TPU v7x, 512 devices: a whole 4x4x16 slice. The times are simulated.
512 devices in a mesh: dp: 16 (over x_lo, y, core), tensor: 32 (over x_hi, z).
Axes of the slice: x: 4 (x_hi: 2, x_lo: 2; x = x_hi * 2 + x_lo), y: 4, z: 16, core: 2. Of those that a mesh axis runs over, the one named last changes fastest.
Arguments:
- queries: bfloat16 [256, 128, 4096], P('dp', None, 'tensor'), may hold values from -6 to 6
- keys_values: bfloat16 [256, 128, 1024], P('dp', 'tensor'), may hold values from -6 to 6
- grad_out: bfloat16 [256, 128, 4096], P('dp', None, 'tensor'), may hold values from -6 to 6
- send_tiles: int32 [16, 16, 2], P('dp'), may hold values from 0 to 15, as said below
- recv_slot: int32 [16, 16], replicated, may hold values from 0 to 31, as said below
- tile_seq: int32 [16, 16], P('dp'), may hold values from 0 to 5, never falling along the last dimension, each value on 1 to 8 neighbouring positions
Outputs:
- grad_queries: bfloat16 [256, 128, 4096], P('dp', None, 'tensor')
- grad_keys_values: bfloat16 [256, 128, 1024], P('dp', 'tensor')
Inputs may be any that keep to these rules, and one draw needn't show every extreme that they name: Every tile of shard s is named by exactly one used slot send_tiles[s, d, c]; slots that no recv_slot entry names hold 0. Which slots are used from shard s to replica d depends only on (s - d) mod 16; used slots of one pair run from c = 0 upward, and some pair uses all 2. recv_slot is consistent with send_tiles: entry s * 2 + c names shard s's slot c towards replica d; each replica's row names distinct slots, and 2 is reached.
All inputs are finite; a program needn't handle non-finite values.
Results may differ from a plain program's by a relative error of at most 0.0072.
Values may be sent and summed in bfloat16 or wider, within the bound.
No kernel may reach another device: no remote copies, remote signals or barrier semaphores. Data moves between devices by JAX's collectives and lax.ppermute only.
A program may use at most 64 MiB of HBM per device.

v0:
```python
import jax
import jax.numpy as jnp
from jax import lax
from jax.sharding import PartitionSpec as P

HD = 128
KV = 4


block_limit = 512


def group_backward(query_rows, grad_rows, key_head, value_head, seq_rows):
    row_count, head_count, head_size = query_rows.shape
    block_size = min(block_limit, row_count)
    block_count = row_count // block_size
    scaling = head_size ** (-0.5)
    positions = jnp.arange(row_count)
    query_blocks = query_rows.reshape(block_count, block_size, head_count, head_size)
    grad_blocks = grad_rows.reshape(block_count, block_size, head_count, head_size)
    offsets = jnp.arange(block_count) * block_size

    def advance(totals, inputs):
        query_block, grad_block, offset = inputs
        query_pos = offset + jnp.arange(block_size)
        query_seq = lax.dynamic_slice_in_dim(seq_rows, offset, block_size)
        allowed = (query_seq[:, None] == seq_rows[None, :]) & (
            positions[None, :] <= query_pos[:, None]
        )
        scores = (
            jnp.einsum("bhd,kd->hbk", query_block, key_head, preferred_element_type=jnp.float32)
            * scaling
        )
        scores = jnp.where(allowed[None], scores, -jnp.inf)
        row_peak = jnp.max(scores, axis=-1, keepdims=True)
        weights = jnp.exp(scores - row_peak)
        attn_probs = weights / jnp.sum(weights, axis=-1, keepdims=True)
        probs_low = attn_probs.astype(jnp.bfloat16)
        grad_probs = jnp.einsum(
            "bhd,kd->hbk", grad_block, value_head, preferred_element_type=jnp.float32
        )
        row_delta = jnp.sum(attn_probs * grad_probs, axis=-1, keepdims=True)
        grad_scores = (attn_probs * (grad_probs - row_delta)).astype(jnp.bfloat16)
        grad_query = (
            jnp.einsum("hbk,kd->bhd", grad_scores, key_head, preferred_element_type=jnp.float32)
            * scaling
        ).astype(jnp.bfloat16)
        grad_key = (
            totals[0]
            + jnp.einsum(
                "hbk,bhd->kd", grad_scores, query_block, preferred_element_type=jnp.float32
            )
            * scaling
        )
        grad_value = totals[1] + jnp.einsum(
            "hbk,bhd->kd", probs_low, grad_block, preferred_element_type=jnp.float32
        )
        return ((grad_key, grad_value), grad_query)

    zeros = jnp.zeros((row_count, head_size), jnp.float32)
    sums, grad_queries = lax.scan(advance, (zeros, zeros), (query_blocks, grad_blocks, offsets))
    return (grad_queries.reshape(row_count, head_count * head_size), sums[0], sums[1])


def on_device(queries, keys_values, grad_out, send_tiles, recv_slot, tile_seq):
    n_replicas = lax.axis_size("dp")
    n_members = lax.axis_size("tensor")
    replica = lax.axis_index("dp")
    member = lax.axis_index("tensor")
    tile_count, tile_rows, row_width = queries.shape
    sliver = keys_values.shape[1]
    slot_cap = send_tiles.shape[2]
    head_count = row_width // HD
    sharers = n_members // KV
    row_count = tile_count * tile_rows
    my_send = send_tiles[0]
    outgoing = my_send.reshape(-1)
    packed = (
        queries[outgoing].reshape(n_replicas, slot_cap, tile_rows, row_width),
        grad_out[outgoing].reshape(n_replicas, slot_cap, tile_rows, row_width),
        keys_values[outgoing].reshape(n_replicas, slot_cap, sliver, 2 * KV * HD),
    )
    arrived = (
        lax.all_to_all(packed[0], "dp", split_axis=0, concat_axis=0, tiled=True),
        lax.all_to_all(packed[1], "dp", split_axis=0, concat_axis=0, tiled=True),
        lax.all_to_all(packed[2], "dp", split_axis=0, concat_axis=0, tiled=True),
    )
    my_recv = lax.dynamic_index_in_dim(recv_slot, replica, 0, keepdims=False)
    query_here = arrived[0].reshape(n_replicas * slot_cap, tile_rows, row_width)[my_recv]
    grad_here = arrived[1].reshape(n_replicas * slot_cap, tile_rows, row_width)[my_recv]
    kv_here = arrived[2].reshape(n_replicas * slot_cap, sliver, 2 * KV * HD)[my_recv]
    group_index = member // sharers
    gathered = lax.all_gather(kv_here, "tensor", axis=1, tiled=True)
    kv_pair = lax.dynamic_index_in_dim(
        gathered.reshape(tile_count, tile_rows, 2, KV, HD), group_index, 3, keepdims=False
    )
    key_head = kv_pair[:, :, 0].reshape(row_count, HD)
    value_head = kv_pair[:, :, 1].reshape(row_count, HD)
    seq_rows = jnp.repeat(tile_seq[0], tile_rows)
    grad_query, grad_key, grad_value = group_backward(
        query_here.reshape(row_count, head_count, HD),
        grad_here.reshape(row_count, head_count, HD),
        key_head,
        value_head,
        seq_rows,
    )
    grad_terms = jnp.stack([grad_key, grad_value], 1).reshape(tile_count, n_members, sliver, 2, HD)
    collected = lax.all_to_all(grad_terms, "tensor", split_axis=1, concat_axis=1, tiled=True)
    summed = jnp.sum(collected.reshape(tile_count, KV, sharers, sliver, 2, HD), axis=2)
    kv_grad_here = (
        summed.transpose(0, 2, 3, 1, 4)
        .reshape(tile_count, sliver, 2 * KV * HD)
        .astype(jnp.bfloat16)
    )
    query_grad_here = grad_query.reshape(tile_count, tile_rows, row_width)
    flat_slots = jnp.arange(n_replicas * slot_cap)
    slot_hits = my_recv[:, None] == flat_slots[None, :]
    back_index = jnp.sum(jnp.where(slot_hits, jnp.arange(tile_count)[:, None], 0), axis=0)
    outgoing_back = (
        query_grad_here[back_index].reshape(n_replicas, slot_cap, tile_rows, row_width),
        kv_grad_here[back_index].reshape(n_replicas, slot_cap, sliver, 2 * KV * HD),
    )
    returned = (
        lax.all_to_all(outgoing_back[0], "dp", split_axis=0, concat_axis=0, tiled=True),
        lax.all_to_all(outgoing_back[1], "dp", split_axis=0, concat_axis=0, tiled=True),
    )
    own_slots = replica * slot_cap + jnp.arange(slot_cap)
    slot_used = jnp.any(recv_slot[:, None, :] == own_slots[None, :, None], axis=2)
    matched = slot_used[:, :, None] & (my_send[:, :, None] == jnp.arange(tile_count)[None, None, :])
    anchor = jnp.sum(
        jnp.where(matched, flat_slots.reshape(n_replicas, slot_cap)[:, :, None], 0), axis=(0, 1)
    )
    grad_queries = returned[0].reshape(n_replicas * slot_cap, tile_rows, row_width)[anchor]
    grad_keys_values = returned[1].reshape(n_replicas * slot_cap, sliver, 2 * KV * HD)[anchor]
    return (grad_queries, grad_keys_values)


def solution(mesh):
    in_specs = (
        P("dp", None, "tensor"),
        P("dp", "tensor", None),
        P("dp", None, "tensor"),
        P("dp", None, None),
        P(),
        P("dp", None),
    )
    out_specs = (P("dp", None, "tensor"), P("dp", "tensor", None))
    return jax.shard_map(
        on_device, mesh=mesh, in_specs=in_specs, out_specs=out_specs, check_vma=False
    )
```

profile of v0, /device:TPU:1, one launch (start us, length us, event | category | flops | bytes accessed | tf_op | source)
XLA Modules:
  0.0 418.2 jit_solution(18385804675254092831)
XLA Ops:
  8.9 2.4 gather_fusion.2
  11.3 10.2 %all-to-all-start.1 = ((bf16[16,2,4,1024]{3,2,1,0:T(4,128)(2,1)}), bf16[16,2,4,1024]{3,2,1,0:T(4,128)(2,1)S(1)}, u32[]{:S(2)}, u32[]{:S(2)}) async-start(bf16[16,2,4,1024]{3,2,1,0:T(4,128)(2,1)} %bitcast.9), calls=%async_computation.1 | async-start | bytes 524288 | tf_op jit(solution)/shard_map/all_to_all | solution.py:86
  22.2 6.5 %all-to-all-done.1 = bf16[16,2,4,1024]{3,2,1,0:T(4,128)(2,1)S(1)} async-done(((bf16[16,2,4,1024]{3,2,1,0:T(4,128)(2,1)}), bf16[16,2,4,1024]{3,2,1,0:T(4,128)(2,1)S(1)}, u32[]{:S(2)}, u32[]{:S(2)}) %all-to-all-start.1) | async-done | bytes 262176 | tf_op jit(solution)/shard_map/all_to_all | solution.py:86
  31.8 4.4 %all-to-all-start.2 = ((bf16[16,2,128,128]{3,2,1,0:T(8,128)(2,1)}), bf16[16,2,128,128]{3,2,1,0:T(8,128)(2,1)S(1)}, u32[]{:S(2)}, u32[]{:S(2)}) async-start(bf16[16,2,128,128]{3,2,1,0:T(8,128)(2,1)} %bitcast.14), calls=%async_computation.2 | async-start | bytes 2097152 | tf_op jit(solution)/shard_map/all_to_all | solution.py:85
  37.9 15.7 %all-to-all-done.2 = bf16[16,2,128,128]{3,2,1,0:T(8,128)(2,1)S(1)} async-done(((bf16[16,2,128,128]{3,2,1,0:T(8,128)(2,1)}), bf16[16,2,128,128]{3,2,1,0:T(8,128)(2,1)S(1)}, u32[]{:S(2)}, u32[]{:S(2)}) %all-to-all-start.2) | async-done | bytes 1048608 | tf_op jit(solution)/shard_map/all_to_all | solution.py:85
  53.6 4.9 %all-to-all-start = ((bf16[16,2,128,128]{3,2,1,0:T(8,128)(2,1)}), bf16[16,2,128,128]{3,2,1,0:T(8,128)(2,1)}, u32[]{:S(2)}, u32[]{:S(2)}) async-start(bf16[16,2,128,128]{3,2,1,0:T(8,128)(2,1)} %bitcast.3), calls=%async_computation | async-start | bytes 2097152 | tf_op jit(solution)/shard_map/all_to_all | solution.py:84
  60.1 14.5 %all-to-all-done = bf16[16,2,128,128]{3,2,1,0:T(8,128)(2,1)} async-done(((bf16[16,2,128,128]{3,2,1,0:T(8,128)(2,1)}), bf16[16,2,128,128]{3,2,1,0:T(8,128)(2,1)}, u32[]{:S(2)}, u32[]{:S(2)}) %all-to-all-start) | async-done | bytes 1048608 | tf_op jit(solution)/shard_map/all_to_all | solution.py:84
  76.4 108.4 %all-gather.3.cloned.1.call-done = bf16[16,128,1024]{2,0,1:T(8,128)(2,1)} async-done(((bf16[16,4,1024]{2,0,1:T(8,128)(2,1)}), bf16[16,128,1024]{2,0,1:T(8,128)(2,1)}) %all-gather.3.cloned.1.call-update) | async-done | bytes 4194320 | tf_op jit(solution)/shard_map/all_gather | solution.py:93
  184.8 6.6 %copy.45 = bf16[16,128,1024]{1,2,0:T(8,128)(2,1)} copy(bf16[16,128,1024]{2,0,1:T(8,128)(2,1)} %all-gather.3.cloned.1.call-done) | data formatting | bytes 8388608 | tf_op jit(solution)/shard_map/all_gather | solution.py:93
  194.0 2.3 fusion.39
  196.3 72.8 %while.15 = (s32[]{:T(128)}, f32[2048,128]{1,0:T(8,128)S(1)}, f32[2048,128]{1,0:T(8,128)}, bf16[4,512,1,128]{3,1,2,0:T(8,128)(2,1)}, s32[4]{0:T(128)S(1)}, /*ind...) while((s32[]{:T(128)}, f32[2048,128]{1,0:T(8,128)S(1)}, ...), condition=%wide.region_4.5_spmd.clone, body=%wide.region_0.4_spmd.clone.sunk | while | flops 1364589568 | bytes 88262592 | solution.py:61
  199.6 2.4 fusion.67
  202.0 2.0 copy-done.1
  204.7 3.7 convolution_add_fusion.2
  208.4 2.2 fusion.69
  217.8 2.4 fusion.67
  222.9 3.7 convolution_add_fusion.2
  226.6 2.2 fusion.69
  236.0 2.4 fusion.67
  238.4 2.0 copy-done.1
  241.1 3.7 convolution_add_fusion.2
  244.8 2.2 fusion.69
  254.2 2.4 fusion.67
  259.3 3.7 convolution_add_fusion.2
  263.0 2.2 fusion.69
  272.8 7.3 %all-to-all-start.4 = ((f32[16,32,4,2,128]{4,2,0,3,1:T(4,128)}), f32[16,32,4,2,128]{4,2,0,3,1:T(4,128)S(1)}, u32[]{:S(2)}, u32[]{:S(2)}) async-start(f32[16,32,4,2,128]{4,2,0,3,1:T(4,128)} %copy.49), calls=%async_computation.4 | async-start | bytes 4194304 | tf_op jit(solution)/shard_map/all_to_all | solution.py:108
  281.8 87.3 %all-to-all-done.4 = f32[16,32,4,2,128]{4,2,0,3,1:T(4,128)S(1)} async-done(((f32[16,32,4,2,128]{4,2,0,3,1:T(4,128)}), f32[16,32,4,2,128]{4,2,0,3,1:T(4,128)S(1)}, u32[]{:S(2)}, u32[]{:S(2)}) %all-to-all-start.4) | async-done | bytes 2097184 | tf_op jit(solution)/shard_map/all_to_all | solution.py:108
  369.1 13.6 %all-to-all-start.3 = ((bf16[16,2,128,128]{3,2,1,0:T(8,128)(2,1)}), bf16[16,2,128,128]{3,2,1,0:T(8,128)(2,1)}, u32[]{:S(2)}, u32[]{:S(2)}) async-start(bf16[16,2,128,128]{3,2,1,0:T(8,128)(2,1)} %bitcast.140), calls=%async_computation.3 | async-start | bytes 2097152 | tf_op jit(solution)/shard_map/all_to_all | solution.py:124
  384.9 13.7 %all-to-all-done.3 = bf16[16,2,128,128]{3,2,1,0:T(8,128)(2,1)} async-done(((bf16[16,2,128,128]{3,2,1,0:T(8,128)(2,1)}), bf16[16,2,128,128]{3,2,1,0:T(8,128)(2,1)}, u32[]{:S(2)}, u32[]{:S(2)}) %all-to-all-start.3) | async-done | bytes 1048608 | tf_op jit(solution)/shard_map/all_to_all | solution.py:124
  398.6 4.2 %all-to-all-start.5 = ((bf16[16,2,4,1024]{3,2,1,0:T(4,128)(2,1)}), bf16[16,2,4,1024]{3,2,1,0:T(4,128)(2,1)S(1)}, u32[]{:S(2)}, u32[]{:S(2)}) async-start(bf16[16,2,4,1024]{3,2,1,0:T(4,128)(2,1)} %bitcast.32), calls=%async_computation.5 | async-start | bytes 524288 | tf_op jit(solution)/shard_map/all_to_all | solution.py:125
  402.8 2.6 gather_fusion.7
  405.4 4.6 %all-to-all-done.5 = bf16[16,2,4,1024]{3,2,1,0:T(4,128)(2,1)S(1)} async-done(((bf16[16,2,4,1024]{3,2,1,0:T(4,128)(2,1)}), bf16[16,2,4,1024]{3,2,1,0:T(4,128)(2,1)S(1)}, u32[]{:S(2)}, u32[]{:S(2)}) %all-to-all-start.5) | async-done | bytes 262176 | tf_op jit(solution)/shard_map/all_to_all | solution.py:125
  (129 shorter events, 49.6 us)
Async XLA Ops:
  7.2 23.0 %copy-start = (bf16[16,128,128]{2,1,0:T(8,128)(2,1)S(1)}, bf16[16,128,128]{2,1,0:T(8,128)(2,1)}, u32[]{:S(2)}) copy-start(bf16[16,128,128]{2,1,0:T(8,128)(2,1)} %param.10) | copy-start | bytes 1572868
  7.2 29.1 %copy-start.3 = (bf16[16,128,128]{2,1,0:T(8,128)(2,1)S(1)}, bf16[16,128,128]{2,1,0:T(8,128)(2,1)}, u32[]{:S(2)}) copy-start(bf16[16,128,128]{2,1,0:T(8,128)(2,1)} %param.8) | copy-start | bytes 1572868
  11.3 17.4 %all-to-all-start.1 = ((bf16[16,2,4,1024]{3,2,1,0:T(4,128)(2,1)}), bf16[16,2,4,1024]{3,2,1,0:T(4,128)(2,1)S(1)}, u32[]{:S(2)}, u32[]{:S(2)}) async-start(bf16[16,2,4,1024]{3,2,1,0:T(4,128)(2,1)} %bitcast.9), calls=%async_computation.1 | async-start | bytes 524288 | tf_op jit(solution)/shard_map/all_to_all | solution.py:86
  21.5 163.3 %all-gather.3.cloned.1.call-start = ((), (), s32[]{:S(2)}) async-start(), calls=%async_computation.6 | async-start | bytes 4325376 | tf_op jit(solution)/shard_map/all_gather | solution.py:93
  30.1 28.4 %copy-start.9 = (s32[1,16]{1,0:T(1,128)S(1)}, s32[1,16]{1,0:T(1,128)}, u32[]{:S(2)}) copy-start(s32[1,16]{1,0:T(1,128)} %param.13) | copy-start | bytes 196
  31.8 21.7 %all-to-all-start.2 = ((bf16[16,2,128,128]{3,2,1,0:T(8,128)(2,1)}), bf16[16,2,128,128]{3,2,1,0:T(8,128)(2,1)S(1)}, u32[]{:S(2)}, u32[]{:S(2)}) async-start(bf16[16,2,128,128]{3,2,1,0:T(8,128)(2,1)} %bitcast.14), calls=%async_computation.2 | async-start | bytes 2097152 | tf_op jit(solution)/shard_map/all_to_all | solution.py:85
  53.6 20.9 %all-to-all-start = ((bf16[16,2,128,128]{3,2,1,0:T(8,128)(2,1)}), bf16[16,2,128,128]{3,2,1,0:T(8,128)(2,1)}, u32[]{:S(2)}, u32[]{:S(2)}) async-start(bf16[16,2,128,128]{3,2,1,0:T(8,128)(2,1)} %bitcast.3), calls=%async_computation | async-start | bytes 2097152 | tf_op jit(solution)/shard_map/all_to_all | solution.py:84
  199.6 5.1 %copy-start.5 = (f32[2048,128]{1,0:T(8,128)S(1)}, f32[2048,128]{1,0:T(8,128)}, u32[]{:S(2)}) copy-start(f32[2048,128]{1,0:T(8,128)} %get-tuple-element.286) | copy-start | bytes 3145732 | tf_op jit(solution)/shard_map/while
  202.0 2.0 copy-start.1
  204.7 3.7 copy-start.2
  204.7 3.7 copy-start.7
  208.4 2.2 copy-start.6
  217.8 5.1 %copy-start.5 = (f32[2048,128]{1,0:T(8,128)S(1)}, f32[2048,128]{1,0:T(8,128)}, u32[]{:S(2)}) copy-start(f32[2048,128]{1,0:T(8,128)} %get-tuple-element.286) | copy-start | bytes 3145732 | tf_op jit(solution)/shard_map/while
  220.2 2.0 copy-start.1
  222.9 3.7 copy-start.2
  222.9 3.7 copy-start.7
  226.6 2.2 copy-start.6
  236.0 5.1 %copy-start.5 = (f32[2048,128]{1,0:T(8,128)S(1)}, f32[2048,128]{1,0:T(8,128)}, u32[]{:S(2)}) copy-start(f32[2048,128]{1,0:T(8,128)} %get-tuple-element.286) | copy-start | bytes 3145732 | tf_op jit(solution)/shard_map/while
  238.4 2.0 copy-start.1
  241.1 3.7 copy-start.2
  241.1 3.7 copy-start.7
  244.8 2.2 copy-start.6
  254.2 5.1 %copy-start.5 = (f32[2048,128]{1,0:T(8,128)S(1)}, f32[2048,128]{1,0:T(8,128)}, u32[]{:S(2)}) copy-start(f32[2048,128]{1,0:T(8,128)} %get-tuple-element.286) | copy-start | bytes 3145732 | tf_op jit(solution)/shard_map/while
  259.3 3.7 copy-start.2
  259.3 3.7 copy-start.7
  263.0 2.2 copy-start.6
  270.8 9.3 %copy-start.4 = (bf16[4,512,1,128]{3,1,2,0:T(8,128)(2,1)S(1)}, bf16[4,512,1,128]{3,1,2,0:T(8,128)(2,1)}, u32[]{:S(2)}) copy-start(bf16[4,512,1,128]{3,1,2,0:T(8,128)(2,1)} %get-tuple-element.66) | copy-start | bytes 1572868
  272.8 109.9 %copy-start.10 = (s32[16,16]{1,0:T(8,128)S(1)}, s32[16,16]{1,0:T(8,128)}, u32[]{:S(2)}) copy-start(s32[16,16]{1,0:T(8,128)} %param.12) | copy-start | bytes 3076
  272.8 110.1 %copy-start.11 = (s32[1,16,2]{1,2,0:T(2,128)S(1)}, s32[1,16,2]{1,2,0:T(2,128)}, u32[]{:S(2)}) copy-start(s32[1,16,2]{1,2,0:T(2,128)} %param.11) | copy-start | bytes 388
  272.8 96.3 %all-to-all-start.4 = ((f32[16,32,4,2,128]{4,2,0,3,1:T(4,128)}), f32[16,32,4,2,128]{4,2,0,3,1:T(4,128)S(1)}, u32[]{:S(2)}, u32[]{:S(2)}) async-start(f32[16,32,4,2,128]{4,2,0,3,1:T(4,128)} %copy.49), calls=%async_computation.4 | async-start | bytes 4194304 | tf_op jit(solution)/shard_map/all_to_all | solution.py:108
  369.1 29.5 %all-to-all-start.3 = ((bf16[16,2,128,128]{3,2,1,0:T(8,128)(2,1)}), bf16[16,2,128,128]{3,2,1,0:T(8,128)(2,1)}, u32[]{:S(2)}, u32[]{:S(2)}) async-start(bf16[16,2,128,128]{3,2,1,0:T(8,128)(2,1)} %bitcast.140), calls=%async_computation.3 | async-start | bytes 2097152 | tf_op jit(solution)/shard_map/all_to_all | solution.py:124
  398.6 11.4 %all-to-all-start.5 = ((bf16[16,2,4,1024]{3,2,1,0:T(4,128)(2,1)}), bf16[16,2,4,1024]{3,2,1,0:T(4,128)(2,1)S(1)}, u32[]{:S(2)}, u32[]{:S(2)}) async-start(bf16[16,2,4,1024]{3,2,1,0:T(4,128)(2,1)} %bitcast.32), calls=%async_computation.5 | async-start | bytes 524288 | tf_op jit(solution)/shard_map/all_to_all | solution.py:125
  (5 other events, 6.3 us)
Sparse Core Ops, SparseCore 0:
  30.2 154.5 all-gather.2
where the time goes:
time: 423 us; the launch traced here: 418 us
  waiting for transfers between devices  251 us (59%)
  starting transfers between devices  44.7 us (11%)
  local copies, waits for them, and re-layouts  43.5 us (10%)
  matrix products  42.9 us (10%)
  between operations  14.3 us (3%)
  other arithmetic  14 us (3%)
  loops' own time  8.22 us (2%)
    all_gather x1, waiting for transfers between devices, on_device(): gathered = lax.all_gather(kv_here, 'tensor', axis=1, tiled=True)  108 us
    all_to_all x1, waiting for transfers between devices, on_device(): lax.all_to_all(grad_terms, 'tensor', split_axis=1, concat_axis=1, tiled=T...  87.3 us
    all_to_all x1, waiting for transfers between devices, on_device(): lax.all_to_all(packed[1], 'dp', split_axis=0, concat_axis=0, tiled=True)  15.7 us
    dot_general x4, matrix products, advance(): jnp.einsum('hbk,bhd->kd', probs_low, grad_block, preferred_element_type=j...  14.7 us
    all_to_all x1, waiting for transfers between devices, on_device(): lax.all_to_all(packed[0], 'dp', split_axis=0, concat_axis=0, tiled=True)  14.5 us
    all_to_all x1, waiting for transfers between devices, on_device(): lax.all_to_all(outgoing_back[0], 'dp', split_axis=0, concat_axis=0, tiled...  13.7 us
    all_to_all x1, starting transfers between devices, on_device(): lax.all_to_all(outgoing_back[0], 'dp', split_axis=0, concat_axis=0, tiled...  13.6 us
    all_to_all x1, starting transfers between devices, on_device(): lax.all_to_all(packed[2], 'dp', split_axis=0, concat_axis=0, tiled=True)  10.2 us
  transfers between devices with their start and end apart: 7, of which 7 were waited for; matrix products, arithmetic and copies ran while one was open for 3% of the time, Pallas kernels for 0%

commit v1 on v0

v1 whole, which is shorter than its diff:
```python
import functools

import jax
import jax.numpy as jnp
from jax import lax
from jax.experimental import pallas as pl
from jax.experimental.pallas import tpu as pltpu
from jax.sharding import Mesh
from jax.sharding import PartitionSpec as P

HD = 128
KV = 4
PAIR = 2
SCALING = HD ** (-0.5)
LOG2E = 1.4426950408889634
FAR = ("xh", "zh", "zm")


def matmul(a, b, contract):
    return lax.dot_general(a, b, (contract, ((), ())), preferred_element_type=jnp.float32)


def pack_kernel(index_ref, q_ref, g_ref, out_ref):
    def body(slot, _):
        tile = index_ref[slot]
        out_ref[slot, 0] = q_ref[tile]
        out_ref[slot, 1] = g_ref[tile]
        return 0

    lax.fori_loop(0, out_ref.shape[0], body, 0)


def pack(index, queries, grad_out):
    slots = index.shape[0]
    return pl.pallas_call(
        pack_kernel,
        out_shape=jax.ShapeDtypeStruct((slots, 2) + queries.shape[1:], queries.dtype),
        in_specs=[
            pl.BlockSpec(memory_space=pltpu.SMEM),
            pl.BlockSpec(memory_space=pltpu.VMEM),
            pl.BlockSpec(memory_space=pltpu.VMEM),
        ],
        out_specs=pl.BlockSpec(memory_space=pltpu.VMEM),
        compiler_params=pltpu.CompilerParams(vmem_limit_bytes=24 * 2**20),
        name="pack_rows",
    )(index, queries, grad_out)


def attention_kernel(
    recv_ref, start_ref, place_ref, qg_ref, kv0, kv1, kv2, kv3, dq_ref, dkv0, dkv1, dkv2, dkv3,
    k_all, kt_all, v_all, dk_all, dv_all, scores, dprobs, dqt,
):
    blocks = k_all.shape[0]
    width = k_all.shape[1]
    tile_rows = width // PAIR
    part = width // 4
    factor = SCALING * LOG2E

    def stage(block, _):
        for place, ref in enumerate((kv0, kv1, kv2, kv3)):
            rows = slice(place * part, (place + 1) * part)
            key = ref[:, 0, block].astype(jnp.float32).reshape(part, HD)
            value = ref[:, 1, block].astype(jnp.float32).reshape(part, HD)
            k_all[block, rows] = key.astype(jnp.bfloat16)
            v_all[block, rows] = value.astype(jnp.bfloat16)
        kt_all[block] = k_all[block].astype(jnp.float32).T.astype(jnp.bfloat16)
        return 0

    lax.fori_loop(0, blocks, stage, 0)

    row = lax.broadcasted_iota(jnp.int32, (width, 1), 0)
    key_offset = (
        ((row >> 2) & 1) * tile_rows
        + ((row >> 3) & 7) * 16
        + ((place_ref[0] - (row >> 6)) & 3) * 4
        + (row & 3)
    )
    lane = lax.broadcasted_iota(jnp.int32, (1, width), 1)

    def query_block(block, _):
        first = recv_ref[PAIR * block]
        second = recv_ref[PAIR * block + 1]
        query = jnp.concatenate([qg_ref[first, 0], qg_ref[second, 0]], axis=0)
        grad = jnp.concatenate([qg_ref[first, 1], qg_ref[second, 1]], axis=0)
        start_low = start_ref[PAIR * block]
        start_high = start_ref[PAIR * block + 1]
        lowest = start_low // PAIR
        row_start = jnp.where(lane < tile_rows, start_low, start_high) * tile_rows

        def products(other, masked_by_order, peak):
            score = matmul(k_all[other], query, ((1,), (1,)))
            key_pos = key_offset + other * width
            allowed = key_pos >= row_start
            if masked_by_order:
                allowed = allowed & (key_offset <= lane)
            score = jnp.where(allowed, score, -jnp.inf)
            scores[other] = score
            dprobs[other] = matmul(v_all[other], grad, ((1,), (1,)))
            return jnp.maximum(peak, jnp.max(score, axis=0, keepdims=True))

        peak = products(block, True, jnp.full((1, width), -jnp.inf, jnp.float32))
        peak = lax.fori_loop(lowest, block, lambda other, m: products(other, False, m), peak)
        shift = peak * factor

        def sums(other, totals):
            weights = jnp.exp2(scores[other] * factor - shift)
            scores[other] = weights
            return (
                totals[0] + jnp.sum(weights, axis=0, keepdims=True),
                totals[1] + jnp.sum(weights * dprobs[other], axis=0, keepdims=True),
            )

        zeros = jnp.zeros((1, width), jnp.float32)
        total, weighted = lax.fori_loop(lowest, block + 1, sums, (zeros, zeros))
        inverse = 1.0 / total
        delta = weighted * inverse

        def terms(other):
            probs = scores[other] * inverse
            dscores = (probs * (dprobs[other] - delta)).astype(jnp.bfloat16)
            grad_value = matmul(probs.astype(jnp.bfloat16), grad, ((1,), (0,)))
            grad_key = matmul(dscores, query, ((1,), (0,)))
            grad_query = matmul(kt_all[other], dscores, ((1,), (0,)))
            return grad_key, grad_value, grad_query

        grad_key, grad_value, grad_query = terms(block)
        dk_all[block] = grad_key
        dv_all[block] = grad_value
        dqt[...] = grad_query

        def earlier(other, _):
            grad_key, grad_value, grad_query = terms(other)
            dk_all[other] += grad_key
            dv_all[other] += grad_value
            dqt[...] += grad_query
            return 0

        lax.fori_loop(lowest, block, earlier, 0)
        result = (dqt[...] * SCALING).T.astype(jnp.bfloat16)
        dq_ref[first] = result[:tile_rows]
        dq_ref[second] = result[tile_rows:]
        return 0

    lax.fori_loop(0, blocks, query_block, 0)

    def unstage(block, _):
        for place, ref in enumerate((dkv0, dkv1, dkv2, dkv3)):
            rows = slice(place * part, (place + 1) * part)
            shape = (ref.shape[0],) + ref.shape[3:]
            ref[:, 0, block] = (dk_all[block, rows] * SCALING).reshape(shape).astype(jnp.bfloat16)
            ref[:, 1, block] = dv_all[block, rows].reshape(shape).astype(jnp.bfloat16)
        return 0

    lax.fori_loop(0, blocks, unstage, 0)


def attention(my_recv, start, place, qg, kv_parts):
    slots, _, tile_rows, _ = qg.shape
    blocks = my_recv.shape[0] // PAIR
    width = PAIR * tile_rows
    vmem = pl.BlockSpec(memory_space=pltpu.VMEM)
    smem = pl.BlockSpec(memory_space=pltpu.SMEM)
    part = jax.ShapeDtypeStruct(kv_parts[0].shape, jnp.bfloat16)
    return pl.pallas_call(
        attention_kernel,
        out_shape=(jax.ShapeDtypeStruct((slots, tile_rows, HD), jnp.bfloat16),) + (part,) * 4,
        in_specs=[smem, smem, smem] + [vmem] * 5,
        out_specs=(vmem,) * 5,
        scratch_shapes=[
            pltpu.VMEM((blocks, width, HD), jnp.bfloat16),
            pltpu.VMEM((blocks, HD, width), jnp.bfloat16),
            pltpu.VMEM((blocks, width, HD), jnp.bfloat16),
            pltpu.VMEM((blocks, width, HD), jnp.float32),
            pltpu.VMEM((blocks, width, HD), jnp.float32),
            pltpu.VMEM((blocks, width, width), jnp.float32),
            pltpu.VMEM((blocks, width, width), jnp.float32),
            pltpu.VMEM((HD, width), jnp.float32),
        ],
        compiler_params=pltpu.CompilerParams(vmem_limit_bytes=40 * 2**20),
        cost_estimate=pl.CostEstimate(
            flops=2 * 10**9, bytes_accessed=6 * 2**20, transcendentals=2 * 10**6
        ),
        name="attention_backward",
    )(my_recv, start, place, qg, *kv_parts)


def near_shift(values, step):
    size = lax.axis_size("zl")
    return lax.ppermute(values, "zl", [(source, (source + step) % size) for source in range(size)])


def on_device(queries, keys_values, grad_out, send_tiles, recv_slot, tile_seq):
    n_replicas = lax.axis_size("dp")
    replica = lax.axis_index("dp")
    tile_count, tile_rows, row_width = queries.shape
    sliver = keys_values.shape[1]
    slot_cap = send_tiles.shape[2]
    slots = n_replicas * slot_cap
    pairs = tile_count // PAIR
    my_send = send_tiles[0]
    outgoing = my_send.reshape(-1)

    kv_packed = keys_values[outgoing].reshape(n_replicas, slot_cap, sliver, 2 * KV * HD)
    kv_arrived = lax.all_to_all(kv_packed, "dp", split_axis=0, concat_axis=0, tiled=True)
    qg_packed = pack(outgoing, queries, grad_out)
    qg_arrived = lax.all_to_all(
        qg_packed.reshape(n_replicas, slot_cap, 2, tile_rows, row_width),
        "dp", split_axis=0, concat_axis=0, tiled=True,
    ).reshape(slots, 2, tile_rows, row_width)

    my_recv = lax.dynamic_index_in_dim(recv_slot, replica, 0, keepdims=False)
    kv_here = kv_arrived.reshape(slots, sliver, 2 * KV * HD)[my_recv]
    by_head = kv_here.reshape(pairs, PAIR * sliver, 2, KV, HD).transpose(3, 2, 0, 1, 4)
    far_out = jnp.broadcast_to(by_head[:, None], (KV, 2) + by_head.shape[1:]).reshape(
        (2 * KV,) + by_head.shape[1:]
    )
    far_in = lax.all_to_all(far_out, FAR, split_axis=0, concat_axis=0, tiled=True)
    kv_parts = [far_in] + [near_shift(far_in, step) for step in range(1, 4)]

    seq = tile_seq[0]
    start = jnp.sum((seq[None, :] < seq[:, None]).astype(jnp.int32), axis=1)
    place = lax.axis_index("zl").astype(jnp.int32).reshape(1)
    query_back, *dkv_parts = attention(my_recv, start, place, qg_arrived, kv_parts)
    query_returned = lax.all_to_all(
        query_back.reshape(n_replicas, slot_cap, tile_rows, row_width),
        "dp", split_axis=0, concat_axis=0, tiled=True,
    )

    near = [dkv_parts[0]] + [near_shift(dkv_parts[step], -step) for step in range(1, 4)]
    near_sum = sum(term.astype(jnp.float32) for term in near).astype(jnp.bfloat16)
    near_sum, query_returned = lax.optimization_barrier((near_sum, query_returned))
    far = lax.all_to_all(near_sum, FAR, split_axis=0, concat_axis=0, tiled=True)
    far_sum = jnp.sum(
        far.reshape((KV, 2) + far.shape[1:]).astype(jnp.float32), axis=1
    ).astype(jnp.bfloat16)
    kv_grad_here = far_sum.transpose(2, 3, 1, 0, 4).reshape(tile_count, sliver, 2 * KV * HD)

    flat_slots = jnp.arange(slots)
    slot_hits = my_recv[:, None] == flat_slots[None, :]
    back_index = jnp.sum(jnp.where(slot_hits, jnp.arange(tile_count)[:, None], 0), axis=0)
    kv_returned = lax.all_to_all(
        kv_grad_here[back_index].reshape(n_replicas, slot_cap, sliver, 2 * KV * HD),
        "dp", split_axis=0, concat_axis=0, tiled=True,
    )
    own_slots = replica * slot_cap + jnp.arange(slot_cap)
    slot_used = jnp.any(recv_slot[:, None, :] == own_slots[None, :, None], axis=2)
    matched = slot_used[:, :, None] & (my_send[:, :, None] == jnp.arange(tile_count)[None, None, :])
    anchor = jnp.sum(
        jnp.where(matched, flat_slots.reshape(n_replicas, slot_cap)[:, :, None], 0), axis=(0, 1)
    )
    grad_queries = query_returned.reshape(slots, tile_rows, row_width)[anchor]
    grad_keys_values = kv_returned.reshape(slots, sliver, 2 * KV * HD)[anchor]
    return (grad_queries, grad_keys_values)


def solution(mesh):
    names = ("dp",) + FAR + ("zl",)
    fine = Mesh(mesh.devices.reshape(mesh.devices.shape[0], 2, 2, 2, 4), names)
    tensor = FAR + ("zl",)
    in_specs = (
        P("dp", None, tensor),
        P("dp", tensor, None),
        P("dp", None, tensor),
        P("dp", None, None),
        P(),
        P("dp", None),
    )
    out_specs = (P("dp", None, tensor), P("dp", tensor, None))
    return jax.shard_map(
        on_device, mesh=fine, in_specs=in_specs, out_specs=out_specs, check_vma=False
    )
```

time: 423 us -> 185 us (0.44)
  the two profiles are of different devices: /device:TPU:1 before, /device:TPU:32 now
where the time goes in v1:
time: 185 us; the launch traced here: 184 us
  waiting for transfers between devices  94.4 us (51%)
  starting transfers between devices  58.2 us (31%)
  Pallas kernels  16.8 us (9%)
  local copies, waits for them, and re-layouts  11.4 us (6%)
  other arithmetic  2.22 us (1%)
    ppermute x6, waiting for transfers between devices, near_shift(): lax.ppermute(values, 'zl', [(source, (source + step) % size) for source i...  35.2 us
    all_to_all x1, waiting for transfers between devices, on_device(): far = lax.all_to_all(near_sum, FAR, split_axis=0, concat_axis=0, tiled=True)  22.2 us
    all_to_all x1, waiting for transfers between devices, on_device(): lax.all_to_all(far_out, FAR, split_axis=0, concat_axis=0, tiled=True)  20.8 us
    ppermute x6, starting transfers between devices, near_shift(): lax.ppermute(values, 'zl', [(source, (source + step) % size) for source i...  17.3 us
    all_to_all x1, starting transfers between devices, on_device(): lax.all_to_all(far_out, FAR, split_axis=0, concat_axis=0, tiled=True)  16.4 us
    pallas_call x1, Pallas kernels, attention(): pl.pallas_call(attention_kernel, out_shape=(jax.ShapeDtypeStruct((slots,...  14.6 us
    all_to_all x1, waiting for transfers between devices, on_device(): lax.all_to_all(kv_packed, 'dp', split_axis=0, concat_axis=0, tiled=True)  7.34 us
    all_to_all x1, waiting for transfers between devices, on_device(): lax.all_to_all(kv_grad_here[back_index].reshape(n_replicas, slot_cap, sli...  6.62 us
  transfers between devices with their start and end apart: 12, of which 10 were waited for; matrix products, arithmetic and copies ran while one was open for 2% of the time, Pallas kernels for 1%

profile of v1, /device:TPU:32, one launch (start us, length us, event | category | flops | bytes accessed | tf_op | source)
XLA Modules:
  0.0 183.9 jit_solution(4338800138432823146)
XLA Ops:
  0.7 0.9 copy.20
  1.6 1.5 gather_fusion
  3.1 5.5 %all-to-all-start.1 = ((bf16[16,2,4,1024]{3,2,1,0:T(4,128)(2,1)}), bf16[16,2,4,1024]{3,2,1,0:T(4,128)(2,1)S(1)}, u32[]{:S(2)}, u32[]{:S(2)}) async-start(bf16[16,2,4,1024]{3,2,1,0:T(4,128)(2,1)} %bitcast.6), calls=%async_computation.1 | async-start | bytes 524288 | tf_op jit(solution)/shard_map/all_to_all | solution.py:204
  9.3 7.3 %all-to-all-done.1 = bf16[16,2,4,1024]{3,2,1,0:T(4,128)(2,1)S(1)} async-done(((bf16[16,2,4,1024]{3,2,1,0:T(4,128)(2,1)}), bf16[16,2,4,1024]{3,2,1,0:T(4,128)(2,1)S(1)}, u32[]{:S(2)}, u32[]{:S(2)}) %all-to-all-start.1) | async-done | bytes 262176 | tf_op jit(solution)/shard_map/all_to_all | solution.py:204
  17.4 0.8 broadcast_in_dim.22
  18.2 16.4 %all-to-all-start.2 = ((bf16[8,2,8,8,128]{4,3,2,1,0:T(8,128)(2,1)}), bf16[8,2,8,8,128]{4,3,2,1,0:T(8,128)(2,1)S(1)}, u32[]{:S(2)}, u32[]{:S(2)}) async-start(bf16[8,2,8,8,128]{4,3,2,1,0:T(8,128)(2,1)} %bitcast.11), calls=%async_computation.2 | async-start | bytes 524288 | tf_op jit(solution)/shard_map/all_to_all | solution.py:217
  34.6 2.2 %pack_rows.1 = bf16[32,2,128,128]{3,2,1,0:T(8,128)(2,1)} custom-call(s32[32]{0:T(128)S(1)} %reshape_squeeze.5.index_ref, bf16[16,128,128]{2,1,0:T(8,128)(2,1)S(1)} %copy-done.1, bf16[16,128,128]{2,1,0:T(8,128)(2,1)S(1)} %copy-done.2), custom_call_target="tpu_custom_call" | custom-call | tf_op jit(solution)/shard_map/pack_rows/pallas_call | solution.py:35
  36.8 20.8 %all-to-all-done.2.kv0 = bf16[8,2,8,8,128]{4,3,2,1,0:T(8,128)(2,1)S(1)} async-done(((bf16[8,2,8,8,128]{4,3,2,1,0:T(8,128)(2,1)}), bf16[8,2,8,8,128]{4,3,2,1,0:T(8,128)(2,1)S(1)}, u32[]{:S(2)}, u32[]{:S(2)}) %all-to-all-start.2) | async-done | bytes 262176 | tf_op jit(solution)/shard_map/all_to_all | solution.py:217
  57.6 3.8 %all-to-all-start = ((bf16[16,2,2,128,128]{4,3,2,1,0:T(8,128)(2,1)}), bf16[16,2,2,128,128]{4,3,2,1,0:T(8,128)(2,1)S(1)}, u32[]{:S(2)}, u32[]{:S(2)}) async-start(bf16[16,2,2,128,128]{4,3,2,1,0:T(8,128)(2,1)} %bitcast.3), calls=%async_computation | async-start | bytes 4194304 | tf_op jit(solution)/shard_map/all_to_all | solution.py:206
  61.5 3.0 %collective-permute-start = (bf16[8,2,8,8,128]{4,3,2,1,0:T(8,128)(2,1)S(1)}, bf16[8,2,8,8,128]{4,3,2,1,0:T(8,128)(2,1)S(1)}, u32[]{:S(2)}, u32[]{:S(2)}) collective-permute-start(bf16[8,2,8,8,128]{4,3,2,1,0:T(8,128)(2,1)S(1)} %all-to-all-done.2.kv0), channel_id=1, source_target_pairs={{0,1},{1,2},{2,3},{3,0},{4,5},{5,6},{6,7},{7,4},{8,9},{9,10},{10,1... | collective-permute-start | bytes 786440 | tf_op jit(solution)/shard_map/ppermute | solution.py:189
  64.5 1.9 %collective-permute-start.1 = (bf16[8,2,8,8,128]{4,3,2,1,0:T(8,128)(2,1)S(1)}, bf16[8,2,8,8,128]{4,3,2,1,0:T(8,128)(2,1)S(1)}, u32[]{:S(2)}, u32[]{:S(2)}) collective-permute-start(bf16[8,2,8,8,128]{4,3,2,1,0:T(8,128)(2,1)S(1)} %all-to-all-done.2.kv0), channel_id=1, source_target_pairs={{0,2},{1,3},{2,0},{3,1},{4,6},{5,7},{6,4},{7,5},{8,10},{9,11},{10,... | collective-permute-start | bytes 786440 | tf_op jit(solution)/shard_map/ppermute | solution.py:189
  66.4 3.4 %collective-permute-start.2 = (bf16[8,2,8,8,128]{4,3,2,1,0:T(8,128)(2,1)S(1)}, bf16[8,2,8,8,128]{4,3,2,1,0:T(8,128)(2,1)S(1)}, u32[]{:S(2)}, u32[]{:S(2)}) collective-permute-start(bf16[8,2,8,8,128]{4,3,2,1,0:T(8,128)(2,1)S(1)} %all-to-all-done.2.kv0), channel_id=1, source_target_pairs={{0,3},{1,0},{2,1},{3,2},{4,7},{5,4},{6,5},{7,6},{8,11},{9,8},{10,9... | collective-permute-start | bytes 786440 | tf_op jit(solution)/shard_map/ppermute | solution.py:189
  70.0 2.5 %collective-permute-done.kv1 = bf16[8,2,8,8,128]{4,3,2,1,0:T(8,128)(2,1)S(1)} collective-permute-done((bf16[8,2,8,8,128]{4,3,2,1,0:T(8,128)(2,1)S(1)}, bf16[8,2,8,8,128]{4,3,2,1,0:T(8,128)(2,1)S(1)}, u32[]{:S(2)}, u32[]{:S(2)}) %collective-permute-start) | collective-permute-done | bytes 262176 | tf_op jit(solution)/shard_map/ppermute | solution.py:189
  72.5 14.8 %collective-permute-done.1.kv2 = bf16[8,2,8,8,128]{4,3,2,1,0:T(8,128)(2,1)S(1)} collective-permute-done((bf16[8,2,8,8,128]{4,3,2,1,0:T(8,128)(2,1)S(1)}, bf16[8,2,8,8,128]{4,3,2,1,0:T(8,128)(2,1)S(1)}, u32[]{:S(2)}, u32[]{:S(2)}) %collective-permute-start.1) | collective-permute-done | bytes 262176 | tf_op jit(solution)/shard_map/ppermute | solution.py:189
  88.0 2.2 %all-to-all-done = bf16[16,2,2,128,128]{4,3,2,1,0:T(8,128)(2,1)S(1)} async-done(((bf16[16,2,2,128,128]{4,3,2,1,0:T(8,128)(2,1)}), bf16[16,2,2,128,128]{4,3,2,1,0:T(8,128)(2,1)S(1)}, u32[]{:S(2)}, u32[]{:S(2)}) %all-to-all-start) | async-done | bytes 2097184 | tf_op jit(solution)/shard_map/all_to_all | solution.py:206
  90.3 0.9 copy-done.4
  91.2 14.6 %attention_backward.1 = (bf16[32,128,128]{2,1,0:T(8,128)(2,1)}, bf16[8,2,8,8,128]{4,3,2,1,0:T(8,128)(2,1)S(1)}, bf16[8,2,8,8,128]{4,3,2,1,0:T(8,128)(2,1)S(1)}, ...) custom-call(s32[16]{0:T(128)S(1)} %fusion.5.recv_ref, s32[16]{0:T(128)S(1)} %convert_reduce_fusion.start_ref, ...), custom_call_target="tpu_custom_call" | custom-call | flops 2000000000 | bytes 6291456 | tf_op jit(solution)/shard_map/attention_backward/pallas_call | solution.py:164
  107.3 4.8 %all-to-all-start.3 = ((bf16[16,2,128,128]{3,2,1,0:T(8,128)(2,1)}), bf16[16,2,128,128]{3,2,1,0:T(8,128)(2,1)S(1)}, u32[]{:S(2)}, u32[]{:S(2)}) async-start(bf16[16,2,128,128]{3,2,1,0:T(8,128)(2,1)} %bitcast.12), calls=%async_computation.3 | async-start | bytes 2097152 | tf_op jit(solution)/shard_map/all_to_all | solution.py:224
  112.1 3.0 %collective-permute-start.5 = (bf16[8,2,8,8,128]{4,3,2,1,0:T(8,128)(2,1)S(1)}, bf16[8,2,8,8,128]{4,3,2,1,0:T(8,128)(2,1)S(1)}, u32[]{:S(2)}, u32[]{:S(2)}) collective-permute-start(bf16[8,2,8,8,128]{4,3,2,1,0:T(8,128)(2,1)S(1)} %copy-done.8), channel_id=1, source_target_pairs={{0,1},{1,2},{2,3},{3,0},{4,5},{5,6},{6,7},{7,4},{8,9},{9,10},{10,1... | collective-permute-start | bytes 786440 | tf_op jit(solution)/shard_map/ppermute | solution.py:189
  115.1 2.0 %collective-permute-start.4 = (bf16[8,2,8,8,128]{4,3,2,1,0:T(8,128)(2,1)S(1)}, bf16[8,2,8,8,128]{4,3,2,1,0:T(8,128)(2,1)S(1)}, u32[]{:S(2)}, u32[]{:S(2)}) collective-permute-start(bf16[8,2,8,8,128]{4,3,2,1,0:T(8,128)(2,1)S(1)} %copy-done.6), channel_id=1, source_target_pairs={{0,2},{1,3},{2,0},{3,1},{4,6},{5,7},{6,4},{7,5},{8,10},{9,11},{10,... | collective-permute-start | bytes 786440 | tf_op jit(solution)/shard_map/ppermute | solution.py:189
  117.1 3.9 %collective-permute-start.3 = (bf16[8,2,8,8,128]{4,3,2,1,0:T(8,128)(2,1)S(1)}, bf16[8,2,8,8,128]{4,3,2,1,0:T(8,128)(2,1)S(1)}, u32[]{:S(2)}, u32[]{:S(2)}) collective-permute-start(bf16[8,2,8,8,128]{4,3,2,1,0:T(8,128)(2,1)S(1)} %get-tuple-element.10), channel_id=1, source_target_pairs={{0,3},{1,0},{2,1},{3,2},{4,7},{5,4},{6,5},{7,6},{8,11},{9,8},{10,9... | collective-permute-start | bytes 786440 | tf_op jit(solution)/shard_map/ppermute | solution.py:189
  121.1 2.0 %collective-permute-done.5 = bf16[8,2,8,8,128]{4,3,2,1,0:T(8,128)(2,1)S(1)} collective-permute-done((bf16[8,2,8,8,128]{4,3,2,1,0:T(8,128)(2,1)S(1)}, bf16[8,2,8,8,128]{4,3,2,1,0:T(8,128)(2,1)S(1)}, u32[]{:S(2)}, u32[]{:S(2)}) %collective-permute-start.5) | collective-permute-done | bytes 262176 | tf_op jit(solution)/shard_map/ppermute | solution.py:189
  123.1 15.0 %collective-permute-done.4 = bf16[8,2,8,8,128]{4,3,2,1,0:T(8,128)(2,1)S(1)} collective-permute-done((bf16[8,2,8,8,128]{4,3,2,1,0:T(8,128)(2,1)S(1)}, bf16[8,2,8,8,128]{4,3,2,1,0:T(8,128)(2,1)S(1)}, u32[]{:S(2)}, u32[]{:S(2)}) %collective-permute-start.4) | collective-permute-done | bytes 262176 | tf_op jit(solution)/shard_map/ppermute | solution.py:189
  138.1 0.9 collective-permute-done.3
  138.9 0.9 add_convert_fusion
  139.8 5.1 %all-to-all-start.4 = ((bf16[8,2,8,8,128]{4,3,2,1,0:T(8,128)(2,1)}), bf16[8,2,8,8,128]{4,3,2,1,0:T(8,128)(2,1)S(1)}, u32[]{:S(2)}, u32[]{:S(2)}) async-start(bf16[8,2,8,8,128]{4,3,2,1,0:T(8,128)(2,1)} %add_convert_fusion), calls=%async_computation.4 | async-start | bytes 524288 | tf_op jit(solution)/shard_map/all_to_all | solution.py:232
  145.4 22.2 %all-to-all-done.4 = bf16[8,2,8,8,128]{4,3,2,1,0:T(8,128)(2,1)S(1)} async-done(((bf16[8,2,8,8,128]{4,3,2,1,0:T(8,128)(2,1)}), bf16[8,2,8,8,128]{4,3,2,1,0:T(8,128)(2,1)S(1)}, u32[]{:S(2)}, u32[]{:S(2)}) %all-to-all-start.4) | async-done | bytes 262176 | tf_op jit(solution)/shard_map/all_to_all | solution.py:232
  167.7 1.4 gather_fusion.3
  169.2 5.4 %all-to-all-start.5 = ((bf16[16,2,4,1024]{3,2,1,0:T(4,128)(2,1)}), bf16[16,2,4,1024]{3,2,1,0:T(4,128)(2,1)S(1)}, u32[]{:S(2)}, u32[]{:S(2)}) async-start(bf16[16,2,4,1024]{3,2,1,0:T(4,128)(2,1)} %bitcast.21), calls=%async_computation.5 | async-start | bytes 524288 | tf_op jit(solution)/shard_map/all_to_all | solution.py:241
  174.6 1.4 gather_fusion.2
  176.0 6.6 %all-to-all-done.5 = bf16[16,2,4,1024]{3,2,1,0:T(4,128)(2,1)S(1)} async-done(((bf16[16,2,4,1024]{3,2,1,0:T(4,128)(2,1)}), bf16[16,2,4,1024]{3,2,1,0:T(4,128)(2,1)S(1)}, u32[]{:S(2)}, u32[]{:S(2)}) %all-to-all-start.5) | async-done | bytes 262176 | tf_op jit(solution)/shard_map/all_to_all | solution.py:241
  182.6 1.3 gather_fusion.4
  (48 shorter events, 4.6 us)
Async XLA Ops:
  0.6 1.0 copy-start
  0.6 34.0 %copy-start.1 = (bf16[16,128,128]{2,1,0:T(8,128)(2,1)S(1)}, bf16[16,128,128]{2,1,0:T(8,128)(2,1)}, u32[]{:S(2)}) copy-start(bf16[16,128,128]{2,1,0:T(8,128)(2,1)} %q_ref.1) | copy-start | bytes 1572868
  0.7 34.0 %copy-start.2 = (bf16[16,128,128]{2,1,0:T(8,128)(2,1)S(1)}, bf16[16,128,128]{2,1,0:T(8,128)(2,1)}, u32[]{:S(2)}) copy-start(bf16[16,128,128]{2,1,0:T(8,128)(2,1)} %g_ref.1) | copy-start | bytes 1572868
  3.1 13.6 %all-to-all-start.1 = ((bf16[16,2,4,1024]{3,2,1,0:T(4,128)(2,1)}), bf16[16,2,4,1024]{3,2,1,0:T(4,128)(2,1)S(1)}, u32[]{:S(2)}, u32[]{:S(2)}) async-start(bf16[16,2,4,1024]{3,2,1,0:T(4,128)(2,1)} %bitcast.6), calls=%async_computation.1 | async-start | bytes 524288 | tf_op jit(solution)/shard_map/all_to_all | solution.py:204
  18.2 39.4 %all-to-all-start.2 = ((bf16[8,2,8,8,128]{4,3,2,1,0:T(8,128)(2,1)}), bf16[8,2,8,8,128]{4,3,2,1,0:T(8,128)(2,1)S(1)}, u32[]{:S(2)}, u32[]{:S(2)}) async-start(bf16[8,2,8,8,128]{4,3,2,1,0:T(8,128)(2,1)} %bitcast.11), calls=%async_computation.2 | async-start | bytes 524288 | tf_op jit(solution)/shard_map/all_to_all | solution.py:217
  57.6 12.2 %copy-start.9 = (s32[16,16]{1,0:T(8,128)S(1)}, s32[16,16]{1,0:T(8,128)}, u32[]{:S(2)}) copy-start(s32[16,16]{1,0:T(8,128)} %param.10) | copy-start | bytes 3076
  57.6 12.2 %copy-start.11 = (s32[1,16]{1,0:T(1,128)S(1)}, s32[1,16]{1,0:T(1,128)}, u32[]{:S(2)}) copy-start(s32[1,16]{1,0:T(1,128)} %param.11) | copy-start | bytes 196
  57.6 32.7 %all-to-all-start = ((bf16[16,2,2,128,128]{4,3,2,1,0:T(8,128)(2,1)}), bf16[16,2,2,128,128]{4,3,2,1,0:T(8,128)(2,1)S(1)}, u32[]{:S(2)}, u32[]{:S(2)}) async-start(bf16[16,2,2,128,128]{4,3,2,1,0:T(8,128)(2,1)} %bitcast.3), calls=%async_computation | async-start | bytes 4194304 | tf_op jit(solution)/shard_map/all_to_all | solution.py:206
  61.5 11.0 %collective-permute-start = (bf16[8,2,8,8,128]{4,3,2,1,0:T(8,128)(2,1)S(1)}, bf16[8,2,8,8,128]{4,3,2,1,0:T(8,128)(2,1)S(1)}, u32[]{:S(2)}, u32[]{:S(2)}) collective-permute-start(bf16[8,2,8,8,128]{4,3,2,1,0:T(8,128)(2,1)S(1)} %all-to-all-done.2.kv0), channel_id=1, source_target_pairs={{0,1},{1,2},{2,3},{3,0},{4,5},{5,6},{6,7},{7,4},{8,9},{9,10},{10,1... | collective-permute-start | bytes 786440 | tf_op jit(solution)/shard_map/ppermute | solution.py:189
  64.5 22.8 %collective-permute-start.1 = (bf16[8,2,8,8,128]{4,3,2,1,0:T(8,128)(2,1)S(1)}, bf16[8,2,8,8,128]{4,3,2,1,0:T(8,128)(2,1)S(1)}, u32[]{:S(2)}, u32[]{:S(2)}) collective-permute-start(bf16[8,2,8,8,128]{4,3,2,1,0:T(8,128)(2,1)S(1)} %all-to-all-done.2.kv0), channel_id=1, source_target_pairs={{0,2},{1,3},{2,0},{3,1},{4,6},{5,7},{6,4},{7,5},{8,10},{9,11},{10,... | collective-permute-start | bytes 786440 | tf_op jit(solution)/shard_map/ppermute | solution.py:189
  66.4 20.9 %collective-permute-start.2 = (bf16[8,2,8,8,128]{4,3,2,1,0:T(8,128)(2,1)S(1)}, bf16[8,2,8,8,128]{4,3,2,1,0:T(8,128)(2,1)S(1)}, u32[]{:S(2)}, u32[]{:S(2)}) collective-permute-start(bf16[8,2,8,8,128]{4,3,2,1,0:T(8,128)(2,1)S(1)} %all-to-all-done.2.kv0), channel_id=1, source_target_pairs={{0,3},{1,0},{2,1},{3,2},{4,7},{5,4},{6,5},{7,6},{8,11},{9,8},{10,9... | collective-permute-start | bytes 786440 | tf_op jit(solution)/shard_map/ppermute | solution.py:189
  87.3 0.7 copy-start.3
  90.3 1.0 copy-start.4
  105.8 0.7 copy-start.5
  106.6 0.7 copy-start.7
  107.3 38.0 %copy-start.10 = (s32[1,16,2]{1,2,0:T(2,128)S(1)}, s32[1,16,2]{1,2,0:T(2,128)}, u32[]{:S(2)}) copy-start(s32[1,16,2]{1,2,0:T(2,128)} %param.9) | copy-start | bytes 388
  107.3 4.8 %copy-start.8 = (bf16[8,2,8,8,128]{4,3,2,1,0:T(8,128)(2,1)S(1)}, bf16[8,2,8,8,128]{4,3,2,1,0:T(8,128)(2,1)}, u32[]{:S(2)}) copy-start(bf16[8,2,8,8,128]{4,3,2,1,0:T(8,128)(2,1)} %copy-done.7) | copy-start | bytes 786436
  107.3 7.8 %copy-start.6 = (bf16[8,2,8,8,128]{4,3,2,1,0:T(8,128)(2,1)S(1)}, bf16[8,2,8,8,128]{4,3,2,1,0:T(8,128)(2,1)}, u32[]{:S(2)}) copy-start(bf16[8,2,8,8,128]{4,3,2,1,0:T(8,128)(2,1)} %copy-done.5) | copy-start | bytes 786436
  107.3 32.6 %all-to-all-start.3 = ((bf16[16,2,128,128]{3,2,1,0:T(8,128)(2,1)}), bf16[16,2,128,128]{3,2,1,0:T(8,128)(2,1)S(1)}, u32[]{:S(2)}, u32[]{:S(2)}) async-start(bf16[16,2,128,128]{3,2,1,0:T(8,128)(2,1)} %bitcast.12), calls=%async_computation.3 | async-start | bytes 2097152 | tf_op jit(solution)/shard_map/all_to_all | solution.py:224
  112.1 11.0 %collective-permute-start.5 = (bf16[8,2,8,8,128]{4,3,2,1,0:T(8,128)(2,1)S(1)}, bf16[8,2,8,8,128]{4,3,2,1,0:T(8,128)(2,1)S(1)}, u32[]{:S(2)}, u32[]{:S(2)}) collective-permute-start(bf16[8,2,8,8,128]{4,3,2,1,0:T(8,128)(2,1)S(1)} %copy-done.8), channel_id=1, source_target_pairs={{0,1},{1,2},{2,3},{3,0},{4,5},{5,6},{6,7},{7,4},{8,9},{9,10},{10,1... | collective-permute-start | bytes 786440 | tf_op jit(solution)/shard_map/ppermute | solution.py:189
  115.1 23.0 %collective-permute-start.4 = (bf16[8,2,8,8,128]{4,3,2,1,0:T(8,128)(2,1)S(1)}, bf16[8,2,8,8,128]{4,3,2,1,0:T(8,128)(2,1)S(1)}, u32[]{:S(2)}, u32[]{:S(2)}) collective-permute-start(bf16[8,2,8,8,128]{4,3,2,1,0:T(8,128)(2,1)S(1)} %copy-done.6), channel_id=1, source_target_pairs={{0,2},{1,3},{2,0},{3,1},{4,6},{5,7},{6,4},{7,5},{8,10},{9,11},{10,... | collective-permute-start | bytes 786440 | tf_op jit(solution)/shard_map/ppermute | solution.py:189
  117.1 21.8 %collective-permute-start.3 = (bf16[8,2,8,8,128]{4,3,2,1,0:T(8,128)(2,1)S(1)}, bf16[8,2,8,8,128]{4,3,2,1,0:T(8,128)(2,1)S(1)}, u32[]{:S(2)}, u32[]{:S(2)}) collective-permute-start(bf16[8,2,8,8,128]{4,3,2,1,0:T(8,128)(2,1)S(1)} %get-tuple-element.10), channel_id=1, source_target_pairs={{0,3},{1,0},{2,1},{3,2},{4,7},{5,4},{6,5},{7,6},{8,11},{9,8},{10,9... | collective-permute-start | bytes 786440 | tf_op jit(solution)/shard_map/ppermute | solution.py:189
  139.8 27.7 %all-to-all-start.4 = ((bf16[8,2,8,8,128]{4,3,2,1,0:T(8,128)(2,1)}), bf16[8,2,8,8,128]{4,3,2,1,0:T(8,128)(2,1)S(1)}, u32[]{:S(2)}, u32[]{:S(2)}) async-start(bf16[8,2,8,8,128]{4,3,2,1,0:T(8,128)(2,1)} %add_convert_fusion), calls=%async_computation.4 | async-start | bytes 524288 | tf_op jit(solution)/shard_map/all_to_all | solution.py:232
  169.2 13.4 %all-to-all-start.5 = ((bf16[16,2,4,1024]{3,2,1,0:T(4,128)(2,1)}), bf16[16,2,4,1024]{3,2,1,0:T(4,128)(2,1)S(1)}, u32[]{:S(2)}, u32[]{:S(2)}) async-start(bf16[16,2,4,1024]{3,2,1,0:T(4,128)(2,1)} %bitcast.21), calls=%async_computation.5 | async-start | bytes 524288 | tf_op jit(solution)/shard_map/all_to_all | solution.py:241

commit v2 on v1

--- a/solution.py
+++ b/solution.py
@@ -13,7 +13,9 @@
 PAIR = 2
 SCALING = HD ** (-0.5)
 LOG2E = 1.4426950408889634
-FAR = ("xh", "zh", "zm")
+PLANE = ("dp", "xh")
+COLUMN = ("zh", "zm", "zl")
+LINE = ("zm", "zl")
 
 
 def matmul(a, b, contract):
@@ -22,7 +24,7 @@
 
 def pack_kernel(index_ref, q_ref, g_ref, out_ref):
     def body(slot, _):
-        tile = index_ref[slot]
+        tile = index_ref[slot & 1, slot >> 1]
         out_ref[slot, 0] = q_ref[tile]
         out_ref[slot, 1] = g_ref[tile]
         return 0
@@ -31,7 +33,7 @@
 
 
 def pack(index, queries, grad_out):
-    slots = index.shape[0]
+    slots = index.size
     return pl.pallas_call(
         pack_kernel,
         out_shape=jax.ShapeDtypeStruct((slots, 2) + queries.shape[1:], queries.dtype),
@@ -47,33 +49,28 @@
 
 
 def attention_kernel(
-    recv_ref, start_ref, place_ref, qg_ref, kv0, kv1, kv2, kv3, dq_ref, dkv0, dkv1, dkv2, dkv3,
+    recv_ref, start_ref, place_ref, qg_ref, kv_ref, dq_ref, dkv_ref,
     k_all, kt_all, v_all, dk_all, dv_all, scores, dprobs, dqt,
 ):
     blocks = k_all.shape[0]
     width = k_all.shape[1]
     tile_rows = width // PAIR
-    part = width // 4
     factor = SCALING * LOG2E
 
     def stage(block, _):
-        for place, ref in enumerate((kv0, kv1, kv2, kv3)):
-            rows = slice(place * part, (place + 1) * part)
-            key = ref[:, 0, block].astype(jnp.float32).reshape(part, HD)
-            value = ref[:, 1, block].astype(jnp.float32).reshape(part, HD)
-            k_all[block, rows] = key.astype(jnp.bfloat16)
-            v_all[block, rows] = value.astype(jnp.bfloat16)
-        kt_all[block] = k_all[block].astype(jnp.float32).T.astype(jnp.bfloat16)
+        key = kv_ref[:, :, :, 0, block].astype(jnp.float32).reshape(width, HD)
+        value = kv_ref[:, :, :, 1, block].astype(jnp.float32).reshape(width, HD)
+        k_all[block] = key.astype(jnp.bfloat16)
+        v_all[block] = value.astype(jnp.bfloat16)
+        kt_all[block] = key.T.astype(jnp.bfloat16)
         return 0
 
     lax.fori_loop(0, blocks, stage, 0)
 
     row = lax.broadcasted_iota(jnp.int32, (width, 1), 0)
+    source = ((place_ref[0] & 8) | (row >> 5)) ^ (((row >> 4) & 1) * 15)
     key_offset = (
-        ((row >> 2) & 1) * tile_rows
-        + ((row >> 3) & 7) * 16
-        + ((place_ref[0] - (row >> 6)) & 3) * 4
-        + (row & 3)
+        ((row >> 2) & 1) * tile_rows + ((row >> 3) & 1) * 64 + source * 4 + (row & 3)
     )
     lane = lax.broadcasted_iota(jnp.int32, (1, width), 1)
 
@@ -144,28 +141,28 @@
     lax.fori_loop(0, blocks, query_block, 0)
 
     def unstage(block, _):
-        for place, ref in enumerate((dkv0, dkv1, dkv2, dkv3)):
-            rows = slice(place * part, (place + 1) * part)
-            shape = (ref.shape[0],) + ref.shape[3:]
-            ref[:, 0, block] = (dk_all[block, rows] * SCALING).reshape(shape).astype(jnp.bfloat16)
-            ref[:, 1, block] = dv_all[block, rows].reshape(shape).astype(jnp.bfloat16)
+        shape = kv_ref.shape[:3] + kv_ref.shape[5:]
+        dkv_ref[:, :, :, 0, block] = (dk_all[block] * SCALING).reshape(shape).astype(jnp.bfloat16)
+        dkv_ref[:, :, :, 1, block] = dv_all[block].reshape(shape).astype(jnp.bfloat16)
         return 0
 
     lax.fori_loop(0, blocks, unstage, 0)
 
 
-def attention(my_recv, start, place, qg, kv_parts):
+def attention(my_recv, start, place, qg, kv):
     slots, _, tile_rows, _ = qg.shape
     blocks = my_recv.shape[0] // PAIR
     width = PAIR * tile_rows
     vmem = pl.BlockSpec(memory_space=pltpu.VMEM)
     smem = pl.BlockSpec(memory_space=pltpu.SMEM)
-    part = jax.ShapeDtypeStruct(kv_parts[0].shape, jnp.bfloat16)
     return pl.pallas_call(
         attention_kernel,
-        out_shape=(jax.ShapeDtypeStruct((slots, tile_rows, HD), jnp.bfloat16),) + (part,) * 4,
-        in_specs=[smem, smem, smem] + [vmem] * 5,
-        out_specs=(vmem,) * 5,
+        out_shape=(
+            jax.ShapeDtypeStruct((slots, tile_rows, HD), jnp.bfloat16),
+            jax.ShapeDtypeStruct(kv.shape, jnp.bfloat16),
+        ),
+        in_specs=[smem, smem, smem, vmem, vmem],
+        out_specs=(vmem, vmem),
         scratch_shapes=[
             pltpu.VMEM((blocks, width, HD), jnp.bfloat16),
             pltpu.VMEM((blocks, HD, width), jnp.bfloat16),
@@ -176,17 +173,90 @@
             pltpu.VMEM((blocks, width, width), jnp.float32),
             pltpu.VMEM((HD, width), jnp.float32),
         ],
-        compiler_params=pltpu.CompilerParams(vmem_limit_bytes=40 * 2**20),
+        compiler_params=pltpu.CompilerParams(vmem_limit_bytes=24 * 2**20),
         cost_estimate=pl.CostEstimate(
             flops=2 * 10**9, bytes_accessed=6 * 2**20, transcendentals=2 * 10**6
         ),
         name="attention_backward",
-    )(my_recv, start, place, qg, *kv_parts)
-
-
-def near_shift(values, step):
-    size = lax.axis_size("zl")
-    return lax.ppermute(values, "zl", [(source, (source + step) % size) for source in range(size)])
+    )(my_recv, start, place, qg, kv)
+
+
+def kv_pack_kernel(index_ref, kv_ref, out_ref):
+    def body(slot, _):
+        tile = index_ref[slot & 1, slot >> 1]
+        piece = kv_ref[tile].reshape((2, 2, 2) + kv_ref.shape[2:])
+        for half in range(2):
+            out_ref[slot >> 1, half, slot & 1] = piece[:, half]
+        return 0
+
+    lax.fori_loop(0, 2 * index_ref.shape[1], body, 0, unroll=4)
+
+
+def kv_unpack_kernel(recv_ref, place_ref, kv_ref, own_ref, other_ref):
+    head = place_ref[0] >> 3
+
+    def body(pair, _):
+        low = recv_ref[PAIR * pair]
+        high = recv_ref[PAIR * pair + 1]
+        for half in range(2):
+            for kind in range(2):
+                for ref, which in ((own_ref, head), (other_ref, 1 - head)):
+                    rows = [
+                        kv_ref[slot >> 1, half, slot & 1, kind, which].astype(jnp.float32)
+                        for slot in (low, high)
+                    ]
+                    ref[half, kind, pair] = jnp.concatenate(rows, axis=0).astype(jnp.bfloat16)
+        return 0
+
+    lax.fori_loop(0, recv_ref.shape[0] // PAIR, body, 0)
+
+
+def kv_back_kernel(recv_ref, place_ref, own_ref, other_ref, out_ref):
+    head = place_ref[0] >> 3
+    sliver = out_ref.shape[-2]
+
+    def body(pair, _):
+        slots = (recv_ref[PAIR * pair], recv_ref[PAIR * pair + 1])
+        for half in range(2):
+            for kind in range(2):
+                for ref, which in ((own_ref, head), (other_ref, 1 - head)):
+                    total = ref[half, kind, pair].astype(jnp.float32)
+                    for order, slot in enumerate(slots):
+                        rows = total[order * sliver : (order + 1) * sliver]
+                        out_ref[slot >> 1, half, slot & 1, kind, which] = rows.astype(jnp.bfloat16)
+        return 0
+
+    lax.fori_loop(0, recv_ref.shape[0] // PAIR, body, 0)
+
+
+def kv_final_kernel(anchor_ref, kv_ref, out_ref):
+    def body(tile, _):
+        slot = anchor_ref[tile]
+        piece = kv_ref[slot >> 1, :, slot & 1]
+        for half in range(2):
+            for kind in range(2):
+                for head in range(2):
+                    out_ref[tile, kind * 4 + half * 2 + head] = piece[half, kind, head]
+        return 0
+
+    lax.fori_loop(0, anchor_ref.shape[0], body, 0)
+
+
+def local_call(kernel, name, scalars, arrays, out_shape):
+    vmem = pl.BlockSpec(memory_space=pltpu.VMEM)
+    smem = pl.BlockSpec(memory_space=pltpu.SMEM)
+    return pl.pallas_call(
+        kernel,
+        out_shape=out_shape,
+        in_specs=[smem] * len(scalars) + [vmem] * len(arrays),
+        out_specs=jax.tree.map(lambda _: vmem, out_shape),
+        compiler_params=pltpu.CompilerParams(vmem_limit_bytes=16 * 2**20),
+        name=name,
+    )(*scalars, *arrays)
+
+
+def mirror(values):
+    return lax.ppermute(values, COLUMN, [(source, 15 - source) for source in range(16)])
 
 
 def on_device(queries, keys_values, grad_out, send_tiles, recv_slot, tile_seq):
@@ -198,50 +268,52 @@
     slots = n_replicas * slot_cap
     pairs = tile_count // PAIR
     my_send = send_tiles[0]
-    outgoing = my_send.reshape(-1)
-
-    kv_packed = keys_values[outgoing].reshape(n_replicas, slot_cap, sliver, 2 * KV * HD)
-    kv_arrived = lax.all_to_all(kv_packed, "dp", split_axis=0, concat_axis=0, tiled=True)
+    outgoing = my_send.T
+    my_recv = lax.dynamic_index_in_dim(recv_slot, replica, 0, keepdims=False)
+    place = lax.axis_index(COLUMN).astype(jnp.int32).reshape(1)
+    traveling = jax.ShapeDtypeStruct(
+        (n_replicas, 2, slot_cap, 2, 2, sliver, HD), keys_values.dtype
+    )
+    half_shape = jax.ShapeDtypeStruct((2, 2, pairs, PAIR * sliver, HD), keys_values.dtype)
+
+    def over_plane(values):
+        return lax.all_to_all(
+            values.reshape((2 * n_replicas,) + values.shape[2:]),
+            PLANE, split_axis=0, concat_axis=0, tiled=True,
+        ).reshape(values.shape)
+
+    kv_blocks = keys_values.reshape(tile_count, sliver, 2 * KV, HD).transpose(0, 2, 1, 3)
+    kv_arrived = over_plane(
+        local_call(kv_pack_kernel, "kv_pack", [outgoing], [kv_blocks], traveling)
+    )
+    own, other = local_call(
+        kv_unpack_kernel, "kv_unpack", [my_recv, place], [kv_arrived], (half_shape, half_shape)
+    )
     qg_packed = pack(outgoing, queries, grad_out)
+    mirrored = mirror(other)
+    qg_packed, mirrored = lax.optimization_barrier((qg_packed, mirrored))
     qg_arrived = lax.all_to_all(
         qg_packed.reshape(n_replicas, slot_cap, 2, tile_rows, row_width),
         "dp", split_axis=0, concat_axis=0, tiled=True,
     ).reshape(slots, 2, tile_rows, row_width)
-
-    my_recv = lax.dynamic_index_in_dim(recv_slot, replica, 0, keepdims=False)
-    kv_here = kv_arrived.reshape(slots, sliver, 2 * KV * HD)[my_recv]
-    by_head = kv_here.reshape(pairs, PAIR * sliver, 2, KV, HD).transpose(3, 2, 0, 1, 4)
-    far_out = jnp.broadcast_to(by_head[:, None], (KV, 2) + by_head.shape[1:]).reshape(
-        (2 * KV,) + by_head.shape[1:]
-    )
-    far_in = lax.all_to_all(far_out, FAR, split_axis=0, concat_axis=0, tiled=True)
-    kv_parts = [far_in] + [near_shift(far_in, step) for step in range(1, 4)]
+    kv_all = lax.all_gather(jnp.stack([own, mirrored]), LINE)
 
     seq = tile_seq[0]
     start = jnp.sum((seq[None, :] < seq[:, None]).astype(jnp.int32), axis=1)
-    place = lax.axis_index("zl").astype(jnp.int32).reshape(1)
-    query_back, *dkv_parts = attention(my_recv, start, place, qg_arrived, kv_parts)
+    query_back, dkv = attention(my_recv, start, place, qg_arrived, kv_all)
     query_returned = lax.all_to_all(
         query_back.reshape(n_replicas, slot_cap, tile_rows, row_width),
         "dp", split_axis=0, concat_axis=0, tiled=True,
     )
 
-    near = [dkv_parts[0]] + [near_shift(dkv_parts[step], -step) for step in range(1, 4)]
-    near_sum = sum(term.astype(jnp.float32) for term in near).astype(jnp.bfloat16)
-    near_sum, query_returned = lax.optimization_barrier((near_sum, query_returned))
-    far = lax.all_to_all(near_sum, FAR, split_axis=0, concat_axis=0, tiled=True)
-    far_sum = jnp.sum(
-        far.reshape((KV, 2) + far.shape[1:]).astype(jnp.float32), axis=1
-    ).astype(jnp.bfloat16)
-    kv_grad_here = far_sum.transpose(2, 3, 1, 0, 4).reshape(tile_count, sliver, 2 * KV * HD)
+    summed = lax.psum_scatter(dkv, LINE, scatter_dimension=0)
+    summed, query_returned = lax.optimization_barrier((summed, query_returned))
+    swapped = [summed[0], mirror(summed[1])]
+    kv_returned = over_plane(
+        local_call(kv_back_kernel, "kv_back", [my_recv, place], swapped, traveling)
+    )
 
     flat_slots = jnp.arange(slots)
-    slot_hits = my_recv[:, None] == flat_slots[None, :]
-    back_index = jnp.sum(jnp.where(slot_hits, jnp.arange(tile_count)[:, None], 0), axis=0)
-    kv_returned = lax.all_to_all(
-        kv_grad_here[back_index].reshape(n_replicas, slot_cap, sliver, 2 * KV * HD),
-        "dp", split_axis=0, concat_axis=0, tiled=True,
-    )
     own_slots = replica * slot_cap + jnp.arange(slot_cap)
     slot_used = jnp.any(recv_slot[:, None, :] == own_slots[None, :, None], axis=2)
     matched = slot_used[:, :, None] & (my_send[:, :, None] == jnp.arange(tile_count)[None, None, :])
@@ -249,14 +321,18 @@
         jnp.where(matched, flat_slots.reshape(n_replicas, slot_cap)[:, :, None], 0), axis=(0, 1)
     )
     grad_queries = query_returned.reshape(slots, tile_rows, row_width)[anchor]
-    grad_keys_values = kv_returned.reshape(slots, sliver, 2 * KV * HD)[anchor]
+    kv_final = local_call(
+        kv_final_kernel, "kv_final", [anchor], [kv_returned],
+        jax.ShapeDtypeStruct(kv_blocks.shape, keys_values.dtype),
+    )
+    grad_keys_values = kv_final.transpose(0, 2, 1, 3).reshape(keys_values.shape)
     return (grad_queries, grad_keys_values)
 
 
 def solution(mesh):
-    names = ("dp",) + FAR + ("zl",)
+    names = PLANE + COLUMN
     fine = Mesh(mesh.devices.reshape(mesh.devices.shape[0], 2, 2, 2, 4), names)
-    tensor = FAR + ("zl",)
+    tensor = ("xh",) + COLUMN
     in_specs = (
         P("dp", None, tensor),
         P("dp", tensor, None),

time: 185 us -> 231 us (1.25)
  the two profiles are of different devices: /device:TPU:32 before, /device:TPU:1 now
where the time goes in v2:
time: 231 us
  waiting for transfers between devices  129 us (56%)
  starting transfers between devices  58.2 us (25%)
  Pallas kernels  19.3 us (8%)
  between operations  14.2 us (6%)
  local copies, waits for them, and re-layouts  8.55 us (4%)
    all_gather x1, waiting for transfers between devices, on_device(): kv_all = lax.all_gather(jnp.stack([own, mirrored]), LINE)  59.8 us
    reduce_scatter x1, waiting for transfers between devices, on_device(): summed = lax.psum_scatter(dkv, LINE, scatter_dimension=0)  34.5 us
    all_to_all x2, starting transfers between devices, over_plane(): lax.all_to_all(values.reshape((2 * n_replicas,) + values.shape[2:]), PLAN...  25.3 us
    all_to_all x1, waiting for transfers between devices, on_device(): lax.all_to_all(query_back.reshape(n_replicas, slot_cap, tile_rows, row_wi...  15.7 us
    all_to_all x2, waiting for transfers between devices, over_plane(): lax.all_to_all(values.reshape((2 * n_replicas,) + values.shape[2:]), PLAN...  15.6 us
    all_to_all x1, starting transfers between devices, on_device(): lax.all_to_all(query_back.reshape(n_replicas, slot_cap, tile_rows, row_wi...  14.2 us
    ppermute x2, starting transfers between devices, mirror(): lax.ppermute(values, COLUMN, [(source, 15 - source) for source in range(1...  14.1 us
    pallas_call x1, Pallas kernels, attention(): pl.pallas_call(attention_kernel, out_shape=(jax.ShapeDtypeStruct((slots,...  12.2 us
  transfers between devices with their start and end apart: 8, of which 7 were waited for; matrix products, arithmetic and copies ran while one was open for 1% of the time, Pallas kernels for 1%

profile of v2, /device:TPU:1, one launch (start us, length us, event | category | flops | bytes accessed | tf_op | source)
XLA Modules:
  0.0 230.6 jit_solution(4065314356769311822)
XLA Ops:
  7.2 0.9 copy-done.2
  8.1 0.7 copy-done.3
  8.7 1.4 kv_pack.1
  10.2 10.4 %all-to-all-start = ((bf16[32,2,2,2,4,128]{5,4,3,2,1,0:T(4,128)(2,1)}), bf16[32,2,2,2,4,128]{5,4,3,2,1,0:T(4,128)(2,1)S(1)}, u32[]{:S(2)}, u32[]{:S(2)}) async-start(bf16[32,2,2,2,4,128]{5,4,3,2,1,0:T(4,128)(2,1)} %bitcast.8), calls=%async_computation | async-start | bytes 524288 | tf_op jit(solution)/shard_map/all_to_all | solution.py:280
  20.6 0.7 dynamic-slice_bitcast_fusion.recv_ref
  21.3 8.2 %all-to-all-done = bf16[32,2,2,2,4,128]{5,4,3,2,1,0:T(4,128)(2,1)S(1)} async-done(((bf16[32,2,2,2,4,128]{5,4,3,2,1,0:T(4,128)(2,1)}), bf16[32,2,2,2,4,128]{5,4,3,2,1,0:T(4,128)(2,1)S(1)}, u32[]{:S(2)}, u32[]{:S(2)}) %all-to-all-start) | async-done | bytes 262176 | tf_op jit(solution)/shard_map/all_to_all | solution.py:280
  29.5 0.7 kv_unpack.1
  30.2 9.3 %collective-permute-start = (bf16[2,2,8,8,128]{4,3,2,1,0:T(8,128)(2,1)S(1)}, bf16[2,2,8,8,128]{4,3,2,1,0:T(8,128)(2,1)S(1)}, u32[]{:S(2)}, u32[]{:S(2)}) collective-permute-start(bf16[2,2,8,8,128]{4,3,2,1,0:T(8,128)(2,1)S(1)} %get-tuple-element.10), channel_id=1, source_target_pairs={{0,15},{1,14},{2,13},{3,12},{4,11},{5,10},{6,9},{7,8},{8,7},{9,6},... | collective-permute-start | bytes 196616 | tf_op jit(solution)/shard_map/ppermute | solution.py:259
  39.5 1.0 copy-done
  40.5 1.0 copy-done.1
  41.6 0.7 copy-done.4
  42.2 2.2 pack_rows.1
  44.5 1.4 collective-permute-done
  45.8 4.5 %all-to-all-start.1 = ((bf16[16,2,2,128,128]{4,3,2,1,0:T(8,128)(2,1)}), bf16[16,2,2,128,128]{4,3,2,1,0:T(8,128)(2,1)S(1)}, u32[]{:S(2)}, u32[]{:S(2)}) async-start(bf16[16,2,2,128,128]{4,3,2,1,0:T(8,128)(2,1)} %bitcast.10), calls=%async_computation.1 | async-start | bytes 4194304 | tf_op jit(solution)/shard_map/all_to_all | solution.py:295
  50.4 0.7 pad_maximum_fusion
  51.1 0.2 convert_reduce_fusion.start_ref
  51.3 59.8 %all-gather.3.cloned.1.call-done = bf16[16,2,2,8,8,128]{5,4,3,2,1,0:T(8,128)(2,1)} async-done(((bf16[2,2,2,8,8,128]{5,4,3,2,1,0:T(8,128)(2,1)}), bf16[16,2,2,8,8,128]{5,4,3,2,1,0:T(8,128)(2,1)}) %all-gather.3.cloned.1.call-update) | async-done | bytes 1048592 | tf_op jit(solution)/shard_map/all_gather | solution.py:299
  111.1 1.2 copy-done.6
  112.4 12.2 %attention_backward.1 = (bf16[32,128,128]{2,1,0:T(8,128)(2,1)}, bf16[8,2,2,2,8,8,128]{6,5,4,3,2,1,0:T(8,128)(2,1)}) custom-call(s32[16]{0:T(128)S(1)} %dynamic-slice_bitcast_fusion.recv_ref, s32[16]{0:T(128)S(1)} %convert_reduce_fusion.start_ref, s32[1]{0:T(128)} %bitcast.2.place_ref, bf16[32,2,128,128]{3,2,1,0:T(8,128)(2,1)S(1)} %bitcast.33, ...), custom_call_target="tpu_custom_call" | custom-call | flops 2000000000 | bytes 6291456 | tf_op jit(solution)/shard_map/attention_backward/pallas_call | solution.py:158
  124.6 14.2 %all-to-all-start.2 = ((bf16[16,2,128,128]{3,2,1,0:T(8,128)(2,1)}), bf16[16,2,128,128]{3,2,1,0:T(8,128)(2,1)S(1)}, u32[]{:S(2)}, u32[]{:S(2)}) async-start(bf16[16,2,128,128]{3,2,1,0:T(8,128)(2,1)} %bitcast.16), calls=%async_computation.3 | async-start | bytes 2097152 | tf_op jit(solution)/shard_map/all_to_all | solution.py:304
  138.9 0.2 compare_reduce_fusion
  139.1 15.7 %all-to-all-done.2 = bf16[16,2,128,128]{3,2,1,0:T(8,128)(2,1)S(1)} async-done(((bf16[16,2,128,128]{3,2,1,0:T(8,128)(2,1)}), bf16[16,2,128,128]{3,2,1,0:T(8,128)(2,1)S(1)}, u32[]{:S(2)}, u32[]{:S(2)}) %all-to-all-start.2) | async-done | bytes 1048608 | tf_op jit(solution)/shard_map/all_to_all | solution.py:304
  154.8 34.5 %reduce-scatter.2.cloned.1.call-done = bf16[1,2,2,2,8,8,128]{6,5,4,3,2,1,0:T(8,128)(2,1)} async-done(((bf16[8,2,2,2,8,8,128]{6,5,4,3,2,1,0:T(8,128)(2,1)}), bf16[1,2,2,2,8,8,128]{6,5,4,3,2,1,0:T(8,128)(2,1)}) %reduce-scatter.2.cloned.1.call-update) | async-done | bytes 131088 | tf_op jit(solution)/shard_map/reduce_scatter | solution.py:309
  189.3 0.9 slice_bitcast_fusion
  190.2 4.8 %collective-permute-start.1 = (bf16[2,2,8,8,128]{4,3,2,1,0:T(8,128)(2,1)S(1)}, bf16[2,2,8,8,128]{4,3,2,1,0:T(8,128)(2,1)S(1)}, u32[]{:S(2)}, u32[]{:S(2)}) collective-permute-start(bf16[2,2,8,8,128]{4,3,2,1,0:T(8,128)(2,1)S(1)} %get-tuple-element.18), channel_id=1, source_target_pairs={{0,15},{1,14},{2,13},{3,12},{4,11},{5,10},{6,9},{7,8},{8,7},{9,6},... | collective-permute-start | bytes 196616 | tf_op jit(solution)/shard_map/ppermute | solution.py:259
  195.0 0.1 select_reduce_fusion.anchor_ref
  195.1 2.2 collective-permute-done.1.other_ref
  197.3 1.4 kv_back.1
  198.7 14.9 %all-to-all-start.3 = ((bf16[32,2,2,2,4,128]{5,4,3,2,1,0:T(4,128)(2,1)}), bf16[32,2,2,2,4,128]{5,4,3,2,1,0:T(4,128)(2,1)S(1)}, u32[]{:S(2)}, u32[]{:S(2)}) async-start(bf16[32,2,2,2,4,128]{5,4,3,2,1,0:T(4,128)(2,1)} %bitcast.22), calls=%async_computation.4 | async-start | bytes 524288 | tf_op jit(solution)/shard_map/all_to_all | solution.py:280
  213.6 1.4 gather_fusion
  215.0 7.4 %all-to-all-done.3 = bf16[32,2,2,2,4,128]{5,4,3,2,1,0:T(4,128)(2,1)S(1)} async-done(((bf16[32,2,2,2,4,128]{5,4,3,2,1,0:T(4,128)(2,1)}), bf16[32,2,2,2,4,128]{5,4,3,2,1,0:T(4,128)(2,1)S(1)}, u32[]{:S(2)}, u32[]{:S(2)}) %all-to-all-start.3) | async-done | bytes 262176 | tf_op jit(solution)/shard_map/all_to_all | solution.py:280
  222.5 1.3 kv_final.1
  (21 shorter events, 0.2 us)
Async XLA Ops:
  7.2 0.9 copy-start.2
  8.1 0.7 copy-start.3
  10.2 19.3 %all-to-all-start = ((bf16[32,2,2,2,4,128]{5,4,3,2,1,0:T(4,128)(2,1)}), bf16[32,2,2,2,4,128]{5,4,3,2,1,0:T(4,128)(2,1)S(1)}, u32[]{:S(2)}, u32[]{:S(2)}) async-start(bf16[32,2,2,2,4,128]{5,4,3,2,1,0:T(4,128)(2,1)} %bitcast.8), calls=%async_computation | async-start | bytes 524288 | tf_op jit(solution)/shard_map/all_to_all | solution.py:280
  30.2 15.6 %collective-permute-start = (bf16[2,2,8,8,128]{4,3,2,1,0:T(8,128)(2,1)S(1)}, bf16[2,2,8,8,128]{4,3,2,1,0:T(8,128)(2,1)S(1)}, u32[]{:S(2)}, u32[]{:S(2)}) collective-permute-start(bf16[2,2,8,8,128]{4,3,2,1,0:T(8,128)(2,1)S(1)} %get-tuple-element.10), channel_id=1, source_target_pairs={{0,15},{1,14},{2,13},{3,12},{4,11},{5,10},{6,9},{7,8},{8,7},{9,6},... | collective-permute-start | bytes 196616 | tf_op jit(solution)/shard_map/ppermute | solution.py:259
  39.5 1.0 copy-start
  40.5 1.0 copy-start.1
  41.6 0.7 copy-start.4
  45.8 5.3 %copy-start.8 = (s32[1,16]{1,0:T(1,128)S(1)}, s32[1,16]{1,0:T(1,128)}, u32[]{:S(2)}) copy-start(s32[1,16]{1,0:T(1,128)} %param.11) | copy-start | bytes 196
  45.8 65.3 %all-to-all-start.1 = ((bf16[16,2,2,128,128]{4,3,2,1,0:T(8,128)(2,1)}), bf16[16,2,2,128,128]{4,3,2,1,0:T(8,128)(2,1)S(1)}, u32[]{:S(2)}, u32[]{:S(2)}) async-start(bf16[16,2,2,128,128]{4,3,2,1,0:T(8,128)(2,1)} %bitcast.10), calls=%async_computation.1 | async-start | bytes 4194304 | tf_op jit(solution)/shard_map/all_to_all | solution.py:295
  50.4 60.8 %all-gather.3.cloned.1.call-start = ((), (), s32[]{:S(2)}) async-start(), calls=%async_computation.6 | async-start | bytes 1179648 | tf_op jit(solution)/shard_map/all_gather | solution.py:299
  51.1 138.2 %reduce-scatter.2.cloned.1.call-start = ((), (), s32[]{:S(2)}) async-start(), calls=%async_computation.5 | async-start | bytes 1179648 | tf_op jit(solution)/shard_map/reduce_scatter | solution.py:309
  111.1 1.2 copy-start.6
  124.6 14.3 %copy-start.7 = (s32[16,16]{1,0:T(8,128)S(1)}, s32[16,16]{1,0:T(8,128)}, u32[]{:S(2)}) copy-start(s32[16,16]{1,0:T(8,128)} %param.10) | copy-start | bytes 3076
  124.6 70.4 %copy-start.5 = (s32[1,16,2]{1,2,0:T(2,128)S(1)}, s32[1,16,2]{1,2,0:T(2,128)}, u32[]{:S(2)}) copy-start(s32[1,16,2]{1,2,0:T(2,128)} %param.9) | copy-start | bytes 388
  124.6 30.2 %all-to-all-start.2 = ((bf16[16,2,128,128]{3,2,1,0:T(8,128)(2,1)}), bf16[16,2,128,128]{3,2,1,0:T(8,128)(2,1)S(1)}, u32[]{:S(2)}, u32[]{:S(2)}) async-start(bf16[16,2,128,128]{3,2,1,0:T(8,128)(2,1)} %bitcast.16), calls=%async_computation.3 | async-start | bytes 2097152 | tf_op jit(solution)/shard_map/all_to_all | solution.py:304
  190.2 7.2 %collective-permute-start.1 = (bf16[2,2,8,8,128]{4,3,2,1,0:T(8,128)(2,1)S(1)}, bf16[2,2,8,8,128]{4,3,2,1,0:T(8,128)(2,1)S(1)}, u32[]{:S(2)}, u32[]{:S(2)}) collective-permute-start(bf16[2,2,8,8,128]{4,3,2,1,0:T(8,128)(2,1)S(1)} %get-tuple-element.18), channel_id=1, source_target_pairs={{0,15},{1,14},{2,13},{3,12},{4,11},{5,10},{6,9},{7,8},{8,7},{9,6},... | collective-permute-start | bytes 196616 | tf_op jit(solution)/shard_map/ppermute | solution.py:259
  198.7 23.7 %all-to-all-start.3 = ((bf16[32,2,2,2,4,128]{5,4,3,2,1,0:T(4,128)(2,1)}), bf16[32,2,2,2,4,128]{5,4,3,2,1,0:T(4,128)(2,1)S(1)}, u32[]{:S(2)}, u32[]{:S(2)}) async-start(bf16[32,2,2,2,4,128]{5,4,3,2,1,0:T(4,128)(2,1)} %bitcast.22), calls=%async_computation.4 | async-start | bytes 524288 | tf_op jit(solution)/shard_map/all_to_all | solution.py:280
Sparse Core Ops, SparseCore 0:
  53.8 57.2 all-gather.2
  124.8 64.4 reduce-scatter.1

commit v3 on v2

--- a/solution.py
+++ b/solution.py
@@ -15,7 +15,8 @@
 LOG2E = 1.4426950408889634
 PLANE = ("dp", "xh")
 COLUMN = ("zh", "zm", "zl")
-LINE = ("zm", "zl")
+RING = 8
+FOLD = (0, 2, 4, 6, 7, 5, 3, 1)
 
 
 def matmul(a, b, contract):
@@ -49,26 +50,36 @@
 
 
 def attention_kernel(
-    recv_ref, start_ref, place_ref, qg_ref, kv_ref, dq_ref, dkv_ref,
-    k_all, kt_all, v_all, dk_all, dv_all, scores, dprobs, dqt,
+    recv_ref, start_ref, place_ref, qg_ref, *refs
 ):
+    kv_refs, dq_ref, dkv_refs = refs[:RING], refs[RING], refs[RING + 1 : 2 * RING + 1]
+    k_all, kt_all, v_all, dk_all, dv_all, scores, dprobs, dqt = refs[2 * RING + 1 :]
     blocks = k_all.shape[0]
     width = k_all.shape[1]
     tile_rows = width // PAIR
+    part = width // RING
     factor = SCALING * LOG2E
 
     def stage(block, _):
-        key = kv_ref[:, :, :, 0, block].astype(jnp.float32).reshape(width, HD)
-        value = kv_ref[:, :, :, 1, block].astype(jnp.float32).reshape(width, HD)
-        k_all[block] = key.astype(jnp.bfloat16)
-        v_all[block] = value.astype(jnp.bfloat16)
-        kt_all[block] = key.T.astype(jnp.bfloat16)
+        for slot, ref in enumerate(kv_refs):
+            rows = slice(slot * part, (slot + 1) * part)
+            key = ref[:, :, 0, block].astype(jnp.float32).reshape(part, HD)
+            value = ref[:, :, 1, block].astype(jnp.float32).reshape(part, HD)
+            k_all[block, rows] = key.astype(jnp.bfloat16)
+            v_all[block, rows] = value.astype(jnp.bfloat16)
+        kt_all[block] = k_all[block].astype(jnp.float32).T.astype(jnp.bfloat16)
         return 0
 
     lax.fori_loop(0, blocks, stage, 0)
 
     row = lax.broadcasted_iota(jnp.int32, (width, 1), 0)
-    source = ((place_ref[0] & 8) | (row >> 5)) ^ (((row >> 4) & 1) * 15)
+    slot = row >> 5
+    step = (slot + 1) >> 1
+    ahead = jnp.where((slot & 1) == 1, -step, step)
+    member = place_ref[0] & (RING - 1)
+    index = (jnp.where((member & 1) == 1, 15 - member, member) >> 1) + ahead & (RING - 1)
+    column = jnp.where(index < RING // 2, 2 * index, 15 - 2 * index)
+    source = ((place_ref[0] & 8) | column) ^ (((row >> 4) & 1) * 15)
     key_offset = (
         ((row >> 2) & 1) * tile_rows + ((row >> 3) & 1) * 64 + source * 4 + (row & 3)
     )
@@ -141,15 +152,17 @@
     lax.fori_loop(0, blocks, query_block, 0)
 
     def unstage(block, _):
-        shape = kv_ref.shape[:3] + kv_ref.shape[5:]
-        dkv_ref[:, :, :, 0, block] = (dk_all[block] * SCALING).reshape(shape).astype(jnp.bfloat16)
-        dkv_ref[:, :, :, 1, block] = dv_all[block].reshape(shape).astype(jnp.bfloat16)
+        for slot, ref in enumerate(dkv_refs):
+            rows = slice(slot * part, (slot + 1) * part)
+            shape = ref.shape[:2] + ref.shape[4:]
+            ref[:, :, 0, block] = (dk_all[block, rows] * SCALING).reshape(shape).astype(jnp.bfloat16)
+            ref[:, :, 1, block] = dv_all[block, rows].reshape(shape).astype(jnp.bfloat16)
         return 0
 
     lax.fori_loop(0, blocks, unstage, 0)
 
 
-def attention(my_recv, start, place, qg, kv):
+def attention(my_recv, start, place, qg, chunks):
     slots, _, tile_rows, _ = qg.shape
     blocks = my_recv.shape[0] // PAIR
     width = PAIR * tile_rows
@@ -157,12 +170,10 @@
     smem = pl.BlockSpec(memory_space=pltpu.SMEM)
     return pl.pallas_call(
         attention_kernel,
-        out_shape=(
-            jax.ShapeDtypeStruct((slots, tile_rows, HD), jnp.bfloat16),
-            jax.ShapeDtypeStruct(kv.shape, jnp.bfloat16),
-        ),
-        in_specs=[smem, smem, smem, vmem, vmem],
-        out_specs=(vmem, vmem),
+        out_shape=(jax.ShapeDtypeStruct((slots, tile_rows, HD), jnp.bfloat16),)
+        + (jax.ShapeDtypeStruct(chunks[0].shape, jnp.bfloat16),) * RING,
+        in_specs=[smem] * 3 + [vmem] * (1 + RING),
+        out_specs=(vmem,) * (1 + RING),
         scratch_shapes=[
             pltpu.VMEM((blocks, width, HD), jnp.bfloat16),
             pltpu.VMEM((blocks, HD, width), jnp.bfloat16),
@@ -178,7 +189,7 @@
             flops=2 * 10**9, bytes_accessed=6 * 2**20, transcendentals=2 * 10**6
         ),
         name="attention_backward",
-    )(my_recv, start, place, qg, kv)
+    )(my_recv, start, place, qg, *chunks)
 
 
 def kv_pack_kernel(index_ref, kv_ref, out_ref):
@@ -257,6 +268,43 @@
 
 def mirror(values):
     return lax.ppermute(values, COLUMN, [(source, 15 - source) for source in range(16)])
+
+
+def turn(values, step):
+    pairs = [
+        (base + FOLD[index], base + FOLD[(index + step) % RING])
+        for base in (0, RING)
+        for index in range(RING)
+    ]
+    return lax.ppermute(values, COLUMN, pairs)
+
+
+def ring_gather(mine):
+    chunks = [mine]
+    before = after = mine
+    for step in range(1, RING // 2 + 1):
+        before = turn(before, 1)
+        chunks.append(before)
+        if step < RING // 2:
+            after = turn(after, -1)
+            chunks.append(after)
+    return chunks
+
+
+def ring_reduce(terms):
+    def plus(arrived, term):
+        return (arrived.astype(jnp.float32) + term.astype(jnp.float32)).astype(term.dtype)
+
+    half = RING // 2
+    onward = turn(terms[RING - 1], 1)
+    first = onward
+    back = turn(terms[2 * half - 3], -1)
+    for step in range(half - 1, 0, -1):
+        onward = turn(plus(onward, terms[2 * step]), 1)
+        if step > 1:
+            back = turn(plus(back, terms[2 * step - 3]), -1)
+    total = onward.astype(jnp.float32) + back.astype(jnp.float32) + terms[0].astype(jnp.float32)
+    return total.astype(terms[0].dtype), first
 
 
 def on_device(queries, keys_values, grad_out, send_tiles, recv_slot, tile_seq):
@@ -296,17 +344,17 @@
         qg_packed.reshape(n_replicas, slot_cap, 2, tile_rows, row_width),
         "dp", split_axis=0, concat_axis=0, tiled=True,
     ).reshape(slots, 2, tile_rows, row_width)
-    kv_all = lax.all_gather(jnp.stack([own, mirrored]), LINE)
+    chunks = ring_gather(jnp.stack([own, mirrored]))
 
     seq = tile_seq[0]
     start = jnp.sum((seq[None, :] < seq[:, None]).astype(jnp.int32), axis=1)
-    query_back, dkv = attention(my_recv, start, place, qg_arrived, kv_all)
+    query_back, *terms = attention(my_recv, start, place, qg_arrived, chunks)
+    summed, first = ring_reduce(terms)
+    query_back, _ = lax.optimization_barrier((query_back, first))
     query_returned = lax.all_to_all(
         query_back.reshape(n_replicas, slot_cap, tile_rows, row_width),
         "dp", split_axis=0, concat_axis=0, tiled=True,
     )
-
-    summed = lax.psum_scatter(dkv, LINE, scatter_dimension=0)
     summed, query_returned = lax.optimization_barrier((summed, query_returned))
     swapped = [summed[0], mirror(summed[1])]
     kv_returned = over_plane(

time: 231 us -> 178 us (0.77)
  the two profiles are of different devices: /device:TPU:1 before, /device:TPU:129 now
where the time goes in v3:
time: 178 us; the launch traced here: 177 us
  starting transfers between devices  96.9 us (54%)
  waiting for transfers between devices  44.9 us (25%)
  Pallas kernels  21.3 us (12%)
  local copies, waits for them, and re-layouts  11.8 us (7%)
    ppermute x14, starting transfers between devices, turn(): return lax.ppermute(values, COLUMN, pairs)  48.3 us
    ppermute x14, waiting for transfers between devices, turn(): return lax.ppermute(values, COLUMN, pairs)  26.2 us
    ppermute x2, starting transfers between devices, mirror(): lax.ppermute(values, COLUMN, [(source, 15 - source) for source in range(1...  18.6 us
    all_to_all x2, starting transfers between devices, over_plane(): lax.all_to_all(values.reshape((2 * n_replicas,) + values.shape[2:]), PLAN...  16.6 us
    all_to_all x2, waiting for transfers between devices, over_plane(): lax.all_to_all(values.reshape((2 * n_replicas,) + values.shape[2:]), PLAN...  15.6 us
    pallas_call x1, Pallas kernels, attention(): pl.pallas_call(attention_kernel, out_shape=(jax.ShapeDtypeStruct((slots,...  14.2 us
    unnamed x30, local copies, waits for them, and re-layouts  9.66 us
    all_to_all x1, starting transfers between devices, on_device(): lax.all_to_all(query_back.reshape(n_replicas, slot_cap, tile_rows, row_wi...  9.11 us
  transfers between devices with their start and end apart: 20, of which 10 were waited for; matrix products, arithmetic and copies ran while one was open for 2% of the time, Pallas kernels for 1%

profile of v3, /device:TPU:129, one launch (start us, length us, event | category | flops | bytes accessed | tf_op | source)
XLA Modules:
  0.0 176.7 jit_solution(13685303230804875626)
XLA Ops:
  3.7 7.8 %all-to-all-start = ((bf16[32,2,2,2,4,128]{5,4,3,2,1,0:T(4,128)(2,1)}), bf16[32,2,2,2,4,128]{5,4,3,2,1,0:T(4,128)(2,1)S(1)}, u32[]{:S(2)}, u32[]{:S(2)}) async-start(bf16[32,2,2,2,4,128]{5,4,3,2,1,0:T(4,128)(2,1)} %bitcast.8), calls=%async_computation | async-start | bytes 524288 | tf_op jit(solution)/shard_map/all_to_all | solution.py:328
  12.1 8.2 %all-to-all-done = bf16[32,2,2,2,4,128]{5,4,3,2,1,0:T(4,128)(2,1)S(1)} async-done(((bf16[32,2,2,2,4,128]{5,4,3,2,1,0:T(4,128)(2,1)}), bf16[32,2,2,2,4,128]{5,4,3,2,1,0:T(4,128)(2,1)S(1)}, u32[]{:S(2)}, u32[]{:S(2)}) %all-to-all-start) | async-done | bytes 262176 | tf_op jit(solution)/shard_map/all_to_all | solution.py:328
  21.0 10.2 %collective-permute-start = (bf16[2,2,8,8,128]{4,3,2,1,0:T(8,128)(2,1)S(1)}, bf16[2,2,8,8,128]{4,3,2,1,0:T(8,128)(2,1)S(1)}, u32[]{:S(2)}, u32[]{:S(2)}) collective-permute-start(bf16[2,2,8,8,128]{4,3,2,1,0:T(8,128)(2,1)S(1)} %get-tuple-element.18), channel_id=1, source_target_pairs={{0,15},{1,14},{2,13},{3,12},{4,11},{5,10},{6,9},{7,8},{8,7},{9,6},... | collective-permute-start | bytes 196616 | tf_op jit(solution)/shard_map/ppermute | solution.py:270
  33.9 2.3 %pack_rows.1 = bf16[32,2,128,128]{3,2,1,0:T(8,128)(2,1)} custom-call(s32[2,16]{1,0:T(2,128)S(1)} %bitcast.37, bf16[16,128,128]{2,1,0:T(8,128)(2,1)S(1)} %copy-done, bf16[16,128,128]{2,1,0:T(8,128)(2,1)S(1)} %copy-done.1), custom_call_target="tpu_custom_call" | custom-call | tf_op jit(solution)/shard_map/pack_rows/pallas_call | solution.py:38
  36.2 4.3 %all-to-all-start.1 = ((bf16[16,2,2,128,128]{4,3,2,1,0:T(8,128)(2,1)}), bf16[16,2,2,128,128]{4,3,2,1,0:T(8,128)(2,1)S(1)}, u32[]{:S(2)}, u32[]{:S(2)}) async-start(bf16[16,2,2,128,128]{4,3,2,1,0:T(8,128)(2,1)} %bitcast.10), calls=%async_computation.1 | async-start | bytes 4194304 | tf_op jit(solution)/shard_map/all_to_all | solution.py:343
  40.5 1.9 %collective-permute-start.1 = (bf16[2,2,2,8,8,128]{5,4,3,2,1,0:T(8,128)(2,1)S(1)}, bf16[2,2,2,8,8,128]{5,4,3,2,1,0:T(8,128)(2,1)S(1)}, u32[]{:S(2)}, u32[]{:S(2)}) collective-permute-start(bf16[2,2,2,8,8,128]{5,4,3,2,1,0:T(8,128)(2,1)S(1)} %pad_maximum_fusion.refs_0_), channel_id=1, source_target_pairs={{0,2},{2,4},{4,6},{6,7},{7,5},{5,3},{3,1},{1,0},{8,10},{10,12},{12... | collective-permute-start | bytes 393224 | tf_op jit(solution)/shard_map/ppermute | solution.py:279
  42.5 5.5 %collective-permute-start.2 = (bf16[2,2,2,8,8,128]{5,4,3,2,1,0:T(8,128)(2,1)S(1)}, bf16[2,2,2,8,8,128]{5,4,3,2,1,0:T(8,128)(2,1)S(1)}, u32[]{:S(2)}, u32[]{:S(2)}) collective-permute-start(bf16[2,2,2,8,8,128]{5,4,3,2,1,0:T(8,128)(2,1)S(1)} %pad_maximum_fusion.refs_0_), channel_id=1, source_target_pairs={{0,1},{2,0},{4,2},{6,4},{7,6},{5,7},{3,5},{1,3},{8,9},{10,8},{12,1... | collective-permute-start | bytes 393224 | tf_op jit(solution)/shard_map/ppermute | solution.py:279
  48.0 4.3 %collective-permute-done.1.refs_1_ = bf16[2,2,2,8,8,128]{5,4,3,2,1,0:T(8,128)(2,1)S(1)} collective-permute-done((bf16[2,2,2,8,8,128]{5,4,3,2,1,0:T(8,128)(2,1)S(1)}, bf16[2,2,2,8,8,128]{5,4,3,2,1,0:T(8,128)(2,1)S(1)}, u32[]{:S(2)}, u32[]{:S(2)}) %collective-permute-start.1) | collective-permute-done | bytes 131104 | tf_op jit(solution)/shard_map/ppermute | solution.py:279
  52.2 1.9 %collective-permute-start.3 = (bf16[2,2,2,8,8,128]{5,4,3,2,1,0:T(8,128)(2,1)S(1)}, bf16[2,2,2,8,8,128]{5,4,3,2,1,0:T(8,128)(2,1)S(1)}, u32[]{:S(2)}, u32[]{:S(2)}) collective-permute-start(bf16[2,2,2,8,8,128]{5,4,3,2,1,0:T(8,128)(2,1)S(1)} %collective-permute-done.1.refs_1_), channel_id=1, source_target_pairs={{0,2},{2,4},{4,6},{6,7},{7,5},{5,3},{3,1},{1,0},{8,10},{10,12},{12... | collective-permute-start | bytes 393224 | tf_op jit(solution)/shard_map/ppermute | solution.py:279
  54.2 5.5 %collective-permute-start.4 = (bf16[2,2,2,8,8,128]{5,4,3,2,1,0:T(8,128)(2,1)S(1)}, bf16[2,2,2,8,8,128]{5,4,3,2,1,0:T(8,128)(2,1)S(1)}, u32[]{:S(2)}, u32[]{:S(2)}) collective-permute-start(bf16[2,2,2,8,8,128]{5,4,3,2,1,0:T(8,128)(2,1)S(1)} %collective-permute-done.2.refs_2_), channel_id=1, source_target_pairs={{0,1},{2,0},{4,2},{6,4},{7,6},{5,7},{3,5},{1,3},{8,9},{10,8},{12,1... | collective-permute-start | bytes 393224 | tf_op jit(solution)/shard_map/ppermute | solution.py:279
  59.6 3.0 %collective-permute-done.3.refs_3_ = bf16[2,2,2,8,8,128]{5,4,3,2,1,0:T(8,128)(2,1)S(1)} collective-permute-done((bf16[2,2,2,8,8,128]{5,4,3,2,1,0:T(8,128)(2,1)S(1)}, bf16[2,2,2,8,8,128]{5,4,3,2,1,0:T(8,128)(2,1)S(1)}, u32[]{:S(2)}, u32[]{:S(2)}) %collective-permute-start.3) | collective-permute-done | bytes 131104 | tf_op jit(solution)/shard_map/ppermute | solution.py:279
  62.6 1.9 %collective-permute-start.5 = (bf16[2,2,2,8,8,128]{5,4,3,2,1,0:T(8,128)(2,1)S(1)}, bf16[2,2,2,8,8,128]{5,4,3,2,1,0:T(8,128)(2,1)S(1)}, u32[]{:S(2)}, u32[]{:S(2)}) collective-permute-start(bf16[2,2,2,8,8,128]{5,4,3,2,1,0:T(8,128)(2,1)S(1)} %collective-permute-done.3.refs_3_), channel_id=1, source_target_pairs={{0,2},{2,4},{4,6},{6,7},{7,5},{5,3},{3,1},{1,0},{8,10},{10,12},{12... | collective-permute-start | bytes 393224 | tf_op jit(solution)/shard_map/ppermute | solution.py:279
  64.6 5.5 %collective-permute-start.6 = (bf16[2,2,2,8,8,128]{5,4,3,2,1,0:T(8,128)(2,1)S(1)}, bf16[2,2,2,8,8,128]{5,4,3,2,1,0:T(8,128)(2,1)S(1)}, u32[]{:S(2)}, u32[]{:S(2)}) collective-permute-start(bf16[2,2,2,8,8,128]{5,4,3,2,1,0:T(8,128)(2,1)S(1)} %collective-permute-done.4.refs_4_), channel_id=1, source_target_pairs={{0,1},{2,0},{4,2},{6,4},{7,6},{5,7},{3,5},{1,3},{8,9},{10,8},{12,1... | collective-permute-start | bytes 393224 | tf_op jit(solution)/shard_map/ppermute | solution.py:279
  70.1 1.6 collective-permute-done.5.refs_5_
  71.7 1.9 %collective-permute-start.7 = (bf16[2,2,2,8,8,128]{5,4,3,2,1,0:T(8,128)(2,1)S(1)}, bf16[2,2,2,8,8,128]{5,4,3,2,1,0:T(8,128)(2,1)S(1)}, u32[]{:S(2)}, u32[]{:S(2)}) collective-permute-start(bf16[2,2,2,8,8,128]{5,4,3,2,1,0:T(8,128)(2,1)S(1)} %collective-permute-done.5.refs_5_), channel_id=1, source_target_pairs={{0,2},{2,4},{4,6},{6,7},{7,5},{5,3},{3,1},{1,0},{8,10},{10,12},{12... | collective-permute-start | bytes 393224 | tf_op jit(solution)/shard_map/ppermute | solution.py:279
  75.1 4.4 %collective-permute-done.7.refs_7_ = bf16[2,2,2,8,8,128]{5,4,3,2,1,0:T(8,128)(2,1)S(1)} collective-permute-done((bf16[2,2,2,8,8,128]{5,4,3,2,1,0:T(8,128)(2,1)S(1)}, bf16[2,2,2,8,8,128]{5,4,3,2,1,0:T(8,128)(2,1)S(1)}, u32[]{:S(2)}, u32[]{:S(2)}) %collective-permute-start.7) | collective-permute-done | bytes 131104 | tf_op jit(solution)/shard_map/ppermute | solution.py:279
  82.9 14.2 %attention_backward.1 = (bf16[32,128,128]{2,1,0:T(8,128)(2,1)}, bf16[2,2,2,8,8,128]{5,4,3,2,1,0:T(8,128)(2,1)S(1)}, bf16[2,2,2,8,8,128]{5,4,3,2,1,0:T(8,128)(2,1...) custom-call(s32[16]{0:T(128)S(1)} %dynamic-slice_bitcast_fusion.recv, ...), custom_call_target="tpu_custom_call" | custom-call | flops 2000000000 | bytes 6291456 | tf_op jit(solution)/shard_map/attention_backward/pallas_call | solution.py:171
  97.8 2.0 %collective-permute-start.8 = (bf16[2,2,2,8,8,128]{5,4,3,2,1,0:T(8,128)(2,1)}, bf16[2,2,2,8,8,128]{5,4,3,2,1,0:T(8,128)(2,1)S(1)}, u32[]{:S(2)}, u32[]{:S(2)}) collective-permute-start(bf16[2,2,2,8,8,128]{5,4,3,2,1,0:T(8,128)(2,1)} %get-tuple-element.22), channel_id=1, source_target_pairs={{0,2},{2,4},{4,6},{6,7},{7,5},{5,3},{3,1},{1,0},{8,10},{10,12},{12... | collective-permute-start | bytes 393224 | tf_op jit(solution)/shard_map/ppermute | solution.py:279
  99.8 5.5 %collective-permute-start.12 = (bf16[2,2,2,8,8,128]{5,4,3,2,1,0:T(8,128)(2,1)}, bf16[2,2,2,8,8,128]{5,4,3,2,1,0:T(8,128)(2,1)S(1)}, u32[]{:S(2)}, u32[]{:S(2)}) collective-permute-start(bf16[2,2,2,8,8,128]{5,4,3,2,1,0:T(8,128)(2,1)} %copy-done.8), channel_id=1, source_target_pairs={{0,1},{2,0},{4,2},{6,4},{7,6},{5,7},{3,5},{1,3},{8,9},{10,8},{12,1... | collective-permute-start | bytes 393224 | tf_op jit(solution)/shard_map/ppermute | solution.py:279
  105.3 2.9 %collective-permute-done.8 = bf16[2,2,2,8,8,128]{5,4,3,2,1,0:T(8,128)(2,1)S(1)} collective-permute-done((bf16[2,2,2,8,8,128]{5,4,3,2,1,0:T(8,128)(2,1)}, bf16[2,2,2,8,8,128]{5,4,3,2,1,0:T(8,128)(2,1)S(1)}, u32[]{:S(2)}, u32[]{:S(2)}) %collective-permute-start.8) | collective-permute-done | bytes 131104 | tf_op jit(solution)/shard_map/ppermute | solution.py:279
  108.2 1.9 %collective-permute-start.9 = (bf16[2,2,2,8,8,128]{5,4,3,2,1,0:T(8,128)(2,1)S(1)}, bf16[2,2,2,8,8,128]{5,4,3,2,1,0:T(8,128)(2,1)S(1)}, u32[]{:S(2)}, u32[]{:S(2)}) collective-permute-start(bf16[2,2,2,8,8,128]{5,4,3,2,1,0:T(8,128)(2,1)S(1)} %add_convert_fusion.5), channel_id=1, source_target_pairs={{0,2},{2,4},{4,6},{6,7},{7,5},{5,3},{3,1},{1,0},{8,10},{10,12},{12... | collective-permute-start | bytes 393224 | tf_op jit(solution)/shard_map/ppermute | solution.py:279
  110.2 5.5 %collective-permute-start.13 = (bf16[2,2,2,8,8,128]{5,4,3,2,1,0:T(8,128)(2,1)S(1)}, bf16[2,2,2,8,8,128]{5,4,3,2,1,0:T(8,128)(2,1)S(1)}, u32[]{:S(2)}, u32[]{:S(2)}) collective-permute-start(bf16[2,2,2,8,8,128]{5,4,3,2,1,0:T(8,128)(2,1)S(1)} %add_convert_fusion.2), channel_id=1, source_target_pairs={{0,1},{2,0},{4,2},{6,4},{7,6},{5,7},{3,5},{1,3},{8,9},{10,8},{12,1... | collective-permute-start | bytes 393224 | tf_op jit(solution)/shard_map/ppermute | solution.py:279
  115.7 9.1 %all-to-all-start.2 = ((bf16[16,2,128,128]{3,2,1,0:T(8,128)(2,1)}), bf16[16,2,128,128]{3,2,1,0:T(8,128)(2,1)S(1)}, u32[]{:S(2)}, u32[]{:S(2)}) async-start(bf16[16,2,128,128]{3,2,1,0:T(8,128)(2,1)} %bitcast.14), calls=%async_computation.2 | async-start | bytes 2097152 | tf_op jit(solution)/shard_map/all_to_all | solution.py:354
  124.9 1.9 %collective-permute-start.10 = (bf16[2,2,2,8,8,128]{5,4,3,2,1,0:T(8,128)(2,1)S(1)}, bf16[2,2,2,8,8,128]{5,4,3,2,1,0:T(8,128)(2,1)S(1)}, u32[]{:S(2)}, u32[]{:S(2)}) collective-permute-start(bf16[2,2,2,8,8,128]{5,4,3,2,1,0:T(8,128)(2,1)S(1)} %add_convert_fusion.4), channel_id=1, source_target_pairs={{0,2},{2,4},{4,6},{6,7},{7,5},{5,3},{3,1},{1,0},{8,10},{10,12},{12... | collective-permute-start | bytes 393224 | tf_op jit(solution)/shard_map/ppermute | solution.py:279
  126.8 5.5 %collective-permute-start.14 = (bf16[2,2,2,8,8,128]{5,4,3,2,1,0:T(8,128)(2,1)S(1)}, bf16[2,2,2,8,8,128]{5,4,3,2,1,0:T(8,128)(2,1)S(1)}, u32[]{:S(2)}, u32[]{:S(2)}) collective-permute-start(bf16[2,2,2,8,8,128]{5,4,3,2,1,0:T(8,128)(2,1)S(1)} %add_convert_fusion.1), channel_id=1, source_target_pairs={{0,1},{2,0},{4,2},{6,4},{7,6},{5,7},{3,5},{1,3},{8,9},{10,8},{12,1... | collective-permute-start | bytes 393224 | tf_op jit(solution)/shard_map/ppermute | solution.py:279
  132.3 4.3 %collective-permute-done.10 = bf16[2,2,2,8,8,128]{5,4,3,2,1,0:T(8,128)(2,1)S(1)} collective-permute-done((bf16[2,2,2,8,8,128]{5,4,3,2,1,0:T(8,128)(2,1)S(1)}, bf16[2,2,2,8,8,128]{5,4,3,2,1,0:T(8,128)(2,1)S(1)}, u32[]{:S(2)}, u32[]{:S(2)}) %collective-permute-start.10) | collective-permute-done | bytes 131104 | tf_op jit(solution)/shard_map/ppermute | solution.py:279
  136.7 1.9 %collective-permute-start.11 = (bf16[2,2,2,8,8,128]{5,4,3,2,1,0:T(8,128)(2,1)S(1)}, bf16[2,2,2,8,8,128]{5,4,3,2,1,0:T(8,128)(2,1)S(1)}, u32[]{:S(2)}, u32[]{:S(2)}) collective-permute-start(bf16[2,2,2,8,8,128]{5,4,3,2,1,0:T(8,128)(2,1)S(1)} %add_convert_fusion.3), channel_id=1, source_target_pairs={{0,2},{2,4},{4,6},{6,7},{7,5},{5,3},{3,1},{1,0},{8,10},{10,12},{12... | collective-permute-start | bytes 393224 | tf_op jit(solution)/shard_map/ppermute | solution.py:279
  138.9 5.7 %collective-permute-done.11 = bf16[2,2,2,8,8,128]{5,4,3,2,1,0:T(8,128)(2,1)S(1)} collective-permute-done((bf16[2,2,2,8,8,128]{5,4,3,2,1,0:T(8,128)(2,1)S(1)}, bf16[2,2,2,8,8,128]{5,4,3,2,1,0:T(8,128)(2,1)S(1)}, u32[]{:S(2)}, u32[]{:S(2)}) %collective-permute-start.11) | collective-permute-done | bytes 131104 | tf_op jit(solution)/shard_map/ppermute | solution.py:279
  144.6 8.4 %collective-permute-start.15 = (bf16[2,2,8,8,128]{4,3,2,1,0:T(8,128)(2,1)S(1)}, bf16[2,2,8,8,128]{4,3,2,1,0:T(8,128)(2,1)S(1)}, u32[]{:S(2)}, u32[]{:S(2)}) collective-permute-start(bf16[2,2,8,8,128]{4,3,2,1,0:T(8,128)(2,1)S(1)} %get-tuple-element.34), channel_id=1, source_target_pairs={{0,15},{1,14},{2,13},{3,12},{4,11},{5,10},{6,9},{7,8},{8,7},{9,6},... | collective-permute-start | bytes 196616 | tf_op jit(solution)/shard_map/ppermute | solution.py:270
  153.1 3.1 %collective-permute-done.15.other_ref = bf16[2,2,8,8,128]{4,3,2,1,0:T(8,128)(2,1)S(1)} collective-permute-done((bf16[2,2,8,8,128]{4,3,2,1,0:T(8,128)(2,1)S(1)}, bf16[2,2,8,8,128]{4,3,2,1,0:T(8,128)(2,1)S(1)}, u32[]{:S(2)}, u32[]{:S(2)}) %collective-permute-start.15) | collective-permute-done | bytes 65568 | tf_op jit(solution)/shard_map/ppermute | solution.py:270
  157.6 8.9 %all-to-all-start.3 = ((bf16[32,2,2,2,4,128]{5,4,3,2,1,0:T(4,128)(2,1)}), bf16[32,2,2,2,4,128]{5,4,3,2,1,0:T(4,128)(2,1)S(1)}, u32[]{:S(2)}, u32[]{:S(2)}) async-start(bf16[32,2,2,2,4,128]{5,4,3,2,1,0:T(4,128)(2,1)} %bitcast.20), calls=%async_computation.3 | async-start | bytes 524288 | tf_op jit(solution)/shard_map/all_to_all | solution.py:328
  167.9 7.4 %all-to-all-done.3 = bf16[32,2,2,2,4,128]{5,4,3,2,1,0:T(4,128)(2,1)S(1)} async-done(((bf16[32,2,2,2,4,128]{5,4,3,2,1,0:T(4,128)(2,1)}), bf16[32,2,2,2,4,128]{5,4,3,2,1,0:T(4,128)(2,1)S(1)}, u32[]{:S(2)}, u32[]{:S(2)}) %all-to-all-start.3) | async-done | bytes 262176 | tf_op jit(solution)/shard_map/all_to_all | solution.py:328
  (61 shorter events, 17.4 us)
Async XLA Ops:
  0.6 0.9 copy-start.2
  1.5 0.7 copy-start.3
  3.7 16.6 %all-to-all-start = ((bf16[32,2,2,2,4,128]{5,4,3,2,1,0:T(4,128)(2,1)}), bf16[32,2,2,2,4,128]{5,4,3,2,1,0:T(4,128)(2,1)S(1)}, u32[]{:S(2)}, u32[]{:S(2)}) async-start(bf16[32,2,2,2,4,128]{5,4,3,2,1,0:T(4,128)(2,1)} %bitcast.8), calls=%async_computation | async-start | bytes 524288 | tf_op jit(solution)/shard_map/all_to_all | solution.py:328
  21.0 15.2 %collective-permute-start = (bf16[2,2,8,8,128]{4,3,2,1,0:T(8,128)(2,1)S(1)}, bf16[2,2,8,8,128]{4,3,2,1,0:T(8,128)(2,1)S(1)}, u32[]{:S(2)}, u32[]{:S(2)}) collective-permute-start(bf16[2,2,8,8,128]{4,3,2,1,0:T(8,128)(2,1)S(1)} %get-tuple-element.18), channel_id=1, source_target_pairs={{0,15},{1,14},{2,13},{3,12},{4,11},{5,10},{6,9},{7,8},{8,7},{9,6},... | collective-permute-start | bytes 196616 | tf_op jit(solution)/shard_map/ppermute | solution.py:270
  31.2 1.0 copy-start
  32.2 1.0 copy-start.1
  33.3 0.7 copy-start.4
  36.2 38.1 %copy-start.14 = (s32[1,16]{1,0:T(1,128)S(1)}, s32[1,16]{1,0:T(1,128)}, u32[]{:S(2)}) copy-start(s32[1,16]{1,0:T(1,128)} %param.11) | copy-start | bytes 196
  36.2 43.9 %all-to-all-start.1 = ((bf16[16,2,2,128,128]{4,3,2,1,0:T(8,128)(2,1)}), bf16[16,2,2,128,128]{4,3,2,1,0:T(8,128)(2,1)S(1)}, u32[]{:S(2)}, u32[]{:S(2)}) async-start(bf16[16,2,2,128,128]{4,3,2,1,0:T(8,128)(2,1)} %bitcast.10), calls=%async_computation.1 | async-start | bytes 4194304 | tf_op jit(solution)/shard_map/all_to_all | solution.py:343
  40.5 11.7 %collective-permute-start.1 = (bf16[2,2,2,8,8,128]{5,4,3,2,1,0:T(8,128)(2,1)S(1)}, bf16[2,2,2,8,8,128]{5,4,3,2,1,0:T(8,128)(2,1)S(1)}, u32[]{:S(2)}, u32[]{:S(2)}) collective-permute-start(bf16[2,2,2,8,8,128]{5,4,3,2,1,0:T(8,128)(2,1)S(1)} %pad_maximum_fusion.refs_0_), channel_id=1, source_target_pairs={{0,2},{2,4},{4,6},{6,7},{7,5},{5,3},{3,1},{1,0},{8,10},{10,12},{12... | collective-permute-start | bytes 393224 | tf_op jit(solution)/shard_map/ppermute | solution.py:279
  42.5 11.7 %collective-permute-start.2 = (bf16[2,2,2,8,8,128]{5,4,3,2,1,0:T(8,128)(2,1)S(1)}, bf16[2,2,2,8,8,128]{5,4,3,2,1,0:T(8,128)(2,1)S(1)}, u32[]{:S(2)}, u32[]{:S(2)}) collective-permute-start(bf16[2,2,2,8,8,128]{5,4,3,2,1,0:T(8,128)(2,1)S(1)} %pad_maximum_fusion.refs_0_), channel_id=1, source_target_pairs={{0,1},{2,0},{4,2},{6,4},{7,6},{5,7},{3,5},{1,3},{8,9},{10,8},{12,1... | collective-permute-start | bytes 393224 | tf_op jit(solution)/shard_map/ppermute | solution.py:279
  52.2 10.4 %collective-permute-start.3 = (bf16[2,2,2,8,8,128]{5,4,3,2,1,0:T(8,128)(2,1)S(1)}, bf16[2,2,2,8,8,128]{5,4,3,2,1,0:T(8,128)(2,1)S(1)}, u32[]{:S(2)}, u32[]{:S(2)}) collective-permute-start(bf16[2,2,2,8,8,128]{5,4,3,2,1,0:T(8,128)(2,1)S(1)} %collective-permute-done.1.refs_1_), channel_id=1, source_target_pairs={{0,2},{2,4},{4,6},{6,7},{7,5},{5,3},{3,1},{1,0},{8,10},{10,12},{12... | collective-permute-start | bytes 393224 | tf_op jit(solution)/shard_map/ppermute | solution.py:279
  54.2 10.4 %collective-permute-start.4 = (bf16[2,2,2,8,8,128]{5,4,3,2,1,0:T(8,128)(2,1)S(1)}, bf16[2,2,2,8,8,128]{5,4,3,2,1,0:T(8,128)(2,1)S(1)}, u32[]{:S(2)}, u32[]{:S(2)}) collective-permute-start(bf16[2,2,2,8,8,128]{5,4,3,2,1,0:T(8,128)(2,1)S(1)} %collective-permute-done.2.refs_2_), channel_id=1, source_target_pairs={{0,1},{2,0},{4,2},{6,4},{7,6},{5,7},{3,5},{1,3},{8,9},{10,8},{12,1... | collective-permute-start | bytes 393224 | tf_op jit(solution)/shard_map/ppermute | solution.py:279
  62.6 9.1 %collective-permute-start.5 = (bf16[2,2,2,8,8,128]{5,4,3,2,1,0:T(8,128)(2,1)S(1)}, bf16[2,2,2,8,8,128]{5,4,3,2,1,0:T(8,128)(2,1)S(1)}, u32[]{:S(2)}, u32[]{:S(2)}) collective-permute-start(bf16[2,2,2,8,8,128]{5,4,3,2,1,0:T(8,128)(2,1)S(1)} %collective-permute-done.3.refs_3_), channel_id=1, source_target_pairs={{0,2},{2,4},{4,6},{6,7},{7,5},{5,3},{3,1},{1,0},{8,10},{10,12},{12... | collective-permute-start | bytes 393224 | tf_op jit(solution)/shard_map/ppermute | solution.py:279
  64.6 9.9 %collective-permute-start.6 = (bf16[2,2,2,8,8,128]{5,4,3,2,1,0:T(8,128)(2,1)S(1)}, bf16[2,2,2,8,8,128]{5,4,3,2,1,0:T(8,128)(2,1)S(1)}, u32[]{:S(2)}, u32[]{:S(2)}) collective-permute-start(bf16[2,2,2,8,8,128]{5,4,3,2,1,0:T(8,128)(2,1)S(1)} %collective-permute-done.4.refs_4_), channel_id=1, source_target_pairs={{0,1},{2,0},{4,2},{6,4},{7,6},{5,7},{3,5},{1,3},{8,9},{10,8},{12,1... | collective-permute-start | bytes 393224 | tf_op jit(solution)/shard_map/ppermute | solution.py:279
  71.7 7.8 %collective-permute-start.7 = (bf16[2,2,2,8,8,128]{5,4,3,2,1,0:T(8,128)(2,1)S(1)}, bf16[2,2,2,8,8,128]{5,4,3,2,1,0:T(8,128)(2,1)S(1)}, u32[]{:S(2)}, u32[]{:S(2)}) collective-permute-start(bf16[2,2,2,8,8,128]{5,4,3,2,1,0:T(8,128)(2,1)S(1)} %collective-permute-done.5.refs_5_), channel_id=1, source_target_pairs={{0,2},{2,4},{4,6},{6,7},{7,5},{5,3},{3,1},{1,0},{8,10},{10,12},{12... | collective-permute-start | bytes 393224 | tf_op jit(solution)/shard_map/ppermute | solution.py:279
  74.5 0.7 copy-start.9
  80.2 0.9 copy-start.7
  81.1 0.9 copy-start.10
  82.0 0.9 copy-start.12
  97.8 40.9 %copy-start.13 = (s32[16,16]{1,0:T(8,128)S(1)}, s32[16,16]{1,0:T(8,128)}, u32[]{:S(2)}) copy-start(s32[16,16]{1,0:T(8,128)} %param.10) | copy-start | bytes 3076
  97.8 10.4 %collective-permute-start.8 = (bf16[2,2,2,8,8,128]{5,4,3,2,1,0:T(8,128)(2,1)}, bf16[2,2,2,8,8,128]{5,4,3,2,1,0:T(8,128)(2,1)S(1)}, u32[]{:S(2)}, u32[]{:S(2)}) collective-permute-start(bf16[2,2,2,8,8,128]{5,4,3,2,1,0:T(8,128)(2,1)} %get-tuple-element.22), channel_id=1, source_target_pairs={{0,2},{2,4},{4,6},{6,7},{7,5},{5,3},{3,1},{1,0},{8,10},{10,12},{12... | collective-permute-start | bytes 393224 | tf_op jit(solution)/shard_map/ppermute | solution.py:279
  99.8 10.3 %collective-permute-start.12 = (bf16[2,2,2,8,8,128]{5,4,3,2,1,0:T(8,128)(2,1)}, bf16[2,2,2,8,8,128]{5,4,3,2,1,0:T(8,128)(2,1)S(1)}, u32[]{:S(2)}, u32[]{:S(2)}) collective-permute-start(bf16[2,2,2,8,8,128]{5,4,3,2,1,0:T(8,128)(2,1)} %copy-done.8), channel_id=1, source_target_pairs={{0,1},{2,0},{4,2},{6,4},{7,6},{5,7},{3,5},{1,3},{8,9},{10,8},{12,1... | collective-permute-start | bytes 393224 | tf_op jit(solution)/shard_map/ppermute | solution.py:279
  108.2 16.6 %collective-permute-start.9 = (bf16[2,2,2,8,8,128]{5,4,3,2,1,0:T(8,128)(2,1)S(1)}, bf16[2,2,2,8,8,128]{5,4,3,2,1,0:T(8,128)(2,1)S(1)}, u32[]{:S(2)}, u32[]{:S(2)}) collective-permute-start(bf16[2,2,2,8,8,128]{5,4,3,2,1,0:T(8,128)(2,1)S(1)} %add_convert_fusion.5), channel_id=1, source_target_pairs={{0,2},{2,4},{4,6},{6,7},{7,5},{5,3},{3,1},{1,0},{8,10},{10,12},{12... | collective-permute-start | bytes 393224 | tf_op jit(solution)/shard_map/ppermute | solution.py:279
  110.2 42.8 %copy-start.5 = (s32[1,16,2]{1,2,0:T(2,128)S(1)}, s32[1,16,2]{1,2,0:T(2,128)}, u32[]{:S(2)}) copy-start(s32[1,16,2]{1,2,0:T(2,128)} %param.9) | copy-start | bytes 388
  110.2 16.6 %collective-permute-start.13 = (bf16[2,2,2,8,8,128]{5,4,3,2,1,0:T(8,128)(2,1)S(1)}, bf16[2,2,2,8,8,128]{5,4,3,2,1,0:T(8,128)(2,1)S(1)}, u32[]{:S(2)}, u32[]{:S(2)}) collective-permute-start(bf16[2,2,2,8,8,128]{5,4,3,2,1,0:T(8,128)(2,1)S(1)} %add_convert_fusion.2), channel_id=1, source_target_pairs={{0,1},{2,0},{4,2},{6,4},{7,6},{5,7},{3,5},{1,3},{8,9},{10,8},{12,1... | collective-permute-start | bytes 393224 | tf_op jit(solution)/shard_map/ppermute | solution.py:279
  115.7 28.9 %all-to-all-start.2 = ((bf16[16,2,128,128]{3,2,1,0:T(8,128)(2,1)}), bf16[16,2,128,128]{3,2,1,0:T(8,128)(2,1)S(1)}, u32[]{:S(2)}, u32[]{:S(2)}) async-start(bf16[16,2,128,128]{3,2,1,0:T(8,128)(2,1)} %bitcast.14), calls=%async_computation.2 | async-start | bytes 2097152 | tf_op jit(solution)/shard_map/all_to_all | solution.py:354
  124.9 11.8 %collective-permute-start.10 = (bf16[2,2,2,8,8,128]{5,4,3,2,1,0:T(8,128)(2,1)S(1)}, bf16[2,2,2,8,8,128]{5,4,3,2,1,0:T(8,128)(2,1)S(1)}, u32[]{:S(2)}, u32[]{:S(2)}) collective-permute-start(bf16[2,2,2,8,8,128]{5,4,3,2,1,0:T(8,128)(2,1)S(1)} %add_convert_fusion.4), channel_id=1, source_target_pairs={{0,2},{2,4},{4,6},{6,7},{7,5},{5,3},{3,1},{1,0},{8,10},{10,12},{12... | collective-permute-start | bytes 393224 | tf_op jit(solution)/shard_map/ppermute | solution.py:279
  126.8 12.0 %collective-permute-start.14 = (bf16[2,2,2,8,8,128]{5,4,3,2,1,0:T(8,128)(2,1)S(1)}, bf16[2,2,2,8,8,128]{5,4,3,2,1,0:T(8,128)(2,1)S(1)}, u32[]{:S(2)}, u32[]{:S(2)}) collective-permute-start(bf16[2,2,2,8,8,128]{5,4,3,2,1,0:T(8,128)(2,1)S(1)} %add_convert_fusion.1), channel_id=1, source_target_pairs={{0,1},{2,0},{4,2},{6,4},{7,6},{5,7},{3,5},{1,3},{8,9},{10,8},{12,1... | collective-permute-start | bytes 393224 | tf_op jit(solution)/shard_map/ppermute | solution.py:279
  136.7 7.8 %collective-permute-start.11 = (bf16[2,2,2,8,8,128]{5,4,3,2,1,0:T(8,128)(2,1)S(1)}, bf16[2,2,2,8,8,128]{5,4,3,2,1,0:T(8,128)(2,1)S(1)}, u32[]{:S(2)}, u32[]{:S(2)}) collective-permute-start(bf16[2,2,2,8,8,128]{5,4,3,2,1,0:T(8,128)(2,1)S(1)} %add_convert_fusion.3), channel_id=1, source_target_pairs={{0,2},{2,4},{4,6},{6,7},{7,5},{5,3},{3,1},{1,0},{8,10},{10,12},{12... | collective-permute-start | bytes 393224 | tf_op jit(solution)/shard_map/ppermute | solution.py:279
  144.6 11.6 %collective-permute-start.15 = (bf16[2,2,8,8,128]{4,3,2,1,0:T(8,128)(2,1)S(1)}, bf16[2,2,8,8,128]{4,3,2,1,0:T(8,128)(2,1)S(1)}, u32[]{:S(2)}, u32[]{:S(2)}) collective-permute-start(bf16[2,2,8,8,128]{4,3,2,1,0:T(8,128)(2,1)S(1)} %get-tuple-element.34), channel_id=1, source_target_pairs={{0,15},{1,14},{2,13},{3,12},{4,11},{5,10},{6,9},{7,8},{8,7},{9,6},... | collective-permute-start | bytes 196616 | tf_op jit(solution)/shard_map/ppermute | solution.py:270
  157.6 17.7 %all-to-all-start.3 = ((bf16[32,2,2,2,4,128]{5,4,3,2,1,0:T(4,128)(2,1)}), bf16[32,2,2,2,4,128]{5,4,3,2,1,0:T(4,128)(2,1)S(1)}, u32[]{:S(2)}, u32[]{:S(2)}) async-start(bf16[32,2,2,2,4,128]{5,4,3,2,1,0:T(4,128)(2,1)} %bitcast.20), calls=%async_computation.3 | async-start | bytes 524288 | tf_op jit(solution)/shard_map/all_to_all | solution.py:328
  (3 other events, 2.0 us)

commit v4 on v2

--- a/solution.py
+++ b/solution.py
@@ -15,7 +15,7 @@
 LOG2E = 1.4426950408889634
 PLANE = ("dp", "xh")
 COLUMN = ("zh", "zm", "zl")
-LINE = ("zm", "zl")
+NEAR = 4
 
 
 def matmul(a, b, contract):
@@ -49,26 +49,49 @@
 
 
 def attention_kernel(
-    recv_ref, start_ref, place_ref, qg_ref, kv_ref, dq_ref, dkv_ref,
-    k_all, kt_all, v_all, dk_all, dv_all, scores, dprobs, dqt,
+    recv_ref, start_ref, place_ref, qg_ref, *refs
 ):
+    kv_refs, dq_ref, dkv_refs = refs[:NEAR], refs[NEAR], refs[NEAR + 1 : 2 * NEAR + 1]
+    k_all, kt_all, v_all, dk_all, dv_all, scores, dprobs, dqt, parts, arrived = refs[2 * NEAR + 1 :]
+    copies = [
+        pltpu.make_async_copy(ref, parts.at[slot], arrived.at[slot])
+        for slot, ref in enumerate(kv_refs)
+    ]
+    for copy in copies:
+        copy.start()
     blocks = k_all.shape[0]
     width = k_all.shape[1]
     tile_rows = width // PAIR
+    part = width // NEAR
     factor = SCALING * LOG2E
 
     def stage(block, _):
-        key = kv_ref[:, :, :, 0, block].astype(jnp.float32).reshape(width, HD)
-        value = kv_ref[:, :, :, 1, block].astype(jnp.float32).reshape(width, HD)
-        k_all[block] = key.astype(jnp.bfloat16)
-        v_all[block] = value.astype(jnp.bfloat16)
-        kt_all[block] = key.T.astype(jnp.bfloat16)
-        return 0
-
+        for slot in range(NEAR):
+            rows = slice(slot * part, (slot + 1) * part)
+            key = parts[slot, :, :, 0, block].astype(jnp.float32).reshape(part, HD)
+            value = parts[slot, :, :, 1, block].astype(jnp.float32).reshape(part, HD)
+            k_all[block, rows] = key.astype(jnp.bfloat16)
+            v_all[block, rows] = value.astype(jnp.bfloat16)
+        kt_all[block] = k_all[block].astype(jnp.float32).T.astype(jnp.bfloat16)
+        return 0
+
+    for copy in copies:
+        copy.wait()
     lax.fori_loop(0, blocks, stage, 0)
 
     row = lax.broadcasted_iota(jnp.int32, (width, 1), 0)
-    source = ((place_ref[0] & 8) | (row >> 5)) ^ (((row >> 4) & 1) * 15)
+    holder = (place_ref[0] & 12) | ((place_ref[0] - (row >> 6)) & 3)
+    origin = (row >> 4) & 3
+    hop = 4 - 8 * (holder & 1)
+    source = jnp.where(
+        origin == 0,
+        holder,
+        jnp.where(
+            origin == 1,
+            (holder - hop) & 15,
+            jnp.where(origin == 2, (holder + hop) & 15, holder ^ 11),
+        ),
+    )
     key_offset = (
         ((row >> 2) & 1) * tile_rows + ((row >> 3) & 1) * 64 + source * 4 + (row & 3)
     )
@@ -141,15 +164,17 @@
     lax.fori_loop(0, blocks, query_block, 0)
 
     def unstage(block, _):
-        shape = kv_ref.shape[:3] + kv_ref.shape[5:]
-        dkv_ref[:, :, :, 0, block] = (dk_all[block] * SCALING).reshape(shape).astype(jnp.bfloat16)
-        dkv_ref[:, :, :, 1, block] = dv_all[block].reshape(shape).astype(jnp.bfloat16)
+        for slot, ref in enumerate(dkv_refs):
+            rows = slice(slot * part, (slot + 1) * part)
+            shape = ref.shape[:2] + ref.shape[4:]
+            ref[:, :, 0, block] = (dk_all[block, rows] * SCALING).reshape(shape).astype(jnp.bfloat16)
+            ref[:, :, 1, block] = dv_all[block, rows].reshape(shape).astype(jnp.bfloat16)
         return 0
 
     lax.fori_loop(0, blocks, unstage, 0)
 
 
-def attention(my_recv, start, place, qg, kv):
+def attention(my_recv, start, place, qg, chunks):
     slots, _, tile_rows, _ = qg.shape
     blocks = my_recv.shape[0] // PAIR
     width = PAIR * tile_rows
@@ -157,12 +182,10 @@
     smem = pl.BlockSpec(memory_space=pltpu.SMEM)
     return pl.pallas_call(
         attention_kernel,
-        out_shape=(
-            jax.ShapeDtypeStruct((slots, tile_rows, HD), jnp.bfloat16),
-            jax.ShapeDtypeStruct(kv.shape, jnp.bfloat16),
-        ),
-        in_specs=[smem, smem, smem, vmem, vmem],
-        out_specs=(vmem, vmem),
+        out_shape=(jax.ShapeDtypeStruct((slots, tile_rows, HD), jnp.bfloat16),)
+        + (jax.ShapeDtypeStruct(chunks[0].shape, jnp.bfloat16),) * NEAR,
+        in_specs=[smem] * 3 + [vmem] + [pl.BlockSpec(memory_space=pl.ANY)] * NEAR,
+        out_specs=(vmem,) * (1 + NEAR),
         scratch_shapes=[
             pltpu.VMEM((blocks, width, HD), jnp.bfloat16),
             pltpu.VMEM((blocks, HD, width), jnp.bfloat16),
@@ -172,13 +195,15 @@
             pltpu.VMEM((blocks, width, width), jnp.float32),
             pltpu.VMEM((blocks, width, width), jnp.float32),
             pltpu.VMEM((HD, width), jnp.float32),
+            pltpu.VMEM((NEAR,) + chunks[0].shape, jnp.bfloat16),
+            pltpu.SemaphoreType.DMA((NEAR,)),
         ],
         compiler_params=pltpu.CompilerParams(vmem_limit_bytes=24 * 2**20),
         cost_estimate=pl.CostEstimate(
             flops=2 * 10**9, bytes_accessed=6 * 2**20, transcendentals=2 * 10**6
         ),
         name="attention_backward",
-    )(my_recv, start, place, qg, kv)
+    )(my_recv, start, place, qg, *chunks)
 
 
 def kv_pack_kernel(index_ref, kv_ref, out_ref):
@@ -192,15 +217,25 @@
     lax.fori_loop(0, 2 * index_ref.shape[1], body, 0, unroll=4)
 
 
-def kv_unpack_kernel(recv_ref, place_ref, kv_ref, own_ref, other_ref):
+def plus_stays(place):
+    return ((place & 1) == 0) == ((place & 4) == 0)
+
+
+def kv_unpack_kernel(recv_ref, place_ref, kv_ref, own_ref, other_ref, plus_ref, minus_ref):
     head = place_ref[0] >> 3
+    plus_head = jnp.where(plus_stays(place_ref[0]), head, 1 - head)
 
     def body(pair, _):
         low = recv_ref[PAIR * pair]
         high = recv_ref[PAIR * pair + 1]
         for half in range(2):
             for kind in range(2):
-                for ref, which in ((own_ref, head), (other_ref, 1 - head)):
+                for ref, which in (
+                    (own_ref, head),
+                    (other_ref, 1 - head),
+                    (plus_ref, plus_head),
+                    (minus_ref, 1 - plus_head),
+                ):
                     rows = [
                         kv_ref[slot >> 1, half, slot & 1, kind, which].astype(jnp.float32)
                         for slot in (low, high)
@@ -211,16 +246,22 @@
     lax.fori_loop(0, recv_ref.shape[0] // PAIR, body, 0)
 
 
-def kv_back_kernel(recv_ref, place_ref, own_ref, other_ref, out_ref):
+def kv_back_kernel(recv_ref, place_ref, own_ref, from_plus, from_minus, other_ref, out_ref):
     head = place_ref[0] >> 3
+    stays = plus_stays(place_ref[0])
     sliver = out_ref.shape[-2]
 
     def body(pair, _):
         slots = (recv_ref[PAIR * pair], recv_ref[PAIR * pair + 1])
         for half in range(2):
             for kind in range(2):
-                for ref, which in ((own_ref, head), (other_ref, 1 - head)):
-                    total = ref[half, kind, pair].astype(jnp.float32)
+                plus = from_plus[half, kind, pair].astype(jnp.float32)
+                minus = from_minus[half, kind, pair].astype(jnp.float32)
+                for ref, far, which in (
+                    (own_ref, jnp.where(stays, plus, minus), head),
+                    (other_ref, jnp.where(stays, minus, plus), 1 - head),
+                ):
+                    total = ref[half, kind, pair].astype(jnp.float32) + far
                     for order, slot in enumerate(slots):
                         rows = total[order * sliver : (order + 1) * sliver]
                         out_ref[slot >> 1, half, slot & 1, kind, which] = rows.astype(jnp.bfloat16)
@@ -255,8 +296,23 @@
     )(*scalars, *arrays)
 
 
-def mirror(values):
-    return lax.ppermute(values, COLUMN, [(source, 15 - source) for source in range(16)])
+def plus_four(values):
+    pairs = [(place, (place + 4 - 8 * (place & 1)) & 15) for place in range(16)]
+    return lax.ppermute(values, COLUMN, pairs)
+
+
+def minus_four(values):
+    pairs = [(place, (place - 4 + 8 * (place & 1)) & 15) for place in range(16)]
+    return lax.ppermute(values, COLUMN, pairs)
+
+
+def across(values):
+    return lax.ppermute(values, COLUMN, [(place, place ^ 11) for place in range(16)])
+
+
+def near_shift(values, step):
+    pairs = [(place, (place & 12) | ((place + step) & 3)) for place in range(16)]
+    return lax.ppermute(values, COLUMN, pairs)
 
 
 def on_device(queries, keys_values, grad_out, send_tiles, recv_slot, tile_seq):
@@ -286,29 +342,34 @@
     kv_arrived = over_plane(
         local_call(kv_pack_kernel, "kv_pack", [outgoing], [kv_blocks], traveling)
     )
-    own, other = local_call(
-        kv_unpack_kernel, "kv_unpack", [my_recv, place], [kv_arrived], (half_shape, half_shape)
+    own, other, plus, minus = local_call(
+        kv_unpack_kernel, "kv_unpack", [my_recv, place], [kv_arrived], (half_shape,) * 4
     )
     qg_packed = pack(outgoing, queries, grad_out)
-    mirrored = mirror(other)
-    qg_packed, mirrored = lax.optimization_barrier((qg_packed, mirrored))
+    far_plus, far_minus, far_across = plus_four(plus), minus_four(minus), across(other)
+    qg_packed, far_plus = lax.optimization_barrier((qg_packed, far_plus))
     qg_arrived = lax.all_to_all(
         qg_packed.reshape(n_replicas, slot_cap, 2, tile_rows, row_width),
         "dp", split_axis=0, concat_axis=0, tiled=True,
     ).reshape(slots, 2, tile_rows, row_width)
-    kv_all = lax.all_gather(jnp.stack([own, mirrored]), LINE)
+    mine = jnp.stack([own, far_plus, far_minus, far_across])
+    chunks = [mine] + [near_shift(mine, step) for step in range(1, NEAR)]
 
     seq = tile_seq[0]
     start = jnp.sum((seq[None, :] < seq[:, None]).astype(jnp.int32), axis=1)
-    query_back, dkv = attention(my_recv, start, place, qg_arrived, kv_all)
+    query_back, *terms = attention(my_recv, start, place, qg_arrived, chunks)
+    near = [terms[0]] + [near_shift(terms[step], -step) for step in range(1, NEAR)]
+    near[1], query_back = lax.optimization_barrier((near[1], query_back))
     query_returned = lax.all_to_all(
         query_back.reshape(n_replicas, slot_cap, tile_rows, row_width),
         "dp", split_axis=0, concat_axis=0, tiled=True,
     )
-
-    summed = lax.psum_scatter(dkv, LINE, scatter_dimension=0)
-    summed, query_returned = lax.optimization_barrier((summed, query_returned))
-    swapped = [summed[0], mirror(summed[1])]
+    sums = [
+        sum(term[origin].astype(jnp.float32) for term in near).astype(jnp.bfloat16)
+        for origin in range(4)
+    ]
+    swapped = [sums[0], minus_four(sums[1]), plus_four(sums[2]), across(sums[3])]
+    swapped, query_returned = lax.optimization_barrier((swapped, query_returned))
     kv_returned = over_plane(
         local_call(kv_back_kernel, "kv_back", [my_recv, place], swapped, traveling)
     )

time: 231 us -> 187 us (0.81)
  waiting for transfers between devices: 129 us -> 61.9 us
  starting transfers between devices: 58.2 us -> 93.7 us
  between operations: 14.2 us -> 0.89 us
    all_gather x1 -> x0, waiting for transfers between devices: 59.8 us -> none  [on_device(): kv_all = lax.all_gather(jnp.stack([own, mirrored]), LINE)]
    ppermute x2 -> x12, starting transfers between devices: 14.1 us -> 60.5 us  [the longest x6 28.3 us: near_shift(): return lax.ppermute(values, COLUMN, pairs)]
    ppermute x2 -> x12, waiting for transfers between devices: 3.59 us -> 46.3 us  [the longest x6 31.1 us: near_shift(): return lax.ppermute(values, COLUMN, pairs)]
    reduce_scatter x1 -> x0, waiting for transfers between devices: 34.5 us -> none  [on_device(): summed = lax.psum_scatter(dkv, LINE, scatter_dimension=0)]
    all_to_all x1, waiting for transfers between devices: 15.7 us -> 0.01 us  [on_device(): lax.all_to_all(query_back.reshape(n_replicas, slot_cap, tile_rows, row_wi...]
    all_to_all x2, starting transfers between devices: 25.3 us -> 18.1 us  [over_plane(): lax.all_to_all(values.reshape((2 * n_replicas,) + values.shape[2:]), PLAN...]
    all_to_all x1, starting transfers between devices: 14.2 us -> 10.5 us  [on_device(): lax.all_to_all(query_back.reshape(n_replicas, slot_cap, tile_rows, row_wi...]
    unnamed x18 -> x24, local copies, waits for them, and re-layouts: 5.57 us -> 7.66 us
  transfers between devices with their start and end apart: 8 -> 16, of which waited for: 7 -> 11; matrix products, arithmetic and copies ran while one was open for 1% -> 2% of each run, Pallas kernels for 1% -> 1%
where the time goes in v4:
time: 187 us; the launch traced here: 186 us
  starting transfers between devices  93.7 us (50%)
  waiting for transfers between devices  61.9 us (33%)
  Pallas kernels  18.8 us (10%)
  local copies, waits for them, and re-layouts  9.76 us (5%)
    ppermute x6, waiting for transfers between devices, near_shift(): return lax.ppermute(values, COLUMN, pairs)  31.1 us
    ppermute x6, starting transfers between devices, near_shift(): return lax.ppermute(values, COLUMN, pairs)  28.3 us
    all_to_all x2, starting transfers between devices, over_plane(): lax.all_to_all(values.reshape((2 * n_replicas,) + values.shape[2:]), PLAN...  18.1 us
    all_to_all x2, waiting for transfers between devices, over_plane(): lax.all_to_all(values.reshape((2 * n_replicas,) + values.shape[2:]), PLAN...  15.6 us
    ppermute x2, starting transfers between devices, across(): lax.ppermute(values, COLUMN, [(place, place ^ 11) for place in range(16)])  13.8 us
    pallas_call x1, Pallas kernels, attention(): pl.pallas_call(attention_kernel, out_shape=(jax.ShapeDtypeStruct((slots,...  11.7 us
    ppermute x2, starting transfers between devices, plus_four(): return lax.ppermute(values, COLUMN, pairs)  11.1 us
    all_to_all x1, starting transfers between devices, on_device(): lax.all_to_all(query_back.reshape(n_replicas, slot_cap, tile_rows, row_wi...  10.5 us
  transfers between devices with their start and end apart: 16, of which 11 were waited for; matrix products, arithmetic and copies ran while one was open for 2% of the time, Pallas kernels for 1%

profile of v4, /device:TPU:1, one launch (start us, length us, event | category | flops | bytes accessed | tf_op | source)
XLA Modules:
  0.0 185.7 jit_solution(1373852288008193718)
XLA Ops:
  2.2 1.4 kv_pack.1
  3.7 10.4 %all-to-all-start = ((bf16[32,2,2,2,4,128]{5,4,3,2,1,0:T(4,128)(2,1)}), bf16[32,2,2,2,4,128]{5,4,3,2,1,0:T(4,128)(2,1)S(1)}, u32[]{:S(2)}, u32[]{:S(2)}) async-start(bf16[32,2,2,2,4,128]{5,4,3,2,1,0:T(4,128)(2,1)} %bitcast.8), calls=%async_computation | async-start | bytes 524288 | tf_op jit(solution)/shard_map/all_to_all | solution.py:336
  14.8 8.2 %all-to-all-done = bf16[32,2,2,2,4,128]{5,4,3,2,1,0:T(4,128)(2,1)S(1)} async-done(((bf16[32,2,2,2,4,128]{5,4,3,2,1,0:T(4,128)(2,1)}), bf16[32,2,2,2,4,128]{5,4,3,2,1,0:T(4,128)(2,1)S(1)}, u32[]{:S(2)}, u32[]{:S(2)}) %all-to-all-start) | async-done | bytes 262176 | tf_op jit(solution)/shard_map/all_to_all | solution.py:336
  23.7 7.0 %collective-permute-start = (bf16[2,2,8,8,128]{4,3,2,1,0:T(8,128)(2,1)S(1)}, bf16[2,2,8,8,128]{4,3,2,1,0:T(8,128)(2,1)S(1)}, u32[]{:S(2)}, u32[]{:S(2)}) collective-permute-start(bf16[2,2,8,8,128]{4,3,2,1,0:T(8,128)(2,1)S(1)} %get-tuple-element.20), channel_id=1, source_target_pairs={{0,4},{1,13},{2,6},{3,15},{4,8},{5,1},{6,10},{7,3},{8,12},{9,5},{1... | collective-permute-start | bytes 196616 | tf_op jit(solution)/shard_map/ppermute | solution.py:301
  31.7 1.0 copy-done.1
  33.4 2.2 %pack_rows.1 = bf16[32,2,128,128]{3,2,1,0:T(8,128)(2,1)} custom-call(s32[2,16]{1,0:T(2,128)S(1)} %bitcast.43, bf16[16,128,128]{2,1,0:T(8,128)(2,1)S(1)} %copy-done, bf16[16,128,128]{2,1,0:T(8,128)(2,1)S(1)} %copy-done.1), custom_call_target="tpu_custom_call" | custom-call | tf_op jit(solution)/shard_map/pack_rows/pallas_call | solution.py:37
  36.4 4.7 %all-to-all-start.1 = ((bf16[16,2,2,128,128]{4,3,2,1,0:T(8,128)(2,1)}), bf16[16,2,2,128,128]{4,3,2,1,0:T(8,128)(2,1)S(1)}, u32[]{:S(2)}, u32[]{:S(2)}) async-start(bf16[16,2,2,128,128]{4,3,2,1,0:T(8,128)(2,1)} %bitcast.10), calls=%async_computation.1 | async-start | bytes 4194304 | tf_op jit(solution)/shard_map/all_to_all | solution.py:351
  41.1 9.8 %collective-permute-start.2 = (bf16[2,2,8,8,128]{4,3,2,1,0:T(8,128)(2,1)S(1)}, bf16[2,2,8,8,128]{4,3,2,1,0:T(8,128)(2,1)S(1)}, u32[]{:S(2)}, u32[]{:S(2)}) collective-permute-start(bf16[2,2,8,8,128]{4,3,2,1,0:T(8,128)(2,1)S(1)} %get-tuple-element.25), channel_id=1, source_target_pairs={{0,11},{1,10},{2,9},{3,8},{4,15},{5,14},{6,13},{7,12},{8,3},{9,2},... | collective-permute-start | bytes 196616 | tf_op jit(solution)/shard_map/ppermute | solution.py:310
  50.9 2.2 %collective-permute-start.1 = (bf16[2,2,8,8,128]{4,3,2,1,0:T(8,128)(2,1)S(1)}, bf16[2,2,8,8,128]{4,3,2,1,0:T(8,128)(2,1)S(1)}, u32[]{:S(2)}, u32[]{:S(2)}) collective-permute-start(bf16[2,2,8,8,128]{4,3,2,1,0:T(8,128)(2,1)S(1)} %get-tuple-element.24), channel_id=1, source_target_pairs={{0,12},{1,5},{2,14},{3,7},{4,0},{5,9},{6,2},{7,11},{8,4},{9,13},{1... | collective-permute-start | bytes 196616 | tf_op jit(solution)/shard_map/ppermute | solution.py:306
  53.2 7.5 %collective-permute-done.1 = bf16[2,2,8,8,128]{4,3,2,1,0:T(8,128)(2,1)S(1)} collective-permute-done((bf16[2,2,8,8,128]{4,3,2,1,0:T(8,128)(2,1)S(1)}, bf16[2,2,8,8,128]{4,3,2,1,0:T(8,128)(2,1)S(1)}, u32[]{:S(2)}, u32[]{:S(2)}) %collective-permute-start.1) | collective-permute-done | bytes 65568 | tf_op jit(solution)/shard_map/ppermute | solution.py:306
  60.7 2.2 %collective-permute-start.3 = (bf16[4,2,2,8,8,128]{5,4,3,2,1,0:T(8,128)(2,1)S(1)}, bf16[4,2,2,8,8,128]{5,4,3,2,1,0:T(8,128)(2,1)S(1)}, u32[]{:S(2)}, u32[]{:S(2)}) collective-permute-start(bf16[4,2,2,8,8,128]{5,4,3,2,1,0:T(8,128)(2,1)S(1)} %pad_maximum_fusion.refs_0_), channel_id=1, source_target_pairs={{0,1},{1,2},{2,3},{3,0},{4,5},{5,6},{6,7},{7,4},{8,9},{9,10},{10,1... | collective-permute-start | bytes 786440 | tf_op jit(solution)/shard_map/ppermute | solution.py:315
  62.9 5.0 %collective-permute-start.4 = (bf16[4,2,2,8,8,128]{5,4,3,2,1,0:T(8,128)(2,1)S(1)}, bf16[4,2,2,8,8,128]{5,4,3,2,1,0:T(8,128)(2,1)S(1)}, u32[]{:S(2)}, u32[]{:S(2)}) collective-permute-start(bf16[4,2,2,8,8,128]{5,4,3,2,1,0:T(8,128)(2,1)S(1)} %pad_maximum_fusion.refs_0_), channel_id=1, source_target_pairs={{0,2},{1,3},{2,0},{3,1},{4,6},{5,7},{6,4},{7,5},{8,10},{9,11},{10,... | collective-permute-start | bytes 786440 | tf_op jit(solution)/shard_map/ppermute | solution.py:315
  67.9 4.3 %collective-permute-start.5 = (bf16[4,2,2,8,8,128]{5,4,3,2,1,0:T(8,128)(2,1)S(1)}, bf16[4,2,2,8,8,128]{5,4,3,2,1,0:T(8,128)(2,1)S(1)}, u32[]{:S(2)}, u32[]{:S(2)}) collective-permute-start(bf16[4,2,2,8,8,128]{5,4,3,2,1,0:T(8,128)(2,1)S(1)} %pad_maximum_fusion.refs_0_), channel_id=1, source_target_pairs={{0,3},{1,0},{2,1},{3,2},{4,7},{5,4},{6,5},{7,6},{8,11},{9,8},{10,9... | collective-permute-start | bytes 786440 | tf_op jit(solution)/shard_map/ppermute | solution.py:315
  72.3 11.6 %collective-permute-done.4.refs_2_ = bf16[4,2,2,8,8,128]{5,4,3,2,1,0:T(8,128)(2,1)S(1)} collective-permute-done((bf16[4,2,2,8,8,128]{5,4,3,2,1,0:T(8,128)(2,1)S(1)}, bf16[4,2,2,8,8,128]{5,4,3,2,1,0:T(8,128)(2,1)S(1)}, u32[]{:S(2)}, u32[]{:S(2)}) %collective-permute-start.4) | collective-permute-done | bytes 262176 | tf_op jit(solution)/shard_map/ppermute | solution.py:315
  87.2 11.7 %attention_backward.1 = (bf16[32,128,128]{2,1,0:T(8,128)(2,1)}, bf16[4,2,2,8,8,128]{5,4,3,2,1,0:T(8,128)(2,1)S(1)}, bf16[4,2,2,8,8,128]{5,4,3,2,1,0:T(8,128)(2,1...) custom-call(s32[16]{0:T(128)S(1)} %dynamic-slice_bitcast_fusion.recv_ref, ...), custom_call_target="tpu_custom_call" | custom-call | flops 2000000000 | bytes 6291456 | tf_op jit(solution)/shard_map/attention_backward/pallas_call | solution.py:183
  98.9 8.8 %collective-permute-start.6 = (bf16[4,2,2,8,8,128]{5,4,3,2,1,0:T(8,128)(2,1)S(1)}, bf16[4,2,2,8,8,128]{5,4,3,2,1,0:T(8,128)(2,1)S(1)}, u32[]{:S(2)}, u32[]{:S(2)}) collective-permute-start(bf16[4,2,2,8,8,128]{5,4,3,2,1,0:T(8,128)(2,1)S(1)} %get-tuple-element.27), channel_id=1, source_target_pairs={{0,3},{1,0},{2,1},{3,2},{4,7},{5,4},{6,5},{7,6},{8,11},{9,8},{10,9... | collective-permute-start | bytes 786440 | tf_op jit(solution)/shard_map/ppermute | solution.py:315
  107.8 3.9 %collective-permute-done.6 = bf16[4,2,2,8,8,128]{5,4,3,2,1,0:T(8,128)(2,1)S(1)} collective-permute-done((bf16[4,2,2,8,8,128]{5,4,3,2,1,0:T(8,128)(2,1)S(1)}, bf16[4,2,2,8,8,128]{5,4,3,2,1,0:T(8,128)(2,1)S(1)}, u32[]{:S(2)}, u32[]{:S(2)}) %collective-permute-start.6) | collective-permute-done | bytes 262176 | tf_op jit(solution)/shard_map/ppermute | solution.py:315
  111.6 10.5 %all-to-all-start.2 = ((bf16[16,2,128,128]{3,2,1,0:T(8,128)(2,1)}), bf16[16,2,128,128]{3,2,1,0:T(8,128)(2,1)S(1)}, u32[]{:S(2)}, u32[]{:S(2)}) async-start(bf16[16,2,128,128]{3,2,1,0:T(8,128)(2,1)} %bitcast.20), calls=%async_computation.2 | async-start | bytes 2097152 | tf_op jit(solution)/shard_map/all_to_all | solution.py:363
  122.1 2.2 %collective-permute-start.8 = (bf16[4,2,2,8,8,128]{5,4,3,2,1,0:T(8,128)(2,1)S(1)}, bf16[4,2,2,8,8,128]{5,4,3,2,1,0:T(8,128)(2,1)S(1)}, u32[]{:S(2)}, u32[]{:S(2)}) collective-permute-start(bf16[4,2,2,8,8,128]{5,4,3,2,1,0:T(8,128)(2,1)S(1)} %get-tuple-element.31), channel_id=1, source_target_pairs={{0,1},{1,2},{2,3},{3,0},{4,5},{5,6},{6,7},{7,4},{8,9},{9,10},{10,1... | collective-permute-start | bytes 786440 | tf_op jit(solution)/shard_map/ppermute | solution.py:315
  124.4 5.9 %collective-permute-start.7 = (bf16[4,2,2,8,8,128]{5,4,3,2,1,0:T(8,128)(2,1)S(1)}, bf16[4,2,2,8,8,128]{5,4,3,2,1,0:T(8,128)(2,1)S(1)}, u32[]{:S(2)}, u32[]{:S(2)}) collective-permute-start(bf16[4,2,2,8,8,128]{5,4,3,2,1,0:T(8,128)(2,1)S(1)} %get-tuple-element.30), channel_id=1, source_target_pairs={{0,2},{1,3},{2,0},{3,1},{4,6},{5,7},{6,4},{7,5},{8,10},{9,11},{10,... | collective-permute-start | bytes 786440 | tf_op jit(solution)/shard_map/ppermute | solution.py:315
  130.5 4.2 %collective-permute-done.8 = bf16[4,2,2,8,8,128]{5,4,3,2,1,0:T(8,128)(2,1)S(1)} collective-permute-done((bf16[4,2,2,8,8,128]{5,4,3,2,1,0:T(8,128)(2,1)S(1)}, bf16[4,2,2,8,8,128]{5,4,3,2,1,0:T(8,128)(2,1)S(1)}, u32[]{:S(2)}, u32[]{:S(2)}) %collective-permute-start.8) | collective-permute-done | bytes 262176 | tf_op jit(solution)/shard_map/ppermute | solution.py:315
  134.6 11.4 %collective-permute-done.7 = bf16[4,2,2,8,8,128]{5,4,3,2,1,0:T(8,128)(2,1)S(1)} collective-permute-done((bf16[4,2,2,8,8,128]{5,4,3,2,1,0:T(8,128)(2,1)S(1)}, bf16[4,2,2,8,8,128]{5,4,3,2,1,0:T(8,128)(2,1)S(1)}, u32[]{:S(2)}, u32[]{:S(2)}) %collective-permute-start.7) | collective-permute-done | bytes 262176 | tf_op jit(solution)/shard_map/ppermute | solution.py:315
  146.2 5.0 %collective-permute-start.9 = (bf16[2,2,8,8,128]{4,3,2,1,0:T(8,128)(2,1)S(1)}, bf16[2,2,8,8,128]{4,3,2,1,0:T(8,128)(2,1)S(1)}, u32[]{:S(2)}, u32[]{:S(2)}) collective-permute-start(bf16[2,2,8,8,128]{4,3,2,1,0:T(8,128)(2,1)S(1)} %get-tuple-element.40), channel_id=1, source_target_pairs={{0,12},{1,5},{2,14},{3,7},{4,0},{5,9},{6,2},{7,11},{8,4},{9,13},{1... | collective-permute-start | bytes 196616 | tf_op jit(solution)/shard_map/ppermute | solution.py:306
  151.3 4.2 %collective-permute-start.10 = (bf16[2,2,8,8,128]{4,3,2,1,0:T(8,128)(2,1)S(1)}, bf16[2,2,8,8,128]{4,3,2,1,0:T(8,128)(2,1)S(1)}, u32[]{:S(2)}, u32[]{:S(2)}) collective-permute-start(bf16[2,2,8,8,128]{4,3,2,1,0:T(8,128)(2,1)S(1)} %get-tuple-element.39), channel_id=1, source_target_pairs={{0,4},{1,13},{2,6},{3,15},{4,8},{5,1},{6,10},{7,3},{8,12},{9,5},{1... | collective-permute-start | bytes 196616 | tf_op jit(solution)/shard_map/ppermute | solution.py:301
  155.5 4.0 %collective-permute-start.11 = (bf16[2,2,8,8,128]{4,3,2,1,0:T(8,128)(2,1)S(1)}, bf16[2,2,8,8,128]{4,3,2,1,0:T(8,128)(2,1)S(1)}, u32[]{:S(2)}, u32[]{:S(2)}) collective-permute-start(bf16[2,2,8,8,128]{4,3,2,1,0:T(8,128)(2,1)S(1)} %get-tuple-element.38), channel_id=1, source_target_pairs={{0,11},{1,10},{2,9},{3,8},{4,15},{5,14},{6,13},{7,12},{8,3},{9,2},... | collective-permute-start | bytes 196616 | tf_op jit(solution)/shard_map/ppermute | solution.py:310
  159.6 1.8 collective-permute-done.10.from_minus
  161.3 5.2 %collective-permute-done.11.other_ref = bf16[2,2,8,8,128]{4,3,2,1,0:T(8,128)(2,1)S(1)} collective-permute-done((bf16[2,2,8,8,128]{4,3,2,1,0:T(8,128)(2,1)S(1)}, bf16[2,2,8,8,128]{4,3,2,1,0:T(8,128)(2,1)S(1)}, u32[]{:S(2)}, u32[]{:S(2)}) %collective-permute-start.11) | collective-permute-done | bytes 65568 | tf_op jit(solution)/shard_map/ppermute | solution.py:310
  166.5 1.4 kv_back.1
  167.9 7.7 %all-to-all-start.3 = ((bf16[32,2,2,2,4,128]{5,4,3,2,1,0:T(4,128)(2,1)}), bf16[32,2,2,2,4,128]{5,4,3,2,1,0:T(4,128)(2,1)S(1)}, u32[]{:S(2)}, u32[]{:S(2)}) async-start(bf16[32,2,2,2,4,128]{5,4,3,2,1,0:T(4,128)(2,1)} %bitcast.24), calls=%async_computation.3 | async-start | bytes 524288 | tf_op jit(solution)/shard_map/all_to_all | solution.py:336
  175.6 1.4 gather_fusion
  177.0 7.4 %all-to-all-done.3 = bf16[32,2,2,2,4,128]{5,4,3,2,1,0:T(4,128)(2,1)S(1)} async-done(((bf16[32,2,2,2,4,128]{5,4,3,2,1,0:T(4,128)(2,1)}), bf16[32,2,2,2,4,128]{5,4,3,2,1,0:T(4,128)(2,1)S(1)}, u32[]{:S(2)}, u32[]{:S(2)}) %all-to-all-start.3) | async-done | bytes 262176 | tf_op jit(solution)/shard_map/all_to_all | solution.py:336
  184.4 1.3 kv_final.1
  (41 shorter events, 9.6 us)
Async XLA Ops:
  0.6 0.9 copy-start.2
  1.5 0.7 copy-start.3
  3.7 19.3 %all-to-all-start = ((bf16[32,2,2,2,4,128]{5,4,3,2,1,0:T(4,128)(2,1)}), bf16[32,2,2,2,4,128]{5,4,3,2,1,0:T(4,128)(2,1)S(1)}, u32[]{:S(2)}, u32[]{:S(2)}) async-start(bf16[32,2,2,2,4,128]{5,4,3,2,1,0:T(4,128)(2,1)} %bitcast.8), calls=%async_computation | async-start | bytes 524288 | tf_op jit(solution)/shard_map/all_to_all | solution.py:336
  23.7 12.7 %collective-permute-start = (bf16[2,2,8,8,128]{4,3,2,1,0:T(8,128)(2,1)S(1)}, bf16[2,2,8,8,128]{4,3,2,1,0:T(8,128)(2,1)S(1)}, u32[]{:S(2)}, u32[]{:S(2)}) collective-permute-start(bf16[2,2,8,8,128]{4,3,2,1,0:T(8,128)(2,1)S(1)} %get-tuple-element.20), channel_id=1, source_target_pairs={{0,4},{1,13},{2,6},{3,15},{4,8},{5,1},{6,10},{7,3},{8,12},{9,5},{1... | collective-permute-start | bytes 196616 | tf_op jit(solution)/shard_map/ppermute | solution.py:301
  30.7 1.0 copy-start
  31.7 1.0 copy-start.1
  32.8 0.7 copy-start.4
  36.4 35.7 %copy-start.11 = (s32[1,16]{1,0:T(1,128)S(1)}, s32[1,16]{1,0:T(1,128)}, u32[]{:S(2)}) copy-start(s32[1,16]{1,0:T(1,128)} %param.11) | copy-start | bytes 196
  36.4 48.9 %all-to-all-start.1 = ((bf16[16,2,2,128,128]{4,3,2,1,0:T(8,128)(2,1)}), bf16[16,2,2,128,128]{4,3,2,1,0:T(8,128)(2,1)S(1)}, u32[]{:S(2)}, u32[]{:S(2)}) async-start(bf16[16,2,2,128,128]{4,3,2,1,0:T(8,128)(2,1)} %bitcast.10), calls=%async_computation.1 | async-start | bytes 4194304 | tf_op jit(solution)/shard_map/all_to_all | solution.py:351
  41.1 12.1 %collective-permute-start.2 = (bf16[2,2,8,8,128]{4,3,2,1,0:T(8,128)(2,1)S(1)}, bf16[2,2,8,8,128]{4,3,2,1,0:T(8,128)(2,1)S(1)}, u32[]{:S(2)}, u32[]{:S(2)}) collective-permute-start(bf16[2,2,8,8,128]{4,3,2,1,0:T(8,128)(2,1)S(1)} %get-tuple-element.25), channel_id=1, source_target_pairs={{0,11},{1,10},{2,9},{3,8},{4,15},{5,14},{6,13},{7,12},{8,3},{9,2},... | collective-permute-start | bytes 196616 | tf_op jit(solution)/shard_map/ppermute | solution.py:310
  50.9 9.8 %collective-permute-start.1 = (bf16[2,2,8,8,128]{4,3,2,1,0:T(8,128)(2,1)S(1)}, bf16[2,2,8,8,128]{4,3,2,1,0:T(8,128)(2,1)S(1)}, u32[]{:S(2)}, u32[]{:S(2)}) collective-permute-start(bf16[2,2,8,8,128]{4,3,2,1,0:T(8,128)(2,1)S(1)} %get-tuple-element.24), channel_id=1, source_target_pairs={{0,12},{1,5},{2,14},{3,7},{4,0},{5,9},{6,2},{7,11},{8,4},{9,13},{1... | collective-permute-start | bytes 196616 | tf_op jit(solution)/shard_map/ppermute | solution.py:306
  60.7 11.6 %collective-permute-start.3 = (bf16[4,2,2,8,8,128]{5,4,3,2,1,0:T(8,128)(2,1)S(1)}, bf16[4,2,2,8,8,128]{5,4,3,2,1,0:T(8,128)(2,1)S(1)}, u32[]{:S(2)}, u32[]{:S(2)}) collective-permute-start(bf16[4,2,2,8,8,128]{5,4,3,2,1,0:T(8,128)(2,1)S(1)} %pad_maximum_fusion.refs_0_), channel_id=1, source_target_pairs={{0,1},{1,2},{2,3},{3,0},{4,5},{5,6},{6,7},{7,4},{8,9},{9,10},{10,1... | collective-permute-start | bytes 786440 | tf_op jit(solution)/shard_map/ppermute | solution.py:315
  62.9 21.0 %collective-permute-start.4 = (bf16[4,2,2,8,8,128]{5,4,3,2,1,0:T(8,128)(2,1)S(1)}, bf16[4,2,2,8,8,128]{5,4,3,2,1,0:T(8,128)(2,1)S(1)}, u32[]{:S(2)}, u32[]{:S(2)}) collective-permute-start(bf16[4,2,2,8,8,128]{5,4,3,2,1,0:T(8,128)(2,1)S(1)} %pad_maximum_fusion.refs_0_), channel_id=1, source_target_pairs={{0,2},{1,3},{2,0},{3,1},{4,6},{5,7},{6,4},{7,5},{8,10},{9,11},{10,... | collective-permute-start | bytes 786440 | tf_op jit(solution)/shard_map/ppermute | solution.py:315
  67.9 16.8 %collective-permute-start.5 = (bf16[4,2,2,8,8,128]{5,4,3,2,1,0:T(8,128)(2,1)S(1)}, bf16[4,2,2,8,8,128]{5,4,3,2,1,0:T(8,128)(2,1)S(1)}, u32[]{:S(2)}, u32[]{:S(2)}) collective-permute-start(bf16[4,2,2,8,8,128]{5,4,3,2,1,0:T(8,128)(2,1)S(1)} %pad_maximum_fusion.refs_0_), channel_id=1, source_target_pairs={{0,3},{1,0},{2,1},{3,2},{4,7},{5,4},{6,5},{7,6},{8,11},{9,8},{10,9... | collective-permute-start | bytes 786440 | tf_op jit(solution)/shard_map/ppermute | solution.py:315
  83.9 0.7 copy-start.6
  84.6 0.7 copy-start.8
  85.3 1.0 copy-start.7
  86.3 0.9 copy-start.9
  98.9 31.4 %copy-start.10 = (s32[16,16]{1,0:T(8,128)S(1)}, s32[16,16]{1,0:T(8,128)}, u32[]{:S(2)}) copy-start(s32[16,16]{1,0:T(8,128)} %param.10) | copy-start | bytes 3076
  98.9 60.5 %copy-start.5 = (s32[1,16,2]{1,2,0:T(2,128)S(1)}, s32[1,16,2]{1,2,0:T(2,128)}, u32[]{:S(2)}) copy-start(s32[1,16,2]{1,2,0:T(2,128)} %param.9) | copy-start | bytes 388
  98.9 12.7 %collective-permute-start.6 = (bf16[4,2,2,8,8,128]{5,4,3,2,1,0:T(8,128)(2,1)S(1)}, bf16[4,2,2,8,8,128]{5,4,3,2,1,0:T(8,128)(2,1)S(1)}, u32[]{:S(2)}, u32[]{:S(2)}) collective-permute-start(bf16[4,2,2,8,8,128]{5,4,3,2,1,0:T(8,128)(2,1)S(1)} %get-tuple-element.27), channel_id=1, source_target_pairs={{0,3},{1,0},{2,1},{3,2},{4,7},{5,4},{6,5},{7,6},{8,11},{9,8},{10,9... | collective-permute-start | bytes 786440 | tf_op jit(solution)/shard_map/ppermute | solution.py:315
  111.6 54.9 %all-to-all-start.2 = ((bf16[16,2,128,128]{3,2,1,0:T(8,128)(2,1)}), bf16[16,2,128,128]{3,2,1,0:T(8,128)(2,1)S(1)}, u32[]{:S(2)}, u32[]{:S(2)}) async-start(bf16[16,2,128,128]{3,2,1,0:T(8,128)(2,1)} %bitcast.20), calls=%async_computation.2 | async-start | bytes 2097152 | tf_op jit(solution)/shard_map/all_to_all | solution.py:363
  122.1 12.5 %collective-permute-start.8 = (bf16[4,2,2,8,8,128]{5,4,3,2,1,0:T(8,128)(2,1)S(1)}, bf16[4,2,2,8,8,128]{5,4,3,2,1,0:T(8,128)(2,1)S(1)}, u32[]{:S(2)}, u32[]{:S(2)}) collective-permute-start(bf16[4,2,2,8,8,128]{5,4,3,2,1,0:T(8,128)(2,1)S(1)} %get-tuple-element.31), channel_id=1, source_target_pairs={{0,1},{1,2},{2,3},{3,0},{4,5},{5,6},{6,7},{7,4},{8,9},{9,10},{10,1... | collective-permute-start | bytes 786440 | tf_op jit(solution)/shard_map/ppermute | solution.py:315
  124.4 21.7 %collective-permute-start.7 = (bf16[4,2,2,8,8,128]{5,4,3,2,1,0:T(8,128)(2,1)S(1)}, bf16[4,2,2,8,8,128]{5,4,3,2,1,0:T(8,128)(2,1)S(1)}, u32[]{:S(2)}, u32[]{:S(2)}) collective-permute-start(bf16[4,2,2,8,8,128]{5,4,3,2,1,0:T(8,128)(2,1)S(1)} %get-tuple-element.30), channel_id=1, source_target_pairs={{0,2},{1,3},{2,0},{3,1},{4,6},{5,7},{6,4},{7,5},{8,10},{9,11},{10,... | collective-permute-start | bytes 786440 | tf_op jit(solution)/shard_map/ppermute | solution.py:315
  146.2 13.3 %collective-permute-start.9 = (bf16[2,2,8,8,128]{4,3,2,1,0:T(8,128)(2,1)S(1)}, bf16[2,2,8,8,128]{4,3,2,1,0:T(8,128)(2,1)S(1)}, u32[]{:S(2)}, u32[]{:S(2)}) collective-permute-start(bf16[2,2,8,8,128]{4,3,2,1,0:T(8,128)(2,1)S(1)} %get-tuple-element.40), channel_id=1, source_target_pairs={{0,12},{1,5},{2,14},{3,7},{4,0},{5,9},{6,2},{7,11},{8,4},{9,13},{1... | collective-permute-start | bytes 196616 | tf_op jit(solution)/shard_map/ppermute | solution.py:306
  151.3 10.1 %collective-permute-start.10 = (bf16[2,2,8,8,128]{4,3,2,1,0:T(8,128)(2,1)S(1)}, bf16[2,2,8,8,128]{4,3,2,1,0:T(8,128)(2,1)S(1)}, u32[]{:S(2)}, u32[]{:S(2)}) collective-permute-start(bf16[2,2,8,8,128]{4,3,2,1,0:T(8,128)(2,1)S(1)} %get-tuple-element.39), channel_id=1, source_target_pairs={{0,4},{1,13},{2,6},{3,15},{4,8},{5,1},{6,10},{7,3},{8,12},{9,5},{1... | collective-permute-start | bytes 196616 | tf_op jit(solution)/shard_map/ppermute | solution.py:301
  155.5 11.0 %collective-permute-start.11 = (bf16[2,2,8,8,128]{4,3,2,1,0:T(8,128)(2,1)S(1)}, bf16[2,2,8,8,128]{4,3,2,1,0:T(8,128)(2,1)S(1)}, u32[]{:S(2)}, u32[]{:S(2)}) collective-permute-start(bf16[2,2,8,8,128]{4,3,2,1,0:T(8,128)(2,1)S(1)} %get-tuple-element.38), channel_id=1, source_target_pairs={{0,11},{1,10},{2,9},{3,8},{4,15},{5,14},{6,13},{7,12},{8,3},{9,2},... | collective-permute-start | bytes 196616 | tf_op jit(solution)/shard_map/ppermute | solution.py:310
  167.9 16.5 %all-to-all-start.3 = ((bf16[32,2,2,2,4,128]{5,4,3,2,1,0:T(4,128)(2,1)}), bf16[32,2,2,2,4,128]{5,4,3,2,1,0:T(4,128)(2,1)S(1)}, u32[]{:S(2)}, u32[]{:S(2)}) async-start(bf16[32,2,2,2,4,128]{5,4,3,2,1,0:T(4,128)(2,1)} %bitcast.24), calls=%async_computation.3 | async-start | bytes 524288 | tf_op jit(solution)/shard_map/all_to_all | solution.py:336

commit v5 on v2

v5 whole, which is shorter than its diff:
```python
import functools

import jax
import jax.numpy as jnp
from jax import lax
from jax.experimental import pallas as pl
from jax.experimental.pallas import tpu as pltpu
from jax.sharding import Mesh
from jax.sharding import PartitionSpec as P

HD = 128
KV = 4
PAIR = 2
SCALING = HD ** (-0.5)
LOG2E = 1.4426950408889634
PLANE = ("dp", "xh")
NEAR = 4


def matmul(a, b, contract):
    return lax.dot_general(a, b, (contract, ((), ())), preferred_element_type=jnp.float32)


def pack_kernel(index_ref, q_ref, g_ref, out_ref):
    def body(slot, _):
        tile = index_ref[slot & 1, slot >> 1]
        out_ref[slot, 0] = q_ref[tile]
        out_ref[slot, 1] = g_ref[tile]
        return 0

    lax.fori_loop(0, out_ref.shape[0], body, 0)


def pack(index, queries, grad_out):
    slots = index.size
    return pl.pallas_call(
        pack_kernel,
        out_shape=jax.ShapeDtypeStruct((slots, 2) + queries.shape[1:], queries.dtype),
        in_specs=[
            pl.BlockSpec(memory_space=pltpu.SMEM),
            pl.BlockSpec(memory_space=pltpu.VMEM),
            pl.BlockSpec(memory_space=pltpu.VMEM),
        ],
        out_specs=pl.BlockSpec(memory_space=pltpu.VMEM),
        compiler_params=pltpu.CompilerParams(vmem_limit_bytes=24 * 2**20),
        name="pack_rows",
    )(index, queries, grad_out)


def attention_kernel(
    recv_ref, start_ref, place_ref, qg_ref, kv0, kv1, kv2, kv3, dq_ref, dkv0, dkv1, dkv2, dkv3,
    qg_all, k_all, kt_all, v_all, dk_all, dv_all, weights_all, dprobs_all, peaks, dqt, arrived,
):
    blocks = k_all.shape[0]
    width = k_all.shape[1]
    tile_rows = width // PAIR
    part = width // NEAR
    factor = SCALING * LOG2E

    def tile_copy(tile, kind):
        return pltpu.make_async_copy(
            qg_ref.at[recv_ref[tile], kind], qg_all.at[kind, tile], arrived.at[kind, tile]
        )

    def fetch(tile, _):
        tile_copy(tile, 0).start()
        tile_copy(tile, 1).start()
        return 0

    lax.fori_loop(0, PAIR * blocks, fetch, 0)

    def stage(block, _):
        for slot, ref in enumerate((kv0, kv1, kv2, kv3)):
            rows = slice(slot * part, (slot + 1) * part)
            key = ref[:, :, 0, block].astype(jnp.float32).reshape(part, HD)
            value = ref[:, :, 1, block].astype(jnp.float32).reshape(part, HD)
            k_all[block, rows] = key.astype(jnp.bfloat16)
            v_all[block, rows] = value.astype(jnp.bfloat16)
        kt_all[block] = k_all[block].astype(jnp.float32).T.astype(jnp.bfloat16)
        return 0

    lax.fori_loop(0, blocks, stage, 0)

    row = lax.broadcasted_iota(jnp.int32, (width, 1), 0)
    holder = (place_ref[0] & 12) | ((place_ref[0] - (row >> 6)) & 3)
    group = jnp.where(holder < 8, holder, 3 - holder) & 3
    origin = (row >> 4) & 3
    source = origin * 4 + jnp.where(origin < 2, group, 3 - group)
    key_offset = (
        ((row >> 2) & 1) * tile_rows + ((row >> 3) & 1) * 64 + source * 4 + (row & 3)
    )
    lane = lax.broadcasted_iota(jnp.int32, (1, width), 1)

    def query_block(block, _):
        for tile in (PAIR * block, PAIR * block + 1):
            tile_copy(tile, 0).wait()
            tile_copy(tile, 1).wait()
        tiles = pl.ds(PAIR * block, PAIR)
        query = qg_all[0, tiles].reshape(width, HD)
        grad = qg_all[1, tiles].reshape(width, HD)
        start_low = start_ref[PAIR * block]
        start_high = start_ref[PAIR * block + 1]
        lowest = start_low // PAIR
        row_start = jnp.where(lane < tile_rows, start_low, start_high) * tile_rows

        def products(other, masked_by_order):
            score = matmul(k_all[other], query, ((1,), (1,)))
            dprobs = matmul(v_all[other], grad, ((1,), (1,)))
            allowed = key_offset >= row_start - other * width
            if masked_by_order:
                allowed = allowed & (key_offset <= lane)
            score = jnp.where(allowed, score, -jnp.inf)
            peak = jnp.maximum(jnp.max(score, axis=0, keepdims=True), -1e30)
            weights = jnp.exp2(score * factor - peak * factor)
            weights_all[other] = weights
            dprobs_all[other] = dprobs
            peaks[other] = jnp.broadcast_to(peak, peaks.shape[1:])
            total = jnp.sum(weights, axis=0, keepdims=True)
            weighted = jnp.sum(weights * dprobs, axis=0, keepdims=True)
            return peak, total, weighted

        def merge(other, state):
            peak, total, weighted = state
            new_peak, new_total, new_weighted = products(other, False)
            top = jnp.maximum(peak, new_peak)
            old, new = jnp.exp2((peak - top) * factor), jnp.exp2((new_peak - top) * factor)
            return top, total * old + new_total * new, weighted * old + new_weighted * new

        peak, total, weighted = lax.fori_loop(lowest, block, merge, products(block, True))
        inverse = 1.0 / total
        delta = weighted * inverse

        def terms(other):
            scale = jnp.exp2((peaks[other][:1] - peak) * factor) * inverse
            probs = weights_all[other] * scale
            dscores = (probs * (dprobs_all[other] - delta)).astype(jnp.bfloat16)
            grad_value = matmul(probs.astype(jnp.bfloat16), grad, ((1,), (0,)))
            grad_key = matmul(dscores, query, ((1,), (0,)))
            grad_query = matmul(kt_all[other], dscores, ((1,), (0,)))
            return grad_key, grad_value, grad_query

        grad_key, grad_value, grad_query = terms(block)
        dk_all[block] = grad_key
        dv_all[block] = grad_value
        dqt[...] = grad_query

        def earlier(other, _):
            grad_key, grad_value, grad_query = terms(other)
            dk_all[other] += grad_key
            dv_all[other] += grad_value
            dqt[...] += grad_query
            return 0

        lax.fori_loop(lowest, block, earlier, 0)
        result = (dqt[...] * SCALING).T.astype(jnp.bfloat16)
        dq_ref[recv_ref[PAIR * block]] = result[:tile_rows]
        dq_ref[recv_ref[PAIR * block + 1]] = result[tile_rows:]
        return 0

    lax.fori_loop(0, blocks, query_block, 0)

    def unstage(block, _):
        for slot, ref in enumerate((dkv0, dkv1, dkv2, dkv3)):
            rows = slice(slot * part, (slot + 1) * part)
            shape = ref.shape[:2] + ref.shape[4:]
            ref[:, :, 0, block] = (dk_all[block, rows] * SCALING).reshape(shape).astype(jnp.bfloat16)
            ref[:, :, 1, block] = dv_all[block, rows].reshape(shape).astype(jnp.bfloat16)
        return 0

    lax.fori_loop(0, blocks, unstage, 0)


def attention(my_recv, start, place, qg, chunks):
    slots, _, tile_rows, _ = qg.shape
    blocks = my_recv.shape[0] // PAIR
    width = PAIR * tile_rows
    vmem = pl.BlockSpec(memory_space=pltpu.VMEM)
    smem = pl.BlockSpec(memory_space=pltpu.SMEM)
    return pl.pallas_call(
        attention_kernel,
        out_shape=(jax.ShapeDtypeStruct((slots, tile_rows, HD), jnp.bfloat16),)
        + (jax.ShapeDtypeStruct(chunks[0].shape, jnp.bfloat16),) * NEAR,
        in_specs=[smem] * 3 + [pl.BlockSpec(memory_space=pl.ANY)] + [vmem] * NEAR,
        out_specs=(vmem,) * (1 + NEAR),
        scratch_shapes=[
            pltpu.VMEM((2, PAIR * blocks, tile_rows, HD), jnp.bfloat16),
            pltpu.VMEM((blocks, width, HD), jnp.bfloat16),
            pltpu.VMEM((blocks, HD, width), jnp.bfloat16),
            pltpu.VMEM((blocks, width, HD), jnp.bfloat16),
            pltpu.VMEM((blocks, width, HD), jnp.float32),
            pltpu.VMEM((blocks, width, HD), jnp.float32),
            pltpu.VMEM((blocks, width, width), jnp.float32),
            pltpu.VMEM((blocks, width, width), jnp.float32),
            pltpu.VMEM((blocks, 8, width), jnp.float32),
            pltpu.VMEM((HD, width), jnp.float32),
            pltpu.SemaphoreType.DMA((2, PAIR * blocks)),
        ],
        compiler_params=pltpu.CompilerParams(vmem_limit_bytes=24 * 2**20),
        cost_estimate=pl.CostEstimate(
            flops=2 * 10**9, bytes_accessed=6 * 2**20, transcendentals=2 * 10**6
        ),
        name="attention_backward",
    )(my_recv, start, place, qg, *chunks)


def kv_pack_kernel(index_ref, kv_ref, out_ref):
    def body(slot, _):
        tile = index_ref[slot & 1, slot >> 1]
        piece = kv_ref[tile].reshape((2, 2, 2) + kv_ref.shape[2:])
        for half in range(2):
            out_ref[slot >> 1, half, slot & 1] = piece[:, half]
        return 0

    lax.fori_loop(0, 2 * index_ref.shape[1], body, 0, unroll=4)


def kv_unpack_kernel(recv_ref, kv_ref, out_ref):
    def body(pair, _):
        slots = (recv_ref[PAIR * pair], recv_ref[PAIR * pair + 1])
        for half in range(2):
            for kind in range(2):
                for head in range(2):
                    rows = [
                        kv_ref[slot >> 1, half, slot & 1, kind, head].astype(jnp.float32)
                        for slot in slots
                    ]
                    both = jnp.concatenate(rows, axis=0).astype(jnp.bfloat16)
                    out_ref[2 * head, half, kind, pair] = both
                    out_ref[2 * head + 1, half, kind, pair] = both
        return 0

    lax.fori_loop(0, recv_ref.shape[0] // PAIR, body, 0)


def kv_back_kernel(recv_ref, terms_ref, out_ref):
    sliver = out_ref.shape[-2]

    def body(pair, _):
        slots = (recv_ref[PAIR * pair], recv_ref[PAIR * pair + 1])
        for half in range(2):
            for kind in range(2):
                for head in range(2):
                    total = terms_ref[2 * head, half, kind, pair].astype(jnp.float32)
                    total += terms_ref[2 * head + 1, half, kind, pair].astype(jnp.float32)
                    for order, slot in enumerate(slots):
                        rows = total[order * sliver : (order + 1) * sliver]
                        out_ref[slot >> 1, half, slot & 1, kind, head] = rows.astype(jnp.bfloat16)
        return 0

    lax.fori_loop(0, recv_ref.shape[0] // PAIR, body, 0)


def kv_final_kernel(anchor_ref, kv_ref, out_ref):
    def body(tile, _):
        slot = anchor_ref[tile]
        piece = kv_ref[slot >> 1, :, slot & 1]
        for half in range(2):
            for kind in range(2):
                for head in range(2):
                    out_ref[tile, kind * 4 + half * 2 + head] = piece[half, kind, head]
        return 0

    lax.fori_loop(0, anchor_ref.shape[0], body, 0)


def local_call(kernel, name, scalars, arrays, out_shape):
    vmem = pl.BlockSpec(memory_space=pltpu.VMEM)
    smem = pl.BlockSpec(memory_space=pltpu.SMEM)
    return pl.pallas_call(
        kernel,
        out_shape=out_shape,
        in_specs=[smem] * len(scalars) + [vmem] * len(arrays),
        out_specs=jax.tree.map(lambda _: vmem, out_shape),
        compiler_params=pltpu.CompilerParams(vmem_limit_bytes=16 * 2**20),
        name=name,
    )(*scalars, *arrays)


def between_cubes(values):
    groups = [[base, base + 4, 11 - base, 15 - base] for base in range(4)]
    return lax.all_to_all(
        values, "z", split_axis=0, concat_axis=0, axis_index_groups=groups, tiled=True
    )


def near_shift(values, step):
    pairs = [(place, (place & 12) | ((place + step) & 3)) for place in range(16)]
    return lax.ppermute(values, "z", pairs)


def on_device(queries, keys_values, grad_out, send_tiles, recv_slot, tile_seq):
    n_replicas = lax.axis_size("dp")
    replica = lax.axis_index("dp")
    tile_count, tile_rows, row_width = queries.shape
    sliver = keys_values.shape[1]
    slot_cap = send_tiles.shape[2]
    slots = n_replicas * slot_cap
    pairs = tile_count // PAIR
    my_send = send_tiles[0]
    outgoing = my_send.T
    my_recv = lax.dynamic_index_in_dim(recv_slot, replica, 0, keepdims=False)
    place = lax.axis_index("z").astype(jnp.int32).reshape(1)
    traveling = jax.ShapeDtypeStruct(
        (n_replicas, 2, slot_cap, 2, 2, sliver, HD), keys_values.dtype
    )
    far_shape = jax.ShapeDtypeStruct((4, 2, 2, pairs, PAIR * sliver, HD), keys_values.dtype)

    def over_plane(values):
        return lax.all_to_all(
            values.reshape((2 * n_replicas,) + values.shape[2:]),
            PLANE, split_axis=0, concat_axis=0, tiled=True,
        ).reshape(values.shape)

    kv_blocks = keys_values.reshape(tile_count, sliver, 2 * KV, HD).transpose(0, 2, 1, 3)
    kv_arrived = over_plane(
        local_call(kv_pack_kernel, "kv_pack", [outgoing], [kv_blocks], traveling)
    )
    mine = between_cubes(
        local_call(kv_unpack_kernel, "kv_unpack", [my_recv], [kv_arrived], far_shape)
    )
    qg_packed = pack(outgoing, queries, grad_out)
    qg_arrived = lax.all_to_all(
        qg_packed.reshape(n_replicas, slot_cap, 2, tile_rows, row_width),
        "dp", split_axis=0, concat_axis=0, tiled=True,
    ).reshape(slots, 2, tile_rows, row_width)
    chunks = [mine] + [near_shift(mine, step) for step in range(1, NEAR)]

    seq = tile_seq[0]
    start = jnp.sum((seq[None, :] < seq[:, None]).astype(jnp.int32), axis=1)
    query_back, *terms = attention(my_recv, start, place, qg_arrived, chunks)
    near = [terms[0]] + [near_shift(terms[step], -step) for step in range(1, NEAR)]
    query_returned = lax.all_to_all(
        query_back.reshape(n_replicas, slot_cap, tile_rows, row_width),
        "dp", split_axis=0, concat_axis=0, tiled=True,
    )
    near_sum = sum(term.astype(jnp.float32) for term in near).astype(jnp.bfloat16)
    near_sum, query_returned = lax.optimization_barrier((near_sum, query_returned))
    far = between_cubes(near_sum)
    kv_returned = over_plane(
        local_call(kv_back_kernel, "kv_back", [my_recv], [far], traveling)
    )

    flat_slots = jnp.arange(slots)
    own_slots = replica * slot_cap + jnp.arange(slot_cap)
    slot_used = jnp.any(recv_slot[:, None, :] == own_slots[None, :, None], axis=2)
    matched = slot_used[:, :, None] & (my_send[:, :, None] == jnp.arange(tile_count)[None, None, :])
    anchor = jnp.sum(
        jnp.where(matched, flat_slots.reshape(n_replicas, slot_cap)[:, :, None], 0), axis=(0, 1)
    )
    grad_queries = query_returned.reshape(slots, tile_rows, row_width)[anchor]
    kv_final = local_call(
        kv_final_kernel, "kv_final", [anchor], [kv_returned],
        jax.ShapeDtypeStruct(kv_blocks.shape, keys_values.dtype),
    )
    grad_keys_values = kv_final.transpose(0, 2, 1, 3).reshape(keys_values.shape)
    return (grad_queries, grad_keys_values)


def solution(mesh):
    fine = Mesh(mesh.devices.reshape(mesh.devices.shape[0], 2, 16), ("dp", "xh", "z"))
    tensor = ("xh", "z")
    in_specs = (
        P("dp", None, tensor),
        P("dp", tensor, None),
        P("dp", None, tensor),
        P("dp", None, None),
        P(),
        P("dp", None),
    )
    out_specs = (P("dp", None, tensor), P("dp", tensor, None))
    return jax.shard_map(
        on_device, mesh=fine, in_specs=in_specs, out_specs=out_specs, check_vma=False
    )
```

time: 231 us -> 181 us (0.78)
  waiting for transfers between devices: 129 us -> 62.4 us
  starting transfers between devices: 58.2 us -> 84 us
  between operations: 14.2 us -> 0.82 us
  Pallas kernels: 19.3 us -> 24.4 us
    all_gather x1 -> x0, waiting for transfers between devices: 59.8 us -> none  [on_device(): kv_all = lax.all_gather(jnp.stack([own, mirrored]), LINE)]
    reduce_scatter x1 -> x0, waiting for transfers between devices: 34.5 us -> none  [on_device(): summed = lax.psum_scatter(dkv, LINE, scatter_dimension=0)]
    all_to_all x0 -> x2, starting transfers between devices: none -> 20.9 us  [between_cubes(): lax.all_to_all(values, 'z', split_axis=0, concat_axis=0, axis_index_group...]
    all_to_all x0 -> x2, waiting for transfers between devices: none -> 20.6 us  [between_cubes(): lax.all_to_all(values, 'z', split_axis=0, concat_axis=0, axis_index_group...]
    ppermute x2 -> x6, waiting for transfers between devices: 3.59 us -> 23.3 us  [near_shift(): return lax.ppermute(values, 'z', pairs)]
    all_to_all x1, waiting for transfers between devices: 15.7 us -> 0.01 us  [on_device(): lax.all_to_all(query_back.reshape(n_replicas, slot_cap, tile_rows, row_wi...]
    ppermute x2 -> x6, starting transfers between devices: 14.1 us -> 26.9 us  [near_shift(): return lax.ppermute(values, 'z', pairs)]
    all_to_all x1, starting transfers between devices: 14.2 us -> 5.96 us  [on_device(): lax.all_to_all(query_back.reshape(n_replicas, slot_cap, tile_rows, row_wi...]
  transfers between devices with their start and end apart: 8 -> 12, of which waited for: 7 -> 8; matrix products, arithmetic and copies ran while one was open for 1% -> 2% of each run, Pallas kernels for 1% -> 1%
where the time goes in v5:
time: 181 us; the launch traced here: 180 us
  starting transfers between devices  84 us (46%)
  waiting for transfers between devices  62.4 us (34%)
  Pallas kernels  24.4 us (13%)
  local copies, waits for them, and re-layouts  7.51 us (4%)
    ppermute x6, starting transfers between devices, near_shift(): return lax.ppermute(values, 'z', pairs)  26.9 us
    ppermute x6, waiting for transfers between devices, near_shift(): return lax.ppermute(values, 'z', pairs)  23.3 us
    all_to_all x2, starting transfers between devices, over_plane(): lax.all_to_all(values.reshape((2 * n_replicas,) + values.shape[2:]), PLAN...  23 us
    all_to_all x2, starting transfers between devices, between_cubes(): lax.all_to_all(values, 'z', split_axis=0, concat_axis=0, axis_index_group...  20.9 us
    all_to_all x2, waiting for transfers between devices, between_cubes(): lax.all_to_all(values, 'z', split_axis=0, concat_axis=0, axis_index_group...  20.6 us
    pallas_call x1, Pallas kernels, attention(): pl.pallas_call(attention_kernel, out_shape=(jax.ShapeDtypeStruct((slots,...  16.6 us
    all_to_all x2, waiting for transfers between devices, over_plane(): lax.all_to_all(values.reshape((2 * n_replicas,) + values.shape[2:]), PLAN...  15.6 us
    all_to_all x1, starting transfers between devices, on_device(): lax.all_to_all(qg_packed.reshape(n_replicas, slot_cap, 2, tile_rows, row_...  7.24 us
  transfers between devices with their start and end apart: 12, of which 8 were waited for; matrix products, arithmetic and copies ran while one was open for 2% of the time, Pallas kernels for 1%

profile of v5, /device:TPU:1, one launch (start us, length us, event | category | flops | bytes accessed | tf_op | source)
XLA Modules:
  0.0 180.5 jit_solution(4262906442315184728)
XLA Ops:
  0.7 1.0 copy-done.2
  2.3 1.4 kv_pack.1
  3.8 10.4 %all-to-all-start.1 = ((bf16[32,2,2,2,4,128]{5,4,3,2,1,0:T(4,128)(2,1)}), bf16[32,2,2,2,4,128]{5,4,3,2,1,0:T(4,128)(2,1)S(1)}, u32[]{:S(2)}, u32[]{:S(2)}) async-start(bf16[32,2,2,2,4,128]{5,4,3,2,1,0:T(4,128)(2,1)} %bitcast.10), calls=%async_computation.1 | async-start | bytes 524288 | tf_op jit(solution)/shard_map/all_to_all | solution.py:309
  14.9 8.2 %all-to-all-done.1 = bf16[32,2,2,2,4,128]{5,4,3,2,1,0:T(4,128)(2,1)S(1)} async-done(((bf16[32,2,2,2,4,128]{5,4,3,2,1,0:T(4,128)(2,1)}), bf16[32,2,2,2,4,128]{5,4,3,2,1,0:T(4,128)(2,1)S(1)}, u32[]{:S(2)}, u32[]{:S(2)}) %all-to-all-start.1) | async-done | bytes 262176 | tf_op jit(solution)/shard_map/all_to_all | solution.py:309
  23.1 1.4 kv_unpack.1
  24.5 11.6 %all-to-all-start.2 = ((bf16[4,2,2,8,8,128]{5,4,3,2,1,0:T(8,128)(2,1)}), bf16[4,2,2,8,8,128]{5,4,3,2,1,0:T(8,128)(2,1)S(1)}, u32[]{:S(2)}, u32[]{:S(2)}) async-start(bf16[4,2,2,8,8,128]{5,4,3,2,1,0:T(8,128)(2,1)} %kv_unpack.1), calls=%async_computation.2 | async-start | bytes 524288 | tf_op jit(solution)/shard_map/all_to_all | solution.py:281
  36.8 2.3 %pack_rows.1 = bf16[32,2,128,128]{3,2,1,0:T(8,128)(2,1)} custom-call(s32[2,16]{1,0:T(2,128)S(1)} %bitcast.30, bf16[16,128,128]{2,1,0:T(8,128)(2,1)S(1)} %copy-done, bf16[16,128,128]{2,1,0:T(8,128)(2,1)S(1)} %copy-done.1), custom_call_target="tpu_custom_call" | custom-call | tf_op jit(solution)/shard_map/pack_rows/pallas_call | solution.py:36
  39.0 8.8 %all-to-all-done.2.kv0 = bf16[4,2,2,8,8,128]{5,4,3,2,1,0:T(8,128)(2,1)S(1)} async-done(((bf16[4,2,2,8,8,128]{5,4,3,2,1,0:T(8,128)(2,1)}), bf16[4,2,2,8,8,128]{5,4,3,2,1,0:T(8,128)(2,1)S(1)}, u32[]{:S(2)}, u32[]{:S(2)}) %all-to-all-start.2) | async-done | bytes 262176 | tf_op jit(solution)/shard_map/all_to_all | solution.py:281
  47.8 7.2 %all-to-all-start = ((bf16[16,2,2,128,128]{4,3,2,1,0:T(8,128)(2,1)}), bf16[16,2,2,128,128]{4,3,2,1,0:T(8,128)(2,1)S(1)}, u32[]{:S(2)}, u32[]{:S(2)}) async-start(bf16[16,2,2,128,128]{4,3,2,1,0:T(8,128)(2,1)} %bitcast.5), calls=%async_computation | async-start | bytes 4194304 | tf_op jit(solution)/shard_map/all_to_all | solution.py:322
  55.1 7.5 %collective-permute-start = (bf16[4,2,2,8,8,128]{5,4,3,2,1,0:T(8,128)(2,1)S(1)}, bf16[4,2,2,8,8,128]{5,4,3,2,1,0:T(8,128)(2,1)S(1)}, u32[]{:S(2)}, u32[]{:S(2)}) collective-permute-start(bf16[4,2,2,8,8,128]{5,4,3,2,1,0:T(8,128)(2,1)S(1)} %all-to-all-done.2.kv0), channel_id=1, source_target_pairs={{0,1},{1,2},{2,3},{3,0},{4,5},{5,6},{6,7},{7,4},{8,9},{9,10},{10,1... | collective-permute-start | bytes 786440 | tf_op jit(solution)/shard_map/ppermute | solution.py:288
  62.6 1.9 %collective-permute-start.1 = (bf16[4,2,2,8,8,128]{5,4,3,2,1,0:T(8,128)(2,1)S(1)}, bf16[4,2,2,8,8,128]{5,4,3,2,1,0:T(8,128)(2,1)S(1)}, u32[]{:S(2)}, u32[]{:S(2)}) collective-permute-start(bf16[4,2,2,8,8,128]{5,4,3,2,1,0:T(8,128)(2,1)S(1)} %all-to-all-done.2.kv0), channel_id=1, source_target_pairs={{0,2},{1,3},{2,0},{3,1},{4,6},{5,7},{6,4},{7,5},{8,10},{9,11},{10,... | collective-permute-start | bytes 786440 | tf_op jit(solution)/shard_map/ppermute | solution.py:288
  64.5 4.0 %collective-permute-start.2 = (bf16[4,2,2,8,8,128]{5,4,3,2,1,0:T(8,128)(2,1)S(1)}, bf16[4,2,2,8,8,128]{5,4,3,2,1,0:T(8,128)(2,1)S(1)}, u32[]{:S(2)}, u32[]{:S(2)}) collective-permute-start(bf16[4,2,2,8,8,128]{5,4,3,2,1,0:T(8,128)(2,1)S(1)} %all-to-all-done.2.kv0), channel_id=1, source_target_pairs={{0,3},{1,0},{2,1},{3,2},{4,7},{5,4},{6,5},{7,6},{8,11},{9,8},{10,9... | collective-permute-start | bytes 786440 | tf_op jit(solution)/shard_map/ppermute | solution.py:288
  68.7 11.0 %collective-permute-done.1.kv2 = bf16[4,2,2,8,8,128]{5,4,3,2,1,0:T(8,128)(2,1)S(1)} collective-permute-done((bf16[4,2,2,8,8,128]{5,4,3,2,1,0:T(8,128)(2,1)S(1)}, bf16[4,2,2,8,8,128]{5,4,3,2,1,0:T(8,128)(2,1)S(1)}, u32[]{:S(2)}, u32[]{:S(2)}) %collective-permute-start.1) | collective-permute-done | bytes 262176 | tf_op jit(solution)/shard_map/ppermute | solution.py:288
  79.7 0.7 copy-done.8
  80.4 2.8 %all-to-all-done = bf16[16,2,2,128,128]{4,3,2,1,0:T(8,128)(2,1)S(1)} async-done(((bf16[16,2,2,128,128]{4,3,2,1,0:T(8,128)(2,1)}), bf16[16,2,2,128,128]{4,3,2,1,0:T(8,128)(2,1)S(1)}, u32[]{:S(2)}, u32[]{:S(2)}) %all-to-all-start) | async-done | bytes 2097184 | tf_op jit(solution)/shard_map/all_to_all | solution.py:322
  83.2 0.9 copy-done.9
  84.2 16.6 %attention_backward.1 = (bf16[32,128,128]{2,1,0:T(8,128)(2,1)}, bf16[4,2,2,8,8,128]{5,4,3,2,1,0:T(8,128)(2,1)S(1)}, bf16[4,2,2,8,8,128]{5,4,3,2,1,0:T(8,128)(2,1...) custom-call(s32[16]{0:T(128)S(1)} %dynamic-slice_bitcast_fusion.recv_ref, ...), custom_call_target="tpu_custom_call" | custom-call | flops 2000000000 | bytes 6291456 | tf_op jit(solution)/shard_map/attention_backward/pallas_call | solution.py:179
  101.5 0.7 copy-done.10
  102.2 6.0 %all-to-all-start.3 = ((bf16[16,2,128,128]{3,2,1,0:T(8,128)(2,1)}), bf16[16,2,128,128]{3,2,1,0:T(8,128)(2,1)S(1)}, u32[]{:S(2)}, u32[]{:S(2)}) async-start(bf16[16,2,128,128]{3,2,1,0:T(8,128)(2,1)} %bitcast.12), calls=%async_computation.3 | async-start | bytes 2097152 | tf_op jit(solution)/shard_map/all_to_all | solution.py:332
  108.2 7.6 %collective-permute-start.5 = (bf16[4,2,2,8,8,128]{5,4,3,2,1,0:T(8,128)(2,1)S(1)}, bf16[4,2,2,8,8,128]{5,4,3,2,1,0:T(8,128)(2,1)S(1)}, u32[]{:S(2)}, u32[]{:S(2)}) collective-permute-start(bf16[4,2,2,8,8,128]{5,4,3,2,1,0:T(8,128)(2,1)S(1)} %copy-done.11), channel_id=1, source_target_pairs={{0,1},{1,2},{2,3},{3,0},{4,5},{5,6},{6,7},{7,4},{8,9},{9,10},{10,1... | collective-permute-start | bytes 786440 | tf_op jit(solution)/shard_map/ppermute | solution.py:288
  115.8 2.4 %collective-permute-start.4 = (bf16[4,2,2,8,8,128]{5,4,3,2,1,0:T(8,128)(2,1)S(1)}, bf16[4,2,2,8,8,128]{5,4,3,2,1,0:T(8,128)(2,1)S(1)}, u32[]{:S(2)}, u32[]{:S(2)}) collective-permute-start(bf16[4,2,2,8,8,128]{5,4,3,2,1,0:T(8,128)(2,1)S(1)} %copy-done.7), channel_id=1, source_target_pairs={{0,2},{1,3},{2,0},{3,1},{4,6},{5,7},{6,4},{7,5},{8,10},{9,11},{10,... | collective-permute-start | bytes 786440 | tf_op jit(solution)/shard_map/ppermute | solution.py:288
  118.2 3.5 %collective-permute-start.3 = (bf16[4,2,2,8,8,128]{5,4,3,2,1,0:T(8,128)(2,1)S(1)}, bf16[4,2,2,8,8,128]{5,4,3,2,1,0:T(8,128)(2,1)S(1)}, u32[]{:S(2)}, u32[]{:S(2)}) collective-permute-start(bf16[4,2,2,8,8,128]{5,4,3,2,1,0:T(8,128)(2,1)S(1)} %get-tuple-element.10), channel_id=1, source_target_pairs={{0,3},{1,0},{2,1},{3,2},{4,7},{5,4},{6,5},{7,6},{8,11},{9,8},{10,9... | collective-permute-start | bytes 786440 | tf_op jit(solution)/shard_map/ppermute | solution.py:288
  121.7 0.9 collective-permute-done.5
  122.6 11.5 %collective-permute-done.4 = bf16[4,2,2,8,8,128]{5,4,3,2,1,0:T(8,128)(2,1)S(1)} collective-permute-done((bf16[4,2,2,8,8,128]{5,4,3,2,1,0:T(8,128)(2,1)S(1)}, bf16[4,2,2,8,8,128]{5,4,3,2,1,0:T(8,128)(2,1)S(1)}, u32[]{:S(2)}, u32[]{:S(2)}) %collective-permute-start.4) | collective-permute-done | bytes 262176 | tf_op jit(solution)/shard_map/ppermute | solution.py:288
  134.0 0.9 add_convert_fusion
  134.9 9.3 %all-to-all-start.4 = ((bf16[4,2,2,8,8,128]{5,4,3,2,1,0:T(8,128)(2,1)}), bf16[4,2,2,8,8,128]{5,4,3,2,1,0:T(8,128)(2,1)S(1)}, u32[]{:S(2)}, u32[]{:S(2)}) async-start(bf16[4,2,2,8,8,128]{5,4,3,2,1,0:T(8,128)(2,1)} %add_convert_fusion), calls=%async_computation.4 | async-start | bytes 524288 | tf_op jit(solution)/shard_map/all_to_all | solution.py:281
  144.5 11.8 %all-to-all-done.4.terms_ref = bf16[4,2,2,8,8,128]{5,4,3,2,1,0:T(8,128)(2,1)S(1)} async-done(((bf16[4,2,2,8,8,128]{5,4,3,2,1,0:T(8,128)(2,1)}), bf16[4,2,2,8,8,128]{5,4,3,2,1,0:T(8,128)(2,1)S(1)}, u32[]{:S(2)}, u32[]{:S(2)}) %all-to-all-start.4) | async-done | bytes 262176 | tf_op jit(solution)/shard_map/all_to_all | solution.py:281
  156.3 1.4 kv_back.1
  157.7 12.6 %all-to-all-start.5 = ((bf16[32,2,2,2,4,128]{5,4,3,2,1,0:T(4,128)(2,1)}), bf16[32,2,2,2,4,128]{5,4,3,2,1,0:T(4,128)(2,1)S(1)}, u32[]{:S(2)}, u32[]{:S(2)}) async-start(bf16[32,2,2,2,4,128]{5,4,3,2,1,0:T(4,128)(2,1)} %bitcast.16), calls=%async_computation.5 | async-start | bytes 524288 | tf_op jit(solution)/shard_map/all_to_all | solution.py:309
  170.3 1.4 gather_fusion
  171.7 7.4 %all-to-all-done.5 = bf16[32,2,2,2,4,128]{5,4,3,2,1,0:T(4,128)(2,1)S(1)} async-done(((bf16[32,2,2,2,4,128]{5,4,3,2,1,0:T(4,128)(2,1)}), bf16[32,2,2,2,4,128]{5,4,3,2,1,0:T(4,128)(2,1)S(1)}, u32[]{:S(2)}, u32[]{:S(2)}) %all-to-all-start.5) | async-done | bytes 262176 | tf_op jit(solution)/shard_map/all_to_all | solution.py:309
  179.2 1.3 kv_final.1
  (36 shorter events, 3.3 us)
Async XLA Ops:
  0.6 35.4 %copy-start = (bf16[16,128,128]{2,1,0:T(8,128)(2,1)S(1)}, bf16[16,128,128]{2,1,0:T(8,128)(2,1)}, u32[]{:S(2)}) copy-start(bf16[16,128,128]{2,1,0:T(8,128)(2,1)} %q_ref.1) | copy-start | bytes 1572868
  0.6 35.4 %copy-start.1 = (bf16[16,128,128]{2,1,0:T(8,128)(2,1)S(1)}, bf16[16,128,128]{2,1,0:T(8,128)(2,1)}, u32[]{:S(2)}) copy-start(bf16[16,128,128]{2,1,0:T(8,128)(2,1)} %g_ref.1) | copy-start | bytes 1572868
  0.6 1.0 copy-start.2
  1.6 0.7 copy-start.3
  3.8 19.3 %all-to-all-start.1 = ((bf16[32,2,2,2,4,128]{5,4,3,2,1,0:T(4,128)(2,1)}), bf16[32,2,2,2,4,128]{5,4,3,2,1,0:T(4,128)(2,1)S(1)}, u32[]{:S(2)}, u32[]{:S(2)}) async-start(bf16[32,2,2,2,4,128]{5,4,3,2,1,0:T(4,128)(2,1)} %bitcast.10), calls=%async_computation.1 | async-start | bytes 524288 | tf_op jit(solution)/shard_map/all_to_all | solution.py:309
  24.5 23.4 %all-to-all-start.2 = ((bf16[4,2,2,8,8,128]{5,4,3,2,1,0:T(8,128)(2,1)}), bf16[4,2,2,8,8,128]{5,4,3,2,1,0:T(8,128)(2,1)S(1)}, u32[]{:S(2)}, u32[]{:S(2)}) async-start(bf16[4,2,2,8,8,128]{5,4,3,2,1,0:T(8,128)(2,1)} %kv_unpack.1), calls=%async_computation.2 | async-start | bytes 524288 | tf_op jit(solution)/shard_map/all_to_all | solution.py:281
  36.1 0.7 copy-start.4
  47.8 20.7 %copy-start.13 = (s32[1,16]{1,0:T(1,128)S(1)}, s32[1,16]{1,0:T(1,128)}, u32[]{:S(2)}) copy-start(s32[1,16]{1,0:T(1,128)} %param.11) | copy-start | bytes 196
  47.8 35.4 %all-to-all-start = ((bf16[16,2,2,128,128]{4,3,2,1,0:T(8,128)(2,1)}), bf16[16,2,2,128,128]{4,3,2,1,0:T(8,128)(2,1)S(1)}, u32[]{:S(2)}, u32[]{:S(2)}) async-start(bf16[16,2,2,128,128]{4,3,2,1,0:T(8,128)(2,1)} %bitcast.5), calls=%async_computation | async-start | bytes 4194304 | tf_op jit(solution)/shard_map/all_to_all | solution.py:322
  55.1 13.6 %collective-permute-start = (bf16[4,2,2,8,8,128]{5,4,3,2,1,0:T(8,128)(2,1)S(1)}, bf16[4,2,2,8,8,128]{5,4,3,2,1,0:T(8,128)(2,1)S(1)}, u32[]{:S(2)}, u32[]{:S(2)}) collective-permute-start(bf16[4,2,2,8,8,128]{5,4,3,2,1,0:T(8,128)(2,1)S(1)} %all-to-all-done.2.kv0), channel_id=1, source_target_pairs={{0,1},{1,2},{2,3},{3,0},{4,5},{5,6},{6,7},{7,4},{8,9},{9,10},{10,1... | collective-permute-start | bytes 786440 | tf_op jit(solution)/shard_map/ppermute | solution.py:288
  62.6 17.1 %collective-permute-start.1 = (bf16[4,2,2,8,8,128]{5,4,3,2,1,0:T(8,128)(2,1)S(1)}, bf16[4,2,2,8,8,128]{5,4,3,2,1,0:T(8,128)(2,1)S(1)}, u32[]{:S(2)}, u32[]{:S(2)}) collective-permute-start(bf16[4,2,2,8,8,128]{5,4,3,2,1,0:T(8,128)(2,1)S(1)} %all-to-all-done.2.kv0), channel_id=1, source_target_pairs={{0,2},{1,3},{2,0},{3,1},{4,6},{5,7},{6,4},{7,5},{8,10},{9,11},{10,... | collective-permute-start | bytes 786440 | tf_op jit(solution)/shard_map/ppermute | solution.py:288
  64.5 15.2 %collective-permute-start.2 = (bf16[4,2,2,8,8,128]{5,4,3,2,1,0:T(8,128)(2,1)S(1)}, bf16[4,2,2,8,8,128]{5,4,3,2,1,0:T(8,128)(2,1)S(1)}, u32[]{:S(2)}, u32[]{:S(2)}) collective-permute-start(bf16[4,2,2,8,8,128]{5,4,3,2,1,0:T(8,128)(2,1)S(1)} %all-to-all-done.2.kv0), channel_id=1, source_target_pairs={{0,3},{1,0},{2,1},{3,2},{4,7},{5,4},{6,5},{7,6},{8,11},{9,8},{10,9... | collective-permute-start | bytes 786440 | tf_op jit(solution)/shard_map/ppermute | solution.py:288
  79.7 0.7 copy-start.8
  83.2 1.0 copy-start.9
  100.8 0.7 copy-start.6
  101.5 0.7 copy-start.10
  102.2 42.0 %copy-start.12 = (s32[16,16]{1,0:T(8,128)S(1)}, s32[16,16]{1,0:T(8,128)}, u32[]{:S(2)}) copy-start(s32[16,16]{1,0:T(8,128)} %param.10) | copy-start | bytes 3076
  102.2 42.2 %copy-start.5 = (s32[1,16,2]{1,2,0:T(2,128)S(1)}, s32[1,16,2]{1,2,0:T(2,128)}, u32[]{:S(2)}) copy-start(s32[1,16,2]{1,2,0:T(2,128)} %param.9) | copy-start | bytes 388
  102.2 6.0 %copy-start.11 = (bf16[4,2,2,8,8,128]{5,4,3,2,1,0:T(8,128)(2,1)S(1)}, bf16[4,2,2,8,8,128]{5,4,3,2,1,0:T(8,128)(2,1)}, u32[]{:S(2)}) copy-start(bf16[4,2,2,8,8,128]{5,4,3,2,1,0:T(8,128)(2,1)} %copy-done.10) | copy-start | bytes 786436
  102.2 13.5 %copy-start.7 = (bf16[4,2,2,8,8,128]{5,4,3,2,1,0:T(8,128)(2,1)S(1)}, bf16[4,2,2,8,8,128]{5,4,3,2,1,0:T(8,128)(2,1)}, u32[]{:S(2)}) copy-start(bf16[4,2,2,8,8,128]{5,4,3,2,1,0:T(8,128)(2,1)} %copy-done.6) | copy-start | bytes 786436
  102.2 32.7 %all-to-all-start.3 = ((bf16[16,2,128,128]{3,2,1,0:T(8,128)(2,1)}), bf16[16,2,128,128]{3,2,1,0:T(8,128)(2,1)S(1)}, u32[]{:S(2)}, u32[]{:S(2)}) async-start(bf16[16,2,128,128]{3,2,1,0:T(8,128)(2,1)} %bitcast.12), calls=%async_computation.3 | async-start | bytes 2097152 | tf_op jit(solution)/shard_map/all_to_all | solution.py:332
  108.2 14.4 %collective-permute-start.5 = (bf16[4,2,2,8,8,128]{5,4,3,2,1,0:T(8,128)(2,1)S(1)}, bf16[4,2,2,8,8,128]{5,4,3,2,1,0:T(8,128)(2,1)S(1)}, u32[]{:S(2)}, u32[]{:S(2)}) collective-permute-start(bf16[4,2,2,8,8,128]{5,4,3,2,1,0:T(8,128)(2,1)S(1)} %copy-done.11), channel_id=1, source_target_pairs={{0,1},{1,2},{2,3},{3,0},{4,5},{5,6},{6,7},{7,4},{8,9},{9,10},{10,1... | collective-permute-start | bytes 786440 | tf_op jit(solution)/shard_map/ppermute | solution.py:288
  115.8 18.3 %collective-permute-start.4 = (bf16[4,2,2,8,8,128]{5,4,3,2,1,0:T(8,128)(2,1)S(1)}, bf16[4,2,2,8,8,128]{5,4,3,2,1,0:T(8,128)(2,1)S(1)}, u32[]{:S(2)}, u32[]{:S(2)}) collective-permute-start(bf16[4,2,2,8,8,128]{5,4,3,2,1,0:T(8,128)(2,1)S(1)} %copy-done.7), channel_id=1, source_target_pairs={{0,2},{1,3},{2,0},{3,1},{4,6},{5,7},{6,4},{7,5},{8,10},{9,11},{10,... | collective-permute-start | bytes 786440 | tf_op jit(solution)/shard_map/ppermute | solution.py:288
  118.2 15.8 %collective-permute-start.3 = (bf16[4,2,2,8,8,128]{5,4,3,2,1,0:T(8,128)(2,1)S(1)}, bf16[4,2,2,8,8,128]{5,4,3,2,1,0:T(8,128)(2,1)S(1)}, u32[]{:S(2)}, u32[]{:S(2)}) collective-permute-start(bf16[4,2,2,8,8,128]{5,4,3,2,1,0:T(8,128)(2,1)S(1)} %get-tuple-element.10), channel_id=1, source_target_pairs={{0,3},{1,0},{2,1},{3,2},{4,7},{5,4},{6,5},{7,6},{8,11},{9,8},{10,9... | collective-permute-start | bytes 786440 | tf_op jit(solution)/shard_map/ppermute | solution.py:288
  134.9 21.4 %all-to-all-start.4 = ((bf16[4,2,2,8,8,128]{5,4,3,2,1,0:T(8,128)(2,1)}), bf16[4,2,2,8,8,128]{5,4,3,2,1,0:T(8,128)(2,1)S(1)}, u32[]{:S(2)}, u32[]{:S(2)}) async-start(bf16[4,2,2,8,8,128]{5,4,3,2,1,0:T(8,128)(2,1)} %add_convert_fusion), calls=%async_computation.4 | async-start | bytes 524288 | tf_op jit(solution)/shard_map/all_to_all | solution.py:281
  157.7 21.4 %all-to-all-start.5 = ((bf16[32,2,2,2,4,128]{5,4,3,2,1,0:T(4,128)(2,1)}), bf16[32,2,2,2,4,128]{5,4,3,2,1,0:T(4,128)(2,1)S(1)}, u32[]{:S(2)}, u32[]{:S(2)}) async-start(bf16[32,2,2,2,4,128]{5,4,3,2,1,0:T(4,128)(2,1)} %bitcast.16), calls=%async_computation.5 | async-start | bytes 524288 | tf_op jit(solution)/shard_map/all_to_all | solution.py:309

commit v6 on v2

--- a/solution.py
+++ b/solution.py
@@ -14,8 +14,8 @@
 SCALING = HD ** (-0.5)
 LOG2E = 1.4426950408889634
 PLANE = ("dp", "xh")
-COLUMN = ("zh", "zm", "zl")
-LINE = ("zm", "zl")
+FAR = (4, 15, 11)
+NEAR = 4
 
 
 def matmul(a, b, contract):
@@ -49,26 +49,39 @@
 
 
 def attention_kernel(
-    recv_ref, start_ref, place_ref, qg_ref, kv_ref, dq_ref, dkv_ref,
-    k_all, kt_all, v_all, dk_all, dv_all, scores, dprobs, dqt,
+    recv_ref, start_ref, place_ref, qg_ref, *refs
 ):
+    kv_refs, dq_ref, dkv_refs = refs[: 2 * NEAR], refs[2 * NEAR], refs[2 * NEAR + 1 : 4 * NEAR + 1]
+    k_all, kt_all, v_all, dk_all, dv_all, scores, dprobs, dqt = refs[4 * NEAR + 1 :]
     blocks = k_all.shape[0]
     width = k_all.shape[1]
     tile_rows = width // PAIR
+    part = width // NEAR
+    own_part = part // 4
     factor = SCALING * LOG2E
 
+    def rows_of(slot):
+        begin = (slot % NEAR) * part
+        if slot < NEAR:
+            return slice(begin, begin + own_part)
+        return slice(begin + own_part, begin + part)
+
     def stage(block, _):
-        key = kv_ref[:, :, :, 0, block].astype(jnp.float32).reshape(width, HD)
-        value = kv_ref[:, :, :, 1, block].astype(jnp.float32).reshape(width, HD)
-        k_all[block] = key.astype(jnp.bfloat16)
-        v_all[block] = value.astype(jnp.bfloat16)
-        kt_all[block] = key.T.astype(jnp.bfloat16)
+        for slot, ref in enumerate(kv_refs):
+            rows = rows_of(slot)
+            count = rows.stop - rows.start
+            key = ref[:, :, 0, block].astype(jnp.float32).reshape(count, HD)
+            value = ref[:, :, 1, block].astype(jnp.float32).reshape(count, HD)
+            k_all[block, rows] = key.astype(jnp.bfloat16)
+            v_all[block, rows] = value.astype(jnp.bfloat16)
+        kt_all[block] = k_all[block].astype(jnp.float32).T.astype(jnp.bfloat16)
         return 0
 
     lax.fori_loop(0, blocks, stage, 0)
 
     row = lax.broadcasted_iota(jnp.int32, (width, 1), 0)
-    source = ((place_ref[0] & 8) | (row >> 5)) ^ (((row >> 4) & 1) * 15)
+    holder = (place_ref[0] & 12) | ((place_ref[0] - (row >> 6)) & 3)
+    source = holder ^ (((row >> 4) & 1) * 4) ^ (((row >> 5) & 1) * 15)
     key_offset = (
         ((row >> 2) & 1) * tile_rows + ((row >> 3) & 1) * 64 + source * 4 + (row & 3)
     )
@@ -141,15 +154,17 @@
     lax.fori_loop(0, blocks, query_block, 0)
 
     def unstage(block, _):
-        shape = kv_ref.shape[:3] + kv_ref.shape[5:]
-        dkv_ref[:, :, :, 0, block] = (dk_all[block] * SCALING).reshape(shape).astype(jnp.bfloat16)
-        dkv_ref[:, :, :, 1, block] = dv_all[block].reshape(shape).astype(jnp.bfloat16)
+        for slot, ref in enumerate(dkv_refs):
+            rows = rows_of(slot)
+            shape = ref.shape[:2] + ref.shape[4:]
+            ref[:, :, 0, block] = (dk_all[block, rows] * SCALING).reshape(shape).astype(jnp.bfloat16)
+            ref[:, :, 1, block] = dv_all[block, rows].reshape(shape).astype(jnp.bfloat16)
         return 0
 
     lax.fori_loop(0, blocks, unstage, 0)
 
 
-def attention(my_recv, start, place, qg, kv):
+def attention(my_recv, start, place, qg, chunks):
     slots, _, tile_rows, _ = qg.shape
     blocks = my_recv.shape[0] // PAIR
     width = PAIR * tile_rows
@@ -157,12 +172,10 @@
     smem = pl.BlockSpec(memory_space=pltpu.SMEM)
     return pl.pallas_call(
         attention_kernel,
-        out_shape=(
-            jax.ShapeDtypeStruct((slots, tile_rows, HD), jnp.bfloat16),
-            jax.ShapeDtypeStruct(kv.shape, jnp.bfloat16),
-        ),
-        in_specs=[smem, smem, smem, vmem, vmem],
-        out_specs=(vmem, vmem),
+        out_shape=(jax.ShapeDtypeStruct((slots, tile_rows, HD), jnp.bfloat16),)
+        + tuple(jax.ShapeDtypeStruct(chunk.shape, jnp.bfloat16) for chunk in chunks),
+        in_specs=[smem] * 3 + [vmem] * (1 + 2 * NEAR),
+        out_specs=(vmem,) * (1 + 2 * NEAR),
         scratch_shapes=[
             pltpu.VMEM((blocks, width, HD), jnp.bfloat16),
             pltpu.VMEM((blocks, HD, width), jnp.bfloat16),
@@ -178,7 +191,7 @@
             flops=2 * 10**9, bytes_accessed=6 * 2**20, transcendentals=2 * 10**6
         ),
         name="attention_backward",
-    )(my_recv, start, place, qg, kv)
+    )(my_recv, start, place, qg, *chunks)
 
 
 def kv_pack_kernel(index_ref, kv_ref, out_ref):
@@ -211,7 +224,7 @@
     lax.fori_loop(0, recv_ref.shape[0] // PAIR, body, 0)
 
 
-def kv_back_kernel(recv_ref, place_ref, own_ref, other_ref, out_ref):
+def kv_back_kernel(recv_ref, place_ref, p0, p1, p2, p3, out_ref):
     head = place_ref[0] >> 3
     sliver = out_ref.shape[-2]
 
@@ -219,8 +232,8 @@
         slots = (recv_ref[PAIR * pair], recv_ref[PAIR * pair + 1])
         for half in range(2):
             for kind in range(2):
-                for ref, which in ((own_ref, head), (other_ref, 1 - head)):
-                    total = ref[half, kind, pair].astype(jnp.float32)
+                for a, b, which in ((p0, p1, head), (p2, p3, 1 - head)):
+                    total = a[half, kind, pair].astype(jnp.float32) + b[half, kind, pair].astype(jnp.float32)
                     for order, slot in enumerate(slots):
                         rows = total[order * sliver : (order + 1) * sliver]
                         out_ref[slot >> 1, half, slot & 1, kind, which] = rows.astype(jnp.bfloat16)
@@ -255,8 +268,25 @@
     )(*scalars, *arrays)
 
 
-def mirror(values):
-    return lax.ppermute(values, COLUMN, [(source, 15 - source) for source in range(16)])
+def far_swap(values, flip):
+    return lax.ppermute(values, "z", [(place, place ^ flip) for place in range(16)])
+
+
+def near_shift(values, step):
+    pairs = [(place, (place & 12) | ((place + step) & 3)) for place in range(16)]
+    return lax.ppermute(values, "z", pairs)
+
+
+def near_gather(values):
+    return [values] + [near_shift(values, step) for step in range(1, NEAR)]
+
+
+def near_terms(terms):
+    return [terms[0]] + [near_shift(terms[step], -step) for step in range(1, NEAR)]
+
+
+def total(terms, index):
+    return sum(term[index].astype(jnp.float32) for term in terms).astype(jnp.bfloat16)
 
 
 def on_device(queries, keys_values, grad_out, send_tiles, recv_slot, tile_seq):
@@ -270,7 +300,7 @@
     my_send = send_tiles[0]
     outgoing = my_send.T
     my_recv = lax.dynamic_index_in_dim(recv_slot, replica, 0, keepdims=False)
-    place = lax.axis_index(COLUMN).astype(jnp.int32).reshape(1)
+    place = lax.axis_index("z").astype(jnp.int32).reshape(1)
     traveling = jax.ShapeDtypeStruct(
         (n_replicas, 2, slot_cap, 2, 2, sliver, HD), keys_values.dtype
     )
@@ -290,25 +320,26 @@
         kv_unpack_kernel, "kv_unpack", [my_recv, place], [kv_arrived], (half_shape, half_shape)
     )
     qg_packed = pack(outgoing, queries, grad_out)
-    mirrored = mirror(other)
-    qg_packed, mirrored = lax.optimization_barrier((qg_packed, mirrored))
     qg_arrived = lax.all_to_all(
         qg_packed.reshape(n_replicas, slot_cap, 2, tile_rows, row_width),
         "dp", split_axis=0, concat_axis=0, tiled=True,
     ).reshape(slots, 2, tile_rows, row_width)
-    kv_all = lax.all_gather(jnp.stack([own, mirrored]), LINE)
+    far = jnp.stack([far_swap(own, FAR[0]), far_swap(other, FAR[1]), far_swap(other, FAR[2])])
+    own_chunks = near_gather(own[None])
+    far, own_chunks, qg_arrived = lax.optimization_barrier((far, own_chunks, qg_arrived))
+    chunks = own_chunks + near_gather(far)
 
     seq = tile_seq[0]
     start = jnp.sum((seq[None, :] < seq[:, None]).astype(jnp.int32), axis=1)
-    query_back, dkv = attention(my_recv, start, place, qg_arrived, kv_all)
+    query_back, *terms = attention(my_recv, start, place, qg_arrived, chunks)
     query_returned = lax.all_to_all(
         query_back.reshape(n_replicas, slot_cap, tile_rows, row_width),
         "dp", split_axis=0, concat_axis=0, tiled=True,
     )
-
-    summed = lax.psum_scatter(dkv, LINE, scatter_dimension=0)
-    summed, query_returned = lax.optimization_barrier((summed, query_returned))
-    swapped = [summed[0], mirror(summed[1])]
+    far_terms = near_terms(terms[NEAR:])
+    back = [far_swap(total(far_terms, index), flip) for index, flip in enumerate(FAR)]
+    own_sum = total(near_terms(terms[:NEAR]), 0)
+    swapped, query_returned = lax.optimization_barrier(([own_sum] + back, query_returned))
     kv_returned = over_plane(
         local_call(kv_back_kernel, "kv_back", [my_recv, place], swapped, traveling)
     )
@@ -330,9 +361,8 @@
 
 
 def solution(mesh):
-    names = PLANE + COLUMN
-    fine = Mesh(mesh.devices.reshape(mesh.devices.shape[0], 2, 2, 2, 4), names)
-    tensor = ("xh",) + COLUMN
+    fine = Mesh(mesh.devices.reshape(mesh.devices.shape[0], 2, 16), ("dp", "xh", "z"))
+    tensor = ("xh", "z")
     in_specs = (
         P("dp", None, tensor),
         P("dp", tensor, None),

time: 231 us -> 173 us (0.75)
  the two profiles are of different devices: /device:TPU:1 before, /device:TPU:97 now
where the time goes in v6:
time: 173 us; the launch traced here: 172 us
  starting transfers between devices  101 us (58%)
  waiting for transfers between devices  42.4 us (25%)
  Pallas kernels  19.1 us (11%)
  local copies, waits for them, and re-layouts  7.23 us (4%)
    ppermute x6, starting transfers between devices, far_swap(): lax.ppermute(values, 'z', [(place, place ^ flip) for place in range(16)])  38.5 us
    ppermute x12, starting transfers between devices, near_shift(): return lax.ppermute(values, 'z', pairs)  36.4 us
    ppermute x12, waiting for transfers between devices, near_shift(): return lax.ppermute(values, 'z', pairs)  17.5 us
    all_to_all x2, starting transfers between devices, over_plane(): lax.all_to_all(values.reshape((2 * n_replicas,) + values.shape[2:]), PLAN...  13.8 us
    ppermute x6, waiting for transfers between devices, far_swap(): lax.ppermute(values, 'z', [(place, place ^ flip) for place in range(16)])  13.6 us
    pallas_call x1, Pallas kernels, attention(): pl.pallas_call(attention_kernel, out_shape=(jax.ShapeDtypeStruct((slots,...  12 us
    all_to_all x2, waiting for transfers between devices, over_plane(): lax.all_to_all(values.reshape((2 * n_replicas,) + values.shape[2:]), PLAN...  11.3 us
    all_to_all x1, starting transfers between devices, on_device(): lax.all_to_all(query_back.reshape(n_replicas, slot_cap, tile_rows, row_wi...  8.43 us
  transfers between devices with their start and end apart: 22, of which 9 were waited for; matrix products, arithmetic and copies ran while one was open for 1% of the time, Pallas kernels for 2%

profile of v6, /device:TPU:97, one launch (start us, length us, event | category | flops | bytes accessed | tf_op | source)
XLA Modules:
  0.0 171.5 jit_solution(4770882385328974126)
XLA Ops:
  2.2 1.4 kv_pack.1
  3.7 7.8 %all-to-all-start = ((bf16[32,2,2,2,4,128]{5,4,3,2,1,0:T(4,128)(2,1)}), bf16[32,2,2,2,4,128]{5,4,3,2,1,0:T(4,128)(2,1)S(1)}, u32[]{:S(2)}, u32[]{:S(2)}) async-start(bf16[32,2,2,2,4,128]{5,4,3,2,1,0:T(4,128)(2,1)} %bitcast.7), calls=%async_computation | async-start | bytes 524288 | tf_op jit(solution)/shard_map/all_to_all | solution.py:310
  14.2 2.3 %pack_rows.1 = bf16[32,2,128,128]{3,2,1,0:T(8,128)(2,1)} custom-call(s32[2,16]{1,0:T(2,128)S(1)} %bitcast.42, bf16[16,128,128]{2,1,0:T(8,128)(2,1)S(1)} %copy-done, bf16[16,128,128]{2,1,0:T(8,128)(2,1)S(1)} %copy-done.1), custom_call_target="tpu_custom_call" | custom-call | tf_op jit(solution)/shard_map/pack_rows/pallas_call | solution.py:37
  16.5 3.8 %all-to-all-done = bf16[32,2,2,2,4,128]{5,4,3,2,1,0:T(4,128)(2,1)S(1)} async-done(((bf16[32,2,2,2,4,128]{5,4,3,2,1,0:T(4,128)(2,1)}), bf16[32,2,2,2,4,128]{5,4,3,2,1,0:T(4,128)(2,1)S(1)}, u32[]{:S(2)}, u32[]{:S(2)}) %all-to-all-start) | async-done | bytes 262176 | tf_op jit(solution)/shard_map/all_to_all | solution.py:310
  20.3 4.0 %all-to-all-start.1 = ((bf16[16,2,2,128,128]{4,3,2,1,0:T(8,128)(2,1)}), bf16[16,2,2,128,128]{4,3,2,1,0:T(8,128)(2,1)S(1)}, u32[]{:S(2)}, u32[]{:S(2)}) async-start(bf16[16,2,2,128,128]{4,3,2,1,0:T(8,128)(2,1)} %bitcast.14), calls=%async_computation.1 | async-start | bytes 4194304 | tf_op jit(solution)/shard_map/all_to_all | solution.py:323
  25.0 11.1 %collective-permute-start.1 = (bf16[2,2,8,8,128]{4,3,2,1,0:T(8,128)(2,1)S(1)}, bf16[2,2,8,8,128]{4,3,2,1,0:T(8,128)(2,1)S(1)}, u32[]{:S(2)}, u32[]{:S(2)}) collective-permute-start(bf16[2,2,8,8,128]{4,3,2,1,0:T(8,128)(2,1)S(1)} %get-tuple-element.25), channel_id=1, source_target_pairs={{0,15},{1,14},{2,13},{3,12},{4,11},{5,10},{6,9},{7,8},{8,7},{9,6},... | collective-permute-start | bytes 196616 | tf_op jit(solution)/shard_map/ppermute | solution.py:272
  36.1 2.2 %collective-permute-start.2 = (bf16[2,2,8,8,128]{4,3,2,1,0:T(8,128)(2,1)S(1)}, bf16[2,2,8,8,128]{4,3,2,1,0:T(8,128)(2,1)S(1)}, u32[]{:S(2)}, u32[]{:S(2)}) collective-permute-start(bf16[2,2,8,8,128]{4,3,2,1,0:T(8,128)(2,1)S(1)} %get-tuple-element.25), channel_id=1, source_target_pairs={{0,11},{1,10},{2,9},{3,8},{4,15},{5,14},{6,13},{7,12},{8,3},{9,2},... | collective-permute-start | bytes 196616 | tf_op jit(solution)/shard_map/ppermute | solution.py:272
  38.4 4.0 %collective-permute-start = (bf16[2,2,8,8,128]{4,3,2,1,0:T(8,128)(2,1)S(1)}, bf16[2,2,8,8,128]{4,3,2,1,0:T(8,128)(2,1)S(1)}, u32[]{:S(2)}, u32[]{:S(2)}) collective-permute-start(bf16[2,2,8,8,128]{4,3,2,1,0:T(8,128)(2,1)S(1)} %get-tuple-element.24), channel_id=1, source_target_pairs={{0,4},{1,5},{2,6},{3,7},{4,0},{5,1},{6,2},{7,3},{8,12},{9,13},{10,... | collective-permute-start | bytes 196616 | tf_op jit(solution)/shard_map/ppermute | solution.py:272
  42.4 4.4 %collective-permute-start.3 = (bf16[1,2,2,8,8,128]{5,4,3,2,1,0:T(8,128)(2,1)S(1)}, bf16[1,2,2,8,8,128]{5,4,3,2,1,0:T(8,128)(2,1)S(1)}, u32[]{:S(2)}, u32[]{:S(2)}) collective-permute-start(bf16[1,2,2,8,8,128]{5,4,3,2,1,0:T(8,128)(2,1)S(1)} %bitcast.44), channel_id=1, source_target_pairs={{0,1},{1,2},{2,3},{3,0},{4,5},{5,6},{6,7},{7,4},{8,9},{9,10},{10,1... | collective-permute-start | bytes 196616 | tf_op jit(solution)/shard_map/ppermute | solution.py:277
  46.8 2.2 %collective-permute-start.4 = (bf16[1,2,2,8,8,128]{5,4,3,2,1,0:T(8,128)(2,1)S(1)}, bf16[1,2,2,8,8,128]{5,4,3,2,1,0:T(8,128)(2,1)S(1)}, u32[]{:S(2)}, u32[]{:S(2)}) collective-permute-start(bf16[1,2,2,8,8,128]{5,4,3,2,1,0:T(8,128)(2,1)S(1)} %bitcast.45), channel_id=1, source_target_pairs={{0,2},{1,3},{2,0},{3,1},{4,6},{5,7},{6,4},{7,5},{8,10},{9,11},{10,... | collective-permute-start | bytes 196616 | tf_op jit(solution)/shard_map/ppermute | solution.py:277
  49.0 2.6 %collective-permute-start.5 = (bf16[1,2,2,8,8,128]{5,4,3,2,1,0:T(8,128)(2,1)S(1)}, bf16[1,2,2,8,8,128]{5,4,3,2,1,0:T(8,128)(2,1)S(1)}, u32[]{:S(2)}, u32[]{:S(2)}) collective-permute-start(bf16[1,2,2,8,8,128]{5,4,3,2,1,0:T(8,128)(2,1)S(1)} %bitcast.46), channel_id=1, source_target_pairs={{0,3},{1,0},{2,1},{3,2},{4,7},{5,4},{6,5},{7,6},{8,11},{9,8},{10,9... | collective-permute-start | bytes 196616 | tf_op jit(solution)/shard_map/ppermute | solution.py:277
  51.7 1.7 %collective-permute-done.3.refs_1_ = bf16[1,2,2,8,8,128]{5,4,3,2,1,0:T(8,128)(2,1)S(1)} collective-permute-done((bf16[1,2,2,8,8,128]{5,4,3,2,1,0:T(8,128)(2,1)S(1)}, bf16[1,2,2,8,8,128]{5,4,3,2,1,0:T(8,128)(2,1)S(1)}, u32[]{:S(2)}, u32[]{:S(2)}) %collective-permute-start.3) | collective-permute-done | bytes 65568 | tf_op jit(solution)/shard_map/ppermute | solution.py:277
  53.5 1.6 collective-permute-done.4.refs_2_
  56.6 2.4 %collective-permute-start.6 = (bf16[3,2,2,8,8,128]{5,4,3,2,1,0:T(8,128)(2,1)S(1)}, bf16[3,2,2,8,8,128]{5,4,3,2,1,0:T(8,128)(2,1)S(1)}, u32[]{:S(2)}, u32[]{:S(2)}) collective-permute-start(bf16[3,2,2,8,8,128]{5,4,3,2,1,0:T(8,128)(2,1)S(1)} %pad_maximum_fusion.refs_4_), channel_id=1, source_target_pairs={{0,1},{1,2},{2,3},{3,0},{4,5},{5,6},{6,7},{7,4},{8,9},{9,10},{10,1... | collective-permute-start | bytes 589832 | tf_op jit(solution)/shard_map/ppermute | solution.py:277
  58.9 4.2 %collective-permute-start.7 = (bf16[3,2,2,8,8,128]{5,4,3,2,1,0:T(8,128)(2,1)S(1)}, bf16[3,2,2,8,8,128]{5,4,3,2,1,0:T(8,128)(2,1)S(1)}, u32[]{:S(2)}, u32[]{:S(2)}) collective-permute-start(bf16[3,2,2,8,8,128]{5,4,3,2,1,0:T(8,128)(2,1)S(1)} %pad_maximum_fusion.refs_4_), channel_id=1, source_target_pairs={{0,2},{1,3},{2,0},{3,1},{4,6},{5,7},{6,4},{7,5},{8,10},{9,11},{10,... | collective-permute-start | bytes 589832 | tf_op jit(solution)/shard_map/ppermute | solution.py:277
  63.2 2.9 %collective-permute-start.8 = (bf16[3,2,2,8,8,128]{5,4,3,2,1,0:T(8,128)(2,1)S(1)}, bf16[3,2,2,8,8,128]{5,4,3,2,1,0:T(8,128)(2,1)S(1)}, u32[]{:S(2)}, u32[]{:S(2)}) collective-permute-start(bf16[3,2,2,8,8,128]{5,4,3,2,1,0:T(8,128)(2,1)S(1)} %pad_maximum_fusion.refs_4_), channel_id=1, source_target_pairs={{0,3},{1,0},{2,1},{3,2},{4,7},{5,4},{6,5},{7,6},{8,11},{9,8},{10,9... | collective-permute-start | bytes 589832 | tf_op jit(solution)/shard_map/ppermute | solution.py:277
  66.3 11.7 %collective-permute-done.7.refs_6_ = bf16[3,2,2,8,8,128]{5,4,3,2,1,0:T(8,128)(2,1)S(1)} collective-permute-done((bf16[3,2,2,8,8,128]{5,4,3,2,1,0:T(8,128)(2,1)S(1)}, bf16[3,2,2,8,8,128]{5,4,3,2,1,0:T(8,128)(2,1)S(1)}, u32[]{:S(2)}, u32[]{:S(2)}) %collective-permute-start.7) | collective-permute-done | bytes 196640 | tf_op jit(solution)/shard_map/ppermute | solution.py:277
  78.8 12.0 %attention_backward.1 = (bf16[32,128,128]{2,1,0:T(8,128)(2,1)}, bf16[1,2,2,8,8,128]{5,4,3,2,1,0:T(8,128)(2,1)S(1)}, bf16[1,2,2,8,8,128]{5,4,3,2,1,0:T(8,128)(2,1...) custom-call(s32[16]{0:T(128)S(1)} %dynamic-slice_bitcast_fusion.recv, ...), custom_call_target="tpu_custom_call" | custom-call | flops 2000000000 | bytes 6291456 | tf_op jit(solution)/shard_map/attention_backward/pallas_call | solution.py:173
  90.8 8.4 %all-to-all-start.2 = ((bf16[16,2,128,128]{3,2,1,0:T(8,128)(2,1)}), bf16[16,2,128,128]{3,2,1,0:T(8,128)(2,1)S(1)}, u32[]{:S(2)}, u32[]{:S(2)}) async-start(bf16[16,2,128,128]{3,2,1,0:T(8,128)(2,1)} %bitcast.20), calls=%async_computation.2 | async-start | bytes 2097152 | tf_op jit(solution)/shard_map/all_to_all | solution.py:335
  99.4 1.9 %collective-permute-start.12 = (bf16[3,2,2,8,8,128]{5,4,3,2,1,0:T(8,128)(2,1)S(1)}, bf16[3,2,2,8,8,128]{5,4,3,2,1,0:T(8,128)(2,1)S(1)}, u32[]{:S(2)}, u32[]{:S(2)}) collective-permute-start(bf16[3,2,2,8,8,128]{5,4,3,2,1,0:T(8,128)(2,1)S(1)} %get-tuple-element.37), channel_id=1, source_target_pairs={{0,3},{1,0},{2,1},{3,2},{4,7},{5,4},{6,5},{7,6},{8,11},{9,8},{10,9... | collective-permute-start | bytes 589832 | tf_op jit(solution)/shard_map/ppermute | solution.py:277
  101.3 2.2 %collective-permute-start.13 = (bf16[3,2,2,8,8,128]{5,4,3,2,1,0:T(8,128)(2,1)S(1)}, bf16[3,2,2,8,8,128]{5,4,3,2,1,0:T(8,128)(2,1)S(1)}, u32[]{:S(2)}, u32[]{:S(2)}) collective-permute-start(bf16[3,2,2,8,8,128]{5,4,3,2,1,0:T(8,128)(2,1)S(1)} %get-tuple-element.38), channel_id=1, source_target_pairs={{0,2},{1,3},{2,0},{3,1},{4,6},{5,7},{6,4},{7,5},{8,10},{9,11},{10,... | collective-permute-start | bytes 589832 | tf_op jit(solution)/shard_map/ppermute | solution.py:277
  103.5 4.9 %collective-permute-start.14 = (bf16[3,2,2,8,8,128]{5,4,3,2,1,0:T(8,128)(2,1)S(1)}, bf16[3,2,2,8,8,128]{5,4,3,2,1,0:T(8,128)(2,1)S(1)}, u32[]{:S(2)}, u32[]{:S(2)}) collective-permute-start(bf16[3,2,2,8,8,128]{5,4,3,2,1,0:T(8,128)(2,1)S(1)} %get-tuple-element.39), channel_id=1, source_target_pairs={{0,1},{1,2},{2,3},{3,0},{4,5},{5,6},{6,7},{7,4},{8,9},{9,10},{10,1... | collective-permute-start | bytes 589832 | tf_op jit(solution)/shard_map/ppermute | solution.py:277
  108.6 3.4 %collective-permute-start.10 = (bf16[1,2,2,8,8,128]{5,4,3,2,1,0:T(8,128)(2,1)S(1)}, bf16[1,2,2,8,8,128]{5,4,3,2,1,0:T(8,128)(2,1)S(1)}, u32[]{:S(2)}, u32[]{:S(2)}) collective-permute-start(bf16[1,2,2,8,8,128]{5,4,3,2,1,0:T(8,128)(2,1)S(1)} %get-tuple-element.34), channel_id=1, source_target_pairs={{0,2},{1,3},{2,0},{3,1},{4,6},{5,7},{6,4},{7,5},{8,10},{9,11},{10,... | collective-permute-start | bytes 196616 | tf_op jit(solution)/shard_map/ppermute | solution.py:277
  111.9 2.8 %collective-permute-start.11 = (bf16[1,2,2,8,8,128]{5,4,3,2,1,0:T(8,128)(2,1)S(1)}, bf16[1,2,2,8,8,128]{5,4,3,2,1,0:T(8,128)(2,1)S(1)}, u32[]{:S(2)}, u32[]{:S(2)}) collective-permute-start(bf16[1,2,2,8,8,128]{5,4,3,2,1,0:T(8,128)(2,1)S(1)} %get-tuple-element.35), channel_id=1, source_target_pairs={{0,1},{1,2},{2,3},{3,0},{4,5},{5,6},{6,7},{7,4},{8,9},{9,10},{10,1... | collective-permute-start | bytes 196616 | tf_op jit(solution)/shard_map/ppermute | solution.py:277
  114.8 2.5 %collective-permute-start.9 = (bf16[1,2,2,8,8,128]{5,4,3,2,1,0:T(8,128)(2,1)S(1)}, bf16[1,2,2,8,8,128]{5,4,3,2,1,0:T(8,128)(2,1)S(1)}, u32[]{:S(2)}, u32[]{:S(2)}) collective-permute-start(bf16[1,2,2,8,8,128]{5,4,3,2,1,0:T(8,128)(2,1)S(1)} %get-tuple-element.33), channel_id=1, source_target_pairs={{0,3},{1,0},{2,1},{3,2},{4,7},{5,4},{6,5},{7,6},{8,11},{9,8},{10,9... | collective-permute-start | bytes 196616 | tf_op jit(solution)/shard_map/ppermute | solution.py:277
  117.2 1.6 collective-permute-done.13
  119.0 6.7 %collective-permute-start.15 = (bf16[2,2,8,8,128]{4,3,2,1,0:T(8,128)(2,1)S(1)}, bf16[2,2,8,8,128]{4,3,2,1,0:T(8,128)(2,1)S(1)}, u32[]{:S(2)}, u32[]{:S(2)}) collective-permute-start(bf16[2,2,8,8,128]{4,3,2,1,0:T(8,128)(2,1)S(1)} %get-tuple-element.48), channel_id=1, source_target_pairs={{0,4},{1,5},{2,6},{3,7},{4,0},{5,1},{6,2},{7,3},{8,12},{9,13},{10,... | collective-permute-start | bytes 196616 | tf_op jit(solution)/shard_map/ppermute | solution.py:272
  125.7 12.6 %collective-permute-start.16 = (bf16[2,2,8,8,128]{4,3,2,1,0:T(8,128)(2,1)S(1)}, bf16[2,2,8,8,128]{4,3,2,1,0:T(8,128)(2,1)S(1)}, u32[]{:S(2)}, u32[]{:S(2)}) collective-permute-start(bf16[2,2,8,8,128]{4,3,2,1,0:T(8,128)(2,1)S(1)} %get-tuple-element.47), channel_id=1, source_target_pairs={{0,15},{1,14},{2,13},{3,12},{4,11},{5,10},{6,9},{7,8},{8,7},{9,6},... | collective-permute-start | bytes 196616 | tf_op jit(solution)/shard_map/ppermute | solution.py:272
  138.3 1.9 %collective-permute-start.17 = (bf16[2,2,8,8,128]{4,3,2,1,0:T(8,128)(2,1)S(1)}, bf16[2,2,8,8,128]{4,3,2,1,0:T(8,128)(2,1)S(1)}, u32[]{:S(2)}, u32[]{:S(2)}) collective-permute-start(bf16[2,2,8,8,128]{4,3,2,1,0:T(8,128)(2,1)S(1)} %get-tuple-element.46), channel_id=1, source_target_pairs={{0,11},{1,10},{2,9},{3,8},{4,15},{5,14},{6,13},{7,12},{8,3},{9,2},... | collective-permute-start | bytes 196616 | tf_op jit(solution)/shard_map/ppermute | solution.py:272
  140.6 13.3 %collective-permute-done.17.p3 = bf16[2,2,8,8,128]{4,3,2,1,0:T(8,128)(2,1)S(1)} collective-permute-done((bf16[2,2,8,8,128]{4,3,2,1,0:T(8,128)(2,1)S(1)}, bf16[2,2,8,8,128]{4,3,2,1,0:T(8,128)(2,1)S(1)}, u32[]{:S(2)}, u32[]{:S(2)}) %collective-permute-start.17) | collective-permute-done | bytes 65568 | tf_op jit(solution)/shard_map/ppermute | solution.py:272
  155.3 6.1 %all-to-all-start.3 = ((bf16[32,2,2,2,4,128]{5,4,3,2,1,0:T(4,128)(2,1)}), bf16[32,2,2,2,4,128]{5,4,3,2,1,0:T(4,128)(2,1)S(1)}, u32[]{:S(2)}, u32[]{:S(2)}) async-start(bf16[32,2,2,2,4,128]{5,4,3,2,1,0:T(4,128)(2,1)} %bitcast.24), calls=%async_computation.3 | async-start | bytes 524288 | tf_op jit(solution)/shard_map/all_to_all | solution.py:310
  162.8 7.4 %all-to-all-done.3 = bf16[32,2,2,2,4,128]{5,4,3,2,1,0:T(4,128)(2,1)S(1)} async-done(((bf16[32,2,2,2,4,128]{5,4,3,2,1,0:T(4,128)(2,1)}), bf16[32,2,2,2,4,128]{5,4,3,2,1,0:T(4,128)(2,1)S(1)}, u32[]{:S(2)}, u32[]{:S(2)}) %all-to-all-start.3) | async-done | bytes 262176 | tf_op jit(solution)/shard_map/all_to_all | solution.py:310
  (50 shorter events, 12.4 us)
Async XLA Ops:
  0.6 0.9 copy-start.2
  1.5 0.7 copy-start.3
  3.7 16.6 %all-to-all-start = ((bf16[32,2,2,2,4,128]{5,4,3,2,1,0:T(4,128)(2,1)}), bf16[32,2,2,2,4,128]{5,4,3,2,1,0:T(4,128)(2,1)S(1)}, u32[]{:S(2)}, u32[]{:S(2)}) async-start(bf16[32,2,2,2,4,128]{5,4,3,2,1,0:T(4,128)(2,1)} %bitcast.7), calls=%async_computation | async-start | bytes 524288 | tf_op jit(solution)/shard_map/all_to_all | solution.py:310
  11.4 1.0 copy-start
  12.5 1.0 copy-start.1
  13.5 0.7 copy-start.4
  20.3 4.0 %copy-start.8 = (s32[16,16]{1,0:T(8,128)S(1)}, s32[16,16]{1,0:T(8,128)}, u32[]{:S(2)}) copy-start(s32[16,16]{1,0:T(8,128)} %param.10) | copy-start | bytes 3076
  20.3 45.8 %copy-start.9 = (s32[1,16]{1,0:T(1,128)S(1)}, s32[1,16]{1,0:T(1,128)}, u32[]{:S(2)}) copy-start(s32[1,16]{1,0:T(1,128)} %param.11) | copy-start | bytes 196
  20.3 36.3 %all-to-all-start.1 = ((bf16[16,2,2,128,128]{4,3,2,1,0:T(8,128)(2,1)}), bf16[16,2,2,128,128]{4,3,2,1,0:T(8,128)(2,1)S(1)}, u32[]{:S(2)}, u32[]{:S(2)}) async-start(bf16[16,2,2,128,128]{4,3,2,1,0:T(8,128)(2,1)} %bitcast.14), calls=%async_computation.1 | async-start | bytes 4194304 | tf_op jit(solution)/shard_map/all_to_all | solution.py:323
  25.0 24.0 %collective-permute-start.1 = (bf16[2,2,8,8,128]{4,3,2,1,0:T(8,128)(2,1)S(1)}, bf16[2,2,8,8,128]{4,3,2,1,0:T(8,128)(2,1)S(1)}, u32[]{:S(2)}, u32[]{:S(2)}) collective-permute-start(bf16[2,2,8,8,128]{4,3,2,1,0:T(8,128)(2,1)S(1)} %get-tuple-element.25), channel_id=1, source_target_pairs={{0,15},{1,14},{2,13},{3,12},{4,11},{5,10},{6,9},{7,8},{8,7},{9,6},... | collective-permute-start | bytes 196616 | tf_op jit(solution)/shard_map/ppermute | solution.py:272
  36.1 15.6 %collective-permute-start.2 = (bf16[2,2,8,8,128]{4,3,2,1,0:T(8,128)(2,1)S(1)}, bf16[2,2,8,8,128]{4,3,2,1,0:T(8,128)(2,1)S(1)}, u32[]{:S(2)}, u32[]{:S(2)}) collective-permute-start(bf16[2,2,8,8,128]{4,3,2,1,0:T(8,128)(2,1)S(1)} %get-tuple-element.25), channel_id=1, source_target_pairs={{0,11},{1,10},{2,9},{3,8},{4,15},{5,14},{6,13},{7,12},{8,3},{9,2},... | collective-permute-start | bytes 196616 | tf_op jit(solution)/shard_map/ppermute | solution.py:272
  38.4 13.3 %collective-permute-start = (bf16[2,2,8,8,128]{4,3,2,1,0:T(8,128)(2,1)S(1)}, bf16[2,2,8,8,128]{4,3,2,1,0:T(8,128)(2,1)S(1)}, u32[]{:S(2)}, u32[]{:S(2)}) collective-permute-start(bf16[2,2,8,8,128]{4,3,2,1,0:T(8,128)(2,1)S(1)} %get-tuple-element.24), channel_id=1, source_target_pairs={{0,4},{1,5},{2,6},{3,7},{4,0},{5,1},{6,2},{7,3},{8,12},{9,13},{10,... | collective-permute-start | bytes 196616 | tf_op jit(solution)/shard_map/ppermute | solution.py:272
  42.4 11.1 %collective-permute-start.3 = (bf16[1,2,2,8,8,128]{5,4,3,2,1,0:T(8,128)(2,1)S(1)}, bf16[1,2,2,8,8,128]{5,4,3,2,1,0:T(8,128)(2,1)S(1)}, u32[]{:S(2)}, u32[]{:S(2)}) collective-permute-start(bf16[1,2,2,8,8,128]{5,4,3,2,1,0:T(8,128)(2,1)S(1)} %bitcast.44), channel_id=1, source_target_pairs={{0,1},{1,2},{2,3},{3,0},{4,5},{5,6},{6,7},{7,4},{8,9},{9,10},{10,1... | collective-permute-start | bytes 196616 | tf_op jit(solution)/shard_map/ppermute | solution.py:277
  46.8 8.3 %collective-permute-start.4 = (bf16[1,2,2,8,8,128]{5,4,3,2,1,0:T(8,128)(2,1)S(1)}, bf16[1,2,2,8,8,128]{5,4,3,2,1,0:T(8,128)(2,1)S(1)}, u32[]{:S(2)}, u32[]{:S(2)}) collective-permute-start(bf16[1,2,2,8,8,128]{5,4,3,2,1,0:T(8,128)(2,1)S(1)} %bitcast.45), channel_id=1, source_target_pairs={{0,2},{1,3},{2,0},{3,1},{4,6},{5,7},{6,4},{7,5},{8,10},{9,11},{10,... | collective-permute-start | bytes 196616 | tf_op jit(solution)/shard_map/ppermute | solution.py:277
  49.0 6.9 %collective-permute-start.5 = (bf16[1,2,2,8,8,128]{5,4,3,2,1,0:T(8,128)(2,1)S(1)}, bf16[1,2,2,8,8,128]{5,4,3,2,1,0:T(8,128)(2,1)S(1)}, u32[]{:S(2)}, u32[]{:S(2)}) collective-permute-start(bf16[1,2,2,8,8,128]{5,4,3,2,1,0:T(8,128)(2,1)S(1)} %bitcast.46), channel_id=1, source_target_pairs={{0,3},{1,0},{2,1},{3,2},{4,7},{5,4},{6,5},{7,6},{8,11},{9,8},{10,9... | collective-permute-start | bytes 196616 | tf_op jit(solution)/shard_map/ppermute | solution.py:277
  55.9 0.6 copy-start.6
  56.6 9.7 %collective-permute-start.6 = (bf16[3,2,2,8,8,128]{5,4,3,2,1,0:T(8,128)(2,1)S(1)}, bf16[3,2,2,8,8,128]{5,4,3,2,1,0:T(8,128)(2,1)S(1)}, u32[]{:S(2)}, u32[]{:S(2)}) collective-permute-start(bf16[3,2,2,8,8,128]{5,4,3,2,1,0:T(8,128)(2,1)S(1)} %pad_maximum_fusion.refs_4_), channel_id=1, source_target_pairs={{0,1},{1,2},{2,3},{3,0},{4,5},{5,6},{6,7},{7,4},{8,9},{9,10},{10,1... | collective-permute-start | bytes 589832 | tf_op jit(solution)/shard_map/ppermute | solution.py:277
  58.9 19.0 %collective-permute-start.7 = (bf16[3,2,2,8,8,128]{5,4,3,2,1,0:T(8,128)(2,1)S(1)}, bf16[3,2,2,8,8,128]{5,4,3,2,1,0:T(8,128)(2,1)S(1)}, u32[]{:S(2)}, u32[]{:S(2)}) collective-permute-start(bf16[3,2,2,8,8,128]{5,4,3,2,1,0:T(8,128)(2,1)S(1)} %pad_maximum_fusion.refs_4_), channel_id=1, source_target_pairs={{0,2},{1,3},{2,0},{3,1},{4,6},{5,7},{6,4},{7,5},{8,10},{9,11},{10,... | collective-permute-start | bytes 589832 | tf_op jit(solution)/shard_map/ppermute | solution.py:277
  63.2 14.8 %collective-permute-start.8 = (bf16[3,2,2,8,8,128]{5,4,3,2,1,0:T(8,128)(2,1)S(1)}, bf16[3,2,2,8,8,128]{5,4,3,2,1,0:T(8,128)(2,1)S(1)}, u32[]{:S(2)}, u32[]{:S(2)}) collective-permute-start(bf16[3,2,2,8,8,128]{5,4,3,2,1,0:T(8,128)(2,1)S(1)} %pad_maximum_fusion.refs_4_), channel_id=1, source_target_pairs={{0,3},{1,0},{2,1},{3,2},{4,7},{5,4},{6,5},{7,6},{8,11},{9,8},{10,9... | collective-permute-start | bytes 589832 | tf_op jit(solution)/shard_map/ppermute | solution.py:277
  78.0 0.8 copy-start.7
  90.8 17.7 %copy-start.5 = (s32[1,16,2]{1,2,0:T(2,128)S(1)}, s32[1,16,2]{1,2,0:T(2,128)}, u32[]{:S(2)}) copy-start(s32[1,16,2]{1,2,0:T(2,128)} %param.9) | copy-start | bytes 388
  90.8 63.1 %all-to-all-start.2 = ((bf16[16,2,128,128]{3,2,1,0:T(8,128)(2,1)}), bf16[16,2,128,128]{3,2,1,0:T(8,128)(2,1)S(1)}, u32[]{:S(2)}, u32[]{:S(2)}) async-start(bf16[16,2,128,128]{3,2,1,0:T(8,128)(2,1)} %bitcast.20), calls=%async_computation.2 | async-start | bytes 2097152 | tf_op jit(solution)/shard_map/all_to_all | solution.py:335
  99.4 15.4 %collective-permute-start.12 = (bf16[3,2,2,8,8,128]{5,4,3,2,1,0:T(8,128)(2,1)S(1)}, bf16[3,2,2,8,8,128]{5,4,3,2,1,0:T(8,128)(2,1)S(1)}, u32[]{:S(2)}, u32[]{:S(2)}) collective-permute-start(bf16[3,2,2,8,8,128]{5,4,3,2,1,0:T(8,128)(2,1)S(1)} %get-tuple-element.37), channel_id=1, source_target_pairs={{0,3},{1,0},{2,1},{3,2},{4,7},{5,4},{6,5},{7,6},{8,11},{9,8},{10,9... | collective-permute-start | bytes 589832 | tf_op jit(solution)/shard_map/ppermute | solution.py:277
  101.3 17.6 %collective-permute-start.13 = (bf16[3,2,2,8,8,128]{5,4,3,2,1,0:T(8,128)(2,1)S(1)}, bf16[3,2,2,8,8,128]{5,4,3,2,1,0:T(8,128)(2,1)S(1)}, u32[]{:S(2)}, u32[]{:S(2)}) collective-permute-start(bf16[3,2,2,8,8,128]{5,4,3,2,1,0:T(8,128)(2,1)S(1)} %get-tuple-element.38), channel_id=1, source_target_pairs={{0,2},{1,3},{2,0},{3,1},{4,6},{5,7},{6,4},{7,5},{8,10},{9,11},{10,... | collective-permute-start | bytes 589832 | tf_op jit(solution)/shard_map/ppermute | solution.py:277
  103.5 15.3 %collective-permute-start.14 = (bf16[3,2,2,8,8,128]{5,4,3,2,1,0:T(8,128)(2,1)S(1)}, bf16[3,2,2,8,8,128]{5,4,3,2,1,0:T(8,128)(2,1)S(1)}, u32[]{:S(2)}, u32[]{:S(2)}) collective-permute-start(bf16[3,2,2,8,8,128]{5,4,3,2,1,0:T(8,128)(2,1)S(1)} %get-tuple-element.39), channel_id=1, source_target_pairs={{0,1},{1,2},{2,3},{3,0},{4,5},{5,6},{6,7},{7,4},{8,9},{9,10},{10,1... | collective-permute-start | bytes 589832 | tf_op jit(solution)/shard_map/ppermute | solution.py:277
  108.6 29.8 %collective-permute-start.10 = (bf16[1,2,2,8,8,128]{5,4,3,2,1,0:T(8,128)(2,1)S(1)}, bf16[1,2,2,8,8,128]{5,4,3,2,1,0:T(8,128)(2,1)S(1)}, u32[]{:S(2)}, u32[]{:S(2)}) collective-permute-start(bf16[1,2,2,8,8,128]{5,4,3,2,1,0:T(8,128)(2,1)S(1)} %get-tuple-element.34), channel_id=1, source_target_pairs={{0,2},{1,3},{2,0},{3,1},{4,6},{5,7},{6,4},{7,5},{8,10},{9,11},{10,... | collective-permute-start | bytes 196616 | tf_op jit(solution)/shard_map/ppermute | solution.py:277
  111.9 28.3 %collective-permute-start.11 = (bf16[1,2,2,8,8,128]{5,4,3,2,1,0:T(8,128)(2,1)S(1)}, bf16[1,2,2,8,8,128]{5,4,3,2,1,0:T(8,128)(2,1)S(1)}, u32[]{:S(2)}, u32[]{:S(2)}) collective-permute-start(bf16[1,2,2,8,8,128]{5,4,3,2,1,0:T(8,128)(2,1)S(1)} %get-tuple-element.35), channel_id=1, source_target_pairs={{0,1},{1,2},{2,3},{3,0},{4,5},{5,6},{6,7},{7,4},{8,9},{9,10},{10,1... | collective-permute-start | bytes 196616 | tf_op jit(solution)/shard_map/ppermute | solution.py:277
  114.8 25.5 %collective-permute-start.9 = (bf16[1,2,2,8,8,128]{5,4,3,2,1,0:T(8,128)(2,1)S(1)}, bf16[1,2,2,8,8,128]{5,4,3,2,1,0:T(8,128)(2,1)S(1)}, u32[]{:S(2)}, u32[]{:S(2)}) collective-permute-start(bf16[1,2,2,8,8,128]{5,4,3,2,1,0:T(8,128)(2,1)S(1)} %get-tuple-element.33), channel_id=1, source_target_pairs={{0,3},{1,0},{2,1},{3,2},{4,7},{5,4},{6,5},{7,6},{8,11},{9,8},{10,9... | collective-permute-start | bytes 196616 | tf_op jit(solution)/shard_map/ppermute | solution.py:277
  119.0 21.3 %collective-permute-start.15 = (bf16[2,2,8,8,128]{4,3,2,1,0:T(8,128)(2,1)S(1)}, bf16[2,2,8,8,128]{4,3,2,1,0:T(8,128)(2,1)S(1)}, u32[]{:S(2)}, u32[]{:S(2)}) collective-permute-start(bf16[2,2,8,8,128]{4,3,2,1,0:T(8,128)(2,1)S(1)} %get-tuple-element.48), channel_id=1, source_target_pairs={{0,4},{1,5},{2,6},{3,7},{4,0},{5,1},{6,2},{7,3},{8,12},{9,13},{10,... | collective-permute-start | bytes 196616 | tf_op jit(solution)/shard_map/ppermute | solution.py:272
  125.7 14.9 %collective-permute-start.16 = (bf16[2,2,8,8,128]{4,3,2,1,0:T(8,128)(2,1)S(1)}, bf16[2,2,8,8,128]{4,3,2,1,0:T(8,128)(2,1)S(1)}, u32[]{:S(2)}, u32[]{:S(2)}) collective-permute-start(bf16[2,2,8,8,128]{4,3,2,1,0:T(8,128)(2,1)S(1)} %get-tuple-element.47), channel_id=1, source_target_pairs={{0,15},{1,14},{2,13},{3,12},{4,11},{5,10},{6,9},{7,8},{8,7},{9,6},... | collective-permute-start | bytes 196616 | tf_op jit(solution)/shard_map/ppermute | solution.py:272
  138.3 15.6 %collective-permute-start.17 = (bf16[2,2,8,8,128]{4,3,2,1,0:T(8,128)(2,1)S(1)}, bf16[2,2,8,8,128]{4,3,2,1,0:T(8,128)(2,1)S(1)}, u32[]{:S(2)}, u32[]{:S(2)}) collective-permute-start(bf16[2,2,8,8,128]{4,3,2,1,0:T(8,128)(2,1)S(1)} %get-tuple-element.46), channel_id=1, source_target_pairs={{0,11},{1,10},{2,9},{3,8},{4,15},{5,14},{6,13},{7,12},{8,3},{9,2},... | collective-permute-start | bytes 196616 | tf_op jit(solution)/shard_map/ppermute | solution.py:272
  155.3 14.9 %all-to-all-start.3 = ((bf16[32,2,2,2,4,128]{5,4,3,2,1,0:T(4,128)(2,1)}), bf16[32,2,2,2,4,128]{5,4,3,2,1,0:T(4,128)(2,1)S(1)}, u32[]{:S(2)}, u32[]{:S(2)}) async-start(bf16[32,2,2,2,4,128]{5,4,3,2,1,0:T(4,128)(2,1)} %bitcast.24), calls=%async_computation.3 | async-start | bytes 524288 | tf_op jit(solution)/shard_map/all_to_all | solution.py:310

commit v7 on v6

--- a/solution.py
+++ b/solution.py
@@ -337,8 +337,9 @@
         "dp", split_axis=0, concat_axis=0, tiled=True,
     )
     far_terms = near_terms(terms[NEAR:])
+    own_terms, far_terms = lax.optimization_barrier((terms[:NEAR], far_terms))
     back = [far_swap(total(far_terms, index), flip) for index, flip in enumerate(FAR)]
-    own_sum = total(near_terms(terms[:NEAR]), 0)
+    own_sum = total(near_terms(own_terms), 0)
     swapped, query_returned = lax.optimization_barrier(([own_sum] + back, query_returned))
     kv_returned = over_plane(
         local_call(kv_back_kernel, "kv_back", [my_recv, place], swapped, traveling)

time: 173 us -> 179 us (1.035)
  the two profiles are of different devices: /device:TPU:97 before, /device:TPU:1 now
where the time goes in v7:
time: 179 us; the launch traced here: 177 us
  starting transfers between devices  108 us (60%)
  waiting for transfers between devices  38.8 us (22%)
  Pallas kernels  21.3 us (12%)
  local copies, waits for them, and re-layouts  7.23 us (4%)
    ppermute x12, starting transfers between devices, near_shift(): return lax.ppermute(values, 'z', pairs)  43.3 us
    ppermute x6, starting transfers between devices, far_swap(): lax.ppermute(values, 'z', [(place, place ^ flip) for place in range(16)])  35.8 us
    ppermute x12, waiting for transfers between devices, near_shift(): return lax.ppermute(values, 'z', pairs)  19.8 us
    all_to_all x2, starting transfers between devices, over_plane(): lax.all_to_all(values.reshape((2 * n_replicas,) + values.shape[2:]), PLAN...  18.6 us
    pallas_call x1, Pallas kernels, attention(): pl.pallas_call(attention_kernel, out_shape=(jax.ShapeDtypeStruct((slots,...  14.2 us
    all_to_all x2, waiting for transfers between devices, over_plane(): lax.all_to_all(values.reshape((2 * n_replicas,) + values.shape[2:]), PLAN...  11.3 us
    ppermute x6, waiting for transfers between devices, far_swap(): lax.ppermute(values, 'z', [(place, place ^ flip) for place in range(16)])  7.64 us
    all_to_all x1, starting transfers between devices, on_device(): lax.all_to_all(query_back.reshape(n_replicas, slot_cap, tile_rows, row_wi...  6.35 us
  transfers between devices with their start and end apart: 22, of which 8 were waited for; matrix products, arithmetic and copies ran while one was open for 1% of the time, Pallas kernels for 2%

profile of v7, /device:TPU:1, one launch (start us, length us, event | category | flops | bytes accessed | tf_op | source)
XLA Modules:
  0.0 177.1 jit_solution(3309270814156519209)
XLA Ops:
  2.2 1.4 kv_pack.1
  3.7 10.4 %all-to-all-start = ((bf16[32,2,2,2,4,128]{5,4,3,2,1,0:T(4,128)(2,1)}), bf16[32,2,2,2,4,128]{5,4,3,2,1,0:T(4,128)(2,1)S(1)}, u32[]{:S(2)}, u32[]{:S(2)}) async-start(bf16[32,2,2,2,4,128]{5,4,3,2,1,0:T(4,128)(2,1)} %bitcast.7), calls=%async_computation | async-start | bytes 524288 | tf_op jit(solution)/shard_map/all_to_all | solution.py:310
  16.8 2.3 %pack_rows.1 = bf16[32,2,128,128]{3,2,1,0:T(8,128)(2,1)} custom-call(s32[2,16]{1,0:T(2,128)S(1)} %bitcast.42, bf16[16,128,128]{2,1,0:T(8,128)(2,1)S(1)} %copy-done, bf16[16,128,128]{2,1,0:T(8,128)(2,1)S(1)} %copy-done.1), custom_call_target="tpu_custom_call" | custom-call | tf_op jit(solution)/shard_map/pack_rows/pallas_call | solution.py:37
  19.1 3.9 %all-to-all-done = bf16[32,2,2,2,4,128]{5,4,3,2,1,0:T(4,128)(2,1)S(1)} async-done(((bf16[32,2,2,2,4,128]{5,4,3,2,1,0:T(4,128)(2,1)}), bf16[32,2,2,2,4,128]{5,4,3,2,1,0:T(4,128)(2,1)S(1)}, u32[]{:S(2)}, u32[]{:S(2)}) %all-to-all-start) | async-done | bytes 262176 | tf_op jit(solution)/shard_map/all_to_all | solution.py:310
  23.0 4.1 %all-to-all-start.1 = ((bf16[16,2,2,128,128]{4,3,2,1,0:T(8,128)(2,1)}), bf16[16,2,2,128,128]{4,3,2,1,0:T(8,128)(2,1)S(1)}, u32[]{:S(2)}, u32[]{:S(2)}) async-start(bf16[16,2,2,128,128]{4,3,2,1,0:T(8,128)(2,1)} %bitcast.14), calls=%async_computation.1 | async-start | bytes 4194304 | tf_op jit(solution)/shard_map/all_to_all | solution.py:323
  27.7 9.2 %collective-permute-start.1 = (bf16[2,2,8,8,128]{4,3,2,1,0:T(8,128)(2,1)S(1)}, bf16[2,2,8,8,128]{4,3,2,1,0:T(8,128)(2,1)S(1)}, u32[]{:S(2)}, u32[]{:S(2)}) collective-permute-start(bf16[2,2,8,8,128]{4,3,2,1,0:T(8,128)(2,1)S(1)} %get-tuple-element.33), channel_id=1, source_target_pairs={{0,15},{1,14},{2,13},{3,12},{4,11},{5,10},{6,9},{7,8},{8,7},{9,6},... | collective-permute-start | bytes 196616 | tf_op jit(solution)/shard_map/ppermute | solution.py:272
  37.0 4.9 %collective-permute-start.2 = (bf16[2,2,8,8,128]{4,3,2,1,0:T(8,128)(2,1)S(1)}, bf16[2,2,8,8,128]{4,3,2,1,0:T(8,128)(2,1)S(1)}, u32[]{:S(2)}, u32[]{:S(2)}) collective-permute-start(bf16[2,2,8,8,128]{4,3,2,1,0:T(8,128)(2,1)S(1)} %get-tuple-element.33), channel_id=1, source_target_pairs={{0,11},{1,10},{2,9},{3,8},{4,15},{5,14},{6,13},{7,12},{8,3},{9,2},... | collective-permute-start | bytes 196616 | tf_op jit(solution)/shard_map/ppermute | solution.py:272
  41.9 4.9 %collective-permute-start = (bf16[2,2,8,8,128]{4,3,2,1,0:T(8,128)(2,1)S(1)}, bf16[2,2,8,8,128]{4,3,2,1,0:T(8,128)(2,1)S(1)}, u32[]{:S(2)}, u32[]{:S(2)}) collective-permute-start(bf16[2,2,8,8,128]{4,3,2,1,0:T(8,128)(2,1)S(1)} %get-tuple-element.32), channel_id=1, source_target_pairs={{0,4},{1,5},{2,6},{3,7},{4,0},{5,1},{6,2},{7,3},{8,12},{9,13},{10,... | collective-permute-start | bytes 196616 | tf_op jit(solution)/shard_map/ppermute | solution.py:272
  46.8 2.7 %collective-permute-start.3 = (bf16[1,2,2,8,8,128]{5,4,3,2,1,0:T(8,128)(2,1)S(1)}, bf16[1,2,2,8,8,128]{5,4,3,2,1,0:T(8,128)(2,1)S(1)}, u32[]{:S(2)}, u32[]{:S(2)}) collective-permute-start(bf16[1,2,2,8,8,128]{5,4,3,2,1,0:T(8,128)(2,1)S(1)} %bitcast.44), channel_id=1, source_target_pairs={{0,1},{1,2},{2,3},{3,0},{4,5},{5,6},{6,7},{7,4},{8,9},{9,10},{10,1... | collective-permute-start | bytes 196616 | tf_op jit(solution)/shard_map/ppermute | solution.py:277
  49.5 2.4 %collective-permute-start.4 = (bf16[1,2,2,8,8,128]{5,4,3,2,1,0:T(8,128)(2,1)S(1)}, bf16[1,2,2,8,8,128]{5,4,3,2,1,0:T(8,128)(2,1)S(1)}, u32[]{:S(2)}, u32[]{:S(2)}) collective-permute-start(bf16[1,2,2,8,8,128]{5,4,3,2,1,0:T(8,128)(2,1)S(1)} %bitcast.45), channel_id=1, source_target_pairs={{0,2},{1,3},{2,0},{3,1},{4,6},{5,7},{6,4},{7,5},{8,10},{9,11},{10,... | collective-permute-start | bytes 196616 | tf_op jit(solution)/shard_map/ppermute | solution.py:277
  51.9 4.3 %collective-permute-start.5 = (bf16[1,2,2,8,8,128]{5,4,3,2,1,0:T(8,128)(2,1)S(1)}, bf16[1,2,2,8,8,128]{5,4,3,2,1,0:T(8,128)(2,1)S(1)}, u32[]{:S(2)}, u32[]{:S(2)}) collective-permute-start(bf16[1,2,2,8,8,128]{5,4,3,2,1,0:T(8,128)(2,1)S(1)} %bitcast.46), channel_id=1, source_target_pairs={{0,3},{1,0},{2,1},{3,2},{4,7},{5,4},{6,5},{7,6},{8,11},{9,8},{10,9... | collective-permute-start | bytes 196616 | tf_op jit(solution)/shard_map/ppermute | solution.py:277
  59.0 4.9 %collective-permute-start.6 = (bf16[3,2,2,8,8,128]{5,4,3,2,1,0:T(8,128)(2,1)S(1)}, bf16[3,2,2,8,8,128]{5,4,3,2,1,0:T(8,128)(2,1)S(1)}, u32[]{:S(2)}, u32[]{:S(2)}) collective-permute-start(bf16[3,2,2,8,8,128]{5,4,3,2,1,0:T(8,128)(2,1)S(1)} %pad_maximum_fusion.refs_4_), channel_id=1, source_target_pairs={{0,1},{1,2},{2,3},{3,0},{4,5},{5,6},{6,7},{7,4},{8,9},{9,10},{10,1... | collective-permute-start | bytes 589832 | tf_op jit(solution)/shard_map/ppermute | solution.py:277
  63.9 2.1 %collective-permute-start.7 = (bf16[3,2,2,8,8,128]{5,4,3,2,1,0:T(8,128)(2,1)S(1)}, bf16[3,2,2,8,8,128]{5,4,3,2,1,0:T(8,128)(2,1)S(1)}, u32[]{:S(2)}, u32[]{:S(2)}) collective-permute-start(bf16[3,2,2,8,8,128]{5,4,3,2,1,0:T(8,128)(2,1)S(1)} %pad_maximum_fusion.refs_4_), channel_id=1, source_target_pairs={{0,2},{1,3},{2,0},{3,1},{4,6},{5,7},{6,4},{7,5},{8,10},{9,11},{10,... | collective-permute-start | bytes 589832 | tf_op jit(solution)/shard_map/ppermute | solution.py:277
  66.0 4.3 %collective-permute-start.8 = (bf16[3,2,2,8,8,128]{5,4,3,2,1,0:T(8,128)(2,1)S(1)}, bf16[3,2,2,8,8,128]{5,4,3,2,1,0:T(8,128)(2,1)S(1)}, u32[]{:S(2)}, u32[]{:S(2)}) collective-permute-start(bf16[3,2,2,8,8,128]{5,4,3,2,1,0:T(8,128)(2,1)S(1)} %pad_maximum_fusion.refs_4_), channel_id=1, source_target_pairs={{0,3},{1,0},{2,1},{3,2},{4,7},{5,4},{6,5},{7,6},{8,11},{9,8},{10,9... | collective-permute-start | bytes 589832 | tf_op jit(solution)/shard_map/ppermute | solution.py:277
  70.5 7.5 %collective-permute-done.7.refs_6_ = bf16[3,2,2,8,8,128]{5,4,3,2,1,0:T(8,128)(2,1)S(1)} collective-permute-done((bf16[3,2,2,8,8,128]{5,4,3,2,1,0:T(8,128)(2,1)S(1)}, bf16[3,2,2,8,8,128]{5,4,3,2,1,0:T(8,128)(2,1)S(1)}, u32[]{:S(2)}, u32[]{:S(2)}) %collective-permute-start.7) | collective-permute-done | bytes 196640 | tf_op jit(solution)/shard_map/ppermute | solution.py:277
  78.8 14.2 %attention_backward.1 = (bf16[32,128,128]{2,1,0:T(8,128)(2,1)}, bf16[1,2,2,8,8,128]{5,4,3,2,1,0:T(8,128)(2,1)S(1)}, bf16[1,2,2,8,8,128]{5,4,3,2,1,0:T(8,128)(2,1...) custom-call(s32[16]{0:T(128)S(1)} %dynamic-slice_bitcast_fusion.recv, ...), custom_call_target="tpu_custom_call" | custom-call | flops 2000000000 | bytes 6291456 | tf_op jit(solution)/shard_map/attention_backward/pallas_call | solution.py:173
  93.0 6.3 %all-to-all-start.2 = ((bf16[16,2,128,128]{3,2,1,0:T(8,128)(2,1)}), bf16[16,2,128,128]{3,2,1,0:T(8,128)(2,1)S(1)}, u32[]{:S(2)}, u32[]{:S(2)}) async-start(bf16[16,2,128,128]{3,2,1,0:T(8,128)(2,1)} %bitcast.20), calls=%async_computation.2 | async-start | bytes 2097152 | tf_op jit(solution)/shard_map/all_to_all | solution.py:335
  99.5 5.4 %collective-permute-start.10 = (bf16[3,2,2,8,8,128]{5,4,3,2,1,0:T(8,128)(2,1)S(1)}, bf16[3,2,2,8,8,128]{5,4,3,2,1,0:T(8,128)(2,1)S(1)}, u32[]{:S(2)}, u32[]{:S(2)}) collective-permute-start(bf16[3,2,2,8,8,128]{5,4,3,2,1,0:T(8,128)(2,1)S(1)} %get-tuple-element.46), channel_id=1, source_target_pairs={{0,2},{1,3},{2,0},{3,1},{4,6},{5,7},{6,4},{7,5},{8,10},{9,11},{10,... | collective-permute-start | bytes 589832 | tf_op jit(solution)/shard_map/ppermute | solution.py:277
  104.9 3.9 %collective-permute-start.11 = (bf16[3,2,2,8,8,128]{5,4,3,2,1,0:T(8,128)(2,1)S(1)}, bf16[3,2,2,8,8,128]{5,4,3,2,1,0:T(8,128)(2,1)S(1)}, u32[]{:S(2)}, u32[]{:S(2)}) collective-permute-start(bf16[3,2,2,8,8,128]{5,4,3,2,1,0:T(8,128)(2,1)S(1)} %get-tuple-element.47), channel_id=1, source_target_pairs={{0,1},{1,2},{2,3},{3,0},{4,5},{5,6},{6,7},{7,4},{8,9},{9,10},{10,1... | collective-permute-start | bytes 589832 | tf_op jit(solution)/shard_map/ppermute | solution.py:277
  108.9 3.1 %collective-permute-start.9 = (bf16[3,2,2,8,8,128]{5,4,3,2,1,0:T(8,128)(2,1)S(1)}, bf16[3,2,2,8,8,128]{5,4,3,2,1,0:T(8,128)(2,1)S(1)}, u32[]{:S(2)}, u32[]{:S(2)}) collective-permute-start(bf16[3,2,2,8,8,128]{5,4,3,2,1,0:T(8,128)(2,1)S(1)} %get-tuple-element.45), channel_id=1, source_target_pairs={{0,3},{1,0},{2,1},{3,2},{4,7},{5,4},{6,5},{7,6},{8,11},{9,8},{10,9... | collective-permute-start | bytes 589832 | tf_op jit(solution)/shard_map/ppermute | solution.py:277
  112.1 6.4 %collective-permute-done.10 = bf16[3,2,2,8,8,128]{5,4,3,2,1,0:T(8,128)(2,1)S(1)} collective-permute-done((bf16[3,2,2,8,8,128]{5,4,3,2,1,0:T(8,128)(2,1)S(1)}, bf16[3,2,2,8,8,128]{5,4,3,2,1,0:T(8,128)(2,1)S(1)}, u32[]{:S(2)}, u32[]{:S(2)}) %collective-permute-start.10) | collective-permute-done | bytes 196640 | tf_op jit(solution)/shard_map/ppermute | solution.py:277
  118.5 3.8 %collective-permute-done.9 = bf16[3,2,2,8,8,128]{5,4,3,2,1,0:T(8,128)(2,1)S(1)} collective-permute-done((bf16[3,2,2,8,8,128]{5,4,3,2,1,0:T(8,128)(2,1)S(1)}, bf16[3,2,2,8,8,128]{5,4,3,2,1,0:T(8,128)(2,1)S(1)}, u32[]{:S(2)}, u32[]{:S(2)}) %collective-permute-start.9) | collective-permute-done | bytes 196640 | tf_op jit(solution)/shard_map/ppermute | solution.py:277
  122.3 3.9 %collective-permute-start.12 = (bf16[1,2,2,8,8,128]{5,4,3,2,1,0:T(8,128)(2,1)S(1)}, bf16[1,2,2,8,8,128]{5,4,3,2,1,0:T(8,128)(2,1)S(1)}, u32[]{:S(2)}, u32[]{:S(2)}) collective-permute-start(bf16[1,2,2,8,8,128]{5,4,3,2,1,0:T(8,128)(2,1)S(1)} %get-tuple-element.49), channel_id=1, source_target_pairs={{0,3},{1,0},{2,1},{3,2},{4,7},{5,4},{6,5},{7,6},{8,11},{9,8},{10,9... | collective-permute-start | bytes 196616 | tf_op jit(solution)/shard_map/ppermute | solution.py:277
  126.3 2.9 %collective-permute-start.13 = (bf16[1,2,2,8,8,128]{5,4,3,2,1,0:T(8,128)(2,1)S(1)}, bf16[1,2,2,8,8,128]{5,4,3,2,1,0:T(8,128)(2,1)S(1)}, u32[]{:S(2)}, u32[]{:S(2)}) collective-permute-start(bf16[1,2,2,8,8,128]{5,4,3,2,1,0:T(8,128)(2,1)S(1)} %get-tuple-element.50), channel_id=1, source_target_pairs={{0,2},{1,3},{2,0},{3,1},{4,6},{5,7},{6,4},{7,5},{8,10},{9,11},{10,... | collective-permute-start | bytes 196616 | tf_op jit(solution)/shard_map/ppermute | solution.py:277
  129.2 3.4 %collective-permute-start.14 = (bf16[1,2,2,8,8,128]{5,4,3,2,1,0:T(8,128)(2,1)S(1)}, bf16[1,2,2,8,8,128]{5,4,3,2,1,0:T(8,128)(2,1)S(1)}, u32[]{:S(2)}, u32[]{:S(2)}) collective-permute-start(bf16[1,2,2,8,8,128]{5,4,3,2,1,0:T(8,128)(2,1)S(1)} %get-tuple-element.51), channel_id=1, source_target_pairs={{0,1},{1,2},{2,3},{3,0},{4,5},{5,6},{6,7},{7,4},{8,9},{9,10},{10,1... | collective-permute-start | bytes 196616 | tf_op jit(solution)/shard_map/ppermute | solution.py:277
  132.7 6.0 %collective-permute-start.15 = (bf16[2,2,8,8,128]{4,3,2,1,0:T(8,128)(2,1)S(1)}, bf16[2,2,8,8,128]{4,3,2,1,0:T(8,128)(2,1)S(1)}, u32[]{:S(2)}, u32[]{:S(2)}) collective-permute-start(bf16[2,2,8,8,128]{4,3,2,1,0:T(8,128)(2,1)S(1)} %get-tuple-element.64), channel_id=1, source_target_pairs={{0,4},{1,5},{2,6},{3,7},{4,0},{5,1},{6,2},{7,3},{8,12},{9,13},{10,... | collective-permute-start | bytes 196616 | tf_op jit(solution)/shard_map/ppermute | solution.py:272
  138.7 6.5 %collective-permute-start.16 = (bf16[2,2,8,8,128]{4,3,2,1,0:T(8,128)(2,1)S(1)}, bf16[2,2,8,8,128]{4,3,2,1,0:T(8,128)(2,1)S(1)}, u32[]{:S(2)}, u32[]{:S(2)}) collective-permute-start(bf16[2,2,8,8,128]{4,3,2,1,0:T(8,128)(2,1)S(1)} %get-tuple-element.63), channel_id=1, source_target_pairs={{0,15},{1,14},{2,13},{3,12},{4,11},{5,10},{6,9},{7,8},{8,7},{9,6},... | collective-permute-start | bytes 196616 | tf_op jit(solution)/shard_map/ppermute | solution.py:272
  145.2 4.3 %collective-permute-start.17 = (bf16[2,2,8,8,128]{4,3,2,1,0:T(8,128)(2,1)S(1)}, bf16[2,2,8,8,128]{4,3,2,1,0:T(8,128)(2,1)S(1)}, u32[]{:S(2)}, u32[]{:S(2)}) collective-permute-start(bf16[2,2,8,8,128]{4,3,2,1,0:T(8,128)(2,1)S(1)} %get-tuple-element.62), channel_id=1, source_target_pairs={{0,11},{1,10},{2,9},{3,8},{4,15},{5,14},{6,13},{7,12},{8,3},{9,2},... | collective-permute-start | bytes 196616 | tf_op jit(solution)/shard_map/ppermute | solution.py:272
  149.6 7.6 %collective-permute-done.17.p3 = bf16[2,2,8,8,128]{4,3,2,1,0:T(8,128)(2,1)S(1)} collective-permute-done((bf16[2,2,8,8,128]{4,3,2,1,0:T(8,128)(2,1)S(1)}, bf16[2,2,8,8,128]{4,3,2,1,0:T(8,128)(2,1)S(1)}, u32[]{:S(2)}, u32[]{:S(2)}) %collective-permute-start.17) | collective-permute-done | bytes 65568 | tf_op jit(solution)/shard_map/ppermute | solution.py:272
  158.6 8.2 %all-to-all-start.3 = ((bf16[32,2,2,2,4,128]{5,4,3,2,1,0:T(4,128)(2,1)}), bf16[32,2,2,2,4,128]{5,4,3,2,1,0:T(4,128)(2,1)S(1)}, u32[]{:S(2)}, u32[]{:S(2)}) async-start(bf16[32,2,2,2,4,128]{5,4,3,2,1,0:T(4,128)(2,1)} %bitcast.24), calls=%async_computation.3 | async-start | bytes 524288 | tf_op jit(solution)/shard_map/all_to_all | solution.py:310
  166.9 1.4 gather_fusion
  168.3 7.4 %all-to-all-done.3 = bf16[32,2,2,2,4,128]{5,4,3,2,1,0:T(4,128)(2,1)S(1)} async-done(((bf16[32,2,2,2,4,128]{5,4,3,2,1,0:T(4,128)(2,1)}), bf16[32,2,2,2,4,128]{5,4,3,2,1,0:T(4,128)(2,1)S(1)}, u32[]{:S(2)}, u32[]{:S(2)}) %all-to-all-start.3) | async-done | bytes 262176 | tf_op jit(solution)/shard_map/all_to_all | solution.py:310
  (50 shorter events, 12.0 us)
Async XLA Ops:
  0.6 0.9 copy-start.2
  1.5 0.7 copy-start.3
  3.7 19.3 %all-to-all-start = ((bf16[32,2,2,2,4,128]{5,4,3,2,1,0:T(4,128)(2,1)}), bf16[32,2,2,2,4,128]{5,4,3,2,1,0:T(4,128)(2,1)S(1)}, u32[]{:S(2)}, u32[]{:S(2)}) async-start(bf16[32,2,2,2,4,128]{5,4,3,2,1,0:T(4,128)(2,1)} %bitcast.7), calls=%async_computation | async-start | bytes 524288 | tf_op jit(solution)/shard_map/all_to_all | solution.py:310
  14.1 1.0 copy-start
  15.1 1.0 copy-start.1
  16.2 0.7 copy-start.4
  23.0 4.1 %copy-start.8 = (s32[16,16]{1,0:T(8,128)S(1)}, s32[16,16]{1,0:T(8,128)}, u32[]{:S(2)}) copy-start(s32[16,16]{1,0:T(8,128)} %param.10) | copy-start | bytes 3076
  23.0 47.3 %copy-start.9 = (s32[1,16]{1,0:T(1,128)S(1)}, s32[1,16]{1,0:T(1,128)}, u32[]{:S(2)}) copy-start(s32[1,16]{1,0:T(1,128)} %param.11) | copy-start | bytes 196
  23.0 36.0 %all-to-all-start.1 = ((bf16[16,2,2,128,128]{4,3,2,1,0:T(8,128)(2,1)}), bf16[16,2,2,128,128]{4,3,2,1,0:T(8,128)(2,1)S(1)}, u32[]{:S(2)}, u32[]{:S(2)}) async-start(bf16[16,2,2,128,128]{4,3,2,1,0:T(8,128)(2,1)} %bitcast.14), calls=%async_computation.1 | async-start | bytes 4194304 | tf_op jit(solution)/shard_map/all_to_all | solution.py:323
  27.7 24.1 %collective-permute-start.1 = (bf16[2,2,8,8,128]{4,3,2,1,0:T(8,128)(2,1)S(1)}, bf16[2,2,8,8,128]{4,3,2,1,0:T(8,128)(2,1)S(1)}, u32[]{:S(2)}, u32[]{:S(2)}) collective-permute-start(bf16[2,2,8,8,128]{4,3,2,1,0:T(8,128)(2,1)S(1)} %get-tuple-element.33), channel_id=1, source_target_pairs={{0,15},{1,14},{2,13},{3,12},{4,11},{5,10},{6,9},{7,8},{8,7},{9,6},... | collective-permute-start | bytes 196616 | tf_op jit(solution)/shard_map/ppermute | solution.py:272
  37.0 19.1 %collective-permute-start.2 = (bf16[2,2,8,8,128]{4,3,2,1,0:T(8,128)(2,1)S(1)}, bf16[2,2,8,8,128]{4,3,2,1,0:T(8,128)(2,1)S(1)}, u32[]{:S(2)}, u32[]{:S(2)}) collective-permute-start(bf16[2,2,8,8,128]{4,3,2,1,0:T(8,128)(2,1)S(1)} %get-tuple-element.33), channel_id=1, source_target_pairs={{0,11},{1,10},{2,9},{3,8},{4,15},{5,14},{6,13},{7,12},{8,3},{9,2},... | collective-permute-start | bytes 196616 | tf_op jit(solution)/shard_map/ppermute | solution.py:272
  41.9 14.2 %collective-permute-start = (bf16[2,2,8,8,128]{4,3,2,1,0:T(8,128)(2,1)S(1)}, bf16[2,2,8,8,128]{4,3,2,1,0:T(8,128)(2,1)S(1)}, u32[]{:S(2)}, u32[]{:S(2)}) collective-permute-start(bf16[2,2,8,8,128]{4,3,2,1,0:T(8,128)(2,1)S(1)} %get-tuple-element.32), channel_id=1, source_target_pairs={{0,4},{1,5},{2,6},{3,7},{4,0},{5,1},{6,2},{7,3},{8,12},{9,13},{10,... | collective-permute-start | bytes 196616 | tf_op jit(solution)/shard_map/ppermute | solution.py:272
  46.8 9.4 %collective-permute-start.3 = (bf16[1,2,2,8,8,128]{5,4,3,2,1,0:T(8,128)(2,1)S(1)}, bf16[1,2,2,8,8,128]{5,4,3,2,1,0:T(8,128)(2,1)S(1)}, u32[]{:S(2)}, u32[]{:S(2)}) collective-permute-start(bf16[1,2,2,8,8,128]{5,4,3,2,1,0:T(8,128)(2,1)S(1)} %bitcast.44), channel_id=1, source_target_pairs={{0,1},{1,2},{2,3},{3,0},{4,5},{5,6},{6,7},{7,4},{8,9},{9,10},{10,1... | collective-permute-start | bytes 196616 | tf_op jit(solution)/shard_map/ppermute | solution.py:277
  49.5 7.4 %collective-permute-start.4 = (bf16[1,2,2,8,8,128]{5,4,3,2,1,0:T(8,128)(2,1)S(1)}, bf16[1,2,2,8,8,128]{5,4,3,2,1,0:T(8,128)(2,1)S(1)}, u32[]{:S(2)}, u32[]{:S(2)}) collective-permute-start(bf16[1,2,2,8,8,128]{5,4,3,2,1,0:T(8,128)(2,1)S(1)} %bitcast.45), channel_id=1, source_target_pairs={{0,2},{1,3},{2,0},{3,1},{4,6},{5,7},{6,4},{7,5},{8,10},{9,11},{10,... | collective-permute-start | bytes 196616 | tf_op jit(solution)/shard_map/ppermute | solution.py:277
  51.9 6.5 %collective-permute-start.5 = (bf16[1,2,2,8,8,128]{5,4,3,2,1,0:T(8,128)(2,1)S(1)}, bf16[1,2,2,8,8,128]{5,4,3,2,1,0:T(8,128)(2,1)S(1)}, u32[]{:S(2)}, u32[]{:S(2)}) collective-permute-start(bf16[1,2,2,8,8,128]{5,4,3,2,1,0:T(8,128)(2,1)S(1)} %bitcast.46), channel_id=1, source_target_pairs={{0,3},{1,0},{2,1},{3,2},{4,7},{5,4},{6,5},{7,6},{8,11},{9,8},{10,9... | collective-permute-start | bytes 196616 | tf_op jit(solution)/shard_map/ppermute | solution.py:277
  58.3 0.6 copy-start.6
  59.0 11.5 %collective-permute-start.6 = (bf16[3,2,2,8,8,128]{5,4,3,2,1,0:T(8,128)(2,1)S(1)}, bf16[3,2,2,8,8,128]{5,4,3,2,1,0:T(8,128)(2,1)S(1)}, u32[]{:S(2)}, u32[]{:S(2)}) collective-permute-start(bf16[3,2,2,8,8,128]{5,4,3,2,1,0:T(8,128)(2,1)S(1)} %pad_maximum_fusion.refs_4_), channel_id=1, source_target_pairs={{0,1},{1,2},{2,3},{3,0},{4,5},{5,6},{6,7},{7,4},{8,9},{9,10},{10,1... | collective-permute-start | bytes 589832 | tf_op jit(solution)/shard_map/ppermute | solution.py:277
  63.9 14.1 %collective-permute-start.7 = (bf16[3,2,2,8,8,128]{5,4,3,2,1,0:T(8,128)(2,1)S(1)}, bf16[3,2,2,8,8,128]{5,4,3,2,1,0:T(8,128)(2,1)S(1)}, u32[]{:S(2)}, u32[]{:S(2)}) collective-permute-start(bf16[3,2,2,8,8,128]{5,4,3,2,1,0:T(8,128)(2,1)S(1)} %pad_maximum_fusion.refs_4_), channel_id=1, source_target_pairs={{0,2},{1,3},{2,0},{3,1},{4,6},{5,7},{6,4},{7,5},{8,10},{9,11},{10,... | collective-permute-start | bytes 589832 | tf_op jit(solution)/shard_map/ppermute | solution.py:277
  66.0 12.0 %collective-permute-start.8 = (bf16[3,2,2,8,8,128]{5,4,3,2,1,0:T(8,128)(2,1)S(1)}, bf16[3,2,2,8,8,128]{5,4,3,2,1,0:T(8,128)(2,1)S(1)}, u32[]{:S(2)}, u32[]{:S(2)}) collective-permute-start(bf16[3,2,2,8,8,128]{5,4,3,2,1,0:T(8,128)(2,1)S(1)} %pad_maximum_fusion.refs_4_), channel_id=1, source_target_pairs={{0,3},{1,0},{2,1},{3,2},{4,7},{5,4},{6,5},{7,6},{8,11},{9,8},{10,9... | collective-permute-start | bytes 589832 | tf_op jit(solution)/shard_map/ppermute | solution.py:277
  78.0 0.8 copy-start.7
  93.0 19.1 %copy-start.5 = (s32[1,16,2]{1,2,0:T(2,128)S(1)}, s32[1,16,2]{1,2,0:T(2,128)}, u32[]{:S(2)}) copy-start(s32[1,16,2]{1,2,0:T(2,128)} %param.9) | copy-start | bytes 388
  93.0 64.3 %all-to-all-start.2 = ((bf16[16,2,128,128]{3,2,1,0:T(8,128)(2,1)}), bf16[16,2,128,128]{3,2,1,0:T(8,128)(2,1)S(1)}, u32[]{:S(2)}, u32[]{:S(2)}) async-start(bf16[16,2,128,128]{3,2,1,0:T(8,128)(2,1)} %bitcast.20), calls=%async_computation.2 | async-start | bytes 2097152 | tf_op jit(solution)/shard_map/all_to_all | solution.py:335
  99.5 19.0 %collective-permute-start.10 = (bf16[3,2,2,8,8,128]{5,4,3,2,1,0:T(8,128)(2,1)S(1)}, bf16[3,2,2,8,8,128]{5,4,3,2,1,0:T(8,128)(2,1)S(1)}, u32[]{:S(2)}, u32[]{:S(2)}) collective-permute-start(bf16[3,2,2,8,8,128]{5,4,3,2,1,0:T(8,128)(2,1)S(1)} %get-tuple-element.46), channel_id=1, source_target_pairs={{0,2},{1,3},{2,0},{3,1},{4,6},{5,7},{6,4},{7,5},{8,10},{9,11},{10,... | collective-permute-start | bytes 589832 | tf_op jit(solution)/shard_map/ppermute | solution.py:277
  104.9 13.6 %collective-permute-start.11 = (bf16[3,2,2,8,8,128]{5,4,3,2,1,0:T(8,128)(2,1)S(1)}, bf16[3,2,2,8,8,128]{5,4,3,2,1,0:T(8,128)(2,1)S(1)}, u32[]{:S(2)}, u32[]{:S(2)}) collective-permute-start(bf16[3,2,2,8,8,128]{5,4,3,2,1,0:T(8,128)(2,1)S(1)} %get-tuple-element.47), channel_id=1, source_target_pairs={{0,1},{1,2},{2,3},{3,0},{4,5},{5,6},{6,7},{7,4},{8,9},{9,10},{10,1... | collective-permute-start | bytes 589832 | tf_op jit(solution)/shard_map/ppermute | solution.py:277
  108.9 13.5 %collective-permute-start.9 = (bf16[3,2,2,8,8,128]{5,4,3,2,1,0:T(8,128)(2,1)S(1)}, bf16[3,2,2,8,8,128]{5,4,3,2,1,0:T(8,128)(2,1)S(1)}, u32[]{:S(2)}, u32[]{:S(2)}) collective-permute-start(bf16[3,2,2,8,8,128]{5,4,3,2,1,0:T(8,128)(2,1)S(1)} %get-tuple-element.45), channel_id=1, source_target_pairs={{0,3},{1,0},{2,1},{3,2},{4,7},{5,4},{6,5},{7,6},{8,11},{9,8},{10,9... | collective-permute-start | bytes 589832 | tf_op jit(solution)/shard_map/ppermute | solution.py:277
  122.3 22.9 %collective-permute-start.12 = (bf16[1,2,2,8,8,128]{5,4,3,2,1,0:T(8,128)(2,1)S(1)}, bf16[1,2,2,8,8,128]{5,4,3,2,1,0:T(8,128)(2,1)S(1)}, u32[]{:S(2)}, u32[]{:S(2)}) collective-permute-start(bf16[1,2,2,8,8,128]{5,4,3,2,1,0:T(8,128)(2,1)S(1)} %get-tuple-element.49), channel_id=1, source_target_pairs={{0,3},{1,0},{2,1},{3,2},{4,7},{5,4},{6,5},{7,6},{8,11},{9,8},{10,9... | collective-permute-start | bytes 196616 | tf_op jit(solution)/shard_map/ppermute | solution.py:277
  126.3 23.3 %collective-permute-start.13 = (bf16[1,2,2,8,8,128]{5,4,3,2,1,0:T(8,128)(2,1)S(1)}, bf16[1,2,2,8,8,128]{5,4,3,2,1,0:T(8,128)(2,1)S(1)}, u32[]{:S(2)}, u32[]{:S(2)}) collective-permute-start(bf16[1,2,2,8,8,128]{5,4,3,2,1,0:T(8,128)(2,1)S(1)} %get-tuple-element.50), channel_id=1, source_target_pairs={{0,2},{1,3},{2,0},{3,1},{4,6},{5,7},{6,4},{7,5},{8,10},{9,11},{10,... | collective-permute-start | bytes 196616 | tf_op jit(solution)/shard_map/ppermute | solution.py:277
  129.2 20.3 %collective-permute-start.14 = (bf16[1,2,2,8,8,128]{5,4,3,2,1,0:T(8,128)(2,1)S(1)}, bf16[1,2,2,8,8,128]{5,4,3,2,1,0:T(8,128)(2,1)S(1)}, u32[]{:S(2)}, u32[]{:S(2)}) collective-permute-start(bf16[1,2,2,8,8,128]{5,4,3,2,1,0:T(8,128)(2,1)S(1)} %get-tuple-element.51), channel_id=1, source_target_pairs={{0,1},{1,2},{2,3},{3,0},{4,5},{5,6},{6,7},{7,4},{8,9},{9,10},{10,1... | collective-permute-start | bytes 196616 | tf_op jit(solution)/shard_map/ppermute | solution.py:277
  132.7 16.9 %collective-permute-start.15 = (bf16[2,2,8,8,128]{4,3,2,1,0:T(8,128)(2,1)S(1)}, bf16[2,2,8,8,128]{4,3,2,1,0:T(8,128)(2,1)S(1)}, u32[]{:S(2)}, u32[]{:S(2)}) collective-permute-start(bf16[2,2,8,8,128]{4,3,2,1,0:T(8,128)(2,1)S(1)} %get-tuple-element.64), channel_id=1, source_target_pairs={{0,4},{1,5},{2,6},{3,7},{4,0},{5,1},{6,2},{7,3},{8,12},{9,13},{10,... | collective-permute-start | bytes 196616 | tf_op jit(solution)/shard_map/ppermute | solution.py:272
  138.7 10.9 %collective-permute-start.16 = (bf16[2,2,8,8,128]{4,3,2,1,0:T(8,128)(2,1)S(1)}, bf16[2,2,8,8,128]{4,3,2,1,0:T(8,128)(2,1)S(1)}, u32[]{:S(2)}, u32[]{:S(2)}) collective-permute-start(bf16[2,2,8,8,128]{4,3,2,1,0:T(8,128)(2,1)S(1)} %get-tuple-element.63), channel_id=1, source_target_pairs={{0,15},{1,14},{2,13},{3,12},{4,11},{5,10},{6,9},{7,8},{8,7},{9,6},... | collective-permute-start | bytes 196616 | tf_op jit(solution)/shard_map/ppermute | solution.py:272
  145.2 12.0 %collective-permute-start.17 = (bf16[2,2,8,8,128]{4,3,2,1,0:T(8,128)(2,1)S(1)}, bf16[2,2,8,8,128]{4,3,2,1,0:T(8,128)(2,1)S(1)}, u32[]{:S(2)}, u32[]{:S(2)}) collective-permute-start(bf16[2,2,8,8,128]{4,3,2,1,0:T(8,128)(2,1)S(1)} %get-tuple-element.62), channel_id=1, source_target_pairs={{0,11},{1,10},{2,9},{3,8},{4,15},{5,14},{6,13},{7,12},{8,3},{9,2},... | collective-permute-start | bytes 196616 | tf_op jit(solution)/shard_map/ppermute | solution.py:272
  158.6 17.1 %all-to-all-start.3 = ((bf16[32,2,2,2,4,128]{5,4,3,2,1,0:T(4,128)(2,1)}), bf16[32,2,2,2,4,128]{5,4,3,2,1,0:T(4,128)(2,1)S(1)}, u32[]{:S(2)}, u32[]{:S(2)}) async-start(bf16[32,2,2,2,4,128]{5,4,3,2,1,0:T(4,128)(2,1)} %bitcast.24), calls=%async_computation.3 | async-start | bytes 524288 | tf_op jit(solution)/shard_map/all_to_all | solution.py:310

commit v8 on v6

--- a/solution.py
+++ b/solution.py
@@ -14,7 +14,8 @@
 SCALING = HD ** (-0.5)
 LOG2E = 1.4426950408889634
 PLANE = ("dp", "xh")
-FAR = (4, 15, 11)
+MIRROR = 15
+ACROSS = 4
 NEAR = 4
 
 
@@ -57,18 +58,17 @@
     width = k_all.shape[1]
     tile_rows = width // PAIR
     part = width // NEAR
-    own_part = part // 4
     factor = SCALING * LOG2E
 
-    def rows_of(slot):
+    def rows_of(slot, first_part):
         begin = (slot % NEAR) * part
         if slot < NEAR:
-            return slice(begin, begin + own_part)
-        return slice(begin + own_part, begin + part)
+            return slice(begin, begin + first_part)
+        return slice(begin + first_part, begin + part)
 
     def stage(block, _):
         for slot, ref in enumerate(kv_refs):
-            rows = rows_of(slot)
+            rows = rows_of(slot, part // 4)
             count = rows.stop - rows.start
             key = ref[:, :, 0, block].astype(jnp.float32).reshape(count, HD)
             value = ref[:, :, 1, block].astype(jnp.float32).reshape(count, HD)
@@ -81,7 +81,7 @@
 
     row = lax.broadcasted_iota(jnp.int32, (width, 1), 0)
     holder = (place_ref[0] & 12) | ((place_ref[0] - (row >> 6)) & 3)
-    source = holder ^ (((row >> 4) & 1) * 4) ^ (((row >> 5) & 1) * 15)
+    source = holder ^ (((row >> 4) & 1) * MIRROR) ^ (((row >> 5) & 1) * ACROSS)
     key_offset = (
         ((row >> 2) & 1) * tile_rows + ((row >> 3) & 1) * 64 + source * 4 + (row & 3)
     )
@@ -155,7 +155,7 @@
 
     def unstage(block, _):
         for slot, ref in enumerate(dkv_refs):
-            rows = rows_of(slot)
+            rows = rows_of(slot, part // 2)
             shape = ref.shape[:2] + ref.shape[4:]
             ref[:, :, 0, block] = (dk_all[block, rows] * SCALING).reshape(shape).astype(jnp.bfloat16)
             ref[:, :, 1, block] = dv_all[block, rows].reshape(shape).astype(jnp.bfloat16)
@@ -173,7 +173,7 @@
     return pl.pallas_call(
         attention_kernel,
         out_shape=(jax.ShapeDtypeStruct((slots, tile_rows, HD), jnp.bfloat16),)
-        + tuple(jax.ShapeDtypeStruct(chunk.shape, jnp.bfloat16) for chunk in chunks),
+        + (jax.ShapeDtypeStruct((2,) + chunks[0].shape[1:], jnp.bfloat16),) * (2 * NEAR),
         in_specs=[smem] * 3 + [vmem] * (1 + 2 * NEAR),
         out_specs=(vmem,) * (1 + 2 * NEAR),
         scratch_shapes=[
@@ -224,7 +224,7 @@
     lax.fori_loop(0, recv_ref.shape[0] // PAIR, body, 0)
 
 
-def kv_back_kernel(recv_ref, place_ref, p0, p1, p2, p3, out_ref):
+def kv_back_kernel(recv_ref, place_ref, own_ref, other_ref, out_ref):
     head = place_ref[0] >> 3
     sliver = out_ref.shape[-2]
 
@@ -232,8 +232,8 @@
         slots = (recv_ref[PAIR * pair], recv_ref[PAIR * pair + 1])
         for half in range(2):
             for kind in range(2):
-                for a, b, which in ((p0, p1, head), (p2, p3, 1 - head)):
-                    total = a[half, kind, pair].astype(jnp.float32) + b[half, kind, pair].astype(jnp.float32)
+                for ref, which in ((own_ref, head), (other_ref, 1 - head)):
+                    total = ref[half, kind, pair].astype(jnp.float32)
                     for order, slot in enumerate(slots):
                         rows = total[order * sliver : (order + 1) * sliver]
                         out_ref[slot >> 1, half, slot & 1, kind, which] = rows.astype(jnp.bfloat16)
@@ -285,8 +285,8 @@
     return [terms[0]] + [near_shift(terms[step], -step) for step in range(1, NEAR)]
 
 
-def total(terms, index):
-    return sum(term[index].astype(jnp.float32) for term in terms).astype(jnp.bfloat16)
+def total(terms):
+    return sum(term.astype(jnp.float32) for term in terms)
 
 
 def on_device(queries, keys_values, grad_out, send_tiles, recv_slot, tile_seq):
@@ -324,7 +324,9 @@
         qg_packed.reshape(n_replicas, slot_cap, 2, tile_rows, row_width),
         "dp", split_axis=0, concat_axis=0, tiled=True,
     ).reshape(slots, 2, tile_rows, row_width)
-    far = jnp.stack([far_swap(own, FAR[0]), far_swap(other, FAR[1]), far_swap(other, FAR[2])])
+    far = jnp.stack(
+        [far_swap(other, MIRROR), far_swap(own, ACROSS), far_swap(other, MIRROR ^ ACROSS)]
+    )
     own_chunks = near_gather(own[None])
     far, own_chunks, qg_arrived = lax.optimization_barrier((far, own_chunks, qg_arrived))
     chunks = own_chunks + near_gather(far)
@@ -336,10 +338,13 @@
         query_back.reshape(n_replicas, slot_cap, tile_rows, row_width),
         "dp", split_axis=0, concat_axis=0, tiled=True,
     )
-    far_terms = near_terms(terms[NEAR:])
-    back = [far_swap(total(far_terms, index), flip) for index, flip in enumerate(FAR)]
-    own_sum = total(near_terms(terms[:NEAR]), 0)
-    swapped, query_returned = lax.optimization_barrier(([own_sum] + back, query_returned))
+    across_terms = near_terms(terms[NEAR:])
+    own_terms, across_terms = lax.optimization_barrier((terms[:NEAR], across_terms))
+    arrived = far_swap(total(across_terms).astype(jnp.bfloat16), ACROSS)
+    base = lax.optimization_barrier(total([arrived, own_terms[0]]))
+    summed = total([base] + near_terms(own_terms)[1:]).astype(jnp.bfloat16)
+    swapped = [summed[0], far_swap(summed[1], MIRROR)]
+    swapped, query_returned = lax.optimization_barrier((swapped, query_returned))
     kv_returned = over_plane(
         local_call(kv_back_kernel, "kv_back", [my_recv, place], swapped, traveling)
     )

time: 173 us -> 171 us (0.988)
  the two profiles are of different devices: /device:TPU:97 before, /device:TPU:1 now
where the time goes in v8:
time: 171 us; the launch traced here: 170 us
  starting transfers between devices  94.4 us (55%)
  waiting for transfers between devices  45 us (26%)
  Pallas kernels  21.8 us (13%)
  local copies, waits for them, and re-layouts  7.24 us (4%)
    ppermute x12, starting transfers between devices, near_shift(): return lax.ppermute(values, 'z', pairs)  40.9 us
    ppermute x5, starting transfers between devices, far_swap(): lax.ppermute(values, 'z', [(place, place ^ flip) for place in range(16)])  26.2 us
    ppermute x12, waiting for transfers between devices, near_shift(): return lax.ppermute(values, 'z', pairs)  19.8 us
    all_to_all x2, starting transfers between devices, over_plane(): lax.all_to_all(values.reshape((2 * n_replicas,) + values.shape[2:]), PLAN...  17.2 us
    pallas_call x1, Pallas kernels, attention(): pl.pallas_call(attention_kernel, out_shape=(jax.ShapeDtypeStruct((slots,...  14.7 us
    ppermute x5, waiting for transfers between devices, far_swap(): lax.ppermute(values, 'z', [(place, place ^ flip) for place in range(16)])  13.8 us
    all_to_all x2, waiting for transfers between devices, over_plane(): lax.all_to_all(values.reshape((2 * n_replicas,) + values.shape[2:]), PLAN...  11.3 us
    all_to_all x1, starting transfers between devices, on_device(): lax.all_to_all(query_back.reshape(n_replicas, slot_cap, tile_rows, row_wi...  5.93 us
  transfers between devices with their start and end apart: 21, of which 9 were waited for; matrix products, arithmetic and copies ran while one was open for 1% of the time, Pallas kernels for 2%

profile of v8, /device:TPU:1, one launch (start us, length us, event | category | flops | bytes accessed | tf_op | source)
XLA Modules:
  0.0 170.0 jit_solution(13668131335908644728)
XLA Ops:
  2.2 1.4 kv_pack.1
  3.7 10.4 %all-to-all-start = ((bf16[32,2,2,2,4,128]{5,4,3,2,1,0:T(4,128)(2,1)}), bf16[32,2,2,2,4,128]{5,4,3,2,1,0:T(4,128)(2,1)S(1)}, u32[]{:S(2)}, u32[]{:S(2)}) async-start(bf16[32,2,2,2,4,128]{5,4,3,2,1,0:T(4,128)(2,1)} %bitcast.7), calls=%async_computation | async-start | bytes 524288 | tf_op jit(solution)/shard_map/all_to_all | solution.py:310
  16.8 2.3 %pack_rows.1 = bf16[32,2,128,128]{3,2,1,0:T(8,128)(2,1)} custom-call(s32[2,16]{1,0:T(2,128)S(1)} %bitcast.38, bf16[16,128,128]{2,1,0:T(8,128)(2,1)S(1)} %copy-done, bf16[16,128,128]{2,1,0:T(8,128)(2,1)S(1)} %copy-done.1), custom_call_target="tpu_custom_call" | custom-call | tf_op jit(solution)/shard_map/pack_rows/pallas_call | solution.py:38
  19.1 3.9 %all-to-all-done = bf16[32,2,2,2,4,128]{5,4,3,2,1,0:T(4,128)(2,1)S(1)} async-done(((bf16[32,2,2,2,4,128]{5,4,3,2,1,0:T(4,128)(2,1)}), bf16[32,2,2,2,4,128]{5,4,3,2,1,0:T(4,128)(2,1)S(1)}, u32[]{:S(2)}, u32[]{:S(2)}) %all-to-all-start) | async-done | bytes 262176 | tf_op jit(solution)/shard_map/all_to_all | solution.py:310
  23.0 4.1 %all-to-all-start.1 = ((bf16[16,2,2,128,128]{4,3,2,1,0:T(8,128)(2,1)}), bf16[16,2,2,128,128]{4,3,2,1,0:T(8,128)(2,1)S(1)}, u32[]{:S(2)}, u32[]{:S(2)}) async-start(bf16[16,2,2,128,128]{4,3,2,1,0:T(8,128)(2,1)} %bitcast.14), calls=%async_computation.1 | async-start | bytes 4194304 | tf_op jit(solution)/shard_map/all_to_all | solution.py:323
  27.7 6.9 %collective-permute-start.1 = (bf16[2,2,8,8,128]{4,3,2,1,0:T(8,128)(2,1)S(1)}, bf16[2,2,8,8,128]{4,3,2,1,0:T(8,128)(2,1)S(1)}, u32[]{:S(2)}, u32[]{:S(2)}) collective-permute-start(bf16[2,2,8,8,128]{4,3,2,1,0:T(8,128)(2,1)S(1)} %get-tuple-element.31), channel_id=1, source_target_pairs={{0,4},{1,5},{2,6},{3,7},{4,0},{5,1},{6,2},{7,3},{8,12},{9,13},{10,... | collective-permute-start | bytes 196616 | tf_op jit(solution)/shard_map/ppermute | solution.py:272
  34.7 9.3 %collective-permute-start.2 = (bf16[2,2,8,8,128]{4,3,2,1,0:T(8,128)(2,1)S(1)}, bf16[2,2,8,8,128]{4,3,2,1,0:T(8,128)(2,1)S(1)}, u32[]{:S(2)}, u32[]{:S(2)}) collective-permute-start(bf16[2,2,8,8,128]{4,3,2,1,0:T(8,128)(2,1)S(1)} %get-tuple-element.30), channel_id=1, source_target_pairs={{0,11},{1,10},{2,9},{3,8},{4,15},{5,14},{6,13},{7,12},{8,3},{9,2},... | collective-permute-start | bytes 196616 | tf_op jit(solution)/shard_map/ppermute | solution.py:272
  44.0 1.9 %collective-permute-start = (bf16[2,2,8,8,128]{4,3,2,1,0:T(8,128)(2,1)S(1)}, bf16[2,2,8,8,128]{4,3,2,1,0:T(8,128)(2,1)S(1)}, u32[]{:S(2)}, u32[]{:S(2)}) collective-permute-start(bf16[2,2,8,8,128]{4,3,2,1,0:T(8,128)(2,1)S(1)} %get-tuple-element.30), channel_id=1, source_target_pairs={{0,15},{1,14},{2,13},{3,12},{4,11},{5,10},{6,9},{7,8},{8,7},{9,6},... | collective-permute-start | bytes 196616 | tf_op jit(solution)/shard_map/ppermute | solution.py:272
  45.9 3.5 %collective-permute-start.3 = (bf16[1,2,2,8,8,128]{5,4,3,2,1,0:T(8,128)(2,1)S(1)}, bf16[1,2,2,8,8,128]{5,4,3,2,1,0:T(8,128)(2,1)S(1)}, u32[]{:S(2)}, u32[]{:S(2)}) collective-permute-start(bf16[1,2,2,8,8,128]{5,4,3,2,1,0:T(8,128)(2,1)S(1)} %bitcast.40), channel_id=1, source_target_pairs={{0,1},{1,2},{2,3},{3,0},{4,5},{5,6},{6,7},{7,4},{8,9},{9,10},{10,1... | collective-permute-start | bytes 196616 | tf_op jit(solution)/shard_map/ppermute | solution.py:277
  49.5 3.1 %collective-permute-start.4 = (bf16[1,2,2,8,8,128]{5,4,3,2,1,0:T(8,128)(2,1)S(1)}, bf16[1,2,2,8,8,128]{5,4,3,2,1,0:T(8,128)(2,1)S(1)}, u32[]{:S(2)}, u32[]{:S(2)}) collective-permute-start(bf16[1,2,2,8,8,128]{5,4,3,2,1,0:T(8,128)(2,1)S(1)} %bitcast.41), channel_id=1, source_target_pairs={{0,2},{1,3},{2,0},{3,1},{4,6},{5,7},{6,4},{7,5},{8,10},{9,11},{10,... | collective-permute-start | bytes 196616 | tf_op jit(solution)/shard_map/ppermute | solution.py:277
  52.6 3.6 %collective-permute-start.5 = (bf16[1,2,2,8,8,128]{5,4,3,2,1,0:T(8,128)(2,1)S(1)}, bf16[1,2,2,8,8,128]{5,4,3,2,1,0:T(8,128)(2,1)S(1)}, u32[]{:S(2)}, u32[]{:S(2)}) collective-permute-start(bf16[1,2,2,8,8,128]{5,4,3,2,1,0:T(8,128)(2,1)S(1)} %bitcast.42), channel_id=1, source_target_pairs={{0,3},{1,0},{2,1},{3,2},{4,7},{5,4},{6,5},{7,6},{8,11},{9,8},{10,9... | collective-permute-start | bytes 196616 | tf_op jit(solution)/shard_map/ppermute | solution.py:277
  56.2 2.5 %collective-permute-done.4.refs_2_ = bf16[1,2,2,8,8,128]{5,4,3,2,1,0:T(8,128)(2,1)S(1)} collective-permute-done((bf16[1,2,2,8,8,128]{5,4,3,2,1,0:T(8,128)(2,1)S(1)}, bf16[1,2,2,8,8,128]{5,4,3,2,1,0:T(8,128)(2,1)S(1)}, u32[]{:S(2)}, u32[]{:S(2)}) %collective-permute-start.4) | collective-permute-done | bytes 65568 | tf_op jit(solution)/shard_map/ppermute | solution.py:277
  59.7 2.6 %collective-permute-start.6 = (bf16[3,2,2,8,8,128]{5,4,3,2,1,0:T(8,128)(2,1)S(1)}, bf16[3,2,2,8,8,128]{5,4,3,2,1,0:T(8,128)(2,1)S(1)}, u32[]{:S(2)}, u32[]{:S(2)}) collective-permute-start(bf16[3,2,2,8,8,128]{5,4,3,2,1,0:T(8,128)(2,1)S(1)} %pad_maximum_fusion.refs_4_), channel_id=1, source_target_pairs={{0,1},{1,2},{2,3},{3,0},{4,5},{5,6},{6,7},{7,4},{8,9},{9,10},{10,1... | collective-permute-start | bytes 589832 | tf_op jit(solution)/shard_map/ppermute | solution.py:277
  62.3 5.9 %collective-permute-start.7 = (bf16[3,2,2,8,8,128]{5,4,3,2,1,0:T(8,128)(2,1)S(1)}, bf16[3,2,2,8,8,128]{5,4,3,2,1,0:T(8,128)(2,1)S(1)}, u32[]{:S(2)}, u32[]{:S(2)}) collective-permute-start(bf16[3,2,2,8,8,128]{5,4,3,2,1,0:T(8,128)(2,1)S(1)} %pad_maximum_fusion.refs_4_), channel_id=1, source_target_pairs={{0,2},{1,3},{2,0},{3,1},{4,6},{5,7},{6,4},{7,5},{8,10},{9,11},{10,... | collective-permute-start | bytes 589832 | tf_op jit(solution)/shard_map/ppermute | solution.py:277
  68.2 1.9 %collective-permute-start.8 = (bf16[3,2,2,8,8,128]{5,4,3,2,1,0:T(8,128)(2,1)S(1)}, bf16[3,2,2,8,8,128]{5,4,3,2,1,0:T(8,128)(2,1)S(1)}, u32[]{:S(2)}, u32[]{:S(2)}) collective-permute-start(bf16[3,2,2,8,8,128]{5,4,3,2,1,0:T(8,128)(2,1)S(1)} %pad_maximum_fusion.refs_4_), channel_id=1, source_target_pairs={{0,3},{1,0},{2,1},{3,2},{4,7},{5,4},{6,5},{7,6},{8,11},{9,8},{10,9... | collective-permute-start | bytes 589832 | tf_op jit(solution)/shard_map/ppermute | solution.py:277
  70.8 9.0 %collective-permute-done.7.refs_6_ = bf16[3,2,2,8,8,128]{5,4,3,2,1,0:T(8,128)(2,1)S(1)} collective-permute-done((bf16[3,2,2,8,8,128]{5,4,3,2,1,0:T(8,128)(2,1)S(1)}, bf16[3,2,2,8,8,128]{5,4,3,2,1,0:T(8,128)(2,1)S(1)}, u32[]{:S(2)}, u32[]{:S(2)}) %collective-permute-start.7) | collective-permute-done | bytes 196640 | tf_op jit(solution)/shard_map/ppermute | solution.py:277
  80.7 14.7 %attention_backward.1 = (bf16[32,128,128]{2,1,0:T(8,128)(2,1)}, bf16[2,2,2,8,8,128]{5,4,3,2,1,0:T(8,128)(2,1)S(1)}, bf16[2,2,2,8,8,128]{5,4,3,2,1,0:T(8,128)(2,1...) custom-call(s32[16]{0:T(128)S(1)} %dynamic-slice_bitcast_fusion.recv, ...), custom_call_target="tpu_custom_call" | custom-call | flops 2000000000 | bytes 6291456 | tf_op jit(solution)/shard_map/attention_backward/pallas_call | solution.py:173
  95.4 5.4 %collective-permute-start.10 = (bf16[2,2,2,8,8,128]{5,4,3,2,1,0:T(8,128)(2,1)S(1)}, bf16[2,2,2,8,8,128]{5,4,3,2,1,0:T(8,128)(2,1)S(1)}, u32[]{:S(2)}, u32[]{:S(2)}) collective-permute-start(bf16[2,2,2,8,8,128]{5,4,3,2,1,0:T(8,128)(2,1)S(1)} %get-tuple-element.44), channel_id=1, source_target_pairs={{0,2},{1,3},{2,0},{3,1},{4,6},{5,7},{6,4},{7,5},{8,10},{9,11},{10,... | collective-permute-start | bytes 393224 | tf_op jit(solution)/shard_map/ppermute | solution.py:277
  100.8 2.9 %collective-permute-start.11 = (bf16[2,2,2,8,8,128]{5,4,3,2,1,0:T(8,128)(2,1)S(1)}, bf16[2,2,2,8,8,128]{5,4,3,2,1,0:T(8,128)(2,1)S(1)}, u32[]{:S(2)}, u32[]{:S(2)}) collective-permute-start(bf16[2,2,2,8,8,128]{5,4,3,2,1,0:T(8,128)(2,1)S(1)} %get-tuple-element.45), channel_id=1, source_target_pairs={{0,1},{1,2},{2,3},{3,0},{4,5},{5,6},{6,7},{7,4},{8,9},{9,10},{10,1... | collective-permute-start | bytes 393224 | tf_op jit(solution)/shard_map/ppermute | solution.py:277
  103.7 4.1 %collective-permute-start.9 = (bf16[2,2,2,8,8,128]{5,4,3,2,1,0:T(8,128)(2,1)S(1)}, bf16[2,2,2,8,8,128]{5,4,3,2,1,0:T(8,128)(2,1)S(1)}, u32[]{:S(2)}, u32[]{:S(2)}) collective-permute-start(bf16[2,2,2,8,8,128]{5,4,3,2,1,0:T(8,128)(2,1)S(1)} %get-tuple-element.43), channel_id=1, source_target_pairs={{0,3},{1,0},{2,1},{3,2},{4,7},{5,4},{6,5},{7,6},{8,11},{9,8},{10,9... | collective-permute-start | bytes 393224 | tf_op jit(solution)/shard_map/ppermute | solution.py:277
  107.9 5.9 %all-to-all-start.2 = ((bf16[16,2,128,128]{3,2,1,0:T(8,128)(2,1)}), bf16[16,2,128,128]{3,2,1,0:T(8,128)(2,1)S(1)}, u32[]{:S(2)}, u32[]{:S(2)}) async-start(bf16[16,2,128,128]{3,2,1,0:T(8,128)(2,1)} %bitcast.18), calls=%async_computation.2 | async-start | bytes 2097152 | tf_op jit(solution)/shard_map/all_to_all | solution.py:337
  113.9 6.2 %collective-permute-start.12 = (bf16[2,2,2,8,8,128]{5,4,3,2,1,0:T(8,128)(2,1)S(1)}, bf16[2,2,2,8,8,128]{5,4,3,2,1,0:T(8,128)(2,1)S(1)}, u32[]{:S(2)}, u32[]{:S(2)}) collective-permute-start(bf16[2,2,2,8,8,128]{5,4,3,2,1,0:T(8,128)(2,1)S(1)} %add_convert_fusion.1), channel_id=1, source_target_pairs={{0,4},{1,5},{2,6},{3,7},{4,0},{5,1},{6,2},{7,3},{8,12},{9,13},{10,... | collective-permute-start | bytes 393224 | tf_op jit(solution)/shard_map/ppermute | solution.py:272
  120.3 3.6 %collective-permute-start.13 = (bf16[2,2,2,8,8,128]{5,4,3,2,1,0:T(8,128)(2,1)S(1)}, bf16[2,2,2,8,8,128]{5,4,3,2,1,0:T(8,128)(2,1)S(1)}, u32[]{:S(2)}, u32[]{:S(2)}) collective-permute-start(bf16[2,2,2,8,8,128]{5,4,3,2,1,0:T(8,128)(2,1)S(1)} %get-tuple-element.51), channel_id=1, source_target_pairs={{0,3},{1,0},{2,1},{3,2},{4,7},{5,4},{6,5},{7,6},{8,11},{9,8},{10,9... | collective-permute-start | bytes 393224 | tf_op jit(solution)/shard_map/ppermute | solution.py:277
  123.9 1.9 %collective-permute-start.14 = (bf16[2,2,2,8,8,128]{5,4,3,2,1,0:T(8,128)(2,1)S(1)}, bf16[2,2,2,8,8,128]{5,4,3,2,1,0:T(8,128)(2,1)S(1)}, u32[]{:S(2)}, u32[]{:S(2)}) collective-permute-start(bf16[2,2,2,8,8,128]{5,4,3,2,1,0:T(8,128)(2,1)S(1)} %get-tuple-element.52), channel_id=1, source_target_pairs={{0,2},{1,3},{2,0},{3,1},{4,6},{5,7},{6,4},{7,5},{8,10},{9,11},{10,... | collective-permute-start | bytes 393224 | tf_op jit(solution)/shard_map/ppermute | solution.py:277
  125.8 2.3 %collective-permute-start.15 = (bf16[2,2,2,8,8,128]{5,4,3,2,1,0:T(8,128)(2,1)S(1)}, bf16[2,2,2,8,8,128]{5,4,3,2,1,0:T(8,128)(2,1)S(1)}, u32[]{:S(2)}, u32[]{:S(2)}) collective-permute-start(bf16[2,2,2,8,8,128]{5,4,3,2,1,0:T(8,128)(2,1)S(1)} %get-tuple-element.53), channel_id=1, source_target_pairs={{0,1},{1,2},{2,3},{3,0},{4,5},{5,6},{6,7},{7,4},{8,9},{9,10},{10,1... | collective-permute-start | bytes 393224 | tf_op jit(solution)/shard_map/ppermute | solution.py:277
  128.2 5.0 %collective-permute-done.12 = bf16[2,2,2,8,8,128]{5,4,3,2,1,0:T(8,128)(2,1)S(1)} collective-permute-done((bf16[2,2,2,8,8,128]{5,4,3,2,1,0:T(8,128)(2,1)S(1)}, bf16[2,2,2,8,8,128]{5,4,3,2,1,0:T(8,128)(2,1)S(1)}, u32[]{:S(2)}, u32[]{:S(2)}) %collective-permute-start.12) | collective-permute-done | bytes 131104 | tf_op jit(solution)/shard_map/ppermute | solution.py:272
  133.3 7.4 %collective-permute-done.14 = bf16[2,2,2,8,8,128]{5,4,3,2,1,0:T(8,128)(2,1)S(1)} collective-permute-done((bf16[2,2,2,8,8,128]{5,4,3,2,1,0:T(8,128)(2,1)S(1)}, bf16[2,2,2,8,8,128]{5,4,3,2,1,0:T(8,128)(2,1)S(1)}, u32[]{:S(2)}, u32[]{:S(2)}) %collective-permute-start.14) | collective-permute-done | bytes 131104 | tf_op jit(solution)/shard_map/ppermute | solution.py:277
  140.8 1.9 %collective-permute-start.16 = (bf16[2,2,8,8,128]{4,3,2,1,0:T(8,128)(2,1)S(1)}, bf16[2,2,8,8,128]{4,3,2,1,0:T(8,128)(2,1)S(1)}, u32[]{:S(2)}, u32[]{:S(2)}) collective-permute-start(bf16[2,2,8,8,128]{4,3,2,1,0:T(8,128)(2,1)S(1)} %get-tuple-element.58), channel_id=1, source_target_pairs={{0,15},{1,14},{2,13},{3,12},{4,11},{5,10},{6,9},{7,8},{8,7},{9,6},... | collective-permute-start | bytes 196616 | tf_op jit(solution)/shard_map/ppermute | solution.py:272
  142.8 8.8 %collective-permute-done.16.other_ref = bf16[2,2,8,8,128]{4,3,2,1,0:T(8,128)(2,1)S(1)} collective-permute-done((bf16[2,2,8,8,128]{4,3,2,1,0:T(8,128)(2,1)S(1)}, bf16[2,2,8,8,128]{4,3,2,1,0:T(8,128)(2,1)S(1)}, u32[]{:S(2)}, u32[]{:S(2)}) %collective-permute-start.16) | collective-permute-done | bytes 65568 | tf_op jit(solution)/shard_map/ppermute | solution.py:272
  153.0 6.8 %all-to-all-start.3 = ((bf16[32,2,2,2,4,128]{5,4,3,2,1,0:T(4,128)(2,1)}), bf16[32,2,2,2,4,128]{5,4,3,2,1,0:T(4,128)(2,1)S(1)}, u32[]{:S(2)}, u32[]{:S(2)}) async-start(bf16[32,2,2,2,4,128]{5,4,3,2,1,0:T(4,128)(2,1)} %bitcast.22), calls=%async_computation.3 | async-start | bytes 524288 | tf_op jit(solution)/shard_map/all_to_all | solution.py:310
  159.9 1.4 gather_fusion
  161.3 7.4 %all-to-all-done.3 = bf16[32,2,2,2,4,128]{5,4,3,2,1,0:T(4,128)(2,1)S(1)} async-done(((bf16[32,2,2,2,4,128]{5,4,3,2,1,0:T(4,128)(2,1)}), bf16[32,2,2,2,4,128]{5,4,3,2,1,0:T(4,128)(2,1)S(1)}, u32[]{:S(2)}, u32[]{:S(2)}) %all-to-all-start.3) | async-done | bytes 262176 | tf_op jit(solution)/shard_map/all_to_all | solution.py:310
  (50 shorter events, 10.8 us)
Async XLA Ops:
  0.6 0.9 copy-start.2
  1.5 0.7 copy-start.3
  3.7 19.3 %all-to-all-start = ((bf16[32,2,2,2,4,128]{5,4,3,2,1,0:T(4,128)(2,1)}), bf16[32,2,2,2,4,128]{5,4,3,2,1,0:T(4,128)(2,1)S(1)}, u32[]{:S(2)}, u32[]{:S(2)}) async-start(bf16[32,2,2,2,4,128]{5,4,3,2,1,0:T(4,128)(2,1)} %bitcast.7), calls=%async_computation | async-start | bytes 524288 | tf_op jit(solution)/shard_map/all_to_all | solution.py:310
  14.1 1.0 copy-start
  15.1 1.0 copy-start.1
  16.2 0.7 copy-start.4
  23.0 4.1 %copy-start.8 = (s32[16,16]{1,0:T(8,128)S(1)}, s32[16,16]{1,0:T(8,128)}, u32[]{:S(2)}) copy-start(s32[16,16]{1,0:T(8,128)} %param.10) | copy-start | bytes 3076
  23.0 47.2 %copy-start.9 = (s32[1,16]{1,0:T(1,128)S(1)}, s32[1,16]{1,0:T(1,128)}, u32[]{:S(2)}) copy-start(s32[1,16]{1,0:T(1,128)} %param.11) | copy-start | bytes 196
  23.0 36.7 %all-to-all-start.1 = ((bf16[16,2,2,128,128]{4,3,2,1,0:T(8,128)(2,1)}), bf16[16,2,2,128,128]{4,3,2,1,0:T(8,128)(2,1)S(1)}, u32[]{:S(2)}, u32[]{:S(2)}) async-start(bf16[16,2,2,128,128]{4,3,2,1,0:T(8,128)(2,1)} %bitcast.14), calls=%async_computation.1 | async-start | bytes 4194304 | tf_op jit(solution)/shard_map/all_to_all | solution.py:323
  27.7 24.8 %collective-permute-start.1 = (bf16[2,2,8,8,128]{4,3,2,1,0:T(8,128)(2,1)S(1)}, bf16[2,2,8,8,128]{4,3,2,1,0:T(8,128)(2,1)S(1)}, u32[]{:S(2)}, u32[]{:S(2)}) collective-permute-start(bf16[2,2,8,8,128]{4,3,2,1,0:T(8,128)(2,1)S(1)} %get-tuple-element.31), channel_id=1, source_target_pairs={{0,4},{1,5},{2,6},{3,7},{4,0},{5,1},{6,2},{7,3},{8,12},{9,13},{10,... | collective-permute-start | bytes 196616 | tf_op jit(solution)/shard_map/ppermute | solution.py:272
  34.7 21.4 %collective-permute-start.2 = (bf16[2,2,8,8,128]{4,3,2,1,0:T(8,128)(2,1)S(1)}, bf16[2,2,8,8,128]{4,3,2,1,0:T(8,128)(2,1)S(1)}, u32[]{:S(2)}, u32[]{:S(2)}) collective-permute-start(bf16[2,2,8,8,128]{4,3,2,1,0:T(8,128)(2,1)S(1)} %get-tuple-element.30), channel_id=1, source_target_pairs={{0,11},{1,10},{2,9},{3,8},{4,15},{5,14},{6,13},{7,12},{8,3},{9,2},... | collective-permute-start | bytes 196616 | tf_op jit(solution)/shard_map/ppermute | solution.py:272
  44.0 12.1 %collective-permute-start = (bf16[2,2,8,8,128]{4,3,2,1,0:T(8,128)(2,1)S(1)}, bf16[2,2,8,8,128]{4,3,2,1,0:T(8,128)(2,1)S(1)}, u32[]{:S(2)}, u32[]{:S(2)}) collective-permute-start(bf16[2,2,8,8,128]{4,3,2,1,0:T(8,128)(2,1)S(1)} %get-tuple-element.30), channel_id=1, source_target_pairs={{0,15},{1,14},{2,13},{3,12},{4,11},{5,10},{6,9},{7,8},{8,7},{9,6},... | collective-permute-start | bytes 196616 | tf_op jit(solution)/shard_map/ppermute | solution.py:272
  45.9 10.3 %collective-permute-start.3 = (bf16[1,2,2,8,8,128]{5,4,3,2,1,0:T(8,128)(2,1)S(1)}, bf16[1,2,2,8,8,128]{5,4,3,2,1,0:T(8,128)(2,1)S(1)}, u32[]{:S(2)}, u32[]{:S(2)}) collective-permute-start(bf16[1,2,2,8,8,128]{5,4,3,2,1,0:T(8,128)(2,1)S(1)} %bitcast.40), channel_id=1, source_target_pairs={{0,1},{1,2},{2,3},{3,0},{4,5},{5,6},{6,7},{7,4},{8,9},{9,10},{10,1... | collective-permute-start | bytes 196616 | tf_op jit(solution)/shard_map/ppermute | solution.py:277
  49.5 9.2 %collective-permute-start.4 = (bf16[1,2,2,8,8,128]{5,4,3,2,1,0:T(8,128)(2,1)S(1)}, bf16[1,2,2,8,8,128]{5,4,3,2,1,0:T(8,128)(2,1)S(1)}, u32[]{:S(2)}, u32[]{:S(2)}) collective-permute-start(bf16[1,2,2,8,8,128]{5,4,3,2,1,0:T(8,128)(2,1)S(1)} %bitcast.41), channel_id=1, source_target_pairs={{0,2},{1,3},{2,0},{3,1},{4,6},{5,7},{6,4},{7,5},{8,10},{9,11},{10,... | collective-permute-start | bytes 196616 | tf_op jit(solution)/shard_map/ppermute | solution.py:277
  52.6 6.5 %collective-permute-start.5 = (bf16[1,2,2,8,8,128]{5,4,3,2,1,0:T(8,128)(2,1)S(1)}, bf16[1,2,2,8,8,128]{5,4,3,2,1,0:T(8,128)(2,1)S(1)}, u32[]{:S(2)}, u32[]{:S(2)}) collective-permute-start(bf16[1,2,2,8,8,128]{5,4,3,2,1,0:T(8,128)(2,1)S(1)} %bitcast.42), channel_id=1, source_target_pairs={{0,3},{1,0},{2,1},{3,2},{4,7},{5,4},{6,5},{7,6},{8,11},{9,8},{10,9... | collective-permute-start | bytes 196616 | tf_op jit(solution)/shard_map/ppermute | solution.py:277
  59.1 0.6 copy-start.6
  59.7 11.1 %collective-permute-start.6 = (bf16[3,2,2,8,8,128]{5,4,3,2,1,0:T(8,128)(2,1)S(1)}, bf16[3,2,2,8,8,128]{5,4,3,2,1,0:T(8,128)(2,1)S(1)}, u32[]{:S(2)}, u32[]{:S(2)}) collective-permute-start(bf16[3,2,2,8,8,128]{5,4,3,2,1,0:T(8,128)(2,1)S(1)} %pad_maximum_fusion.refs_4_), channel_id=1, source_target_pairs={{0,1},{1,2},{2,3},{3,0},{4,5},{5,6},{6,7},{7,4},{8,9},{9,10},{10,1... | collective-permute-start | bytes 589832 | tf_op jit(solution)/shard_map/ppermute | solution.py:277
  62.3 17.5 %collective-permute-start.7 = (bf16[3,2,2,8,8,128]{5,4,3,2,1,0:T(8,128)(2,1)S(1)}, bf16[3,2,2,8,8,128]{5,4,3,2,1,0:T(8,128)(2,1)S(1)}, u32[]{:S(2)}, u32[]{:S(2)}) collective-permute-start(bf16[3,2,2,8,8,128]{5,4,3,2,1,0:T(8,128)(2,1)S(1)} %pad_maximum_fusion.refs_4_), channel_id=1, source_target_pairs={{0,2},{1,3},{2,0},{3,1},{4,6},{5,7},{6,4},{7,5},{8,10},{9,11},{10,... | collective-permute-start | bytes 589832 | tf_op jit(solution)/shard_map/ppermute | solution.py:277
  68.2 11.6 %collective-permute-start.8 = (bf16[3,2,2,8,8,128]{5,4,3,2,1,0:T(8,128)(2,1)S(1)}, bf16[3,2,2,8,8,128]{5,4,3,2,1,0:T(8,128)(2,1)S(1)}, u32[]{:S(2)}, u32[]{:S(2)}) collective-permute-start(bf16[3,2,2,8,8,128]{5,4,3,2,1,0:T(8,128)(2,1)S(1)} %pad_maximum_fusion.refs_4_), channel_id=1, source_target_pairs={{0,3},{1,0},{2,1},{3,2},{4,7},{5,4},{6,5},{7,6},{8,11},{9,8},{10,9... | collective-permute-start | bytes 589832 | tf_op jit(solution)/shard_map/ppermute | solution.py:277
  79.8 0.8 copy-start.7
  95.4 18.4 %collective-permute-start.10 = (bf16[2,2,2,8,8,128]{5,4,3,2,1,0:T(8,128)(2,1)S(1)}, bf16[2,2,2,8,8,128]{5,4,3,2,1,0:T(8,128)(2,1)S(1)}, u32[]{:S(2)}, u32[]{:S(2)}) collective-permute-start(bf16[2,2,2,8,8,128]{5,4,3,2,1,0:T(8,128)(2,1)S(1)} %get-tuple-element.44), channel_id=1, source_target_pairs={{0,2},{1,3},{2,0},{3,1},{4,6},{5,7},{6,4},{7,5},{8,10},{9,11},{10,... | collective-permute-start | bytes 393224 | tf_op jit(solution)/shard_map/ppermute | solution.py:277
  100.8 13.1 %collective-permute-start.11 = (bf16[2,2,2,8,8,128]{5,4,3,2,1,0:T(8,128)(2,1)S(1)}, bf16[2,2,2,8,8,128]{5,4,3,2,1,0:T(8,128)(2,1)S(1)}, u32[]{:S(2)}, u32[]{:S(2)}) collective-permute-start(bf16[2,2,2,8,8,128]{5,4,3,2,1,0:T(8,128)(2,1)S(1)} %get-tuple-element.45), channel_id=1, source_target_pairs={{0,1},{1,2},{2,3},{3,0},{4,5},{5,6},{6,7},{7,4},{8,9},{9,10},{10,1... | collective-permute-start | bytes 393224 | tf_op jit(solution)/shard_map/ppermute | solution.py:277
  103.7 10.1 %collective-permute-start.9 = (bf16[2,2,2,8,8,128]{5,4,3,2,1,0:T(8,128)(2,1)S(1)}, bf16[2,2,2,8,8,128]{5,4,3,2,1,0:T(8,128)(2,1)S(1)}, u32[]{:S(2)}, u32[]{:S(2)}) collective-permute-start(bf16[2,2,2,8,8,128]{5,4,3,2,1,0:T(8,128)(2,1)S(1)} %get-tuple-element.43), channel_id=1, source_target_pairs={{0,3},{1,0},{2,1},{3,2},{4,7},{5,4},{6,5},{7,6},{8,11},{9,8},{10,9... | collective-permute-start | bytes 393224 | tf_op jit(solution)/shard_map/ppermute | solution.py:277
  107.9 34.9 %copy-start.5 = (s32[1,16,2]{1,2,0:T(2,128)S(1)}, s32[1,16,2]{1,2,0:T(2,128)}, u32[]{:S(2)}) copy-start(s32[1,16,2]{1,2,0:T(2,128)} %param.9) | copy-start | bytes 388
  107.9 43.7 %all-to-all-start.2 = ((bf16[16,2,128,128]{3,2,1,0:T(8,128)(2,1)}), bf16[16,2,128,128]{3,2,1,0:T(8,128)(2,1)S(1)}, u32[]{:S(2)}, u32[]{:S(2)}) async-start(bf16[16,2,128,128]{3,2,1,0:T(8,128)(2,1)} %bitcast.18), calls=%async_computation.2 | async-start | bytes 2097152 | tf_op jit(solution)/shard_map/all_to_all | solution.py:337
  113.9 19.3 %collective-permute-start.12 = (bf16[2,2,2,8,8,128]{5,4,3,2,1,0:T(8,128)(2,1)S(1)}, bf16[2,2,2,8,8,128]{5,4,3,2,1,0:T(8,128)(2,1)S(1)}, u32[]{:S(2)}, u32[]{:S(2)}) collective-permute-start(bf16[2,2,2,8,8,128]{5,4,3,2,1,0:T(8,128)(2,1)S(1)} %add_convert_fusion.1), channel_id=1, source_target_pairs={{0,4},{1,5},{2,6},{3,7},{4,0},{5,1},{6,2},{7,3},{8,12},{9,13},{10,... | collective-permute-start | bytes 393224 | tf_op jit(solution)/shard_map/ppermute | solution.py:272
  120.3 13.0 %collective-permute-start.13 = (bf16[2,2,2,8,8,128]{5,4,3,2,1,0:T(8,128)(2,1)S(1)}, bf16[2,2,2,8,8,128]{5,4,3,2,1,0:T(8,128)(2,1)S(1)}, u32[]{:S(2)}, u32[]{:S(2)}) collective-permute-start(bf16[2,2,2,8,8,128]{5,4,3,2,1,0:T(8,128)(2,1)S(1)} %get-tuple-element.51), channel_id=1, source_target_pairs={{0,3},{1,0},{2,1},{3,2},{4,7},{5,4},{6,5},{7,6},{8,11},{9,8},{10,9... | collective-permute-start | bytes 393224 | tf_op jit(solution)/shard_map/ppermute | solution.py:277
  123.9 16.8 %collective-permute-start.14 = (bf16[2,2,2,8,8,128]{5,4,3,2,1,0:T(8,128)(2,1)S(1)}, bf16[2,2,2,8,8,128]{5,4,3,2,1,0:T(8,128)(2,1)S(1)}, u32[]{:S(2)}, u32[]{:S(2)}) collective-permute-start(bf16[2,2,2,8,8,128]{5,4,3,2,1,0:T(8,128)(2,1)S(1)} %get-tuple-element.52), channel_id=1, source_target_pairs={{0,2},{1,3},{2,0},{3,1},{4,6},{5,7},{6,4},{7,5},{8,10},{9,11},{10,... | collective-permute-start | bytes 393224 | tf_op jit(solution)/shard_map/ppermute | solution.py:277
  125.8 14.9 %collective-permute-start.15 = (bf16[2,2,2,8,8,128]{5,4,3,2,1,0:T(8,128)(2,1)S(1)}, bf16[2,2,2,8,8,128]{5,4,3,2,1,0:T(8,128)(2,1)S(1)}, u32[]{:S(2)}, u32[]{:S(2)}) collective-permute-start(bf16[2,2,2,8,8,128]{5,4,3,2,1,0:T(8,128)(2,1)S(1)} %get-tuple-element.53), channel_id=1, source_target_pairs={{0,1},{1,2},{2,3},{3,0},{4,5},{5,6},{6,7},{7,4},{8,9},{9,10},{10,1... | collective-permute-start | bytes 393224 | tf_op jit(solution)/shard_map/ppermute | solution.py:277
  140.8 10.8 %collective-permute-start.16 = (bf16[2,2,8,8,128]{4,3,2,1,0:T(8,128)(2,1)S(1)}, bf16[2,2,8,8,128]{4,3,2,1,0:T(8,128)(2,1)S(1)}, u32[]{:S(2)}, u32[]{:S(2)}) collective-permute-start(bf16[2,2,8,8,128]{4,3,2,1,0:T(8,128)(2,1)S(1)} %get-tuple-element.58), channel_id=1, source_target_pairs={{0,15},{1,14},{2,13},{3,12},{4,11},{5,10},{6,9},{7,8},{8,7},{9,6},... | collective-permute-start | bytes 196616 | tf_op jit(solution)/shard_map/ppermute | solution.py:272
  153.0 15.7 %all-to-all-start.3 = ((bf16[32,2,2,2,4,128]{5,4,3,2,1,0:T(4,128)(2,1)}), bf16[32,2,2,2,4,128]{5,4,3,2,1,0:T(4,128)(2,1)S(1)}, u32[]{:S(2)}, u32[]{:S(2)}) async-start(bf16[32,2,2,2,4,128]{5,4,3,2,1,0:T(4,128)(2,1)} %bitcast.22), calls=%async_computation.3 | async-start | bytes 524288 | tf_op jit(solution)/shard_map/all_to_all | solution.py:310

commit v9 on v8

--- a/solution.py
+++ b/solution.py
@@ -13,8 +13,7 @@
 PAIR = 2
 SCALING = HD ** (-0.5)
 LOG2E = 1.4426950408889634
-PLANE = ("dp", "xh")
-MIRROR = 15
+EVERYONE = ("dp", "xh", "z")
 ACROSS = 4
 NEAR = 4
 
@@ -60,15 +59,13 @@
     part = width // NEAR
     factor = SCALING * LOG2E
 
-    def rows_of(slot, first_part):
-        begin = (slot % NEAR) * part
-        if slot < NEAR:
-            return slice(begin, begin + first_part)
-        return slice(begin + first_part, begin + part)
+    def rows_of(slot):
+        begin = (slot % NEAR) * part + (slot // NEAR) * (part // 2)
+        return slice(begin, begin + part // 2)
 
     def stage(block, _):
         for slot, ref in enumerate(kv_refs):
-            rows = rows_of(slot, part // 4)
+            rows = rows_of(slot)
             count = rows.stop - rows.start
             key = ref[:, :, 0, block].astype(jnp.float32).reshape(count, HD)
             value = ref[:, :, 1, block].astype(jnp.float32).reshape(count, HD)
@@ -81,7 +78,9 @@
 
     row = lax.broadcasted_iota(jnp.int32, (width, 1), 0)
     holder = (place_ref[0] & 12) | ((place_ref[0] - (row >> 6)) & 3)
-    source = holder ^ (((row >> 4) & 1) * MIRROR) ^ (((row >> 5) & 1) * ACROSS)
+    holder = holder ^ (((row >> 5) & 1) * ACROSS)
+    lower = jnp.where(holder < 8, holder, 15 - holder)
+    source = jnp.where(((row >> 4) & 1) == 0, lower, 15 - lower)
     key_offset = (
         ((row >> 2) & 1) * tile_rows + ((row >> 3) & 1) * 64 + source * 4 + (row & 3)
     )
@@ -155,7 +154,7 @@
 
     def unstage(block, _):
         for slot, ref in enumerate(dkv_refs):
-            rows = rows_of(slot, part // 2)
+            rows = rows_of(slot)
             shape = ref.shape[:2] + ref.shape[4:]
             ref[:, :, 0, block] = (dk_all[block, rows] * SCALING).reshape(shape).astype(jnp.bfloat16)
             ref[:, :, 1, block] = dv_all[block, rows].reshape(shape).astype(jnp.bfloat16)
@@ -173,7 +172,7 @@
     return pl.pallas_call(
         attention_kernel,
         out_shape=(jax.ShapeDtypeStruct((slots, tile_rows, HD), jnp.bfloat16),)
-        + (jax.ShapeDtypeStruct((2,) + chunks[0].shape[1:], jnp.bfloat16),) * (2 * NEAR),
+        + (jax.ShapeDtypeStruct(chunks[0].shape, jnp.bfloat16),) * (2 * NEAR),
         in_specs=[smem] * 3 + [vmem] * (1 + 2 * NEAR),
         out_specs=(vmem,) * (1 + 2 * NEAR),
         scratch_shapes=[
@@ -198,45 +197,40 @@
     def body(slot, _):
         tile = index_ref[slot & 1, slot >> 1]
         piece = kv_ref[tile].reshape((2, 2, 2) + kv_ref.shape[2:])
-        for half in range(2):
-            out_ref[slot >> 1, half, slot & 1] = piece[:, half]
+        for across in range(2):
+            for half in range(2):
+                out_ref[slot >> 1, across, half, slot & 1] = piece[:, across, half]
         return 0
 
     lax.fori_loop(0, 2 * index_ref.shape[1], body, 0, unroll=4)
 
 
-def kv_unpack_kernel(recv_ref, place_ref, kv_ref, own_ref, other_ref):
-    head = place_ref[0] >> 3
-
-    def body(pair, _):
-        low = recv_ref[PAIR * pair]
-        high = recv_ref[PAIR * pair + 1]
-        for half in range(2):
-            for kind in range(2):
-                for ref, which in ((own_ref, head), (other_ref, 1 - head)):
-                    rows = [
-                        kv_ref[slot >> 1, half, slot & 1, kind, which].astype(jnp.float32)
-                        for slot in (low, high)
-                    ]
-                    ref[half, kind, pair] = jnp.concatenate(rows, axis=0).astype(jnp.bfloat16)
-        return 0
-
-    lax.fori_loop(0, recv_ref.shape[0] // PAIR, body, 0)
-
-
-def kv_back_kernel(recv_ref, place_ref, own_ref, other_ref, out_ref):
-    head = place_ref[0] >> 3
-    sliver = out_ref.shape[-2]
-
+def kv_unpack_kernel(recv_ref, kv_ref, out_ref):
     def body(pair, _):
         slots = (recv_ref[PAIR * pair], recv_ref[PAIR * pair + 1])
-        for half in range(2):
-            for kind in range(2):
-                for ref, which in ((own_ref, head), (other_ref, 1 - head)):
-                    total = ref[half, kind, pair].astype(jnp.float32)
-                    for order, slot in enumerate(slots):
-                        rows = total[order * sliver : (order + 1) * sliver]
-                        out_ref[slot >> 1, half, slot & 1, kind, which] = rows.astype(jnp.bfloat16)
+        for across in range(2):
+            for half in range(2):
+                rows = [
+                    kv_ref[slot >> 1, across, half, slot & 1].astype(jnp.float32)
+                    for slot in slots
+                ]
+                out_ref[half, across, :, pair] = jnp.concatenate(rows, axis=1).astype(jnp.bfloat16)
+        return 0
+
+    lax.fori_loop(0, recv_ref.shape[0] // PAIR, body, 0)
+
+
+def kv_back_kernel(recv_ref, sum_ref, out_ref):
+    sliver = out_ref.shape[-2]
+
+    def body(pair, _):
+        slots = (recv_ref[PAIR * pair], recv_ref[PAIR * pair + 1])
+        for across in range(2):
+            for half in range(2):
+                both = sum_ref[half, across, :, pair].astype(jnp.float32)
+                for order, slot in enumerate(slots):
+                    rows = both[:, order * sliver : (order + 1) * sliver]
+                    out_ref[slot >> 1, across, half, slot & 1] = rows.astype(jnp.bfloat16)
         return 0
 
     lax.fori_loop(0, recv_ref.shape[0] // PAIR, body, 0)
@@ -245,14 +239,14 @@
 def kv_final_kernel(anchor_ref, kv_ref, out_ref):
     def body(tile, _):
         slot = anchor_ref[tile]
-        piece = kv_ref[slot >> 1, :, slot & 1]
-        for half in range(2):
-            for kind in range(2):
-                for head in range(2):
-                    out_ref[tile, kind * 4 + half * 2 + head] = piece[half, kind, head]
-        return 0
-
-    lax.fori_loop(0, anchor_ref.shape[0], body, 0)
+        for across in range(2):
+            for half in range(2):
+                piece = kv_ref[slot >> 1, across, half, slot & 1]
+                for kind in range(2):
+                    out_ref[tile, kind * 4 + across * 2 + half] = piece[kind]
+        return 0
+
+    lax.fori_loop(0, anchor_ref.shape[0], body, 0, unroll=4)
 
 
 def local_call(kernel, name, scalars, arrays, out_shape):
@@ -302,34 +296,34 @@
     my_recv = lax.dynamic_index_in_dim(recv_slot, replica, 0, keepdims=False)
     place = lax.axis_index("z").astype(jnp.int32).reshape(1)
     traveling = jax.ShapeDtypeStruct(
-        (n_replicas, 2, slot_cap, 2, 2, sliver, HD), keys_values.dtype
-    )
-    half_shape = jax.ShapeDtypeStruct((2, 2, pairs, PAIR * sliver, HD), keys_values.dtype)
-
-    def over_plane(values):
+        (n_replicas, 2, 2, slot_cap, 2, sliver, HD), keys_values.dtype
+    )
+    half_shape = jax.ShapeDtypeStruct((2, 2, 2, pairs, PAIR * sliver, HD), keys_values.dtype)
+    half_groups = [
+        [32 * rank + 16 * across + z for rank in range(n_replicas) for across in range(2) for z in pair]
+        for pair in ((low, 15 - low) for low in range(8))
+    ]
+
+    def by_halves(values):
         return lax.all_to_all(
-            values.reshape((2 * n_replicas,) + values.shape[2:]),
-            PLANE, split_axis=0, concat_axis=0, tiled=True,
+            values.reshape((4 * n_replicas,) + values.shape[3:]), EVERYONE,
+            split_axis=0, concat_axis=0, axis_index_groups=half_groups, tiled=True,
         ).reshape(values.shape)
 
     kv_blocks = keys_values.reshape(tile_count, sliver, 2 * KV, HD).transpose(0, 2, 1, 3)
-    kv_arrived = over_plane(
+    kv_arrived = by_halves(
         local_call(kv_pack_kernel, "kv_pack", [outgoing], [kv_blocks], traveling)
     )
-    own, other = local_call(
-        kv_unpack_kernel, "kv_unpack", [my_recv, place], [kv_arrived], (half_shape, half_shape)
-    )
+    mine = local_call(kv_unpack_kernel, "kv_unpack", [my_recv], [kv_arrived], half_shape)
     qg_packed = pack(outgoing, queries, grad_out)
     qg_arrived = lax.all_to_all(
         qg_packed.reshape(n_replicas, slot_cap, 2, tile_rows, row_width),
         "dp", split_axis=0, concat_axis=0, tiled=True,
     ).reshape(slots, 2, tile_rows, row_width)
-    far = jnp.stack(
-        [far_swap(other, MIRROR), far_swap(own, ACROSS), far_swap(other, MIRROR ^ ACROSS)]
-    )
-    own_chunks = near_gather(own[None])
-    far, own_chunks, qg_arrived = lax.optimization_barrier((far, own_chunks, qg_arrived))
-    chunks = own_chunks + near_gather(far)
+    far = far_swap(mine, ACROSS)
+    chunks = near_gather(mine)
+    far, chunks, qg_arrived = lax.optimization_barrier((far, chunks, qg_arrived))
+    chunks = chunks + near_gather(far)
 
     seq = tile_seq[0]
     start = jnp.sum((seq[None, :] < seq[:, None]).astype(jnp.int32), axis=1)
@@ -343,10 +337,9 @@
     arrived = far_swap(total(across_terms).astype(jnp.bfloat16), ACROSS)
     base = lax.optimization_barrier(total([arrived, own_terms[0]]))
     summed = total([base] + near_terms(own_terms)[1:]).astype(jnp.bfloat16)
-    swapped = [summed[0], far_swap(summed[1], MIRROR)]
-    swapped, query_returned = lax.optimization_barrier((swapped, query_returned))
-    kv_returned = over_plane(
-        local_call(kv_back_kernel, "kv_back", [my_recv, place], swapped, traveling)
+    summed, query_returned = lax.optimization_barrier((summed, query_returned))
+    kv_returned = by_halves(
+        local_call(kv_back_kernel, "kv_back", [my_recv], [summed], traveling)
     )
 
     flat_slots = jnp.arange(slots)

time: 171 us -> 180 us (1.053)
  the two profiles are of different devices: /device:TPU:1 before, /device:TPU:33 now
where the time goes in v9:
time: 180 us; the launch traced here: 179 us
  starting transfers between devices  90.7 us (50%)
  waiting for transfers between devices  57.5 us (32%)
  Pallas kernels  19.1 us (11%)
  local copies, waits for them, and re-layouts  10.4 us (6%)
    ppermute x12, starting transfers between devices, near_shift(): return lax.ppermute(values, 'z', pairs)  35.3 us
    all_to_all x2, starting transfers between devices, by_halves(): lax.all_to_all(values.reshape((4 * n_replicas,) + values.shape[3:]), EVER...  31.5 us
    all_to_all x2, waiting for transfers between devices, by_halves(): lax.all_to_all(values.reshape((4 * n_replicas,) + values.shape[3:]), EVER...  29.6 us
    ppermute x12, waiting for transfers between devices, near_shift(): return lax.ppermute(values, 'z', pairs)  20.6 us
    pallas_call x1, Pallas kernels, attention(): pl.pallas_call(attention_kernel, out_shape=(jax.ShapeDtypeStruct((slots,...  12 us
    ppermute x2, starting transfers between devices, far_swap(): lax.ppermute(values, 'z', [(place, place ^ flip) for place in range(16)])  10.5 us
    all_to_all x1, starting transfers between devices, on_device(): lax.all_to_all(query_back.reshape(n_replicas, slot_cap, tile_rows, row_wi...  9.39 us
    unnamed x28, local copies, waits for them, and re-layouts  9.03 us
  transfers between devices with their start and end apart: 18, of which 12 were waited for; matrix products, arithmetic and copies ran while one was open for 1% of the time, Pallas kernels for 2%

profile of v9, /device:TPU:33, one launch (start us, length us, event | category | flops | bytes accessed | tf_op | source)
XLA Modules:
  0.0 179.3 jit_solution(8889667938500991235)
XLA Ops:
  2.2 1.5 kv_pack.1
  3.7 17.1 %all-to-all-start = ((bf16[64,2,2,4,128]{4,3,2,1,0:T(4,128)(2,1)}), bf16[64,2,2,4,128]{4,3,2,1,0:T(4,128)(2,1)S(1)}, u32[]{:S(2)}, u32[]{:S(2)}) async-start(bf16[64,2,2,4,128]{4,3,2,1,0:T(4,128)(2,1)} %bitcast.7), calls=%async_computation | async-start | bytes 524288 | tf_op jit(solution)/shard_map/all_to_all | solution.py:308
  23.5 2.3 %pack_rows.1 = bf16[32,2,128,128]{3,2,1,0:T(8,128)(2,1)} custom-call(s32[2,16]{1,0:T(2,128)S(1)} %bitcast.30, bf16[16,128,128]{2,1,0:T(8,128)(2,1)S(1)} %copy-done, bf16[16,128,128]{2,1,0:T(8,128)(2,1)S(1)} %copy-done.1), custom_call_target="tpu_custom_call" | custom-call | tf_op jit(solution)/shard_map/pack_rows/pallas_call | solution.py:37
  25.8 13.2 %all-to-all-done = bf16[64,2,2,4,128]{4,3,2,1,0:T(4,128)(2,1)S(1)} async-done(((bf16[64,2,2,4,128]{4,3,2,1,0:T(4,128)(2,1)}), bf16[64,2,2,4,128]{4,3,2,1,0:T(4,128)(2,1)S(1)}, u32[]{:S(2)}, u32[]{:S(2)}) %all-to-all-start) | async-done | bytes 262176 | tf_op jit(solution)/shard_map/all_to_all | solution.py:308
  39.0 4.1 %all-to-all-start.1 = ((bf16[16,2,2,128,128]{4,3,2,1,0:T(8,128)(2,1)}), bf16[16,2,2,128,128]{4,3,2,1,0:T(8,128)(2,1)S(1)}, u32[]{:S(2)}, u32[]{:S(2)}) async-start(bf16[16,2,2,128,128]{4,3,2,1,0:T(8,128)(2,1)} %bitcast.10), calls=%async_computation.1 | async-start | bytes 4194304 | tf_op jit(solution)/shard_map/all_to_all | solution.py:319
  43.9 5.1 %collective-permute-start = (bf16[2,2,2,8,8,128]{5,4,3,2,1,0:T(8,128)(2,1)S(1)}, bf16[2,2,2,8,8,128]{5,4,3,2,1,0:T(8,128)(2,1)S(1)}, u32[]{:S(2)}, u32[]{:S(2)}) collective-permute-start(bf16[2,2,2,8,8,128]{5,4,3,2,1,0:T(8,128)(2,1)S(1)} %kv_unpack.1.refs_0_), channel_id=1, source_target_pairs={{0,4},{1,5},{2,6},{3,7},{4,0},{5,1},{6,2},{7,3},{8,12},{9,13},{10,... | collective-permute-start | bytes 393224 | tf_op jit(solution)/shard_map/ppermute | solution.py:266
  49.0 2.7 %collective-permute-start.1 = (bf16[2,2,2,8,8,128]{5,4,3,2,1,0:T(8,128)(2,1)S(1)}, bf16[2,2,2,8,8,128]{5,4,3,2,1,0:T(8,128)(2,1)S(1)}, u32[]{:S(2)}, u32[]{:S(2)}) collective-permute-start(bf16[2,2,2,8,8,128]{5,4,3,2,1,0:T(8,128)(2,1)S(1)} %kv_unpack.1.refs_0_), channel_id=1, source_target_pairs={{0,1},{1,2},{2,3},{3,0},{4,5},{5,6},{6,7},{7,4},{8,9},{9,10},{10,1... | collective-permute-start | bytes 393224 | tf_op jit(solution)/shard_map/ppermute | solution.py:271
  51.7 3.9 %collective-permute-start.2 = (bf16[2,2,2,8,8,128]{5,4,3,2,1,0:T(8,128)(2,1)S(1)}, bf16[2,2,2,8,8,128]{5,4,3,2,1,0:T(8,128)(2,1)S(1)}, u32[]{:S(2)}, u32[]{:S(2)}) collective-permute-start(bf16[2,2,2,8,8,128]{5,4,3,2,1,0:T(8,128)(2,1)S(1)} %kv_unpack.1.refs_0_), channel_id=1, source_target_pairs={{0,2},{1,3},{2,0},{3,1},{4,6},{5,7},{6,4},{7,5},{8,10},{9,11},{10,... | collective-permute-start | bytes 393224 | tf_op jit(solution)/shard_map/ppermute | solution.py:271
  55.6 1.9 %collective-permute-start.3 = (bf16[2,2,2,8,8,128]{5,4,3,2,1,0:T(8,128)(2,1)S(1)}, bf16[2,2,2,8,8,128]{5,4,3,2,1,0:T(8,128)(2,1)S(1)}, u32[]{:S(2)}, u32[]{:S(2)}) collective-permute-start(bf16[2,2,2,8,8,128]{5,4,3,2,1,0:T(8,128)(2,1)S(1)} %kv_unpack.1.refs_0_), channel_id=1, source_target_pairs={{0,3},{1,0},{2,1},{3,2},{4,7},{5,4},{6,5},{7,6},{8,11},{9,8},{10,9... | collective-permute-start | bytes 393224 | tf_op jit(solution)/shard_map/ppermute | solution.py:271
  57.5 4.2 %collective-permute-done.refs_4_ = bf16[2,2,2,8,8,128]{5,4,3,2,1,0:T(8,128)(2,1)S(1)} collective-permute-done((bf16[2,2,2,8,8,128]{5,4,3,2,1,0:T(8,128)(2,1)S(1)}, bf16[2,2,2,8,8,128]{5,4,3,2,1,0:T(8,128)(2,1)S(1)}, u32[]{:S(2)}, u32[]{:S(2)}) %collective-permute-start) | collective-permute-done | bytes 131104 | tf_op jit(solution)/shard_map/ppermute | solution.py:266
  61.7 1.5 collective-permute-done.1.refs_1_
  63.2 3.4 %collective-permute-done.2.refs_2_ = bf16[2,2,2,8,8,128]{5,4,3,2,1,0:T(8,128)(2,1)S(1)} collective-permute-done((bf16[2,2,2,8,8,128]{5,4,3,2,1,0:T(8,128)(2,1)S(1)}, bf16[2,2,2,8,8,128]{5,4,3,2,1,0:T(8,128)(2,1)S(1)}, u32[]{:S(2)}, u32[]{:S(2)}) %collective-permute-start.2) | collective-permute-done | bytes 131104 | tf_op jit(solution)/shard_map/ppermute | solution.py:271
  66.5 4.0 %collective-permute-done.3.refs_3_ = bf16[2,2,2,8,8,128]{5,4,3,2,1,0:T(8,128)(2,1)S(1)} collective-permute-done((bf16[2,2,2,8,8,128]{5,4,3,2,1,0:T(8,128)(2,1)S(1)}, bf16[2,2,2,8,8,128]{5,4,3,2,1,0:T(8,128)(2,1)S(1)}, u32[]{:S(2)}, u32[]{:S(2)}) %collective-permute-start.3) | collective-permute-done | bytes 131104 | tf_op jit(solution)/shard_map/ppermute | solution.py:271
  71.3 2.6 %collective-permute-start.4 = (bf16[2,2,2,8,8,128]{5,4,3,2,1,0:T(8,128)(2,1)S(1)}, bf16[2,2,2,8,8,128]{5,4,3,2,1,0:T(8,128)(2,1)S(1)}, u32[]{:S(2)}, u32[]{:S(2)}) collective-permute-start(bf16[2,2,2,8,8,128]{5,4,3,2,1,0:T(8,128)(2,1)S(1)} %collective-permute-done.refs_4_), channel_id=1, source_target_pairs={{0,1},{1,2},{2,3},{3,0},{4,5},{5,6},{6,7},{7,4},{8,9},{9,10},{10,1... | collective-permute-start | bytes 393224 | tf_op jit(solution)/shard_map/ppermute | solution.py:271
  73.9 4.1 %collective-permute-start.5 = (bf16[2,2,2,8,8,128]{5,4,3,2,1,0:T(8,128)(2,1)S(1)}, bf16[2,2,2,8,8,128]{5,4,3,2,1,0:T(8,128)(2,1)S(1)}, u32[]{:S(2)}, u32[]{:S(2)}) collective-permute-start(bf16[2,2,2,8,8,128]{5,4,3,2,1,0:T(8,128)(2,1)S(1)} %collective-permute-done.refs_4_), channel_id=1, source_target_pairs={{0,2},{1,3},{2,0},{3,1},{4,6},{5,7},{6,4},{7,5},{8,10},{9,11},{10,... | collective-permute-start | bytes 393224 | tf_op jit(solution)/shard_map/ppermute | solution.py:271
  78.0 1.9 %collective-permute-start.6 = (bf16[2,2,2,8,8,128]{5,4,3,2,1,0:T(8,128)(2,1)S(1)}, bf16[2,2,2,8,8,128]{5,4,3,2,1,0:T(8,128)(2,1)S(1)}, u32[]{:S(2)}, u32[]{:S(2)}) collective-permute-start(bf16[2,2,2,8,8,128]{5,4,3,2,1,0:T(8,128)(2,1)S(1)} %collective-permute-done.refs_4_), channel_id=1, source_target_pairs={{0,3},{1,0},{2,1},{3,2},{4,7},{5,4},{6,5},{7,6},{8,11},{9,8},{10,9... | collective-permute-start | bytes 393224 | tf_op jit(solution)/shard_map/ppermute | solution.py:271
  80.7 5.3 %collective-permute-done.5.refs_6_ = bf16[2,2,2,8,8,128]{5,4,3,2,1,0:T(8,128)(2,1)S(1)} collective-permute-done((bf16[2,2,2,8,8,128]{5,4,3,2,1,0:T(8,128)(2,1)S(1)}, bf16[2,2,2,8,8,128]{5,4,3,2,1,0:T(8,128)(2,1)S(1)}, u32[]{:S(2)}, u32[]{:S(2)}) %collective-permute-start.5) | collective-permute-done | bytes 131104 | tf_op jit(solution)/shard_map/ppermute | solution.py:271
  86.7 1.7 collective-permute-done.6.refs_7_
  91.8 12.0 %attention_backward.1 = (bf16[32,128,128]{2,1,0:T(8,128)(2,1)}, bf16[2,2,2,8,8,128]{5,4,3,2,1,0:T(8,128)(2,1)S(1)}, bf16[2,2,2,8,8,128]{5,4,3,2,1,0:T(8,128)(2,1...) custom-call(s32[16]{0:T(128)S(1)} %dynamic-slice_bitcast_fusion.recv, ...), custom_call_target="tpu_custom_call" | custom-call | flops 2000000000 | bytes 6291456 | tf_op jit(solution)/shard_map/attention_backward/pallas_call | solution.py:172
  103.9 1.9 %collective-permute-start.7 = (bf16[2,2,2,8,8,128]{5,4,3,2,1,0:T(8,128)(2,1)}, bf16[2,2,2,8,8,128]{5,4,3,2,1,0:T(8,128)(2,1)S(1)}, u32[]{:S(2)}, u32[]{:S(2)}) collective-permute-start(bf16[2,2,2,8,8,128]{5,4,3,2,1,0:T(8,128)(2,1)} %get-tuple-element.38), channel_id=1, source_target_pairs={{0,3},{1,0},{2,1},{3,2},{4,7},{5,4},{6,5},{7,6},{8,11},{9,8},{10,9... | collective-permute-start | bytes 393224 | tf_op jit(solution)/shard_map/ppermute | solution.py:271
  105.8 3.3 %collective-permute-start.8 = (bf16[2,2,2,8,8,128]{5,4,3,2,1,0:T(8,128)(2,1)}, bf16[2,2,2,8,8,128]{5,4,3,2,1,0:T(8,128)(2,1)S(1)}, u32[]{:S(2)}, u32[]{:S(2)}) collective-permute-start(bf16[2,2,2,8,8,128]{5,4,3,2,1,0:T(8,128)(2,1)} %get-tuple-element.39), channel_id=1, source_target_pairs={{0,2},{1,3},{2,0},{3,1},{4,6},{5,7},{6,4},{7,5},{8,10},{9,11},{10,... | collective-permute-start | bytes 393224 | tf_op jit(solution)/shard_map/ppermute | solution.py:271
  109.1 4.3 %collective-permute-start.9 = (bf16[2,2,2,8,8,128]{5,4,3,2,1,0:T(8,128)(2,1)S(1)}, bf16[2,2,2,8,8,128]{5,4,3,2,1,0:T(8,128)(2,1)S(1)}, u32[]{:S(2)}, u32[]{:S(2)}) collective-permute-start(bf16[2,2,2,8,8,128]{5,4,3,2,1,0:T(8,128)(2,1)S(1)} %get-tuple-element.40), channel_id=1, source_target_pairs={{0,1},{1,2},{2,3},{3,0},{4,5},{5,6},{6,7},{7,4},{8,9},{9,10},{10,1... | collective-permute-start | bytes 393224 | tf_op jit(solution)/shard_map/ppermute | solution.py:271
  113.4 9.4 %all-to-all-start.2 = ((bf16[16,2,128,128]{3,2,1,0:T(8,128)(2,1)}), bf16[16,2,128,128]{3,2,1,0:T(8,128)(2,1)S(1)}, u32[]{:S(2)}, u32[]{:S(2)}) async-start(bf16[16,2,128,128]{3,2,1,0:T(8,128)(2,1)} %bitcast.12), calls=%async_computation.2 | async-start | bytes 2097152 | tf_op jit(solution)/shard_map/all_to_all | solution.py:331
  122.9 5.3 %collective-permute-start.10 = (bf16[2,2,2,8,8,128]{5,4,3,2,1,0:T(8,128)(2,1)S(1)}, bf16[2,2,2,8,8,128]{5,4,3,2,1,0:T(8,128)(2,1)S(1)}, u32[]{:S(2)}, u32[]{:S(2)}) collective-permute-start(bf16[2,2,2,8,8,128]{5,4,3,2,1,0:T(8,128)(2,1)S(1)} %add_convert_fusion.1), channel_id=1, source_target_pairs={{0,4},{1,5},{2,6},{3,7},{4,0},{5,1},{6,2},{7,3},{8,12},{9,13},{10,... | collective-permute-start | bytes 393224 | tf_op jit(solution)/shard_map/ppermute | solution.py:266
  128.2 1.9 %collective-permute-start.11 = (bf16[2,2,2,8,8,128]{5,4,3,2,1,0:T(8,128)(2,1)S(1)}, bf16[2,2,2,8,8,128]{5,4,3,2,1,0:T(8,128)(2,1)S(1)}, u32[]{:S(2)}, u32[]{:S(2)}) collective-permute-start(bf16[2,2,2,8,8,128]{5,4,3,2,1,0:T(8,128)(2,1)S(1)} %get-tuple-element.46), channel_id=1, source_target_pairs={{0,3},{1,0},{2,1},{3,2},{4,7},{5,4},{6,5},{7,6},{8,11},{9,8},{10,9... | collective-permute-start | bytes 393224 | tf_op jit(solution)/shard_map/ppermute | solution.py:271
  130.1 2.8 %collective-permute-start.12 = (bf16[2,2,2,8,8,128]{5,4,3,2,1,0:T(8,128)(2,1)S(1)}, bf16[2,2,2,8,8,128]{5,4,3,2,1,0:T(8,128)(2,1)S(1)}, u32[]{:S(2)}, u32[]{:S(2)}) collective-permute-start(bf16[2,2,2,8,8,128]{5,4,3,2,1,0:T(8,128)(2,1)S(1)} %get-tuple-element.47), channel_id=1, source_target_pairs={{0,2},{1,3},{2,0},{3,1},{4,6},{5,7},{6,4},{7,5},{8,10},{9,11},{10,... | collective-permute-start | bytes 393224 | tf_op jit(solution)/shard_map/ppermute | solution.py:271
  132.9 4.0 %collective-permute-start.13 = (bf16[2,2,2,8,8,128]{5,4,3,2,1,0:T(8,128)(2,1)S(1)}, bf16[2,2,2,8,8,128]{5,4,3,2,1,0:T(8,128)(2,1)S(1)}, u32[]{:S(2)}, u32[]{:S(2)}) collective-permute-start(bf16[2,2,2,8,8,128]{5,4,3,2,1,0:T(8,128)(2,1)S(1)} %get-tuple-element.48), channel_id=1, source_target_pairs={{0,1},{1,2},{2,3},{3,0},{4,5},{5,6},{6,7},{7,4},{8,9},{9,10},{10,1... | collective-permute-start | bytes 393224 | tf_op jit(solution)/shard_map/ppermute | solution.py:271
  137.0 2.3 %collective-permute-done.10 = bf16[2,2,2,8,8,128]{5,4,3,2,1,0:T(8,128)(2,1)S(1)} collective-permute-done((bf16[2,2,2,8,8,128]{5,4,3,2,1,0:T(8,128)(2,1)S(1)}, bf16[2,2,2,8,8,128]{5,4,3,2,1,0:T(8,128)(2,1)S(1)}, u32[]{:S(2)}, u32[]{:S(2)}) %collective-permute-start.10) | collective-permute-done | bytes 131104 | tf_op jit(solution)/shard_map/ppermute | solution.py:266
  139.3 4.1 %collective-permute-done.12 = bf16[2,2,2,8,8,128]{5,4,3,2,1,0:T(8,128)(2,1)S(1)} collective-permute-done((bf16[2,2,2,8,8,128]{5,4,3,2,1,0:T(8,128)(2,1)S(1)}, bf16[2,2,2,8,8,128]{5,4,3,2,1,0:T(8,128)(2,1)S(1)}, u32[]{:S(2)}, u32[]{:S(2)}) %collective-permute-start.12) | collective-permute-done | bytes 131104 | tf_op jit(solution)/shard_map/ppermute | solution.py:271
  145.5 14.4 %all-to-all-start.3 = ((bf16[64,2,2,4,128]{4,3,2,1,0:T(4,128)(2,1)}), bf16[64,2,2,4,128]{4,3,2,1,0:T(4,128)(2,1)S(1)}, u32[]{:S(2)}, u32[]{:S(2)}) async-start(bf16[64,2,2,4,128]{4,3,2,1,0:T(4,128)(2,1)} %bitcast.16), calls=%async_computation.3 | async-start | bytes 524288 | tf_op jit(solution)/shard_map/all_to_all | solution.py:308
  160.2 1.4 gather_fusion
  161.6 16.4 %all-to-all-done.3 = bf16[64,2,2,4,128]{4,3,2,1,0:T(4,128)(2,1)S(1)} async-done(((bf16[64,2,2,4,128]{4,3,2,1,0:T(4,128)(2,1)}), bf16[64,2,2,4,128]{4,3,2,1,0:T(4,128)(2,1)S(1)}, u32[]{:S(2)}, u32[]{:S(2)}) %all-to-all-start.3) | async-done | bytes 262176 | tf_op jit(solution)/shard_map/all_to_all | solution.py:308
  (50 shorter events, 14.5 us)
Async XLA Ops:
  0.6 0.9 copy-start.2
  1.5 0.7 copy-start.3
  3.7 35.3 %all-to-all-start = ((bf16[64,2,2,4,128]{4,3,2,1,0:T(4,128)(2,1)}), bf16[64,2,2,4,128]{4,3,2,1,0:T(4,128)(2,1)S(1)}, u32[]{:S(2)}, u32[]{:S(2)}) async-start(bf16[64,2,2,4,128]{4,3,2,1,0:T(4,128)(2,1)} %bitcast.7), calls=%async_computation | async-start | bytes 524288 | tf_op jit(solution)/shard_map/all_to_all | solution.py:308
  20.8 1.0 copy-start
  21.8 1.0 copy-start.1
  22.9 0.7 copy-start.4
  39.0 4.2 %copy-start.12 = (s32[16,16]{1,0:T(8,128)S(1)}, s32[16,16]{1,0:T(8,128)}, u32[]{:S(2)}) copy-start(s32[16,16]{1,0:T(8,128)} %param.10) | copy-start | bytes 3076
  39.0 40.9 %copy-start.13 = (s32[1,16]{1,0:T(1,128)S(1)}, s32[1,16]{1,0:T(1,128)}, u32[]{:S(2)}) copy-start(s32[1,16]{1,0:T(1,128)} %param.11) | copy-start | bytes 196
  39.0 32.3 %all-to-all-start.1 = ((bf16[16,2,2,128,128]{4,3,2,1,0:T(8,128)(2,1)}), bf16[16,2,2,128,128]{4,3,2,1,0:T(8,128)(2,1)S(1)}, u32[]{:S(2)}, u32[]{:S(2)}) async-start(bf16[16,2,2,128,128]{4,3,2,1,0:T(8,128)(2,1)} %bitcast.10), calls=%async_computation.1 | async-start | bytes 4194304 | tf_op jit(solution)/shard_map/all_to_all | solution.py:319
  43.9 17.8 %collective-permute-start = (bf16[2,2,2,8,8,128]{5,4,3,2,1,0:T(8,128)(2,1)S(1)}, bf16[2,2,2,8,8,128]{5,4,3,2,1,0:T(8,128)(2,1)S(1)}, u32[]{:S(2)}, u32[]{:S(2)}) collective-permute-start(bf16[2,2,2,8,8,128]{5,4,3,2,1,0:T(8,128)(2,1)S(1)} %kv_unpack.1.refs_0_), channel_id=1, source_target_pairs={{0,4},{1,5},{2,6},{3,7},{4,0},{5,1},{6,2},{7,3},{8,12},{9,13},{10,... | collective-permute-start | bytes 393224 | tf_op jit(solution)/shard_map/ppermute | solution.py:266
  49.0 14.2 %collective-permute-start.1 = (bf16[2,2,2,8,8,128]{5,4,3,2,1,0:T(8,128)(2,1)S(1)}, bf16[2,2,2,8,8,128]{5,4,3,2,1,0:T(8,128)(2,1)S(1)}, u32[]{:S(2)}, u32[]{:S(2)}) collective-permute-start(bf16[2,2,2,8,8,128]{5,4,3,2,1,0:T(8,128)(2,1)S(1)} %kv_unpack.1.refs_0_), channel_id=1, source_target_pairs={{0,1},{1,2},{2,3},{3,0},{4,5},{5,6},{6,7},{7,4},{8,9},{9,10},{10,1... | collective-permute-start | bytes 393224 | tf_op jit(solution)/shard_map/ppermute | solution.py:271
  51.7 14.8 %collective-permute-start.2 = (bf16[2,2,2,8,8,128]{5,4,3,2,1,0:T(8,128)(2,1)S(1)}, bf16[2,2,2,8,8,128]{5,4,3,2,1,0:T(8,128)(2,1)S(1)}, u32[]{:S(2)}, u32[]{:S(2)}) collective-permute-start(bf16[2,2,2,8,8,128]{5,4,3,2,1,0:T(8,128)(2,1)S(1)} %kv_unpack.1.refs_0_), channel_id=1, source_target_pairs={{0,2},{1,3},{2,0},{3,1},{4,6},{5,7},{6,4},{7,5},{8,10},{9,11},{10,... | collective-permute-start | bytes 393224 | tf_op jit(solution)/shard_map/ppermute | solution.py:271
  55.6 14.9 %collective-permute-start.3 = (bf16[2,2,2,8,8,128]{5,4,3,2,1,0:T(8,128)(2,1)S(1)}, bf16[2,2,2,8,8,128]{5,4,3,2,1,0:T(8,128)(2,1)S(1)}, u32[]{:S(2)}, u32[]{:S(2)}) collective-permute-start(bf16[2,2,2,8,8,128]{5,4,3,2,1,0:T(8,128)(2,1)S(1)} %kv_unpack.1.refs_0_), channel_id=1, source_target_pairs={{0,3},{1,0},{2,1},{3,2},{4,7},{5,4},{6,5},{7,6},{8,11},{9,8},{10,9... | collective-permute-start | bytes 393224 | tf_op jit(solution)/shard_map/ppermute | solution.py:271
  71.3 8.8 %collective-permute-start.4 = (bf16[2,2,2,8,8,128]{5,4,3,2,1,0:T(8,128)(2,1)S(1)}, bf16[2,2,2,8,8,128]{5,4,3,2,1,0:T(8,128)(2,1)S(1)}, u32[]{:S(2)}, u32[]{:S(2)}) collective-permute-start(bf16[2,2,2,8,8,128]{5,4,3,2,1,0:T(8,128)(2,1)S(1)} %collective-permute-done.refs_4_), channel_id=1, source_target_pairs={{0,1},{1,2},{2,3},{3,0},{4,5},{5,6},{6,7},{7,4},{8,9},{9,10},{10,1... | collective-permute-start | bytes 393224 | tf_op jit(solution)/shard_map/ppermute | solution.py:271
  73.9 12.2 %collective-permute-start.5 = (bf16[2,2,2,8,8,128]{5,4,3,2,1,0:T(8,128)(2,1)S(1)}, bf16[2,2,2,8,8,128]{5,4,3,2,1,0:T(8,128)(2,1)S(1)}, u32[]{:S(2)}, u32[]{:S(2)}) collective-permute-start(bf16[2,2,2,8,8,128]{5,4,3,2,1,0:T(8,128)(2,1)S(1)} %collective-permute-done.refs_4_), channel_id=1, source_target_pairs={{0,2},{1,3},{2,0},{3,1},{4,6},{5,7},{6,4},{7,5},{8,10},{9,11},{10,... | collective-permute-start | bytes 393224 | tf_op jit(solution)/shard_map/ppermute | solution.py:271
  78.0 10.5 %collective-permute-start.6 = (bf16[2,2,2,8,8,128]{5,4,3,2,1,0:T(8,128)(2,1)S(1)}, bf16[2,2,2,8,8,128]{5,4,3,2,1,0:T(8,128)(2,1)S(1)}, u32[]{:S(2)}, u32[]{:S(2)}) collective-permute-start(bf16[2,2,2,8,8,128]{5,4,3,2,1,0:T(8,128)(2,1)S(1)} %collective-permute-done.refs_4_), channel_id=1, source_target_pairs={{0,3},{1,0},{2,1},{3,2},{4,7},{5,4},{6,5},{7,6},{8,11},{9,8},{10,9... | collective-permute-start | bytes 393224 | tf_op jit(solution)/shard_map/ppermute | solution.py:271
  80.1 0.7 copy-start.6
  86.1 0.7 copy-start.8
  88.4 0.7 copy-start.10
  89.1 0.9 copy-start.7
  90.0 0.9 copy-start.9
  90.9 0.9 copy-start.11
  103.9 18.9 %collective-permute-start.7 = (bf16[2,2,2,8,8,128]{5,4,3,2,1,0:T(8,128)(2,1)}, bf16[2,2,2,8,8,128]{5,4,3,2,1,0:T(8,128)(2,1)S(1)}, u32[]{:S(2)}, u32[]{:S(2)}) collective-permute-start(bf16[2,2,2,8,8,128]{5,4,3,2,1,0:T(8,128)(2,1)} %get-tuple-element.38), channel_id=1, source_target_pairs={{0,3},{1,0},{2,1},{3,2},{4,7},{5,4},{6,5},{7,6},{8,11},{9,8},{10,9... | collective-permute-start | bytes 393224 | tf_op jit(solution)/shard_map/ppermute | solution.py:271
  105.8 17.0 %collective-permute-start.8 = (bf16[2,2,2,8,8,128]{5,4,3,2,1,0:T(8,128)(2,1)}, bf16[2,2,2,8,8,128]{5,4,3,2,1,0:T(8,128)(2,1)S(1)}, u32[]{:S(2)}, u32[]{:S(2)}) collective-permute-start(bf16[2,2,2,8,8,128]{5,4,3,2,1,0:T(8,128)(2,1)} %get-tuple-element.39), channel_id=1, source_target_pairs={{0,2},{1,3},{2,0},{3,1},{4,6},{5,7},{6,4},{7,5},{8,10},{9,11},{10,... | collective-permute-start | bytes 393224 | tf_op jit(solution)/shard_map/ppermute | solution.py:271
  109.1 13.7 %collective-permute-start.9 = (bf16[2,2,2,8,8,128]{5,4,3,2,1,0:T(8,128)(2,1)S(1)}, bf16[2,2,2,8,8,128]{5,4,3,2,1,0:T(8,128)(2,1)S(1)}, u32[]{:S(2)}, u32[]{:S(2)}) collective-permute-start(bf16[2,2,2,8,8,128]{5,4,3,2,1,0:T(8,128)(2,1)S(1)} %get-tuple-element.40), channel_id=1, source_target_pairs={{0,1},{1,2},{2,3},{3,0},{4,5},{5,6},{6,7},{7,4},{8,9},{9,10},{10,1... | collective-permute-start | bytes 393224 | tf_op jit(solution)/shard_map/ppermute | solution.py:271
  113.3 46.8 %copy-start.5 = (s32[1,16,2]{1,2,0:T(2,128)S(1)}, s32[1,16,2]{1,2,0:T(2,128)}, u32[]{:S(2)}) copy-start(s32[1,16,2]{1,2,0:T(2,128)} %param.9) | copy-start | bytes 388
  113.4 30.8 %all-to-all-start.2 = ((bf16[16,2,128,128]{3,2,1,0:T(8,128)(2,1)}), bf16[16,2,128,128]{3,2,1,0:T(8,128)(2,1)S(1)}, u32[]{:S(2)}, u32[]{:S(2)}) async-start(bf16[16,2,128,128]{3,2,1,0:T(8,128)(2,1)} %bitcast.12), calls=%async_computation.2 | async-start | bytes 2097152 | tf_op jit(solution)/shard_map/all_to_all | solution.py:331
  122.9 16.4 %collective-permute-start.10 = (bf16[2,2,2,8,8,128]{5,4,3,2,1,0:T(8,128)(2,1)S(1)}, bf16[2,2,2,8,8,128]{5,4,3,2,1,0:T(8,128)(2,1)S(1)}, u32[]{:S(2)}, u32[]{:S(2)}) collective-permute-start(bf16[2,2,2,8,8,128]{5,4,3,2,1,0:T(8,128)(2,1)S(1)} %add_convert_fusion.1), channel_id=1, source_target_pairs={{0,4},{1,5},{2,6},{3,7},{4,0},{5,1},{6,2},{7,3},{8,12},{9,13},{10,... | collective-permute-start | bytes 393224 | tf_op jit(solution)/shard_map/ppermute | solution.py:266
  128.2 11.1 %collective-permute-start.11 = (bf16[2,2,2,8,8,128]{5,4,3,2,1,0:T(8,128)(2,1)S(1)}, bf16[2,2,2,8,8,128]{5,4,3,2,1,0:T(8,128)(2,1)S(1)}, u32[]{:S(2)}, u32[]{:S(2)}) collective-permute-start(bf16[2,2,2,8,8,128]{5,4,3,2,1,0:T(8,128)(2,1)S(1)} %get-tuple-element.46), channel_id=1, source_target_pairs={{0,3},{1,0},{2,1},{3,2},{4,7},{5,4},{6,5},{7,6},{8,11},{9,8},{10,9... | collective-permute-start | bytes 393224 | tf_op jit(solution)/shard_map/ppermute | solution.py:271
  130.1 13.3 %collective-permute-start.12 = (bf16[2,2,2,8,8,128]{5,4,3,2,1,0:T(8,128)(2,1)S(1)}, bf16[2,2,2,8,8,128]{5,4,3,2,1,0:T(8,128)(2,1)S(1)}, u32[]{:S(2)}, u32[]{:S(2)}) collective-permute-start(bf16[2,2,2,8,8,128]{5,4,3,2,1,0:T(8,128)(2,1)S(1)} %get-tuple-element.47), channel_id=1, source_target_pairs={{0,2},{1,3},{2,0},{3,1},{4,6},{5,7},{6,4},{7,5},{8,10},{9,11},{10,... | collective-permute-start | bytes 393224 | tf_op jit(solution)/shard_map/ppermute | solution.py:271
  132.9 11.1 %collective-permute-start.13 = (bf16[2,2,2,8,8,128]{5,4,3,2,1,0:T(8,128)(2,1)S(1)}, bf16[2,2,2,8,8,128]{5,4,3,2,1,0:T(8,128)(2,1)S(1)}, u32[]{:S(2)}, u32[]{:S(2)}) collective-permute-start(bf16[2,2,2,8,8,128]{5,4,3,2,1,0:T(8,128)(2,1)S(1)} %get-tuple-element.48), channel_id=1, source_target_pairs={{0,1},{1,2},{2,3},{3,0},{4,5},{5,6},{6,7},{7,4},{8,9},{9,10},{10,1... | collective-permute-start | bytes 393224 | tf_op jit(solution)/shard_map/ppermute | solution.py:271
  145.5 32.5 %all-to-all-start.3 = ((bf16[64,2,2,4,128]{4,3,2,1,0:T(4,128)(2,1)}), bf16[64,2,2,4,128]{4,3,2,1,0:T(4,128)(2,1)S(1)}, u32[]{:S(2)}, u32[]{:S(2)}) async-start(bf16[64,2,2,4,128]{4,3,2,1,0:T(4,128)(2,1)} %bitcast.16), calls=%async_computation.3 | async-start | bytes 524288 | tf_op jit(solution)/shard_map/all_to_all | solution.py:308

commit v10 on v8

--- a/solution.py
+++ b/solution.py
@@ -30,7 +30,7 @@
         out_ref[slot, 1] = g_ref[tile]
         return 0
 
-    lax.fori_loop(0, out_ref.shape[0], body, 0)
+    lax.fori_loop(0, out_ref.shape[0], body, 0, unroll=2)
 
 
 def pack(index, queries, grad_out):
@@ -53,7 +53,8 @@
     recv_ref, start_ref, place_ref, qg_ref, *refs
 ):
     kv_refs, dq_ref, dkv_refs = refs[: 2 * NEAR], refs[2 * NEAR], refs[2 * NEAR + 1 : 4 * NEAR + 1]
-    k_all, kt_all, v_all, dk_all, dv_all, scores, dprobs, dqt = refs[4 * NEAR + 1 :]
+    k_all, kt_all, v_all, dk_all, dv_all, *rest = refs[4 * NEAR + 1 :]
+    scores, dprobs, diagonal_scores, diagonal_dprobs, stats, dqt = rest
     blocks = k_all.shape[0]
     width = k_all.shape[1]
     tile_rows = width // PAIR
@@ -77,7 +78,7 @@
         kt_all[block] = k_all[block].astype(jnp.float32).T.astype(jnp.bfloat16)
         return 0
 
-    lax.fori_loop(0, blocks, stage, 0)
+    lax.fori_loop(0, blocks, stage, 0, unroll=2)
 
     row = lax.broadcasted_iota(jnp.int32, (width, 1), 0)
     holder = (place_ref[0] & 12) | ((place_ref[0] - (row >> 6)) & 3)
@@ -87,29 +88,54 @@
     )
     lane = lax.broadcasted_iota(jnp.int32, (1, width), 1)
 
-    def query_block(block, _):
+    def operands(block):
         first = recv_ref[PAIR * block]
         second = recv_ref[PAIR * block + 1]
         query = jnp.concatenate([qg_ref[first, 0], qg_ref[second, 0]], axis=0)
         grad = jnp.concatenate([qg_ref[first, 1], qg_ref[second, 1]], axis=0)
-        start_low = start_ref[PAIR * block]
-        start_high = start_ref[PAIR * block + 1]
-        lowest = start_low // PAIR
-        row_start = jnp.where(lane < tile_rows, start_low, start_high) * tile_rows
-
-        def products(other, masked_by_order, peak):
+        return query, grad
+
+    def first_row(block):
+        low, high = start_ref[PAIR * block], start_ref[PAIR * block + 1]
+        return jnp.where(lane < tile_rows, low, high) * tile_rows
+
+    def terms(weights, dprob, key_t, query, grad, inverse, delta):
+        probs = weights * inverse
+        dscores = (probs * (dprob - delta)).astype(jnp.bfloat16)
+        grad_value = matmul(probs.astype(jnp.bfloat16), grad, ((1,), (0,)))
+        grad_key = matmul(dscores, query, ((1,), (0,)))
+        grad_query = matmul(key_t, dscores, ((1,), (0,)))
+        return grad_key, grad_value, grad_query
+
+    def diagonal_products(block, _):
+        query, grad = operands(block)
+        score = matmul(k_all[block], query, ((1,), (1,)))
+        allowed = (key_offset >= first_row(block) - block * width) & (key_offset <= lane)
+        score = jnp.where(allowed, score, -jnp.inf)
+        diagonal_scores[block] = score
+        diagonal_dprobs[block] = matmul(v_all[block], grad, ((1,), (1,)))
+        peak = jnp.max(score, axis=0, keepdims=True)
+        stats[block, 0] = jnp.broadcast_to(peak, stats.shape[2:])
+        dk_all[block] = jnp.zeros_like(dk_all[block])
+        dv_all[block] = jnp.zeros_like(dv_all[block])
+        dqt[block] = jnp.zeros_like(dqt[block])
+        return 0
+
+    lax.fori_loop(0, blocks, diagonal_products, 0, unroll=2)
+
+    def query_block(block, _):
+        query, grad = operands(block)
+        row_start = first_row(block)
+        lowest = start_ref[PAIR * block] // PAIR
+
+        def products(other, peak):
             score = matmul(k_all[other], query, ((1,), (1,)))
-            key_pos = key_offset + other * width
-            allowed = key_pos >= row_start
-            if masked_by_order:
-                allowed = allowed & (key_offset <= lane)
-            score = jnp.where(allowed, score, -jnp.inf)
+            score = jnp.where(key_offset >= row_start - other * width, score, -jnp.inf)
             scores[other] = score
             dprobs[other] = matmul(v_all[other], grad, ((1,), (1,)))
             return jnp.maximum(peak, jnp.max(score, axis=0, keepdims=True))
 
-        peak = products(block, True, jnp.full((1, width), -jnp.inf, jnp.float32))
-        peak = lax.fori_loop(lowest, block, lambda other, m: products(other, False, m), peak)
+        peak = lax.fori_loop(lowest, block, products, stats[block, 0][:1])
         shift = peak * factor
 
         def sums(other, totals):
@@ -120,38 +146,46 @@
                 totals[1] + jnp.sum(weights * dprobs[other], axis=0, keepdims=True),
             )
 
-        zeros = jnp.zeros((1, width), jnp.float32)
-        total, weighted = lax.fori_loop(lowest, block + 1, sums, (zeros, zeros))
+        weights = jnp.exp2(diagonal_scores[block] * factor - shift)
+        diagonal_scores[block] = weights
+        totals = (
+            jnp.sum(weights, axis=0, keepdims=True),
+            jnp.sum(weights * diagonal_dprobs[block], axis=0, keepdims=True),
+        )
+        total, weighted = lax.fori_loop(lowest, block, sums, totals)
         inverse = 1.0 / total
         delta = weighted * inverse
-
-        def terms(other):
-            probs = scores[other] * inverse
-            dscores = (probs * (dprobs[other] - delta)).astype(jnp.bfloat16)
-            grad_value = matmul(probs.astype(jnp.bfloat16), grad, ((1,), (0,)))
-            grad_key = matmul(dscores, query, ((1,), (0,)))
-            grad_query = matmul(kt_all[other], dscores, ((1,), (0,)))
-            return grad_key, grad_value, grad_query
-
-        grad_key, grad_value, grad_query = terms(block)
-        dk_all[block] = grad_key
-        dv_all[block] = grad_value
-        dqt[...] = grad_query
+        stats[block, 0] = jnp.broadcast_to(inverse, stats.shape[2:])
+        stats[block, 1] = jnp.broadcast_to(delta, stats.shape[2:])
 
         def earlier(other, _):
-            grad_key, grad_value, grad_query = terms(other)
+            grad_key, grad_value, grad_query = terms(
+                scores[other], dprobs[other], kt_all[other], query, grad, inverse, delta
+            )
             dk_all[other] += grad_key
             dv_all[other] += grad_value
-            dqt[...] += grad_query
+            dqt[block] += grad_query
             return 0
 
         lax.fori_loop(lowest, block, earlier, 0)
-        result = (dqt[...] * SCALING).T.astype(jnp.bfloat16)
-        dq_ref[first] = result[:tile_rows]
-        dq_ref[second] = result[tile_rows:]
         return 0
 
     lax.fori_loop(0, blocks, query_block, 0)
+
+    def diagonal_terms(block, _):
+        query, grad = operands(block)
+        grad_key, grad_value, grad_query = terms(
+            diagonal_scores[block], diagonal_dprobs[block], kt_all[block], query, grad,
+            stats[block, 0][:1], stats[block, 1][:1],
+        )
+        dk_all[block] += grad_key
+        dv_all[block] += grad_value
+        result = ((dqt[block] + grad_query) * SCALING).T.astype(jnp.bfloat16)
+        dq_ref[recv_ref[PAIR * block]] = result[:tile_rows]
+        dq_ref[recv_ref[PAIR * block + 1]] = result[tile_rows:]
+        return 0
+
+    lax.fori_loop(0, blocks, diagonal_terms, 0, unroll=2)
 
     def unstage(block, _):
         for slot, ref in enumerate(dkv_refs):
@@ -161,7 +195,7 @@
             ref[:, :, 1, block] = dv_all[block, rows].reshape(shape).astype(jnp.bfloat16)
         return 0
 
-    lax.fori_loop(0, blocks, unstage, 0)
+    lax.fori_loop(0, blocks, unstage, 0, unroll=2)
 
 
 def attention(my_recv, start, place, qg, chunks):
@@ -184,7 +218,10 @@
             pltpu.VMEM((blocks, width, HD), jnp.float32),
             pltpu.VMEM((blocks, width, width), jnp.float32),
             pltpu.VMEM((blocks, width, width), jnp.float32),
-            pltpu.VMEM((HD, width), jnp.float32),
+            pltpu.VMEM((blocks, width, width), jnp.float32),
+            pltpu.VMEM((blocks, width, width), jnp.float32),
+            pltpu.VMEM((blocks, 2, 8, width), jnp.float32),
+            pltpu.VMEM((blocks, HD, width), jnp.float32),
         ],
         compiler_params=pltpu.CompilerParams(vmem_limit_bytes=24 * 2**20),
         cost_estimate=pl.CostEstimate(
@@ -221,7 +258,7 @@
                     ref[half, kind, pair] = jnp.concatenate(rows, axis=0).astype(jnp.bfloat16)
         return 0
 
-    lax.fori_loop(0, recv_ref.shape[0] // PAIR, body, 0)
+    lax.fori_loop(0, recv_ref.shape[0] // PAIR, body, 0, unroll=4)
 
 
 def kv_back_kernel(recv_ref, place_ref, own_ref, other_ref, out_ref):
@@ -239,7 +276,7 @@
                         out_ref[slot >> 1, half, slot & 1, kind, which] = rows.astype(jnp.bfloat16)
         return 0
 
-    lax.fori_loop(0, recv_ref.shape[0] // PAIR, body, 0)
+    lax.fori_loop(0, recv_ref.shape[0] // PAIR, body, 0, unroll=4)
 
 
 def kv_final_kernel(anchor_ref, kv_ref, out_ref):
@@ -252,7 +289,7 @@
                     out_ref[tile, kind * 4 + half * 2 + head] = piece[half, kind, head]
         return 0
 
-    lax.fori_loop(0, anchor_ref.shape[0], body, 0)
+    lax.fori_loop(0, anchor_ref.shape[0], body, 0, unroll=4)
 
 
 def local_call(kernel, name, scalars, arrays, out_shape):

time: 171 us -> 169 us (0.988)
  Pallas kernels: 21.8 us -> 16.8 us
    pallas_call x1, Pallas kernels: 14.7 us -> 10 us  [attention(): pl.pallas_call(attention_kernel, out_shape=(jax.ShapeDtypeStruct((slots,...]
    all_to_all x1, starting transfers between devices: 5.93 us -> 8.89 us  [on_device(): lax.all_to_all(query_back.reshape(n_replicas, slot_cap, tile_rows, row_wi...]
where the time goes in v10:
time: 169 us; the launch traced here: 168 us
  starting transfers between devices  95.8 us (57%)
  waiting for transfers between devices  46.6 us (28%)
  Pallas kernels  16.8 us (10%)
  local copies, waits for them, and re-layouts  7.24 us (4%)
    ppermute x12, starting transfers between devices, near_shift(): return lax.ppermute(values, 'z', pairs)  40.3 us
    ppermute x5, starting transfers between devices, far_swap(): lax.ppermute(values, 'z', [(place, place ^ flip) for place in range(16)])  26.3 us
    ppermute x12, waiting for transfers between devices, near_shift(): return lax.ppermute(values, 'z', pairs)  20.8 us
    all_to_all x2, starting transfers between devices, over_plane(): lax.all_to_all(values.reshape((2 * n_replicas,) + values.shape[2:]), PLAN...  16.3 us
    ppermute x5, waiting for transfers between devices, far_swap(): lax.ppermute(values, 'z', [(place, place ^ flip) for place in range(16)])  14.4 us
    all_to_all x2, waiting for transfers between devices, over_plane(): lax.all_to_all(values.reshape((2 * n_replicas,) + values.shape[2:]), PLAN...  11.4 us
    pallas_call x1, Pallas kernels, attention(): pl.pallas_call(attention_kernel, out_shape=(jax.ShapeDtypeStruct((slots,...  10 us
    all_to_all x1, starting transfers between devices, on_device(): lax.all_to_all(query_back.reshape(n_replicas, slot_cap, tile_rows, row_wi...  8.89 us
  transfers between devices with their start and end apart: 21, of which 9 were waited for; matrix products, arithmetic and copies ran while one was open for 1% of the time, Pallas kernels for 2%

profile of v10, /device:TPU:1, one launch (start us, length us, event | category | flops | bytes accessed | tf_op | source)
XLA Modules:
  0.0 168.2 jit_solution(3689875117376836485)
XLA Ops:
  2.2 1.4 kv_pack.1
  3.7 10.4 %all-to-all-start = ((bf16[32,2,2,2,4,128]{5,4,3,2,1,0:T(4,128)(2,1)}), bf16[32,2,2,2,4,128]{5,4,3,2,1,0:T(4,128)(2,1)S(1)}, u32[]{:S(2)}, u32[]{:S(2)}) async-start(bf16[32,2,2,2,4,128]{5,4,3,2,1,0:T(4,128)(2,1)} %bitcast.7), calls=%async_computation | async-start | bytes 524288 | tf_op jit(solution)/shard_map/all_to_all | solution.py:347
  16.8 2.1 %pack_rows.1 = bf16[32,2,128,128]{3,2,1,0:T(8,128)(2,1)} custom-call(s32[2,16]{1,0:T(2,128)S(1)} %bitcast.38, bf16[16,128,128]{2,1,0:T(8,128)(2,1)S(1)} %copy-done, bf16[16,128,128]{2,1,0:T(8,128)(2,1)S(1)} %copy-done.1), custom_call_target="tpu_custom_call" | custom-call | tf_op jit(solution)/shard_map/pack_rows/pallas_call | solution.py:38
  19.0 4.0 %all-to-all-done = bf16[32,2,2,2,4,128]{5,4,3,2,1,0:T(4,128)(2,1)S(1)} async-done(((bf16[32,2,2,2,4,128]{5,4,3,2,1,0:T(4,128)(2,1)}), bf16[32,2,2,2,4,128]{5,4,3,2,1,0:T(4,128)(2,1)S(1)}, u32[]{:S(2)}, u32[]{:S(2)}) %all-to-all-start) | async-done | bytes 262176 | tf_op jit(solution)/shard_map/all_to_all | solution.py:347
  23.0 4.1 %all-to-all-start.1 = ((bf16[16,2,2,128,128]{4,3,2,1,0:T(8,128)(2,1)}), bf16[16,2,2,128,128]{4,3,2,1,0:T(8,128)(2,1)S(1)}, u32[]{:S(2)}, u32[]{:S(2)}) async-start(bf16[16,2,2,128,128]{4,3,2,1,0:T(8,128)(2,1)} %bitcast.14), calls=%async_computation.1 | async-start | bytes 4194304 | tf_op jit(solution)/shard_map/all_to_all | solution.py:360
  27.7 6.9 %collective-permute-start.1 = (bf16[2,2,8,8,128]{4,3,2,1,0:T(8,128)(2,1)S(1)}, bf16[2,2,8,8,128]{4,3,2,1,0:T(8,128)(2,1)S(1)}, u32[]{:S(2)}, u32[]{:S(2)}) collective-permute-start(bf16[2,2,8,8,128]{4,3,2,1,0:T(8,128)(2,1)S(1)} %get-tuple-element.31), channel_id=1, source_target_pairs={{0,4},{1,5},{2,6},{3,7},{4,0},{5,1},{6,2},{7,3},{8,12},{9,13},{10,... | collective-permute-start | bytes 196616 | tf_op jit(solution)/shard_map/ppermute | solution.py:309
  34.6 9.3 %collective-permute-start.2 = (bf16[2,2,8,8,128]{4,3,2,1,0:T(8,128)(2,1)S(1)}, bf16[2,2,8,8,128]{4,3,2,1,0:T(8,128)(2,1)S(1)}, u32[]{:S(2)}, u32[]{:S(2)}) collective-permute-start(bf16[2,2,8,8,128]{4,3,2,1,0:T(8,128)(2,1)S(1)} %get-tuple-element.30), channel_id=1, source_target_pairs={{0,11},{1,10},{2,9},{3,8},{4,15},{5,14},{6,13},{7,12},{8,3},{9,2},... | collective-permute-start | bytes 196616 | tf_op jit(solution)/shard_map/ppermute | solution.py:309
  43.9 1.9 %collective-permute-start = (bf16[2,2,8,8,128]{4,3,2,1,0:T(8,128)(2,1)S(1)}, bf16[2,2,8,8,128]{4,3,2,1,0:T(8,128)(2,1)S(1)}, u32[]{:S(2)}, u32[]{:S(2)}) collective-permute-start(bf16[2,2,8,8,128]{4,3,2,1,0:T(8,128)(2,1)S(1)} %get-tuple-element.30), channel_id=1, source_target_pairs={{0,15},{1,14},{2,13},{3,12},{4,11},{5,10},{6,9},{7,8},{8,7},{9,6},... | collective-permute-start | bytes 196616 | tf_op jit(solution)/shard_map/ppermute | solution.py:309
  45.9 3.5 %collective-permute-start.3 = (bf16[1,2,2,8,8,128]{5,4,3,2,1,0:T(8,128)(2,1)S(1)}, bf16[1,2,2,8,8,128]{5,4,3,2,1,0:T(8,128)(2,1)S(1)}, u32[]{:S(2)}, u32[]{:S(2)}) collective-permute-start(bf16[1,2,2,8,8,128]{5,4,3,2,1,0:T(8,128)(2,1)S(1)} %bitcast.40), channel_id=1, source_target_pairs={{0,1},{1,2},{2,3},{3,0},{4,5},{5,6},{6,7},{7,4},{8,9},{9,10},{10,1... | collective-permute-start | bytes 196616 | tf_op jit(solution)/shard_map/ppermute | solution.py:314
  49.4 3.1 %collective-permute-start.4 = (bf16[1,2,2,8,8,128]{5,4,3,2,1,0:T(8,128)(2,1)S(1)}, bf16[1,2,2,8,8,128]{5,4,3,2,1,0:T(8,128)(2,1)S(1)}, u32[]{:S(2)}, u32[]{:S(2)}) collective-permute-start(bf16[1,2,2,8,8,128]{5,4,3,2,1,0:T(8,128)(2,1)S(1)} %bitcast.41), channel_id=1, source_target_pairs={{0,2},{1,3},{2,0},{3,1},{4,6},{5,7},{6,4},{7,5},{8,10},{9,11},{10,... | collective-permute-start | bytes 196616 | tf_op jit(solution)/shard_map/ppermute | solution.py:314
  52.5 3.6 %collective-permute-start.5 = (bf16[1,2,2,8,8,128]{5,4,3,2,1,0:T(8,128)(2,1)S(1)}, bf16[1,2,2,8,8,128]{5,4,3,2,1,0:T(8,128)(2,1)S(1)}, u32[]{:S(2)}, u32[]{:S(2)}) collective-permute-start(bf16[1,2,2,8,8,128]{5,4,3,2,1,0:T(8,128)(2,1)S(1)} %bitcast.42), channel_id=1, source_target_pairs={{0,3},{1,0},{2,1},{3,2},{4,7},{5,4},{6,5},{7,6},{8,11},{9,8},{10,9... | collective-permute-start | bytes 196616 | tf_op jit(solution)/shard_map/ppermute | solution.py:314
  56.1 2.5 %collective-permute-done.4.refs_2_ = bf16[1,2,2,8,8,128]{5,4,3,2,1,0:T(8,128)(2,1)S(1)} collective-permute-done((bf16[1,2,2,8,8,128]{5,4,3,2,1,0:T(8,128)(2,1)S(1)}, bf16[1,2,2,8,8,128]{5,4,3,2,1,0:T(8,128)(2,1)S(1)}, u32[]{:S(2)}, u32[]{:S(2)}) %collective-permute-start.4) | collective-permute-done | bytes 65568 | tf_op jit(solution)/shard_map/ppermute | solution.py:314
  59.7 2.6 %collective-permute-start.6 = (bf16[3,2,2,8,8,128]{5,4,3,2,1,0:T(8,128)(2,1)S(1)}, bf16[3,2,2,8,8,128]{5,4,3,2,1,0:T(8,128)(2,1)S(1)}, u32[]{:S(2)}, u32[]{:S(2)}) collective-permute-start(bf16[3,2,2,8,8,128]{5,4,3,2,1,0:T(8,128)(2,1)S(1)} %pad_maximum_fusion.refs_4_), channel_id=1, source_target_pairs={{0,1},{1,2},{2,3},{3,0},{4,5},{5,6},{6,7},{7,4},{8,9},{9,10},{10,1... | collective-permute-start | bytes 589832 | tf_op jit(solution)/shard_map/ppermute | solution.py:314
  62.3 5.9 %collective-permute-start.7 = (bf16[3,2,2,8,8,128]{5,4,3,2,1,0:T(8,128)(2,1)S(1)}, bf16[3,2,2,8,8,128]{5,4,3,2,1,0:T(8,128)(2,1)S(1)}, u32[]{:S(2)}, u32[]{:S(2)}) collective-permute-start(bf16[3,2,2,8,8,128]{5,4,3,2,1,0:T(8,128)(2,1)S(1)} %pad_maximum_fusion.refs_4_), channel_id=1, source_target_pairs={{0,2},{1,3},{2,0},{3,1},{4,6},{5,7},{6,4},{7,5},{8,10},{9,11},{10,... | collective-permute-start | bytes 589832 | tf_op jit(solution)/shard_map/ppermute | solution.py:314
  68.1 1.9 %collective-permute-start.8 = (bf16[3,2,2,8,8,128]{5,4,3,2,1,0:T(8,128)(2,1)S(1)}, bf16[3,2,2,8,8,128]{5,4,3,2,1,0:T(8,128)(2,1)S(1)}, u32[]{:S(2)}, u32[]{:S(2)}) collective-permute-start(bf16[3,2,2,8,8,128]{5,4,3,2,1,0:T(8,128)(2,1)S(1)} %pad_maximum_fusion.refs_4_), channel_id=1, source_target_pairs={{0,3},{1,0},{2,1},{3,2},{4,7},{5,4},{6,5},{7,6},{8,11},{9,8},{10,9... | collective-permute-start | bytes 589832 | tf_op jit(solution)/shard_map/ppermute | solution.py:314
  70.7 9.0 %collective-permute-done.7.refs_6_ = bf16[3,2,2,8,8,128]{5,4,3,2,1,0:T(8,128)(2,1)S(1)} collective-permute-done((bf16[3,2,2,8,8,128]{5,4,3,2,1,0:T(8,128)(2,1)S(1)}, bf16[3,2,2,8,8,128]{5,4,3,2,1,0:T(8,128)(2,1)S(1)}, u32[]{:S(2)}, u32[]{:S(2)}) %collective-permute-start.7) | collective-permute-done | bytes 196640 | tf_op jit(solution)/shard_map/ppermute | solution.py:314
  80.6 10.0 %attention_backward.1 = (bf16[32,128,128]{2,1,0:T(8,128)(2,1)}, bf16[2,2,2,8,8,128]{5,4,3,2,1,0:T(8,128)(2,1)S(1)}, bf16[2,2,2,8,8,128]{5,4,3,2,1,0:T(8,128)(2,1...) custom-call(s32[16]{0:T(128)S(1)} %dynamic-slice_bitcast_fusion.recv, ...), custom_call_target="tpu_custom_call" | custom-call | flops 2000000000 | bytes 6291456 | tf_op jit(solution)/shard_map/attention_backward/pallas_call | solution.py:207
  90.6 5.4 %collective-permute-start.10 = (bf16[2,2,2,8,8,128]{5,4,3,2,1,0:T(8,128)(2,1)S(1)}, bf16[2,2,2,8,8,128]{5,4,3,2,1,0:T(8,128)(2,1)S(1)}, u32[]{:S(2)}, u32[]{:S(2)}) collective-permute-start(bf16[2,2,2,8,8,128]{5,4,3,2,1,0:T(8,128)(2,1)S(1)} %get-tuple-element.44), channel_id=1, source_target_pairs={{0,2},{1,3},{2,0},{3,1},{4,6},{5,7},{6,4},{7,5},{8,10},{9,11},{10,... | collective-permute-start | bytes 393224 | tf_op jit(solution)/shard_map/ppermute | solution.py:314
  96.0 2.9 %collective-permute-start.11 = (bf16[2,2,2,8,8,128]{5,4,3,2,1,0:T(8,128)(2,1)S(1)}, bf16[2,2,2,8,8,128]{5,4,3,2,1,0:T(8,128)(2,1)S(1)}, u32[]{:S(2)}, u32[]{:S(2)}) collective-permute-start(bf16[2,2,2,8,8,128]{5,4,3,2,1,0:T(8,128)(2,1)S(1)} %get-tuple-element.45), channel_id=1, source_target_pairs={{0,1},{1,2},{2,3},{3,0},{4,5},{5,6},{6,7},{7,4},{8,9},{9,10},{10,1... | collective-permute-start | bytes 393224 | tf_op jit(solution)/shard_map/ppermute | solution.py:314
  99.0 4.1 %collective-permute-start.9 = (bf16[2,2,2,8,8,128]{5,4,3,2,1,0:T(8,128)(2,1)S(1)}, bf16[2,2,2,8,8,128]{5,4,3,2,1,0:T(8,128)(2,1)S(1)}, u32[]{:S(2)}, u32[]{:S(2)}) collective-permute-start(bf16[2,2,2,8,8,128]{5,4,3,2,1,0:T(8,128)(2,1)S(1)} %get-tuple-element.43), channel_id=1, source_target_pairs={{0,3},{1,0},{2,1},{3,2},{4,7},{5,4},{6,5},{7,6},{8,11},{9,8},{10,9... | collective-permute-start | bytes 393224 | tf_op jit(solution)/shard_map/ppermute | solution.py:314
  103.1 8.9 %all-to-all-start.2 = ((bf16[16,2,128,128]{3,2,1,0:T(8,128)(2,1)}), bf16[16,2,128,128]{3,2,1,0:T(8,128)(2,1)S(1)}, u32[]{:S(2)}, u32[]{:S(2)}) async-start(bf16[16,2,128,128]{3,2,1,0:T(8,128)(2,1)} %bitcast.18), calls=%async_computation.2 | async-start | bytes 2097152 | tf_op jit(solution)/shard_map/all_to_all | solution.py:374
  112.1 6.2 %collective-permute-start.12 = (bf16[2,2,2,8,8,128]{5,4,3,2,1,0:T(8,128)(2,1)S(1)}, bf16[2,2,2,8,8,128]{5,4,3,2,1,0:T(8,128)(2,1)S(1)}, u32[]{:S(2)}, u32[]{:S(2)}) collective-permute-start(bf16[2,2,2,8,8,128]{5,4,3,2,1,0:T(8,128)(2,1)S(1)} %add_convert_fusion.1), channel_id=1, source_target_pairs={{0,4},{1,5},{2,6},{3,7},{4,0},{5,1},{6,2},{7,3},{8,12},{9,13},{10,... | collective-permute-start | bytes 393224 | tf_op jit(solution)/shard_map/ppermute | solution.py:309
  118.5 3.2 %collective-permute-start.13 = (bf16[2,2,2,8,8,128]{5,4,3,2,1,0:T(8,128)(2,1)S(1)}, bf16[2,2,2,8,8,128]{5,4,3,2,1,0:T(8,128)(2,1)S(1)}, u32[]{:S(2)}, u32[]{:S(2)}) collective-permute-start(bf16[2,2,2,8,8,128]{5,4,3,2,1,0:T(8,128)(2,1)S(1)} %get-tuple-element.51), channel_id=1, source_target_pairs={{0,3},{1,0},{2,1},{3,2},{4,7},{5,4},{6,5},{7,6},{8,11},{9,8},{10,9... | collective-permute-start | bytes 393224 | tf_op jit(solution)/shard_map/ppermute | solution.py:314
  121.7 1.9 %collective-permute-start.14 = (bf16[2,2,2,8,8,128]{5,4,3,2,1,0:T(8,128)(2,1)S(1)}, bf16[2,2,2,8,8,128]{5,4,3,2,1,0:T(8,128)(2,1)S(1)}, u32[]{:S(2)}, u32[]{:S(2)}) collective-permute-start(bf16[2,2,2,8,8,128]{5,4,3,2,1,0:T(8,128)(2,1)S(1)} %get-tuple-element.52), channel_id=1, source_target_pairs={{0,2},{1,3},{2,0},{3,1},{4,6},{5,7},{6,4},{7,5},{8,10},{9,11},{10,... | collective-permute-start | bytes 393224 | tf_op jit(solution)/shard_map/ppermute | solution.py:314
  123.7 2.2 %collective-permute-start.15 = (bf16[2,2,2,8,8,128]{5,4,3,2,1,0:T(8,128)(2,1)S(1)}, bf16[2,2,2,8,8,128]{5,4,3,2,1,0:T(8,128)(2,1)S(1)}, u32[]{:S(2)}, u32[]{:S(2)}) collective-permute-start(bf16[2,2,2,8,8,128]{5,4,3,2,1,0:T(8,128)(2,1)S(1)} %get-tuple-element.53), channel_id=1, source_target_pairs={{0,1},{1,2},{2,3},{3,0},{4,5},{5,6},{6,7},{7,4},{8,9},{9,10},{10,1... | collective-permute-start | bytes 393224 | tf_op jit(solution)/shard_map/ppermute | solution.py:314
  125.8 5.2 %collective-permute-done.12 = bf16[2,2,2,8,8,128]{5,4,3,2,1,0:T(8,128)(2,1)S(1)} collective-permute-done((bf16[2,2,2,8,8,128]{5,4,3,2,1,0:T(8,128)(2,1)S(1)}, bf16[2,2,2,8,8,128]{5,4,3,2,1,0:T(8,128)(2,1)S(1)}, u32[]{:S(2)}, u32[]{:S(2)}) %collective-permute-start.12) | collective-permute-done | bytes 131104 | tf_op jit(solution)/shard_map/ppermute | solution.py:309
  131.1 8.4 %collective-permute-done.14 = bf16[2,2,2,8,8,128]{5,4,3,2,1,0:T(8,128)(2,1)S(1)} collective-permute-done((bf16[2,2,2,8,8,128]{5,4,3,2,1,0:T(8,128)(2,1)S(1)}, bf16[2,2,2,8,8,128]{5,4,3,2,1,0:T(8,128)(2,1)S(1)}, u32[]{:S(2)}, u32[]{:S(2)}) %collective-permute-start.14) | collective-permute-done | bytes 131104 | tf_op jit(solution)/shard_map/ppermute | solution.py:314
  139.5 1.9 %collective-permute-start.16 = (bf16[2,2,8,8,128]{4,3,2,1,0:T(8,128)(2,1)S(1)}, bf16[2,2,8,8,128]{4,3,2,1,0:T(8,128)(2,1)S(1)}, u32[]{:S(2)}, u32[]{:S(2)}) collective-permute-start(bf16[2,2,8,8,128]{4,3,2,1,0:T(8,128)(2,1)S(1)} %get-tuple-element.58), channel_id=1, source_target_pairs={{0,15},{1,14},{2,13},{3,12},{4,11},{5,10},{6,9},{7,8},{8,7},{9,6},... | collective-permute-start | bytes 196616 | tf_op jit(solution)/shard_map/ppermute | solution.py:309
  141.6 9.3 %collective-permute-done.16.other_ref = bf16[2,2,8,8,128]{4,3,2,1,0:T(8,128)(2,1)S(1)} collective-permute-done((bf16[2,2,8,8,128]{4,3,2,1,0:T(8,128)(2,1)S(1)}, bf16[2,2,8,8,128]{4,3,2,1,0:T(8,128)(2,1)S(1)}, u32[]{:S(2)}, u32[]{:S(2)}) %collective-permute-start.16) | collective-permute-done | bytes 65568 | tf_op jit(solution)/shard_map/ppermute | solution.py:309
  152.2 5.9 %all-to-all-start.3 = ((bf16[32,2,2,2,4,128]{5,4,3,2,1,0:T(4,128)(2,1)}), bf16[32,2,2,2,4,128]{5,4,3,2,1,0:T(4,128)(2,1)S(1)}, u32[]{:S(2)}, u32[]{:S(2)}) async-start(bf16[32,2,2,2,4,128]{5,4,3,2,1,0:T(4,128)(2,1)} %bitcast.22), calls=%async_computation.3 | async-start | bytes 524288 | tf_op jit(solution)/shard_map/all_to_all | solution.py:347
  158.1 1.4 gather_fusion
  159.5 7.4 %all-to-all-done.3 = bf16[32,2,2,2,4,128]{5,4,3,2,1,0:T(4,128)(2,1)S(1)} async-done(((bf16[32,2,2,2,4,128]{5,4,3,2,1,0:T(4,128)(2,1)}), bf16[32,2,2,2,4,128]{5,4,3,2,1,0:T(4,128)(2,1)S(1)}, u32[]{:S(2)}, u32[]{:S(2)}) %all-to-all-start.3) | async-done | bytes 262176 | tf_op jit(solution)/shard_map/all_to_all | solution.py:347
  (50 shorter events, 10.6 us)
Async XLA Ops:
  0.6 0.9 copy-start.2
  1.5 0.7 copy-start.3
  3.7 19.3 %all-to-all-start = ((bf16[32,2,2,2,4,128]{5,4,3,2,1,0:T(4,128)(2,1)}), bf16[32,2,2,2,4,128]{5,4,3,2,1,0:T(4,128)(2,1)S(1)}, u32[]{:S(2)}, u32[]{:S(2)}) async-start(bf16[32,2,2,2,4,128]{5,4,3,2,1,0:T(4,128)(2,1)} %bitcast.7), calls=%async_computation | async-start | bytes 524288 | tf_op jit(solution)/shard_map/all_to_all | solution.py:347
  14.1 1.0 copy-start
  15.1 1.0 copy-start.1
  16.2 0.7 copy-start.4
  23.0 4.1 %copy-start.8 = (s32[16,16]{1,0:T(8,128)S(1)}, s32[16,16]{1,0:T(8,128)}, u32[]{:S(2)}) copy-start(s32[16,16]{1,0:T(8,128)} %param.10) | copy-start | bytes 3076
  23.0 47.1 %copy-start.9 = (s32[1,16]{1,0:T(1,128)S(1)}, s32[1,16]{1,0:T(1,128)}, u32[]{:S(2)}) copy-start(s32[1,16]{1,0:T(1,128)} %param.11) | copy-start | bytes 196
  23.0 36.7 %all-to-all-start.1 = ((bf16[16,2,2,128,128]{4,3,2,1,0:T(8,128)(2,1)}), bf16[16,2,2,128,128]{4,3,2,1,0:T(8,128)(2,1)S(1)}, u32[]{:S(2)}, u32[]{:S(2)}) async-start(bf16[16,2,2,128,128]{4,3,2,1,0:T(8,128)(2,1)} %bitcast.14), calls=%async_computation.1 | async-start | bytes 4194304 | tf_op jit(solution)/shard_map/all_to_all | solution.py:360
  27.7 24.8 %collective-permute-start.1 = (bf16[2,2,8,8,128]{4,3,2,1,0:T(8,128)(2,1)S(1)}, bf16[2,2,8,8,128]{4,3,2,1,0:T(8,128)(2,1)S(1)}, u32[]{:S(2)}, u32[]{:S(2)}) collective-permute-start(bf16[2,2,8,8,128]{4,3,2,1,0:T(8,128)(2,1)S(1)} %get-tuple-element.31), channel_id=1, source_target_pairs={{0,4},{1,5},{2,6},{3,7},{4,0},{5,1},{6,2},{7,3},{8,12},{9,13},{10,... | collective-permute-start | bytes 196616 | tf_op jit(solution)/shard_map/ppermute | solution.py:309
  34.6 21.4 %collective-permute-start.2 = (bf16[2,2,8,8,128]{4,3,2,1,0:T(8,128)(2,1)S(1)}, bf16[2,2,8,8,128]{4,3,2,1,0:T(8,128)(2,1)S(1)}, u32[]{:S(2)}, u32[]{:S(2)}) collective-permute-start(bf16[2,2,8,8,128]{4,3,2,1,0:T(8,128)(2,1)S(1)} %get-tuple-element.30), channel_id=1, source_target_pairs={{0,11},{1,10},{2,9},{3,8},{4,15},{5,14},{6,13},{7,12},{8,3},{9,2},... | collective-permute-start | bytes 196616 | tf_op jit(solution)/shard_map/ppermute | solution.py:309
  43.9 12.1 %collective-permute-start = (bf16[2,2,8,8,128]{4,3,2,1,0:T(8,128)(2,1)S(1)}, bf16[2,2,8,8,128]{4,3,2,1,0:T(8,128)(2,1)S(1)}, u32[]{:S(2)}, u32[]{:S(2)}) collective-permute-start(bf16[2,2,8,8,128]{4,3,2,1,0:T(8,128)(2,1)S(1)} %get-tuple-element.30), channel_id=1, source_target_pairs={{0,15},{1,14},{2,13},{3,12},{4,11},{5,10},{6,9},{7,8},{8,7},{9,6},... | collective-permute-start | bytes 196616 | tf_op jit(solution)/shard_map/ppermute | solution.py:309
  45.9 10.3 %collective-permute-start.3 = (bf16[1,2,2,8,8,128]{5,4,3,2,1,0:T(8,128)(2,1)S(1)}, bf16[1,2,2,8,8,128]{5,4,3,2,1,0:T(8,128)(2,1)S(1)}, u32[]{:S(2)}, u32[]{:S(2)}) collective-permute-start(bf16[1,2,2,8,8,128]{5,4,3,2,1,0:T(8,128)(2,1)S(1)} %bitcast.40), channel_id=1, source_target_pairs={{0,1},{1,2},{2,3},{3,0},{4,5},{5,6},{6,7},{7,4},{8,9},{9,10},{10,1... | collective-permute-start | bytes 196616 | tf_op jit(solution)/shard_map/ppermute | solution.py:314
  49.4 9.2 %collective-permute-start.4 = (bf16[1,2,2,8,8,128]{5,4,3,2,1,0:T(8,128)(2,1)S(1)}, bf16[1,2,2,8,8,128]{5,4,3,2,1,0:T(8,128)(2,1)S(1)}, u32[]{:S(2)}, u32[]{:S(2)}) collective-permute-start(bf16[1,2,2,8,8,128]{5,4,3,2,1,0:T(8,128)(2,1)S(1)} %bitcast.41), channel_id=1, source_target_pairs={{0,2},{1,3},{2,0},{3,1},{4,6},{5,7},{6,4},{7,5},{8,10},{9,11},{10,... | collective-permute-start | bytes 196616 | tf_op jit(solution)/shard_map/ppermute | solution.py:314
  52.5 6.5 %collective-permute-start.5 = (bf16[1,2,2,8,8,128]{5,4,3,2,1,0:T(8,128)(2,1)S(1)}, bf16[1,2,2,8,8,128]{5,4,3,2,1,0:T(8,128)(2,1)S(1)}, u32[]{:S(2)}, u32[]{:S(2)}) collective-permute-start(bf16[1,2,2,8,8,128]{5,4,3,2,1,0:T(8,128)(2,1)S(1)} %bitcast.42), channel_id=1, source_target_pairs={{0,3},{1,0},{2,1},{3,2},{4,7},{5,4},{6,5},{7,6},{8,11},{9,8},{10,9... | collective-permute-start | bytes 196616 | tf_op jit(solution)/shard_map/ppermute | solution.py:314
  59.0 0.6 copy-start.6
  59.7 11.1 %collective-permute-start.6 = (bf16[3,2,2,8,8,128]{5,4,3,2,1,0:T(8,128)(2,1)S(1)}, bf16[3,2,2,8,8,128]{5,4,3,2,1,0:T(8,128)(2,1)S(1)}, u32[]{:S(2)}, u32[]{:S(2)}) collective-permute-start(bf16[3,2,2,8,8,128]{5,4,3,2,1,0:T(8,128)(2,1)S(1)} %pad_maximum_fusion.refs_4_), channel_id=1, source_target_pairs={{0,1},{1,2},{2,3},{3,0},{4,5},{5,6},{6,7},{7,4},{8,9},{9,10},{10,1... | collective-permute-start | bytes 589832 | tf_op jit(solution)/shard_map/ppermute | solution.py:314
  62.3 17.5 %collective-permute-start.7 = (bf16[3,2,2,8,8,128]{5,4,3,2,1,0:T(8,128)(2,1)S(1)}, bf16[3,2,2,8,8,128]{5,4,3,2,1,0:T(8,128)(2,1)S(1)}, u32[]{:S(2)}, u32[]{:S(2)}) collective-permute-start(bf16[3,2,2,8,8,128]{5,4,3,2,1,0:T(8,128)(2,1)S(1)} %pad_maximum_fusion.refs_4_), channel_id=1, source_target_pairs={{0,2},{1,3},{2,0},{3,1},{4,6},{5,7},{6,4},{7,5},{8,10},{9,11},{10,... | collective-permute-start | bytes 589832 | tf_op jit(solution)/shard_map/ppermute | solution.py:314
  68.1 11.6 %collective-permute-start.8 = (bf16[3,2,2,8,8,128]{5,4,3,2,1,0:T(8,128)(2,1)S(1)}, bf16[3,2,2,8,8,128]{5,4,3,2,1,0:T(8,128)(2,1)S(1)}, u32[]{:S(2)}, u32[]{:S(2)}) collective-permute-start(bf16[3,2,2,8,8,128]{5,4,3,2,1,0:T(8,128)(2,1)S(1)} %pad_maximum_fusion.refs_4_), channel_id=1, source_target_pairs={{0,3},{1,0},{2,1},{3,2},{4,7},{5,4},{6,5},{7,6},{8,11},{9,8},{10,9... | collective-permute-start | bytes 589832 | tf_op jit(solution)/shard_map/ppermute | solution.py:314
  79.8 0.8 copy-start.7
  90.6 21.4 %collective-permute-start.10 = (bf16[2,2,2,8,8,128]{5,4,3,2,1,0:T(8,128)(2,1)S(1)}, bf16[2,2,2,8,8,128]{5,4,3,2,1,0:T(8,128)(2,1)S(1)}, u32[]{:S(2)}, u32[]{:S(2)}) collective-permute-start(bf16[2,2,2,8,8,128]{5,4,3,2,1,0:T(8,128)(2,1)S(1)} %get-tuple-element.44), channel_id=1, source_target_pairs={{0,2},{1,3},{2,0},{3,1},{4,6},{5,7},{6,4},{7,5},{8,10},{9,11},{10,... | collective-permute-start | bytes 393224 | tf_op jit(solution)/shard_map/ppermute | solution.py:314
  96.0 16.0 %collective-permute-start.11 = (bf16[2,2,2,8,8,128]{5,4,3,2,1,0:T(8,128)(2,1)S(1)}, bf16[2,2,2,8,8,128]{5,4,3,2,1,0:T(8,128)(2,1)S(1)}, u32[]{:S(2)}, u32[]{:S(2)}) collective-permute-start(bf16[2,2,2,8,8,128]{5,4,3,2,1,0:T(8,128)(2,1)S(1)} %get-tuple-element.45), channel_id=1, source_target_pairs={{0,1},{1,2},{2,3},{3,0},{4,5},{5,6},{6,7},{7,4},{8,9},{9,10},{10,1... | collective-permute-start | bytes 393224 | tf_op jit(solution)/shard_map/ppermute | solution.py:314
  99.0 13.1 %collective-permute-start.9 = (bf16[2,2,2,8,8,128]{5,4,3,2,1,0:T(8,128)(2,1)S(1)}, bf16[2,2,2,8,8,128]{5,4,3,2,1,0:T(8,128)(2,1)S(1)}, u32[]{:S(2)}, u32[]{:S(2)}) collective-permute-start(bf16[2,2,2,8,8,128]{5,4,3,2,1,0:T(8,128)(2,1)S(1)} %get-tuple-element.43), channel_id=1, source_target_pairs={{0,3},{1,0},{2,1},{3,2},{4,7},{5,4},{6,5},{7,6},{8,11},{9,8},{10,9... | collective-permute-start | bytes 393224 | tf_op jit(solution)/shard_map/ppermute | solution.py:314
  103.1 38.3 %copy-start.5 = (s32[1,16,2]{1,2,0:T(2,128)S(1)}, s32[1,16,2]{1,2,0:T(2,128)}, u32[]{:S(2)}) copy-start(s32[1,16,2]{1,2,0:T(2,128)} %param.9) | copy-start | bytes 388
  103.1 47.7 %all-to-all-start.2 = ((bf16[16,2,128,128]{3,2,1,0:T(8,128)(2,1)}), bf16[16,2,128,128]{3,2,1,0:T(8,128)(2,1)S(1)}, u32[]{:S(2)}, u32[]{:S(2)}) async-start(bf16[16,2,128,128]{3,2,1,0:T(8,128)(2,1)} %bitcast.18), calls=%async_computation.2 | async-start | bytes 2097152 | tf_op jit(solution)/shard_map/all_to_all | solution.py:374
  112.1 18.9 %collective-permute-start.12 = (bf16[2,2,2,8,8,128]{5,4,3,2,1,0:T(8,128)(2,1)S(1)}, bf16[2,2,2,8,8,128]{5,4,3,2,1,0:T(8,128)(2,1)S(1)}, u32[]{:S(2)}, u32[]{:S(2)}) collective-permute-start(bf16[2,2,2,8,8,128]{5,4,3,2,1,0:T(8,128)(2,1)S(1)} %add_convert_fusion.1), channel_id=1, source_target_pairs={{0,4},{1,5},{2,6},{3,7},{4,0},{5,1},{6,2},{7,3},{8,12},{9,13},{10,... | collective-permute-start | bytes 393224 | tf_op jit(solution)/shard_map/ppermute | solution.py:309
  118.5 12.6 %collective-permute-start.13 = (bf16[2,2,2,8,8,128]{5,4,3,2,1,0:T(8,128)(2,1)S(1)}, bf16[2,2,2,8,8,128]{5,4,3,2,1,0:T(8,128)(2,1)S(1)}, u32[]{:S(2)}, u32[]{:S(2)}) collective-permute-start(bf16[2,2,2,8,8,128]{5,4,3,2,1,0:T(8,128)(2,1)S(1)} %get-tuple-element.51), channel_id=1, source_target_pairs={{0,3},{1,0},{2,1},{3,2},{4,7},{5,4},{6,5},{7,6},{8,11},{9,8},{10,9... | collective-permute-start | bytes 393224 | tf_op jit(solution)/shard_map/ppermute | solution.py:314
  121.7 17.7 %collective-permute-start.14 = (bf16[2,2,2,8,8,128]{5,4,3,2,1,0:T(8,128)(2,1)S(1)}, bf16[2,2,2,8,8,128]{5,4,3,2,1,0:T(8,128)(2,1)S(1)}, u32[]{:S(2)}, u32[]{:S(2)}) collective-permute-start(bf16[2,2,2,8,8,128]{5,4,3,2,1,0:T(8,128)(2,1)S(1)} %get-tuple-element.52), channel_id=1, source_target_pairs={{0,2},{1,3},{2,0},{3,1},{4,6},{5,7},{6,4},{7,5},{8,10},{9,11},{10,... | collective-permute-start | bytes 393224 | tf_op jit(solution)/shard_map/ppermute | solution.py:314
  123.7 15.8 %collective-permute-start.15 = (bf16[2,2,2,8,8,128]{5,4,3,2,1,0:T(8,128)(2,1)S(1)}, bf16[2,2,2,8,8,128]{5,4,3,2,1,0:T(8,128)(2,1)S(1)}, u32[]{:S(2)}, u32[]{:S(2)}) collective-permute-start(bf16[2,2,2,8,8,128]{5,4,3,2,1,0:T(8,128)(2,1)S(1)} %get-tuple-element.53), channel_id=1, source_target_pairs={{0,1},{1,2},{2,3},{3,0},{4,5},{5,6},{6,7},{7,4},{8,9},{9,10},{10,1... | collective-permute-start | bytes 393224 | tf_op jit(solution)/shard_map/ppermute | solution.py:314
  139.5 11.3 %collective-permute-start.16 = (bf16[2,2,8,8,128]{4,3,2,1,0:T(8,128)(2,1)S(1)}, bf16[2,2,8,8,128]{4,3,2,1,0:T(8,128)(2,1)S(1)}, u32[]{:S(2)}, u32[]{:S(2)}) collective-permute-start(bf16[2,2,8,8,128]{4,3,2,1,0:T(8,128)(2,1)S(1)} %get-tuple-element.58), channel_id=1, source_target_pairs={{0,15},{1,14},{2,13},{3,12},{4,11},{5,10},{6,9},{7,8},{8,7},{9,6},... | collective-permute-start | bytes 196616 | tf_op jit(solution)/shard_map/ppermute | solution.py:309
  152.2 14.8 %all-to-all-start.3 = ((bf16[32,2,2,2,4,128]{5,4,3,2,1,0:T(4,128)(2,1)}), bf16[32,2,2,2,4,128]{5,4,3,2,1,0:T(4,128)(2,1)S(1)}, u32[]{:S(2)}, u32[]{:S(2)}) async-start(bf16[32,2,2,2,4,128]{5,4,3,2,1,0:T(4,128)(2,1)} %bitcast.22), calls=%async_computation.3 | async-start | bytes 524288 | tf_op jit(solution)/shard_map/all_to_all | solution.py:347

commit v11 on v10

--- a/solution.py
+++ b/solution.py
@@ -52,8 +52,8 @@
 def attention_kernel(
     recv_ref, start_ref, place_ref, qg_ref, *refs
 ):
-    kv_refs, dq_ref, dkv_refs = refs[: 2 * NEAR], refs[2 * NEAR], refs[2 * NEAR + 1 : 4 * NEAR + 1]
-    k_all, kt_all, v_all, dk_all, dv_all, *rest = refs[4 * NEAR + 1 :]
+    kv_refs, dq_ref, dkv_refs = refs[: 2 * NEAR], refs[2 * NEAR], refs[2 * NEAR + 1 : 5 * NEAR + 1]
+    k_all, kt_all, v_all, dk_all, dv_all, *rest = refs[5 * NEAR + 1 :]
     scores, dprobs, diagonal_scores, diagonal_dprobs, stats, dqt = rest
     blocks = k_all.shape[0]
     width = k_all.shape[1]
@@ -61,15 +61,13 @@
     part = width // NEAR
     factor = SCALING * LOG2E
 
-    def rows_of(slot, first_part):
+    def rows_of(slot, *bounds):
         begin = (slot % NEAR) * part
-        if slot < NEAR:
-            return slice(begin, begin + first_part)
-        return slice(begin + first_part, begin + part)
+        return slice(begin + bounds[slot // NEAR], begin + bounds[slot // NEAR + 1])
 
     def stage(block, _):
         for slot, ref in enumerate(kv_refs):
-            rows = rows_of(slot, part // 4)
+            rows = rows_of(slot, 0, part // 4, part)
             count = rows.stop - rows.start
             key = ref[:, :, 0, block].astype(jnp.float32).reshape(count, HD)
             value = ref[:, :, 1, block].astype(jnp.float32).reshape(count, HD)
@@ -121,7 +119,7 @@
         dqt[block] = jnp.zeros_like(dqt[block])
         return 0
 
-    lax.fori_loop(0, blocks, diagonal_products, 0, unroll=2)
+    lax.fori_loop(0, blocks, diagonal_products, 0, unroll=4)
 
     def query_block(block, _):
         query, grad = operands(block)
@@ -185,11 +183,11 @@
         dq_ref[recv_ref[PAIR * block + 1]] = result[tile_rows:]
         return 0
 
-    lax.fori_loop(0, blocks, diagonal_terms, 0, unroll=2)
+    lax.fori_loop(0, blocks, diagonal_terms, 0, unroll=4)
 
     def unstage(block, _):
         for slot, ref in enumerate(dkv_refs):
-            rows = rows_of(slot, part // 2)
+            rows = rows_of(slot, 0, part // 4, part // 2, part)
             shape = ref.shape[:2] + ref.shape[4:]
             ref[:, :, 0, block] = (dk_all[block, rows] * SCALING).reshape(shape).astype(jnp.bfloat16)
             ref[:, :, 1, block] = dv_all[block, rows].reshape(shape).astype(jnp.bfloat16)
@@ -207,9 +205,13 @@
     return pl.pallas_call(
         attention_kernel,
         out_shape=(jax.ShapeDtypeStruct((slots, tile_rows, HD), jnp.bfloat16),)
-        + (jax.ShapeDtypeStruct((2,) + chunks[0].shape[1:], jnp.bfloat16),) * (2 * NEAR),
+        + tuple(
+            jax.ShapeDtypeStruct((count,) + chunks[0].shape[1:], jnp.bfloat16)
+            for count in (1, 1, 2)
+            for _ in range(NEAR)
+        ),
         in_specs=[smem] * 3 + [vmem] * (1 + 2 * NEAR),
-        out_specs=(vmem,) * (1 + 2 * NEAR),
+        out_specs=(vmem,) * (1 + 3 * NEAR),
         scratch_shapes=[
             pltpu.VMEM((blocks, width, HD), jnp.bfloat16),
             pltpu.VMEM((blocks, HD, width), jnp.bfloat16),
@@ -261,7 +263,8 @@
     lax.fori_loop(0, recv_ref.shape[0] // PAIR, body, 0, unroll=4)
 
 
-def kv_back_kernel(recv_ref, place_ref, own_ref, other_ref, out_ref):
+def kv_back_kernel(recv_ref, place_ref, *refs):
+    own_refs, (across_ref, other_ref, out_ref) = refs[:NEAR], refs[NEAR:]
     head = place_ref[0] >> 3
     sliver = out_ref.shape[-2]
 
@@ -269,8 +272,10 @@
         slots = (recv_ref[PAIR * pair], recv_ref[PAIR * pair + 1])
         for half in range(2):
             for kind in range(2):
-                for ref, which in ((own_ref, head), (other_ref, 1 - head)):
-                    total = ref[half, kind, pair].astype(jnp.float32)
+                own = across_ref[0, half, kind, pair].astype(jnp.float32)
+                for ref in own_refs:
+                    own += ref[0, half, kind, pair].astype(jnp.float32)
+                for total, which in ((own, head), (other_ref[half, kind, pair], 1 - head)):
                     for order, slot in enumerate(slots):
                         rows = total[order * sliver : (order + 1) * sliver]
                         out_ref[slot >> 1, half, slot & 1, kind, which] = rows.astype(jnp.bfloat16)
@@ -375,15 +380,20 @@
         query_back.reshape(n_replicas, slot_cap, tile_rows, row_width),
         "dp", split_axis=0, concat_axis=0, tiled=True,
     )
-    across_terms = near_terms(terms[NEAR:])
-    own_terms, across_terms = lax.optimization_barrier((terms[:NEAR], across_terms))
+    own_terms, mirror_terms = terms[:NEAR], terms[NEAR : 2 * NEAR]
+    across_terms = near_terms(terms[2 * NEAR :])
+    own_terms, mirror_terms, across_terms = lax.optimization_barrier(
+        (own_terms, mirror_terms, across_terms)
+    )
     arrived = far_swap(total(across_terms).astype(jnp.bfloat16), ACROSS)
-    base = lax.optimization_barrier(total([arrived, own_terms[0]]))
-    summed = total([base] + near_terms(own_terms)[1:]).astype(jnp.bfloat16)
-    swapped = [summed[0], far_swap(summed[1], MIRROR)]
-    swapped, query_returned = lax.optimization_barrier((swapped, query_returned))
+    base = lax.optimization_barrier(total([arrived[1:], mirror_terms[0]]))
+    mirror_sum = total([base] + near_terms(mirror_terms)[1:])[0].astype(jnp.bfloat16)
+    own_terms, mirror_sum = lax.optimization_barrier((own_terms, mirror_sum))
+    other = lax.optimization_barrier(far_swap(mirror_sum, MIRROR).astype(jnp.float32))
+    last = near_terms(own_terms) + [arrived, other]
+    last, query_returned = lax.optimization_barrier((last, query_returned))
     kv_returned = over_plane(
-        local_call(kv_back_kernel, "kv_back", [my_recv, place], swapped, traveling)
+        local_call(kv_back_kernel, "kv_back", [my_recv, place], last, traveling)
     )
 
     flat_slots = jnp.arange(slots)

time: 169 us -> 174 us (1.030)
  starting transfers between devices: 95.8 us -> 111 us
  waiting for transfers between devices: 46.6 us -> 36.4 us
    ppermute x12 -> x15, starting transfers between devices: 40.3 us -> 51.6 us  [near_shift(): return lax.ppermute(values, 'z', pairs)]
    ppermute x5, waiting for transfers between devices: 14.4 us -> 5.18 us  [far_swap(): lax.ppermute(values, 'z', [(place, place ^ flip) for place in range(16)])]
    all_to_all x2, starting transfers between devices: 16.3 us -> 21.1 us  [over_plane(): lax.all_to_all(values.reshape((2 * n_replicas,) + values.shape[2:]), PLAN...]
    ppermute x12 -> x15, waiting for transfers between devices: 20.8 us -> 19.8 us  [near_shift(): return lax.ppermute(values, 'z', pairs)]
  transfers between devices with their start and end apart: 21 -> 24, of which waited for: 9 -> 10; matrix products, arithmetic and copies ran while one was open for 1% -> 1% of each run, Pallas kernels for 2% -> 2%
where the time goes in v11:
time: 174 us; the launch traced here: 172 us
  starting transfers between devices  111 us (64%)
  waiting for transfers between devices  36.4 us (21%)
  Pallas kernels  16.1 us (9%)
  local copies, waits for them, and re-layouts  7.23 us (4%)
    ppermute x15, starting transfers between devices, near_shift(): return lax.ppermute(values, 'z', pairs)  51.6 us
    ppermute x5, starting transfers between devices, far_swap(): lax.ppermute(values, 'z', [(place, place ^ flip) for place in range(16)])  26.2 us
    all_to_all x2, starting transfers between devices, over_plane(): lax.all_to_all(values.reshape((2 * n_replicas,) + values.shape[2:]), PLAN...  21.1 us
    ppermute x15, waiting for transfers between devices, near_shift(): return lax.ppermute(values, 'z', pairs)  19.8 us
    all_to_all x2, waiting for transfers between devices, over_plane(): lax.all_to_all(values.reshape((2 * n_replicas,) + values.shape[2:]), PLAN...  11.4 us
    pallas_call x1, Pallas kernels, attention(): pl.pallas_call(attention_kernel, out_shape=(jax.ShapeDtypeStruct((slots,...  9.29 us
    all_to_all x1, starting transfers between devices, on_device(): lax.all_to_all(query_back.reshape(n_replicas, slot_cap, tile_rows, row_wi...  8.09 us
    unnamed x20, local copies, waits for them, and re-layouts  5.81 us
  transfers between devices with their start and end apart: 24, of which 10 were waited for; matrix products, arithmetic and copies ran while one was open for 1% of the time, Pallas kernels for 2%

profile of v11, /device:TPU:1, one launch (start us, length us, event | category | flops | bytes accessed | tf_op | source)
XLA Modules:
  0.0 172.5 jit_solution(8911683461119583278)
XLA Ops:
  3.7 10.4 %all-to-all-start = ((bf16[32,2,2,2,4,128]{5,4,3,2,1,0:T(4,128)(2,1)}), bf16[32,2,2,2,4,128]{5,4,3,2,1,0:T(4,128)(2,1)S(1)}, u32[]{:S(2)}, u32[]{:S(2)}) async-start(bf16[32,2,2,2,4,128]{5,4,3,2,1,0:T(4,128)(2,1)} %bitcast.7), calls=%async_computation | async-start | bytes 524288 | tf_op jit(solution)/shard_map/all_to_all | solution.py:352
  16.8 2.2 %pack_rows.1 = bf16[32,2,128,128]{3,2,1,0:T(8,128)(2,1)} custom-call(s32[2,16]{1,0:T(2,128)S(1)} %bitcast.36, bf16[16,128,128]{2,1,0:T(8,128)(2,1)S(1)} %copy-done, bf16[16,128,128]{2,1,0:T(8,128)(2,1)S(1)} %copy-done.1), custom_call_target="tpu_custom_call" | custom-call | tf_op jit(solution)/shard_map/pack_rows/pallas_call | solution.py:38
  19.0 4.0 %all-to-all-done = bf16[32,2,2,2,4,128]{5,4,3,2,1,0:T(4,128)(2,1)S(1)} async-done(((bf16[32,2,2,2,4,128]{5,4,3,2,1,0:T(4,128)(2,1)}), bf16[32,2,2,2,4,128]{5,4,3,2,1,0:T(4,128)(2,1)S(1)}, u32[]{:S(2)}, u32[]{:S(2)}) %all-to-all-start) | async-done | bytes 262176 | tf_op jit(solution)/shard_map/all_to_all | solution.py:352
  23.0 4.1 %all-to-all-start.1 = ((bf16[16,2,2,128,128]{4,3,2,1,0:T(8,128)(2,1)}), bf16[16,2,2,128,128]{4,3,2,1,0:T(8,128)(2,1)S(1)}, u32[]{:S(2)}, u32[]{:S(2)}) async-start(bf16[16,2,2,128,128]{4,3,2,1,0:T(8,128)(2,1)} %bitcast.14), calls=%async_computation.1 | async-start | bytes 4194304 | tf_op jit(solution)/shard_map/all_to_all | solution.py:365
  27.7 6.9 %collective-permute-start.1 = (bf16[2,2,8,8,128]{4,3,2,1,0:T(8,128)(2,1)S(1)}, bf16[2,2,8,8,128]{4,3,2,1,0:T(8,128)(2,1)S(1)}, u32[]{:S(2)}, u32[]{:S(2)}) collective-permute-start(bf16[2,2,8,8,128]{4,3,2,1,0:T(8,128)(2,1)S(1)} %get-tuple-element.48), channel_id=1, source_target_pairs={{0,4},{1,5},{2,6},{3,7},{4,0},{5,1},{6,2},{7,3},{8,12},{9,13},{10,... | collective-permute-start | bytes 196616 | tf_op jit(solution)/shard_map/ppermute | solution.py:314
  34.6 9.3 %collective-permute-start.2 = (bf16[2,2,8,8,128]{4,3,2,1,0:T(8,128)(2,1)S(1)}, bf16[2,2,8,8,128]{4,3,2,1,0:T(8,128)(2,1)S(1)}, u32[]{:S(2)}, u32[]{:S(2)}) collective-permute-start(bf16[2,2,8,8,128]{4,3,2,1,0:T(8,128)(2,1)S(1)} %get-tuple-element.47), channel_id=1, source_target_pairs={{0,11},{1,10},{2,9},{3,8},{4,15},{5,14},{6,13},{7,12},{8,3},{9,2},... | collective-permute-start | bytes 196616 | tf_op jit(solution)/shard_map/ppermute | solution.py:314
  43.9 1.9 %collective-permute-start = (bf16[2,2,8,8,128]{4,3,2,1,0:T(8,128)(2,1)S(1)}, bf16[2,2,8,8,128]{4,3,2,1,0:T(8,128)(2,1)S(1)}, u32[]{:S(2)}, u32[]{:S(2)}) collective-permute-start(bf16[2,2,8,8,128]{4,3,2,1,0:T(8,128)(2,1)S(1)} %get-tuple-element.47), channel_id=1, source_target_pairs={{0,15},{1,14},{2,13},{3,12},{4,11},{5,10},{6,9},{7,8},{8,7},{9,6},... | collective-permute-start | bytes 196616 | tf_op jit(solution)/shard_map/ppermute | solution.py:314
  45.9 3.5 %collective-permute-start.3 = (bf16[1,2,2,8,8,128]{5,4,3,2,1,0:T(8,128)(2,1)S(1)}, bf16[1,2,2,8,8,128]{5,4,3,2,1,0:T(8,128)(2,1)S(1)}, u32[]{:S(2)}, u32[]{:S(2)}) collective-permute-start(bf16[1,2,2,8,8,128]{5,4,3,2,1,0:T(8,128)(2,1)S(1)} %bitcast.38), channel_id=1, source_target_pairs={{0,1},{1,2},{2,3},{3,0},{4,5},{5,6},{6,7},{7,4},{8,9},{9,10},{10,1... | collective-permute-start | bytes 196616 | tf_op jit(solution)/shard_map/ppermute | solution.py:319
  49.4 3.1 %collective-permute-start.4 = (bf16[1,2,2,8,8,128]{5,4,3,2,1,0:T(8,128)(2,1)S(1)}, bf16[1,2,2,8,8,128]{5,4,3,2,1,0:T(8,128)(2,1)S(1)}, u32[]{:S(2)}, u32[]{:S(2)}) collective-permute-start(bf16[1,2,2,8,8,128]{5,4,3,2,1,0:T(8,128)(2,1)S(1)} %bitcast.39), channel_id=1, source_target_pairs={{0,2},{1,3},{2,0},{3,1},{4,6},{5,7},{6,4},{7,5},{8,10},{9,11},{10,... | collective-permute-start | bytes 196616 | tf_op jit(solution)/shard_map/ppermute | solution.py:319
  52.5 3.6 %collective-permute-start.5 = (bf16[1,2,2,8,8,128]{5,4,3,2,1,0:T(8,128)(2,1)S(1)}, bf16[1,2,2,8,8,128]{5,4,3,2,1,0:T(8,128)(2,1)S(1)}, u32[]{:S(2)}, u32[]{:S(2)}) collective-permute-start(bf16[1,2,2,8,8,128]{5,4,3,2,1,0:T(8,128)(2,1)S(1)} %bitcast.40), channel_id=1, source_target_pairs={{0,3},{1,0},{2,1},{3,2},{4,7},{5,4},{6,5},{7,6},{8,11},{9,8},{10,9... | collective-permute-start | bytes 196616 | tf_op jit(solution)/shard_map/ppermute | solution.py:319
  56.1 2.5 %collective-permute-done.4.refs_2_ = bf16[1,2,2,8,8,128]{5,4,3,2,1,0:T(8,128)(2,1)S(1)} collective-permute-done((bf16[1,2,2,8,8,128]{5,4,3,2,1,0:T(8,128)(2,1)S(1)}, bf16[1,2,2,8,8,128]{5,4,3,2,1,0:T(8,128)(2,1)S(1)}, u32[]{:S(2)}, u32[]{:S(2)}) %collective-permute-start.4) | collective-permute-done | bytes 65568 | tf_op jit(solution)/shard_map/ppermute | solution.py:319
  59.7 2.6 %collective-permute-start.6 = (bf16[3,2,2,8,8,128]{5,4,3,2,1,0:T(8,128)(2,1)S(1)}, bf16[3,2,2,8,8,128]{5,4,3,2,1,0:T(8,128)(2,1)S(1)}, u32[]{:S(2)}, u32[]{:S(2)}) collective-permute-start(bf16[3,2,2,8,8,128]{5,4,3,2,1,0:T(8,128)(2,1)S(1)} %pad_maximum_fusion.refs_4_), channel_id=1, source_target_pairs={{0,1},{1,2},{2,3},{3,0},{4,5},{5,6},{6,7},{7,4},{8,9},{9,10},{10,1... | collective-permute-start | bytes 589832 | tf_op jit(solution)/shard_map/ppermute | solution.py:319
  62.3 5.9 %collective-permute-start.7 = (bf16[3,2,2,8,8,128]{5,4,3,2,1,0:T(8,128)(2,1)S(1)}, bf16[3,2,2,8,8,128]{5,4,3,2,1,0:T(8,128)(2,1)S(1)}, u32[]{:S(2)}, u32[]{:S(2)}) collective-permute-start(bf16[3,2,2,8,8,128]{5,4,3,2,1,0:T(8,128)(2,1)S(1)} %pad_maximum_fusion.refs_4_), channel_id=1, source_target_pairs={{0,2},{1,3},{2,0},{3,1},{4,6},{5,7},{6,4},{7,5},{8,10},{9,11},{10,... | collective-permute-start | bytes 589832 | tf_op jit(solution)/shard_map/ppermute | solution.py:319
  68.1 1.9 %collective-permute-start.8 = (bf16[3,2,2,8,8,128]{5,4,3,2,1,0:T(8,128)(2,1)S(1)}, bf16[3,2,2,8,8,128]{5,4,3,2,1,0:T(8,128)(2,1)S(1)}, u32[]{:S(2)}, u32[]{:S(2)}) collective-permute-start(bf16[3,2,2,8,8,128]{5,4,3,2,1,0:T(8,128)(2,1)S(1)} %pad_maximum_fusion.refs_4_), channel_id=1, source_target_pairs={{0,3},{1,0},{2,1},{3,2},{4,7},{5,4},{6,5},{7,6},{8,11},{9,8},{10,9... | collective-permute-start | bytes 589832 | tf_op jit(solution)/shard_map/ppermute | solution.py:319
  70.7 9.0 %collective-permute-done.7.refs_6_ = bf16[3,2,2,8,8,128]{5,4,3,2,1,0:T(8,128)(2,1)S(1)} collective-permute-done((bf16[3,2,2,8,8,128]{5,4,3,2,1,0:T(8,128)(2,1)S(1)}, bf16[3,2,2,8,8,128]{5,4,3,2,1,0:T(8,128)(2,1)S(1)}, u32[]{:S(2)}, u32[]{:S(2)}) %collective-permute-start.7) | collective-permute-done | bytes 196640 | tf_op jit(solution)/shard_map/ppermute | solution.py:319
  80.6 9.3 %attention_backward.1 = (bf16[32,128,128]{2,1,0:T(8,128)(2,1)}, bf16[1,2,2,8,8,128]{5,4,3,2,1,0:T(8,128)(2,1)S(1)}, bf16[1,2,2,8,8,128]{5,4,3,2,1,0:T(8,128)(2,1...) custom-call(s32[16]{0:T(128)S(1)} %dynamic-slice_bitcast_fusion.recv, ...), custom_call_target="tpu_custom_call" | custom-call | flops 2000000000 | bytes 6291456 | tf_op jit(solution)/shard_map/attention_backward/pallas_call | solution.py:205
  89.9 5.5 %collective-permute-start.10 = (bf16[2,2,2,8,8,128]{5,4,3,2,1,0:T(8,128)(2,1)S(1)}, bf16[2,2,2,8,8,128]{5,4,3,2,1,0:T(8,128)(2,1)S(1)}, u32[]{:S(2)}, u32[]{:S(2)}) collective-permute-start(bf16[2,2,2,8,8,128]{5,4,3,2,1,0:T(8,128)(2,1)S(1)} %get-tuple-element.65), channel_id=1, source_target_pairs={{0,2},{1,3},{2,0},{3,1},{4,6},{5,7},{6,4},{7,5},{8,10},{9,11},{10,... | collective-permute-start | bytes 393224 | tf_op jit(solution)/shard_map/ppermute | solution.py:319
  95.4 2.9 %collective-permute-start.11 = (bf16[2,2,2,8,8,128]{5,4,3,2,1,0:T(8,128)(2,1)S(1)}, bf16[2,2,2,8,8,128]{5,4,3,2,1,0:T(8,128)(2,1)S(1)}, u32[]{:S(2)}, u32[]{:S(2)}) collective-permute-start(bf16[2,2,2,8,8,128]{5,4,3,2,1,0:T(8,128)(2,1)S(1)} %get-tuple-element.66), channel_id=1, source_target_pairs={{0,1},{1,2},{2,3},{3,0},{4,5},{5,6},{6,7},{7,4},{8,9},{9,10},{10,1... | collective-permute-start | bytes 393224 | tf_op jit(solution)/shard_map/ppermute | solution.py:319
  98.4 4.1 %collective-permute-start.9 = (bf16[2,2,2,8,8,128]{5,4,3,2,1,0:T(8,128)(2,1)S(1)}, bf16[2,2,2,8,8,128]{5,4,3,2,1,0:T(8,128)(2,1)S(1)}, u32[]{:S(2)}, u32[]{:S(2)}) collective-permute-start(bf16[2,2,2,8,8,128]{5,4,3,2,1,0:T(8,128)(2,1)S(1)} %get-tuple-element.64), channel_id=1, source_target_pairs={{0,3},{1,0},{2,1},{3,2},{4,7},{5,4},{6,5},{7,6},{8,11},{9,8},{10,9... | collective-permute-start | bytes 393224 | tf_op jit(solution)/shard_map/ppermute | solution.py:319
  102.5 8.1 %all-to-all-start.2 = ((bf16[16,2,128,128]{3,2,1,0:T(8,128)(2,1)}), bf16[16,2,128,128]{3,2,1,0:T(8,128)(2,1)S(1)}, u32[]{:S(2)}, u32[]{:S(2)}) async-start(bf16[16,2,128,128]{3,2,1,0:T(8,128)(2,1)} %bitcast.17), calls=%async_computation.2 | async-start | bytes 2097152 | tf_op jit(solution)/shard_map/all_to_all | solution.py:379
  110.7 6.2 %collective-permute-start.12 = (bf16[2,2,2,8,8,128]{5,4,3,2,1,0:T(8,128)(2,1)S(1)}, bf16[2,2,2,8,8,128]{5,4,3,2,1,0:T(8,128)(2,1)S(1)}, u32[]{:S(2)}, u32[]{:S(2)}) collective-permute-start(bf16[2,2,2,8,8,128]{5,4,3,2,1,0:T(8,128)(2,1)S(1)} %add_convert_fusion), channel_id=1, source_target_pairs={{0,4},{1,5},{2,6},{3,7},{4,0},{5,1},{6,2},{7,3},{8,12},{9,13},{10,... | collective-permute-start | bytes 393224 | tf_op jit(solution)/shard_map/ppermute | solution.py:314
  117.1 3.2 %collective-permute-start.13 = (bf16[1,2,2,8,8,128]{5,4,3,2,1,0:T(8,128)(2,1)S(1)}, bf16[1,2,2,8,8,128]{5,4,3,2,1,0:T(8,128)(2,1)S(1)}, u32[]{:S(2)}, u32[]{:S(2)}) collective-permute-start(bf16[1,2,2,8,8,128]{5,4,3,2,1,0:T(8,128)(2,1)S(1)} %get-tuple-element.76), channel_id=1, source_target_pairs={{0,3},{1,0},{2,1},{3,2},{4,7},{5,4},{6,5},{7,6},{8,11},{9,8},{10,9... | collective-permute-start | bytes 196616 | tf_op jit(solution)/shard_map/ppermute | solution.py:319
  120.3 1.9 %collective-permute-start.14 = (bf16[1,2,2,8,8,128]{5,4,3,2,1,0:T(8,128)(2,1)S(1)}, bf16[1,2,2,8,8,128]{5,4,3,2,1,0:T(8,128)(2,1)S(1)}, u32[]{:S(2)}, u32[]{:S(2)}) collective-permute-start(bf16[1,2,2,8,8,128]{5,4,3,2,1,0:T(8,128)(2,1)S(1)} %get-tuple-element.77), channel_id=1, source_target_pairs={{0,2},{1,3},{2,0},{3,1},{4,6},{5,7},{6,4},{7,5},{8,10},{9,11},{10,... | collective-permute-start | bytes 196616 | tf_op jit(solution)/shard_map/ppermute | solution.py:319
  122.3 2.2 %collective-permute-start.15 = (bf16[1,2,2,8,8,128]{5,4,3,2,1,0:T(8,128)(2,1)S(1)}, bf16[1,2,2,8,8,128]{5,4,3,2,1,0:T(8,128)(2,1)S(1)}, u32[]{:S(2)}, u32[]{:S(2)}) collective-permute-start(bf16[1,2,2,8,8,128]{5,4,3,2,1,0:T(8,128)(2,1)S(1)} %get-tuple-element.78), channel_id=1, source_target_pairs={{0,1},{1,2},{2,3},{3,0},{4,5},{5,6},{6,7},{7,4},{8,9},{9,10},{10,1... | collective-permute-start | bytes 196616 | tf_op jit(solution)/shard_map/ppermute | solution.py:319
  124.5 5.2 %collective-permute-done.12.refs_4_ = bf16[2,2,2,8,8,128]{5,4,3,2,1,0:T(8,128)(2,1)S(1)} collective-permute-done((bf16[2,2,2,8,8,128]{5,4,3,2,1,0:T(8,128)(2,1)S(1)}, bf16[2,2,2,8,8,128]{5,4,3,2,1,0:T(8,128)(2,1)S(1)}, u32[]{:S(2)}, u32[]{:S(2)}) %collective-permute-start.12) | collective-permute-done | bytes 131104 | tf_op jit(solution)/shard_map/ppermute | solution.py:314
  129.7 4.1 %collective-permute-done.14 = bf16[1,2,2,8,8,128]{5,4,3,2,1,0:T(8,128)(2,1)S(1)} collective-permute-done((bf16[1,2,2,8,8,128]{5,4,3,2,1,0:T(8,128)(2,1)S(1)}, bf16[1,2,2,8,8,128]{5,4,3,2,1,0:T(8,128)(2,1)S(1)}, u32[]{:S(2)}, u32[]{:S(2)}) %collective-permute-start.14) | collective-permute-done | bytes 65568 | tf_op jit(solution)/shard_map/ppermute | solution.py:319
  135.7 5.8 %collective-permute-start.16 = (bf16[1,2,2,8,8,128]{5,4,3,2,1,0:T(8,128)(2,1)S(1)}, bf16[1,2,2,8,8,128]{5,4,3,2,1,0:T(8,128)(2,1)S(1)}, u32[]{:S(2)}, u32[]{:S(2)}) collective-permute-start(bf16[1,2,2,8,8,128]{5,4,3,2,1,0:T(8,128)(2,1)S(1)} %get-tuple-element.80), channel_id=1, source_target_pairs={{0,3},{1,0},{2,1},{3,2},{4,7},{5,4},{6,5},{7,6},{8,11},{9,8},{10,9... | collective-permute-start | bytes 196616 | tf_op jit(solution)/shard_map/ppermute | solution.py:319
  141.5 2.0 %collective-permute-start.17 = (bf16[1,2,2,8,8,128]{5,4,3,2,1,0:T(8,128)(2,1)S(1)}, bf16[1,2,2,8,8,128]{5,4,3,2,1,0:T(8,128)(2,1)S(1)}, u32[]{:S(2)}, u32[]{:S(2)}) collective-permute-start(bf16[1,2,2,8,8,128]{5,4,3,2,1,0:T(8,128)(2,1)S(1)} %get-tuple-element.81), channel_id=1, source_target_pairs={{0,2},{1,3},{2,0},{3,1},{4,6},{5,7},{6,4},{7,5},{8,10},{9,11},{10,... | collective-permute-start | bytes 196616 | tf_op jit(solution)/shard_map/ppermute | solution.py:319
  143.5 3.4 %collective-permute-start.18 = (bf16[1,2,2,8,8,128]{5,4,3,2,1,0:T(8,128)(2,1)S(1)}, bf16[1,2,2,8,8,128]{5,4,3,2,1,0:T(8,128)(2,1)S(1)}, u32[]{:S(2)}, u32[]{:S(2)}) collective-permute-start(bf16[1,2,2,8,8,128]{5,4,3,2,1,0:T(8,128)(2,1)S(1)} %get-tuple-element.82), channel_id=1, source_target_pairs={{0,1},{1,2},{2,3},{3,0},{4,5},{5,6},{6,7},{7,4},{8,9},{9,10},{10,1... | collective-permute-start | bytes 196616 | tf_op jit(solution)/shard_map/ppermute | solution.py:319
  148.1 2.2 %collective-permute-done.18.refs_3_ = bf16[1,2,2,8,8,128]{5,4,3,2,1,0:T(8,128)(2,1)S(1)} collective-permute-done((bf16[1,2,2,8,8,128]{5,4,3,2,1,0:T(8,128)(2,1)S(1)}, bf16[1,2,2,8,8,128]{5,4,3,2,1,0:T(8,128)(2,1)S(1)}, u32[]{:S(2)}, u32[]{:S(2)}) %collective-permute-start.18) | collective-permute-done | bytes 65568 | tf_op jit(solution)/shard_map/ppermute | solution.py:319
  151.7 10.7 %all-to-all-start.3 = ((bf16[32,2,2,2,4,128]{5,4,3,2,1,0:T(4,128)(2,1)}), bf16[32,2,2,2,4,128]{5,4,3,2,1,0:T(4,128)(2,1)S(1)}, u32[]{:S(2)}, u32[]{:S(2)}) async-start(bf16[32,2,2,2,4,128]{5,4,3,2,1,0:T(4,128)(2,1)} %bitcast.21), calls=%async_computation.3 | async-start | bytes 524288 | tf_op jit(solution)/shard_map/all_to_all | solution.py:352
  163.8 7.4 %all-to-all-done.3 = bf16[32,2,2,2,4,128]{5,4,3,2,1,0:T(4,128)(2,1)S(1)} async-done(((bf16[32,2,2,2,4,128]{5,4,3,2,1,0:T(4,128)(2,1)}), bf16[32,2,2,2,4,128]{5,4,3,2,1,0:T(4,128)(2,1)S(1)}, u32[]{:S(2)}, u32[]{:S(2)}) %all-to-all-start.3) | async-done | bytes 262176 | tf_op jit(solution)/shard_map/all_to_all | solution.py:352
  (56 shorter events, 16.4 us)
Async XLA Ops:
  0.6 0.9 copy-start.2
  1.5 0.7 copy-start.3
  3.7 19.3 %all-to-all-start = ((bf16[32,2,2,2,4,128]{5,4,3,2,1,0:T(4,128)(2,1)}), bf16[32,2,2,2,4,128]{5,4,3,2,1,0:T(4,128)(2,1)S(1)}, u32[]{:S(2)}, u32[]{:S(2)}) async-start(bf16[32,2,2,2,4,128]{5,4,3,2,1,0:T(4,128)(2,1)} %bitcast.7), calls=%async_computation | async-start | bytes 524288 | tf_op jit(solution)/shard_map/all_to_all | solution.py:352
  14.1 1.0 copy-start
  15.1 1.0 copy-start.1
  23.0 4.1 %copy-start.8 = (s32[16,16]{1,0:T(8,128)S(1)}, s32[16,16]{1,0:T(8,128)}, u32[]{:S(2)}) copy-start(s32[16,16]{1,0:T(8,128)} %param.10) | copy-start | bytes 3076
  23.0 47.1 %copy-start.9 = (s32[1,16]{1,0:T(1,128)S(1)}, s32[1,16]{1,0:T(1,128)}, u32[]{:S(2)}) copy-start(s32[1,16]{1,0:T(1,128)} %param.11) | copy-start | bytes 196
  23.0 36.7 %all-to-all-start.1 = ((bf16[16,2,2,128,128]{4,3,2,1,0:T(8,128)(2,1)}), bf16[16,2,2,128,128]{4,3,2,1,0:T(8,128)(2,1)S(1)}, u32[]{:S(2)}, u32[]{:S(2)}) async-start(bf16[16,2,2,128,128]{4,3,2,1,0:T(8,128)(2,1)} %bitcast.14), calls=%async_computation.1 | async-start | bytes 4194304 | tf_op jit(solution)/shard_map/all_to_all | solution.py:365
  27.7 24.8 %collective-permute-start.1 = (bf16[2,2,8,8,128]{4,3,2,1,0:T(8,128)(2,1)S(1)}, bf16[2,2,8,8,128]{4,3,2,1,0:T(8,128)(2,1)S(1)}, u32[]{:S(2)}, u32[]{:S(2)}) collective-permute-start(bf16[2,2,8,8,128]{4,3,2,1,0:T(8,128)(2,1)S(1)} %get-tuple-element.48), channel_id=1, source_target_pairs={{0,4},{1,5},{2,6},{3,7},{4,0},{5,1},{6,2},{7,3},{8,12},{9,13},{10,... | collective-permute-start | bytes 196616 | tf_op jit(solution)/shard_map/ppermute | solution.py:314
  34.6 21.4 %collective-permute-start.2 = (bf16[2,2,8,8,128]{4,3,2,1,0:T(8,128)(2,1)S(1)}, bf16[2,2,8,8,128]{4,3,2,1,0:T(8,128)(2,1)S(1)}, u32[]{:S(2)}, u32[]{:S(2)}) collective-permute-start(bf16[2,2,8,8,128]{4,3,2,1,0:T(8,128)(2,1)S(1)} %get-tuple-element.47), channel_id=1, source_target_pairs={{0,11},{1,10},{2,9},{3,8},{4,15},{5,14},{6,13},{7,12},{8,3},{9,2},... | collective-permute-start | bytes 196616 | tf_op jit(solution)/shard_map/ppermute | solution.py:314
  43.9 12.1 %collective-permute-start = (bf16[2,2,8,8,128]{4,3,2,1,0:T(8,128)(2,1)S(1)}, bf16[2,2,8,8,128]{4,3,2,1,0:T(8,128)(2,1)S(1)}, u32[]{:S(2)}, u32[]{:S(2)}) collective-permute-start(bf16[2,2,8,8,128]{4,3,2,1,0:T(8,128)(2,1)S(1)} %get-tuple-element.47), channel_id=1, source_target_pairs={{0,15},{1,14},{2,13},{3,12},{4,11},{5,10},{6,9},{7,8},{8,7},{9,6},... | collective-permute-start | bytes 196616 | tf_op jit(solution)/shard_map/ppermute | solution.py:314
  45.9 10.3 %collective-permute-start.3 = (bf16[1,2,2,8,8,128]{5,4,3,2,1,0:T(8,128)(2,1)S(1)}, bf16[1,2,2,8,8,128]{5,4,3,2,1,0:T(8,128)(2,1)S(1)}, u32[]{:S(2)}, u32[]{:S(2)}) collective-permute-start(bf16[1,2,2,8,8,128]{5,4,3,2,1,0:T(8,128)(2,1)S(1)} %bitcast.38), channel_id=1, source_target_pairs={{0,1},{1,2},{2,3},{3,0},{4,5},{5,6},{6,7},{7,4},{8,9},{9,10},{10,1... | collective-permute-start | bytes 196616 | tf_op jit(solution)/shard_map/ppermute | solution.py:319
  49.4 9.2 %collective-permute-start.4 = (bf16[1,2,2,8,8,128]{5,4,3,2,1,0:T(8,128)(2,1)S(1)}, bf16[1,2,2,8,8,128]{5,4,3,2,1,0:T(8,128)(2,1)S(1)}, u32[]{:S(2)}, u32[]{:S(2)}) collective-permute-start(bf16[1,2,2,8,8,128]{5,4,3,2,1,0:T(8,128)(2,1)S(1)} %bitcast.39), channel_id=1, source_target_pairs={{0,2},{1,3},{2,0},{3,1},{4,6},{5,7},{6,4},{7,5},{8,10},{9,11},{10,... | collective-permute-start | bytes 196616 | tf_op jit(solution)/shard_map/ppermute | solution.py:319
  52.5 6.5 %collective-permute-start.5 = (bf16[1,2,2,8,8,128]{5,4,3,2,1,0:T(8,128)(2,1)S(1)}, bf16[1,2,2,8,8,128]{5,4,3,2,1,0:T(8,128)(2,1)S(1)}, u32[]{:S(2)}, u32[]{:S(2)}) collective-permute-start(bf16[1,2,2,8,8,128]{5,4,3,2,1,0:T(8,128)(2,1)S(1)} %bitcast.40), channel_id=1, source_target_pairs={{0,3},{1,0},{2,1},{3,2},{4,7},{5,4},{6,5},{7,6},{8,11},{9,8},{10,9... | collective-permute-start | bytes 196616 | tf_op jit(solution)/shard_map/ppermute | solution.py:319
  59.7 11.1 %collective-permute-start.6 = (bf16[3,2,2,8,8,128]{5,4,3,2,1,0:T(8,128)(2,1)S(1)}, bf16[3,2,2,8,8,128]{5,4,3,2,1,0:T(8,128)(2,1)S(1)}, u32[]{:S(2)}, u32[]{:S(2)}) collective-permute-start(bf16[3,2,2,8,8,128]{5,4,3,2,1,0:T(8,128)(2,1)S(1)} %pad_maximum_fusion.refs_4_), channel_id=1, source_target_pairs={{0,1},{1,2},{2,3},{3,0},{4,5},{5,6},{6,7},{7,4},{8,9},{9,10},{10,1... | collective-permute-start | bytes 589832 | tf_op jit(solution)/shard_map/ppermute | solution.py:319
  62.3 17.5 %collective-permute-start.7 = (bf16[3,2,2,8,8,128]{5,4,3,2,1,0:T(8,128)(2,1)S(1)}, bf16[3,2,2,8,8,128]{5,4,3,2,1,0:T(8,128)(2,1)S(1)}, u32[]{:S(2)}, u32[]{:S(2)}) collective-permute-start(bf16[3,2,2,8,8,128]{5,4,3,2,1,0:T(8,128)(2,1)S(1)} %pad_maximum_fusion.refs_4_), channel_id=1, source_target_pairs={{0,2},{1,3},{2,0},{3,1},{4,6},{5,7},{6,4},{7,5},{8,10},{9,11},{10,... | collective-permute-start | bytes 589832 | tf_op jit(solution)/shard_map/ppermute | solution.py:319
  68.1 11.6 %collective-permute-start.8 = (bf16[3,2,2,8,8,128]{5,4,3,2,1,0:T(8,128)(2,1)S(1)}, bf16[3,2,2,8,8,128]{5,4,3,2,1,0:T(8,128)(2,1)S(1)}, u32[]{:S(2)}, u32[]{:S(2)}) collective-permute-start(bf16[3,2,2,8,8,128]{5,4,3,2,1,0:T(8,128)(2,1)S(1)} %pad_maximum_fusion.refs_4_), channel_id=1, source_target_pairs={{0,3},{1,0},{2,1},{3,2},{4,7},{5,4},{6,5},{7,6},{8,11},{9,8},{10,9... | collective-permute-start | bytes 589832 | tf_op jit(solution)/shard_map/ppermute | solution.py:319
  79.8 0.8 copy-start.7
  89.9 57.0 %copy-start.5 = (s32[1,16,2]{1,2,0:T(2,128)S(1)}, s32[1,16,2]{1,2,0:T(2,128)}, u32[]{:S(2)}) copy-start(s32[1,16,2]{1,2,0:T(2,128)} %param.9) | copy-start | bytes 388
  89.9 20.7 %collective-permute-start.10 = (bf16[2,2,2,8,8,128]{5,4,3,2,1,0:T(8,128)(2,1)S(1)}, bf16[2,2,2,8,8,128]{5,4,3,2,1,0:T(8,128)(2,1)S(1)}, u32[]{:S(2)}, u32[]{:S(2)}) collective-permute-start(bf16[2,2,2,8,8,128]{5,4,3,2,1,0:T(8,128)(2,1)S(1)} %get-tuple-element.65), channel_id=1, source_target_pairs={{0,2},{1,3},{2,0},{3,1},{4,6},{5,7},{6,4},{7,5},{8,10},{9,11},{10,... | collective-permute-start | bytes 393224 | tf_op jit(solution)/shard_map/ppermute | solution.py:319
  95.4 15.2 %collective-permute-start.11 = (bf16[2,2,2,8,8,128]{5,4,3,2,1,0:T(8,128)(2,1)S(1)}, bf16[2,2,2,8,8,128]{5,4,3,2,1,0:T(8,128)(2,1)S(1)}, u32[]{:S(2)}, u32[]{:S(2)}) collective-permute-start(bf16[2,2,2,8,8,128]{5,4,3,2,1,0:T(8,128)(2,1)S(1)} %get-tuple-element.66), channel_id=1, source_target_pairs={{0,1},{1,2},{2,3},{3,0},{4,5},{5,6},{6,7},{7,4},{8,9},{9,10},{10,1... | collective-permute-start | bytes 393224 | tf_op jit(solution)/shard_map/ppermute | solution.py:319
  98.4 12.3 %collective-permute-start.9 = (bf16[2,2,2,8,8,128]{5,4,3,2,1,0:T(8,128)(2,1)S(1)}, bf16[2,2,2,8,8,128]{5,4,3,2,1,0:T(8,128)(2,1)S(1)}, u32[]{:S(2)}, u32[]{:S(2)}) collective-permute-start(bf16[2,2,2,8,8,128]{5,4,3,2,1,0:T(8,128)(2,1)S(1)} %get-tuple-element.64), channel_id=1, source_target_pairs={{0,3},{1,0},{2,1},{3,2},{4,7},{5,4},{6,5},{7,6},{8,11},{9,8},{10,9... | collective-permute-start | bytes 393224 | tf_op jit(solution)/shard_map/ppermute | solution.py:319
  102.5 47.8 %all-to-all-start.2 = ((bf16[16,2,128,128]{3,2,1,0:T(8,128)(2,1)}), bf16[16,2,128,128]{3,2,1,0:T(8,128)(2,1)S(1)}, u32[]{:S(2)}, u32[]{:S(2)}) async-start(bf16[16,2,128,128]{3,2,1,0:T(8,128)(2,1)} %bitcast.17), calls=%async_computation.2 | async-start | bytes 2097152 | tf_op jit(solution)/shard_map/all_to_all | solution.py:379
  110.7 18.9 %collective-permute-start.12 = (bf16[2,2,2,8,8,128]{5,4,3,2,1,0:T(8,128)(2,1)S(1)}, bf16[2,2,2,8,8,128]{5,4,3,2,1,0:T(8,128)(2,1)S(1)}, u32[]{:S(2)}, u32[]{:S(2)}) collective-permute-start(bf16[2,2,2,8,8,128]{5,4,3,2,1,0:T(8,128)(2,1)S(1)} %add_convert_fusion), channel_id=1, source_target_pairs={{0,4},{1,5},{2,6},{3,7},{4,0},{5,1},{6,2},{7,3},{8,12},{9,13},{10,... | collective-permute-start | bytes 393224 | tf_op jit(solution)/shard_map/ppermute | solution.py:314
  117.1 12.5 %collective-permute-start.13 = (bf16[1,2,2,8,8,128]{5,4,3,2,1,0:T(8,128)(2,1)S(1)}, bf16[1,2,2,8,8,128]{5,4,3,2,1,0:T(8,128)(2,1)S(1)}, u32[]{:S(2)}, u32[]{:S(2)}) collective-permute-start(bf16[1,2,2,8,8,128]{5,4,3,2,1,0:T(8,128)(2,1)S(1)} %get-tuple-element.76), channel_id=1, source_target_pairs={{0,3},{1,0},{2,1},{3,2},{4,7},{5,4},{6,5},{7,6},{8,11},{9,8},{10,9... | collective-permute-start | bytes 196616 | tf_op jit(solution)/shard_map/ppermute | solution.py:319
  120.3 13.4 %collective-permute-start.14 = (bf16[1,2,2,8,8,128]{5,4,3,2,1,0:T(8,128)(2,1)S(1)}, bf16[1,2,2,8,8,128]{5,4,3,2,1,0:T(8,128)(2,1)S(1)}, u32[]{:S(2)}, u32[]{:S(2)}) collective-permute-start(bf16[1,2,2,8,8,128]{5,4,3,2,1,0:T(8,128)(2,1)S(1)} %get-tuple-element.77), channel_id=1, source_target_pairs={{0,2},{1,3},{2,0},{3,1},{4,6},{5,7},{6,4},{7,5},{8,10},{9,11},{10,... | collective-permute-start | bytes 196616 | tf_op jit(solution)/shard_map/ppermute | solution.py:319
  122.3 11.5 %collective-permute-start.15 = (bf16[1,2,2,8,8,128]{5,4,3,2,1,0:T(8,128)(2,1)S(1)}, bf16[1,2,2,8,8,128]{5,4,3,2,1,0:T(8,128)(2,1)S(1)}, u32[]{:S(2)}, u32[]{:S(2)}) collective-permute-start(bf16[1,2,2,8,8,128]{5,4,3,2,1,0:T(8,128)(2,1)S(1)} %get-tuple-element.78), channel_id=1, source_target_pairs={{0,1},{1,2},{2,3},{3,0},{4,5},{5,6},{6,7},{7,4},{8,9},{9,10},{10,1... | collective-permute-start | bytes 196616 | tf_op jit(solution)/shard_map/ppermute | solution.py:319
  133.8 13.2 %collective-permute-start.19 = (bf16[2,2,8,8,128]{4,3,2,1,0:T(8,128)(2,1)S(1)}, bf16[2,2,8,8,128]{4,3,2,1,0:T(8,128)(2,1)S(1)}, u32[]{:S(2)}, u32[]{:S(2)}) collective-permute-start(bf16[2,2,8,8,128]{4,3,2,1,0:T(8,128)(2,1)S(1)} %fusion), channel_id=1, source_target_pairs={{0,15},{1,14},{2,13},{3,12},{4,11},{5,10},{6,9},{7,8},{8,7},{9,6},... | collective-permute-start | bytes 196616 | tf_op jit(solution)/shard_map/ppermute | solution.py:314
  135.7 11.3 %collective-permute-start.16 = (bf16[1,2,2,8,8,128]{5,4,3,2,1,0:T(8,128)(2,1)S(1)}, bf16[1,2,2,8,8,128]{5,4,3,2,1,0:T(8,128)(2,1)S(1)}, u32[]{:S(2)}, u32[]{:S(2)}) collective-permute-start(bf16[1,2,2,8,8,128]{5,4,3,2,1,0:T(8,128)(2,1)S(1)} %get-tuple-element.80), channel_id=1, source_target_pairs={{0,3},{1,0},{2,1},{3,2},{4,7},{5,4},{6,5},{7,6},{8,11},{9,8},{10,9... | collective-permute-start | bytes 196616 | tf_op jit(solution)/shard_map/ppermute | solution.py:319
  141.5 6.6 %collective-permute-start.17 = (bf16[1,2,2,8,8,128]{5,4,3,2,1,0:T(8,128)(2,1)S(1)}, bf16[1,2,2,8,8,128]{5,4,3,2,1,0:T(8,128)(2,1)S(1)}, u32[]{:S(2)}, u32[]{:S(2)}) collective-permute-start(bf16[1,2,2,8,8,128]{5,4,3,2,1,0:T(8,128)(2,1)S(1)} %get-tuple-element.81), channel_id=1, source_target_pairs={{0,2},{1,3},{2,0},{3,1},{4,6},{5,7},{6,4},{7,5},{8,10},{9,11},{10,... | collective-permute-start | bytes 196616 | tf_op jit(solution)/shard_map/ppermute | solution.py:319
  143.5 6.8 %collective-permute-start.18 = (bf16[1,2,2,8,8,128]{5,4,3,2,1,0:T(8,128)(2,1)S(1)}, bf16[1,2,2,8,8,128]{5,4,3,2,1,0:T(8,128)(2,1)S(1)}, u32[]{:S(2)}, u32[]{:S(2)}) collective-permute-start(bf16[1,2,2,8,8,128]{5,4,3,2,1,0:T(8,128)(2,1)S(1)} %get-tuple-element.82), channel_id=1, source_target_pairs={{0,1},{1,2},{2,3},{3,0},{4,5},{5,6},{6,7},{7,4},{8,9},{9,10},{10,1... | collective-permute-start | bytes 196616 | tf_op jit(solution)/shard_map/ppermute | solution.py:319
  151.7 19.6 %all-to-all-start.3 = ((bf16[32,2,2,2,4,128]{5,4,3,2,1,0:T(4,128)(2,1)}), bf16[32,2,2,2,4,128]{5,4,3,2,1,0:T(4,128)(2,1)S(1)}, u32[]{:S(2)}, u32[]{:S(2)}) async-start(bf16[32,2,2,2,4,128]{5,4,3,2,1,0:T(4,128)(2,1)} %bitcast.21), calls=%async_computation.3 | async-start | bytes 524288 | tf_op jit(solution)/shard_map/all_to_all | solution.py:352
  (2 other events, 1.3 us)

commit v12 on v10

--- a/solution.py
+++ b/solution.py
@@ -14,8 +14,8 @@
 SCALING = HD ** (-0.5)
 LOG2E = 1.4426950408889634
 PLANE = ("dp", "xh")
-MIRROR = 15
-ACROSS = 4
+MIRROR = 12
+ACROSS = 7
 NEAR = 4
 
 
@@ -121,7 +121,16 @@
         dqt[block] = jnp.zeros_like(dqt[block])
         return 0
 
-    lax.fori_loop(0, blocks, diagonal_products, 0, unroll=2)
+    lax.fori_loop(0, blocks, diagonal_products, 0, unroll=4)
+
+    def sweep(begin, end, step, state):
+        twice = (end - begin) >> 1
+
+        def two(index, state):
+            return step(begin + 2 * index + 1, step(begin + 2 * index, state))
+
+        state = lax.fori_loop(0, twice, two, state)
+        return lax.fori_loop(begin + 2 * twice, end, step, state)
 
     def query_block(block, _):
         query, grad = operands(block)
@@ -135,7 +144,7 @@
             dprobs[other] = matmul(v_all[other], grad, ((1,), (1,)))
             return jnp.maximum(peak, jnp.max(score, axis=0, keepdims=True))
 
-        peak = lax.fori_loop(lowest, block, products, stats[block, 0][:1])
+        peak = sweep(lowest, block, products, stats[block, 0][:1])
         shift = peak * factor
 
         def sums(other, totals):
@@ -152,7 +161,7 @@
             jnp.sum(weights, axis=0, keepdims=True),
             jnp.sum(weights * diagonal_dprobs[block], axis=0, keepdims=True),
         )
-        total, weighted = lax.fori_loop(lowest, block, sums, totals)
+        total, weighted = sweep(lowest, block, sums, totals)
         inverse = 1.0 / total
         delta = weighted * inverse
         stats[block, 0] = jnp.broadcast_to(inverse, stats.shape[2:])
@@ -167,7 +176,7 @@
             dqt[block] += grad_query
             return 0
 
-        lax.fori_loop(lowest, block, earlier, 0)
+        sweep(lowest, block, earlier, 0)
         return 0
 
     lax.fori_loop(0, blocks, query_block, 0)
@@ -185,7 +194,7 @@
         dq_ref[recv_ref[PAIR * block + 1]] = result[tile_rows:]
         return 0
 
-    lax.fori_loop(0, blocks, diagonal_terms, 0, unroll=2)
+    lax.fori_loop(0, blocks, diagonal_terms, 0, unroll=4)
 
     def unstage(block, _):
         for slot, ref in enumerate(dkv_refs):

time: 169 us -> 164 us (0.970)
  waiting for transfers between devices: 46.6 us -> 37.9 us
  starting transfers between devices: 95.8 us -> 99.5 us
    ppermute x5, waiting for transfers between devices: 14.4 us -> 4.32 us  [far_swap(): lax.ppermute(values, 'z', [(place, place ^ flip) for place in range(16)])]
    ppermute x5, starting transfers between devices: 26.3 us -> 30.8 us  [far_swap(): lax.ppermute(values, 'z', [(place, place ^ flip) for place in range(16)])]
    all_to_all x1, starting transfers between devices: 8.89 us -> 5.49 us  [on_device(): lax.all_to_all(query_back.reshape(n_replicas, slot_cap, tile_rows, row_wi...]
    all_to_all x2, starting transfers between devices: 16.3 us -> 18.7 us  [over_plane(): lax.all_to_all(values.reshape((2 * n_replicas,) + values.shape[2:]), PLAN...]
  transfers between devices with their start and end apart: 21 -> 21, of which waited for: 9 -> 8; matrix products, arithmetic and copies ran while one was open for 1% -> 1% of each run, Pallas kernels for 2% -> 2%
where the time goes in v12:
time: 164 us; the launch traced here: 163 us
  starting transfers between devices  99.5 us (61%)
  waiting for transfers between devices  37.9 us (23%)
  Pallas kernels  16.6 us (10%)
  local copies, waits for them, and re-layouts  7.24 us (4%)
    ppermute x12, starting transfers between devices, near_shift(): return lax.ppermute(values, 'z', pairs)  40.4 us
    ppermute x5, starting transfers between devices, far_swap(): lax.ppermute(values, 'z', [(place, place ^ flip) for place in range(16)])  30.8 us
    ppermute x12, waiting for transfers between devices, near_shift(): return lax.ppermute(values, 'z', pairs)  22.1 us
    all_to_all x2, starting transfers between devices, over_plane(): lax.all_to_all(values.reshape((2 * n_replicas,) + values.shape[2:]), PLAN...  18.7 us
    all_to_all x2, waiting for transfers between devices, over_plane(): lax.all_to_all(values.reshape((2 * n_replicas,) + values.shape[2:]), PLAN...  11.4 us
    pallas_call x1, Pallas kernels, attention(): pl.pallas_call(attention_kernel, out_shape=(jax.ShapeDtypeStruct((slots,...  9.78 us
    unnamed x20, local copies, waits for them, and re-layouts  5.82 us
    all_to_all x1, starting transfers between devices, on_device(): lax.all_to_all(query_back.reshape(n_replicas, slot_cap, tile_rows, row_wi...  5.49 us
  transfers between devices with their start and end apart: 21, of which 8 were waited for; matrix products, arithmetic and copies ran while one was open for 1% of the time, Pallas kernels for 2%

profile of v12, /device:TPU:1, one launch (start us, length us, event | category | flops | bytes accessed | tf_op | source)
XLA Modules:
  0.0 162.9 jit_solution(8300012284067007113)
XLA Ops:
  2.2 1.4 kv_pack.1
  3.7 10.4 %all-to-all-start = ((bf16[32,2,2,2,4,128]{5,4,3,2,1,0:T(4,128)(2,1)}), bf16[32,2,2,2,4,128]{5,4,3,2,1,0:T(4,128)(2,1)S(1)}, u32[]{:S(2)}, u32[]{:S(2)}) async-start(bf16[32,2,2,2,4,128]{5,4,3,2,1,0:T(4,128)(2,1)} %bitcast.7), calls=%async_computation | async-start | bytes 524288 | tf_op jit(solution)/shard_map/all_to_all | solution.py:356
  16.8 2.1 %pack_rows.1 = bf16[32,2,128,128]{3,2,1,0:T(8,128)(2,1)} custom-call(s32[2,16]{1,0:T(2,128)S(1)} %bitcast.38, bf16[16,128,128]{2,1,0:T(8,128)(2,1)S(1)} %copy-done, bf16[16,128,128]{2,1,0:T(8,128)(2,1)S(1)} %copy-done.1), custom_call_target="tpu_custom_call" | custom-call | tf_op jit(solution)/shard_map/pack_rows/pallas_call | solution.py:38
  19.0 4.0 %all-to-all-done = bf16[32,2,2,2,4,128]{5,4,3,2,1,0:T(4,128)(2,1)S(1)} async-done(((bf16[32,2,2,2,4,128]{5,4,3,2,1,0:T(4,128)(2,1)}), bf16[32,2,2,2,4,128]{5,4,3,2,1,0:T(4,128)(2,1)S(1)}, u32[]{:S(2)}, u32[]{:S(2)}) %all-to-all-start) | async-done | bytes 262176 | tf_op jit(solution)/shard_map/all_to_all | solution.py:356
  23.0 4.1 %all-to-all-start.1 = ((bf16[16,2,2,128,128]{4,3,2,1,0:T(8,128)(2,1)}), bf16[16,2,2,128,128]{4,3,2,1,0:T(8,128)(2,1)S(1)}, u32[]{:S(2)}, u32[]{:S(2)}) async-start(bf16[16,2,2,128,128]{4,3,2,1,0:T(8,128)(2,1)} %bitcast.14), calls=%async_computation.1 | async-start | bytes 4194304 | tf_op jit(solution)/shard_map/all_to_all | solution.py:369
  27.7 11.0 %collective-permute-start.1 = (bf16[2,2,8,8,128]{4,3,2,1,0:T(8,128)(2,1)S(1)}, bf16[2,2,8,8,128]{4,3,2,1,0:T(8,128)(2,1)S(1)}, u32[]{:S(2)}, u32[]{:S(2)}) collective-permute-start(bf16[2,2,8,8,128]{4,3,2,1,0:T(8,128)(2,1)S(1)} %get-tuple-element.31), channel_id=1, source_target_pairs={{0,7},{1,6},{2,5},{3,4},{4,3},{5,2},{6,1},{7,0},{8,15},{9,14},{10,... | collective-permute-start | bytes 196616 | tf_op jit(solution)/shard_map/ppermute | solution.py:318
  38.7 3.9 %collective-permute-start.2 = (bf16[2,2,8,8,128]{4,3,2,1,0:T(8,128)(2,1)S(1)}, bf16[2,2,8,8,128]{4,3,2,1,0:T(8,128)(2,1)S(1)}, u32[]{:S(2)}, u32[]{:S(2)}) collective-permute-start(bf16[2,2,8,8,128]{4,3,2,1,0:T(8,128)(2,1)S(1)} %get-tuple-element.30), channel_id=1, source_target_pairs={{0,11},{1,10},{2,9},{3,8},{4,15},{5,14},{6,13},{7,12},{8,3},{9,2},... | collective-permute-start | bytes 196616 | tf_op jit(solution)/shard_map/ppermute | solution.py:318
  42.6 2.3 %collective-permute-start = (bf16[2,2,8,8,128]{4,3,2,1,0:T(8,128)(2,1)S(1)}, bf16[2,2,8,8,128]{4,3,2,1,0:T(8,128)(2,1)S(1)}, u32[]{:S(2)}, u32[]{:S(2)}) collective-permute-start(bf16[2,2,8,8,128]{4,3,2,1,0:T(8,128)(2,1)S(1)} %get-tuple-element.30), channel_id=1, source_target_pairs={{0,12},{1,13},{2,14},{3,15},{4,8},{5,9},{6,10},{7,11},{8,4},{9,5},... | collective-permute-start | bytes 196616 | tf_op jit(solution)/shard_map/ppermute | solution.py:318
  44.9 4.0 %collective-permute-start.3 = (bf16[1,2,2,8,8,128]{5,4,3,2,1,0:T(8,128)(2,1)S(1)}, bf16[1,2,2,8,8,128]{5,4,3,2,1,0:T(8,128)(2,1)S(1)}, u32[]{:S(2)}, u32[]{:S(2)}) collective-permute-start(bf16[1,2,2,8,8,128]{5,4,3,2,1,0:T(8,128)(2,1)S(1)} %bitcast.40), channel_id=1, source_target_pairs={{0,1},{1,2},{2,3},{3,0},{4,5},{5,6},{6,7},{7,4},{8,9},{9,10},{10,1... | collective-permute-start | bytes 196616 | tf_op jit(solution)/shard_map/ppermute | solution.py:323
  49.0 4.0 %collective-permute-start.4 = (bf16[1,2,2,8,8,128]{5,4,3,2,1,0:T(8,128)(2,1)S(1)}, bf16[1,2,2,8,8,128]{5,4,3,2,1,0:T(8,128)(2,1)S(1)}, u32[]{:S(2)}, u32[]{:S(2)}) collective-permute-start(bf16[1,2,2,8,8,128]{5,4,3,2,1,0:T(8,128)(2,1)S(1)} %bitcast.41), channel_id=1, source_target_pairs={{0,2},{1,3},{2,0},{3,1},{4,6},{5,7},{6,4},{7,5},{8,10},{9,11},{10,... | collective-permute-start | bytes 196616 | tf_op jit(solution)/shard_map/ppermute | solution.py:323
  53.0 3.5 %collective-permute-start.5 = (bf16[1,2,2,8,8,128]{5,4,3,2,1,0:T(8,128)(2,1)S(1)}, bf16[1,2,2,8,8,128]{5,4,3,2,1,0:T(8,128)(2,1)S(1)}, u32[]{:S(2)}, u32[]{:S(2)}) collective-permute-start(bf16[1,2,2,8,8,128]{5,4,3,2,1,0:T(8,128)(2,1)S(1)} %bitcast.42), channel_id=1, source_target_pairs={{0,3},{1,0},{2,1},{3,2},{4,7},{5,4},{6,5},{7,6},{8,11},{9,8},{10,9... | collective-permute-start | bytes 196616 | tf_op jit(solution)/shard_map/ppermute | solution.py:323
  56.6 2.3 %collective-permute-done.4.refs_2_ = bf16[1,2,2,8,8,128]{5,4,3,2,1,0:T(8,128)(2,1)S(1)} collective-permute-done((bf16[1,2,2,8,8,128]{5,4,3,2,1,0:T(8,128)(2,1)S(1)}, bf16[1,2,2,8,8,128]{5,4,3,2,1,0:T(8,128)(2,1)S(1)}, u32[]{:S(2)}, u32[]{:S(2)}) %collective-permute-start.4) | collective-permute-done | bytes 65568 | tf_op jit(solution)/shard_map/ppermute | solution.py:323
  59.8 3.3 %collective-permute-start.6 = (bf16[3,2,2,8,8,128]{5,4,3,2,1,0:T(8,128)(2,1)S(1)}, bf16[3,2,2,8,8,128]{5,4,3,2,1,0:T(8,128)(2,1)S(1)}, u32[]{:S(2)}, u32[]{:S(2)}) collective-permute-start(bf16[3,2,2,8,8,128]{5,4,3,2,1,0:T(8,128)(2,1)S(1)} %pad_maximum_fusion.refs_4_), channel_id=1, source_target_pairs={{0,1},{1,2},{2,3},{3,0},{4,5},{5,6},{6,7},{7,4},{8,9},{9,10},{10,1... | collective-permute-start | bytes 589832 | tf_op jit(solution)/shard_map/ppermute | solution.py:323
  63.1 3.8 %collective-permute-start.7 = (bf16[3,2,2,8,8,128]{5,4,3,2,1,0:T(8,128)(2,1)S(1)}, bf16[3,2,2,8,8,128]{5,4,3,2,1,0:T(8,128)(2,1)S(1)}, u32[]{:S(2)}, u32[]{:S(2)}) collective-permute-start(bf16[3,2,2,8,8,128]{5,4,3,2,1,0:T(8,128)(2,1)S(1)} %pad_maximum_fusion.refs_4_), channel_id=1, source_target_pairs={{0,2},{1,3},{2,0},{3,1},{4,6},{5,7},{6,4},{7,5},{8,10},{9,11},{10,... | collective-permute-start | bytes 589832 | tf_op jit(solution)/shard_map/ppermute | solution.py:323
  67.0 2.1 %collective-permute-start.8 = (bf16[3,2,2,8,8,128]{5,4,3,2,1,0:T(8,128)(2,1)S(1)}, bf16[3,2,2,8,8,128]{5,4,3,2,1,0:T(8,128)(2,1)S(1)}, u32[]{:S(2)}, u32[]{:S(2)}) collective-permute-start(bf16[3,2,2,8,8,128]{5,4,3,2,1,0:T(8,128)(2,1)S(1)} %pad_maximum_fusion.refs_4_), channel_id=1, source_target_pairs={{0,3},{1,0},{2,1},{3,2},{4,7},{5,4},{6,5},{7,6},{8,11},{9,8},{10,9... | collective-permute-start | bytes 589832 | tf_op jit(solution)/shard_map/ppermute | solution.py:323
  69.3 9.5 %collective-permute-done.7.refs_6_ = bf16[3,2,2,8,8,128]{5,4,3,2,1,0:T(8,128)(2,1)S(1)} collective-permute-done((bf16[3,2,2,8,8,128]{5,4,3,2,1,0:T(8,128)(2,1)S(1)}, bf16[3,2,2,8,8,128]{5,4,3,2,1,0:T(8,128)(2,1)S(1)}, u32[]{:S(2)}, u32[]{:S(2)}) %collective-permute-start.7) | collective-permute-done | bytes 196640 | tf_op jit(solution)/shard_map/ppermute | solution.py:323
  79.6 9.8 %attention_backward.1 = (bf16[32,128,128]{2,1,0:T(8,128)(2,1)}, bf16[2,2,2,8,8,128]{5,4,3,2,1,0:T(8,128)(2,1)S(1)}, bf16[2,2,2,8,8,128]{5,4,3,2,1,0:T(8,128)(2,1...) custom-call(s32[16]{0:T(128)S(1)} %dynamic-slice_bitcast_fusion.recv, ...), custom_call_target="tpu_custom_call" | custom-call | flops 2000000000 | bytes 6291456 | tf_op jit(solution)/shard_map/attention_backward/pallas_call | solution.py:216
  89.4 5.4 %collective-permute-start.10 = (bf16[2,2,2,8,8,128]{5,4,3,2,1,0:T(8,128)(2,1)S(1)}, bf16[2,2,2,8,8,128]{5,4,3,2,1,0:T(8,128)(2,1)S(1)}, u32[]{:S(2)}, u32[]{:S(2)}) collective-permute-start(bf16[2,2,2,8,8,128]{5,4,3,2,1,0:T(8,128)(2,1)S(1)} %get-tuple-element.44), channel_id=1, source_target_pairs={{0,2},{1,3},{2,0},{3,1},{4,6},{5,7},{6,4},{7,5},{8,10},{9,11},{10,... | collective-permute-start | bytes 393224 | tf_op jit(solution)/shard_map/ppermute | solution.py:323
  94.8 2.9 %collective-permute-start.11 = (bf16[2,2,2,8,8,128]{5,4,3,2,1,0:T(8,128)(2,1)S(1)}, bf16[2,2,2,8,8,128]{5,4,3,2,1,0:T(8,128)(2,1)S(1)}, u32[]{:S(2)}, u32[]{:S(2)}) collective-permute-start(bf16[2,2,2,8,8,128]{5,4,3,2,1,0:T(8,128)(2,1)S(1)} %get-tuple-element.45), channel_id=1, source_target_pairs={{0,1},{1,2},{2,3},{3,0},{4,5},{5,6},{6,7},{7,4},{8,9},{9,10},{10,1... | collective-permute-start | bytes 393224 | tf_op jit(solution)/shard_map/ppermute | solution.py:323
  97.7 4.1 %collective-permute-start.9 = (bf16[2,2,2,8,8,128]{5,4,3,2,1,0:T(8,128)(2,1)S(1)}, bf16[2,2,2,8,8,128]{5,4,3,2,1,0:T(8,128)(2,1)S(1)}, u32[]{:S(2)}, u32[]{:S(2)}) collective-permute-start(bf16[2,2,2,8,8,128]{5,4,3,2,1,0:T(8,128)(2,1)S(1)} %get-tuple-element.43), channel_id=1, source_target_pairs={{0,3},{1,0},{2,1},{3,2},{4,7},{5,4},{6,5},{7,6},{8,11},{9,8},{10,9... | collective-permute-start | bytes 393224 | tf_op jit(solution)/shard_map/ppermute | solution.py:323
  101.9 5.5 %all-to-all-start.2 = ((bf16[16,2,128,128]{3,2,1,0:T(8,128)(2,1)}), bf16[16,2,128,128]{3,2,1,0:T(8,128)(2,1)S(1)}, u32[]{:S(2)}, u32[]{:S(2)}) async-start(bf16[16,2,128,128]{3,2,1,0:T(8,128)(2,1)} %bitcast.18), calls=%async_computation.2 | async-start | bytes 2097152 | tf_op jit(solution)/shard_map/all_to_all | solution.py:383
  107.5 9.0 %collective-permute-start.12 = (bf16[2,2,2,8,8,128]{5,4,3,2,1,0:T(8,128)(2,1)S(1)}, bf16[2,2,2,8,8,128]{5,4,3,2,1,0:T(8,128)(2,1)S(1)}, u32[]{:S(2)}, u32[]{:S(2)}) collective-permute-start(bf16[2,2,2,8,8,128]{5,4,3,2,1,0:T(8,128)(2,1)S(1)} %add_convert_fusion.1), channel_id=1, source_target_pairs={{0,7},{1,6},{2,5},{3,4},{4,3},{5,2},{6,1},{7,0},{8,15},{9,14},{10,... | collective-permute-start | bytes 393224 | tf_op jit(solution)/shard_map/ppermute | solution.py:318
  116.8 1.9 %collective-permute-start.13 = (bf16[2,2,2,8,8,128]{5,4,3,2,1,0:T(8,128)(2,1)S(1)}, bf16[2,2,2,8,8,128]{5,4,3,2,1,0:T(8,128)(2,1)S(1)}, u32[]{:S(2)}, u32[]{:S(2)}) collective-permute-start(bf16[2,2,2,8,8,128]{5,4,3,2,1,0:T(8,128)(2,1)S(1)} %get-tuple-element.51), channel_id=1, source_target_pairs={{0,3},{1,0},{2,1},{3,2},{4,7},{5,4},{6,5},{7,6},{8,11},{9,8},{10,9... | collective-permute-start | bytes 393224 | tf_op jit(solution)/shard_map/ppermute | solution.py:323
  118.7 2.5 %collective-permute-start.14 = (bf16[2,2,2,8,8,128]{5,4,3,2,1,0:T(8,128)(2,1)S(1)}, bf16[2,2,2,8,8,128]{5,4,3,2,1,0:T(8,128)(2,1)S(1)}, u32[]{:S(2)}, u32[]{:S(2)}) collective-permute-start(bf16[2,2,2,8,8,128]{5,4,3,2,1,0:T(8,128)(2,1)S(1)} %get-tuple-element.52), channel_id=1, source_target_pairs={{0,2},{1,3},{2,0},{3,1},{4,6},{5,7},{6,4},{7,5},{8,10},{9,11},{10,... | collective-permute-start | bytes 393224 | tf_op jit(solution)/shard_map/ppermute | solution.py:323
  121.2 2.8 %collective-permute-start.15 = (bf16[2,2,2,8,8,128]{5,4,3,2,1,0:T(8,128)(2,1)S(1)}, bf16[2,2,2,8,8,128]{5,4,3,2,1,0:T(8,128)(2,1)S(1)}, u32[]{:S(2)}, u32[]{:S(2)}) collective-permute-start(bf16[2,2,2,8,8,128]{5,4,3,2,1,0:T(8,128)(2,1)S(1)} %get-tuple-element.53), channel_id=1, source_target_pairs={{0,1},{1,2},{2,3},{3,0},{4,5},{5,6},{6,7},{7,4},{8,9},{9,10},{10,1... | collective-permute-start | bytes 393224 | tf_op jit(solution)/shard_map/ppermute | solution.py:323
  124.2 9.8 %collective-permute-done.14 = bf16[2,2,2,8,8,128]{5,4,3,2,1,0:T(8,128)(2,1)S(1)} collective-permute-done((bf16[2,2,2,8,8,128]{5,4,3,2,1,0:T(8,128)(2,1)S(1)}, bf16[2,2,2,8,8,128]{5,4,3,2,1,0:T(8,128)(2,1)S(1)}, u32[]{:S(2)}, u32[]{:S(2)}) %collective-permute-start.14) | collective-permute-done | bytes 131104 | tf_op jit(solution)/shard_map/ppermute | solution.py:323
  134.1 4.6 %collective-permute-start.16 = (bf16[2,2,8,8,128]{4,3,2,1,0:T(8,128)(2,1)S(1)}, bf16[2,2,8,8,128]{4,3,2,1,0:T(8,128)(2,1)S(1)}, u32[]{:S(2)}, u32[]{:S(2)}) collective-permute-start(bf16[2,2,8,8,128]{4,3,2,1,0:T(8,128)(2,1)S(1)} %get-tuple-element.58), channel_id=1, source_target_pairs={{0,12},{1,13},{2,14},{3,15},{4,8},{5,9},{6,10},{7,11},{8,4},{9,5},... | collective-permute-start | bytes 196616 | tf_op jit(solution)/shard_map/ppermute | solution.py:318
  138.8 4.3 %collective-permute-done.16.other_ref = bf16[2,2,8,8,128]{4,3,2,1,0:T(8,128)(2,1)S(1)} collective-permute-done((bf16[2,2,8,8,128]{4,3,2,1,0:T(8,128)(2,1)S(1)}, bf16[2,2,8,8,128]{4,3,2,1,0:T(8,128)(2,1)S(1)}, u32[]{:S(2)}, u32[]{:S(2)}) %collective-permute-start.16) | collective-permute-done | bytes 65568 | tf_op jit(solution)/shard_map/ppermute | solution.py:318
  143.1 1.3 kv_back.1
  144.4 8.3 %all-to-all-start.3 = ((bf16[32,2,2,2,4,128]{5,4,3,2,1,0:T(4,128)(2,1)}), bf16[32,2,2,2,4,128]{5,4,3,2,1,0:T(4,128)(2,1)S(1)}, u32[]{:S(2)}, u32[]{:S(2)}) async-start(bf16[32,2,2,2,4,128]{5,4,3,2,1,0:T(4,128)(2,1)} %bitcast.22), calls=%async_computation.3 | async-start | bytes 524288 | tf_op jit(solution)/shard_map/all_to_all | solution.py:356
  152.8 1.4 gather_fusion
  154.2 7.4 %all-to-all-done.3 = bf16[32,2,2,2,4,128]{5,4,3,2,1,0:T(4,128)(2,1)S(1)} async-done(((bf16[32,2,2,2,4,128]{5,4,3,2,1,0:T(4,128)(2,1)}), bf16[32,2,2,2,4,128]{5,4,3,2,1,0:T(4,128)(2,1)S(1)}, u32[]{:S(2)}, u32[]{:S(2)}) %all-to-all-start.3) | async-done | bytes 262176 | tf_op jit(solution)/shard_map/all_to_all | solution.py:356
  (50 shorter events, 8.9 us)
Async XLA Ops:
  0.6 0.9 copy-start.2
  1.5 0.7 copy-start.3
  3.7 19.3 %all-to-all-start = ((bf16[32,2,2,2,4,128]{5,4,3,2,1,0:T(4,128)(2,1)}), bf16[32,2,2,2,4,128]{5,4,3,2,1,0:T(4,128)(2,1)S(1)}, u32[]{:S(2)}, u32[]{:S(2)}) async-start(bf16[32,2,2,2,4,128]{5,4,3,2,1,0:T(4,128)(2,1)} %bitcast.7), calls=%async_computation | async-start | bytes 524288 | tf_op jit(solution)/shard_map/all_to_all | solution.py:356
  14.1 1.0 copy-start
  15.1 1.0 copy-start.1
  16.2 0.7 copy-start.4
  23.0 4.1 %copy-start.8 = (s32[16,16]{1,0:T(8,128)S(1)}, s32[16,16]{1,0:T(8,128)}, u32[]{:S(2)}) copy-start(s32[16,16]{1,0:T(8,128)} %param.10) | copy-start | bytes 3076
  23.0 46.1 %copy-start.9 = (s32[1,16]{1,0:T(1,128)S(1)}, s32[1,16]{1,0:T(1,128)}, u32[]{:S(2)}) copy-start(s32[1,16]{1,0:T(1,128)} %param.11) | copy-start | bytes 196
  23.0 36.8 %all-to-all-start.1 = ((bf16[16,2,2,128,128]{4,3,2,1,0:T(8,128)(2,1)}), bf16[16,2,2,128,128]{4,3,2,1,0:T(8,128)(2,1)S(1)}, u32[]{:S(2)}, u32[]{:S(2)}) async-start(bf16[16,2,2,128,128]{4,3,2,1,0:T(8,128)(2,1)} %bitcast.14), calls=%async_computation.1 | async-start | bytes 4194304 | tf_op jit(solution)/shard_map/all_to_all | solution.py:369
  27.7 25.3 %collective-permute-start.1 = (bf16[2,2,8,8,128]{4,3,2,1,0:T(8,128)(2,1)S(1)}, bf16[2,2,8,8,128]{4,3,2,1,0:T(8,128)(2,1)S(1)}, u32[]{:S(2)}, u32[]{:S(2)}) collective-permute-start(bf16[2,2,8,8,128]{4,3,2,1,0:T(8,128)(2,1)S(1)} %get-tuple-element.31), channel_id=1, source_target_pairs={{0,7},{1,6},{2,5},{3,4},{4,3},{5,2},{6,1},{7,0},{8,15},{9,14},{10,... | collective-permute-start | bytes 196616 | tf_op jit(solution)/shard_map/ppermute | solution.py:318
  38.7 17.8 %collective-permute-start.2 = (bf16[2,2,8,8,128]{4,3,2,1,0:T(8,128)(2,1)S(1)}, bf16[2,2,8,8,128]{4,3,2,1,0:T(8,128)(2,1)S(1)}, u32[]{:S(2)}, u32[]{:S(2)}) collective-permute-start(bf16[2,2,8,8,128]{4,3,2,1,0:T(8,128)(2,1)S(1)} %get-tuple-element.30), channel_id=1, source_target_pairs={{0,11},{1,10},{2,9},{3,8},{4,15},{5,14},{6,13},{7,12},{8,3},{9,2},... | collective-permute-start | bytes 196616 | tf_op jit(solution)/shard_map/ppermute | solution.py:318
  42.6 14.0 %collective-permute-start = (bf16[2,2,8,8,128]{4,3,2,1,0:T(8,128)(2,1)S(1)}, bf16[2,2,8,8,128]{4,3,2,1,0:T(8,128)(2,1)S(1)}, u32[]{:S(2)}, u32[]{:S(2)}) collective-permute-start(bf16[2,2,8,8,128]{4,3,2,1,0:T(8,128)(2,1)S(1)} %get-tuple-element.30), channel_id=1, source_target_pairs={{0,12},{1,13},{2,14},{3,15},{4,8},{5,9},{6,10},{7,11},{8,4},{9,5},... | collective-permute-start | bytes 196616 | tf_op jit(solution)/shard_map/ppermute | solution.py:318
  44.9 11.6 %collective-permute-start.3 = (bf16[1,2,2,8,8,128]{5,4,3,2,1,0:T(8,128)(2,1)S(1)}, bf16[1,2,2,8,8,128]{5,4,3,2,1,0:T(8,128)(2,1)S(1)}, u32[]{:S(2)}, u32[]{:S(2)}) collective-permute-start(bf16[1,2,2,8,8,128]{5,4,3,2,1,0:T(8,128)(2,1)S(1)} %bitcast.40), channel_id=1, source_target_pairs={{0,1},{1,2},{2,3},{3,0},{4,5},{5,6},{6,7},{7,4},{8,9},{9,10},{10,1... | collective-permute-start | bytes 196616 | tf_op jit(solution)/shard_map/ppermute | solution.py:323
  49.0 10.0 %collective-permute-start.4 = (bf16[1,2,2,8,8,128]{5,4,3,2,1,0:T(8,128)(2,1)S(1)}, bf16[1,2,2,8,8,128]{5,4,3,2,1,0:T(8,128)(2,1)S(1)}, u32[]{:S(2)}, u32[]{:S(2)}) collective-permute-start(bf16[1,2,2,8,8,128]{5,4,3,2,1,0:T(8,128)(2,1)S(1)} %bitcast.41), channel_id=1, source_target_pairs={{0,2},{1,3},{2,0},{3,1},{4,6},{5,7},{6,4},{7,5},{8,10},{9,11},{10,... | collective-permute-start | bytes 196616 | tf_op jit(solution)/shard_map/ppermute | solution.py:323
  53.0 6.2 %collective-permute-start.5 = (bf16[1,2,2,8,8,128]{5,4,3,2,1,0:T(8,128)(2,1)S(1)}, bf16[1,2,2,8,8,128]{5,4,3,2,1,0:T(8,128)(2,1)S(1)}, u32[]{:S(2)}, u32[]{:S(2)}) collective-permute-start(bf16[1,2,2,8,8,128]{5,4,3,2,1,0:T(8,128)(2,1)S(1)} %bitcast.42), channel_id=1, source_target_pairs={{0,3},{1,0},{2,1},{3,2},{4,7},{5,4},{6,5},{7,6},{8,11},{9,8},{10,9... | collective-permute-start | bytes 196616 | tf_op jit(solution)/shard_map/ppermute | solution.py:323
  59.2 0.6 copy-start.6
  59.8 9.4 %collective-permute-start.6 = (bf16[3,2,2,8,8,128]{5,4,3,2,1,0:T(8,128)(2,1)S(1)}, bf16[3,2,2,8,8,128]{5,4,3,2,1,0:T(8,128)(2,1)S(1)}, u32[]{:S(2)}, u32[]{:S(2)}) collective-permute-start(bf16[3,2,2,8,8,128]{5,4,3,2,1,0:T(8,128)(2,1)S(1)} %pad_maximum_fusion.refs_4_), channel_id=1, source_target_pairs={{0,1},{1,2},{2,3},{3,0},{4,5},{5,6},{6,7},{7,4},{8,9},{9,10},{10,1... | collective-permute-start | bytes 589832 | tf_op jit(solution)/shard_map/ppermute | solution.py:323
  63.1 15.6 %collective-permute-start.7 = (bf16[3,2,2,8,8,128]{5,4,3,2,1,0:T(8,128)(2,1)S(1)}, bf16[3,2,2,8,8,128]{5,4,3,2,1,0:T(8,128)(2,1)S(1)}, u32[]{:S(2)}, u32[]{:S(2)}) collective-permute-start(bf16[3,2,2,8,8,128]{5,4,3,2,1,0:T(8,128)(2,1)S(1)} %pad_maximum_fusion.refs_4_), channel_id=1, source_target_pairs={{0,2},{1,3},{2,0},{3,1},{4,6},{5,7},{6,4},{7,5},{8,10},{9,11},{10,... | collective-permute-start | bytes 589832 | tf_op jit(solution)/shard_map/ppermute | solution.py:323
  67.0 11.8 %collective-permute-start.8 = (bf16[3,2,2,8,8,128]{5,4,3,2,1,0:T(8,128)(2,1)S(1)}, bf16[3,2,2,8,8,128]{5,4,3,2,1,0:T(8,128)(2,1)S(1)}, u32[]{:S(2)}, u32[]{:S(2)}) collective-permute-start(bf16[3,2,2,8,8,128]{5,4,3,2,1,0:T(8,128)(2,1)S(1)} %pad_maximum_fusion.refs_4_), channel_id=1, source_target_pairs={{0,3},{1,0},{2,1},{3,2},{4,7},{5,4},{6,5},{7,6},{8,11},{9,8},{10,9... | collective-permute-start | bytes 589832 | tf_op jit(solution)/shard_map/ppermute | solution.py:323
  78.8 0.8 copy-start.7
  89.4 18.0 %collective-permute-start.10 = (bf16[2,2,2,8,8,128]{5,4,3,2,1,0:T(8,128)(2,1)S(1)}, bf16[2,2,2,8,8,128]{5,4,3,2,1,0:T(8,128)(2,1)S(1)}, u32[]{:S(2)}, u32[]{:S(2)}) collective-permute-start(bf16[2,2,2,8,8,128]{5,4,3,2,1,0:T(8,128)(2,1)S(1)} %get-tuple-element.44), channel_id=1, source_target_pairs={{0,2},{1,3},{2,0},{3,1},{4,6},{5,7},{6,4},{7,5},{8,10},{9,11},{10,... | collective-permute-start | bytes 393224 | tf_op jit(solution)/shard_map/ppermute | solution.py:323
  94.8 12.6 %collective-permute-start.11 = (bf16[2,2,2,8,8,128]{5,4,3,2,1,0:T(8,128)(2,1)S(1)}, bf16[2,2,2,8,8,128]{5,4,3,2,1,0:T(8,128)(2,1)S(1)}, u32[]{:S(2)}, u32[]{:S(2)}) collective-permute-start(bf16[2,2,2,8,8,128]{5,4,3,2,1,0:T(8,128)(2,1)S(1)} %get-tuple-element.45), channel_id=1, source_target_pairs={{0,1},{1,2},{2,3},{3,0},{4,5},{5,6},{6,7},{7,4},{8,9},{9,10},{10,1... | collective-permute-start | bytes 393224 | tf_op jit(solution)/shard_map/ppermute | solution.py:323
  97.7 9.7 %collective-permute-start.9 = (bf16[2,2,2,8,8,128]{5,4,3,2,1,0:T(8,128)(2,1)S(1)}, bf16[2,2,2,8,8,128]{5,4,3,2,1,0:T(8,128)(2,1)S(1)}, u32[]{:S(2)}, u32[]{:S(2)}) collective-permute-start(bf16[2,2,2,8,8,128]{5,4,3,2,1,0:T(8,128)(2,1)S(1)} %get-tuple-element.43), channel_id=1, source_target_pairs={{0,3},{1,0},{2,1},{3,2},{4,7},{5,4},{6,5},{7,6},{8,11},{9,8},{10,9... | collective-permute-start | bytes 393224 | tf_op jit(solution)/shard_map/ppermute | solution.py:323
  101.9 36.8 %copy-start.5 = (s32[1,16,2]{1,2,0:T(2,128)S(1)}, s32[1,16,2]{1,2,0:T(2,128)}, u32[]{:S(2)}) copy-start(s32[1,16,2]{1,2,0:T(2,128)} %param.9) | copy-start | bytes 388
  101.9 41.2 %all-to-all-start.2 = ((bf16[16,2,128,128]{3,2,1,0:T(8,128)(2,1)}), bf16[16,2,128,128]{3,2,1,0:T(8,128)(2,1)S(1)}, u32[]{:S(2)}, u32[]{:S(2)}) async-start(bf16[16,2,128,128]{3,2,1,0:T(8,128)(2,1)} %bitcast.18), calls=%async_computation.2 | async-start | bytes 2097152 | tf_op jit(solution)/shard_map/all_to_all | solution.py:383
  107.5 16.5 %collective-permute-start.12 = (bf16[2,2,2,8,8,128]{5,4,3,2,1,0:T(8,128)(2,1)S(1)}, bf16[2,2,2,8,8,128]{5,4,3,2,1,0:T(8,128)(2,1)S(1)}, u32[]{:S(2)}, u32[]{:S(2)}) collective-permute-start(bf16[2,2,2,8,8,128]{5,4,3,2,1,0:T(8,128)(2,1)S(1)} %add_convert_fusion.1), channel_id=1, source_target_pairs={{0,7},{1,6},{2,5},{3,4},{4,3},{5,2},{6,1},{7,0},{8,15},{9,14},{10,... | collective-permute-start | bytes 393224 | tf_op jit(solution)/shard_map/ppermute | solution.py:318
  116.8 7.5 %collective-permute-start.13 = (bf16[2,2,2,8,8,128]{5,4,3,2,1,0:T(8,128)(2,1)S(1)}, bf16[2,2,2,8,8,128]{5,4,3,2,1,0:T(8,128)(2,1)S(1)}, u32[]{:S(2)}, u32[]{:S(2)}) collective-permute-start(bf16[2,2,2,8,8,128]{5,4,3,2,1,0:T(8,128)(2,1)S(1)} %get-tuple-element.51), channel_id=1, source_target_pairs={{0,3},{1,0},{2,1},{3,2},{4,7},{5,4},{6,5},{7,6},{8,11},{9,8},{10,9... | collective-permute-start | bytes 393224 | tf_op jit(solution)/shard_map/ppermute | solution.py:323
  118.7 15.3 %collective-permute-start.14 = (bf16[2,2,2,8,8,128]{5,4,3,2,1,0:T(8,128)(2,1)S(1)}, bf16[2,2,2,8,8,128]{5,4,3,2,1,0:T(8,128)(2,1)S(1)}, u32[]{:S(2)}, u32[]{:S(2)}) collective-permute-start(bf16[2,2,2,8,8,128]{5,4,3,2,1,0:T(8,128)(2,1)S(1)} %get-tuple-element.52), channel_id=1, source_target_pairs={{0,2},{1,3},{2,0},{3,1},{4,6},{5,7},{6,4},{7,5},{8,10},{9,11},{10,... | collective-permute-start | bytes 393224 | tf_op jit(solution)/shard_map/ppermute | solution.py:323
  121.2 12.8 %collective-permute-start.15 = (bf16[2,2,2,8,8,128]{5,4,3,2,1,0:T(8,128)(2,1)S(1)}, bf16[2,2,2,8,8,128]{5,4,3,2,1,0:T(8,128)(2,1)S(1)}, u32[]{:S(2)}, u32[]{:S(2)}) collective-permute-start(bf16[2,2,2,8,8,128]{5,4,3,2,1,0:T(8,128)(2,1)S(1)} %get-tuple-element.53), channel_id=1, source_target_pairs={{0,1},{1,2},{2,3},{3,0},{4,5},{5,6},{6,7},{7,4},{8,9},{9,10},{10,1... | collective-permute-start | bytes 393224 | tf_op jit(solution)/shard_map/ppermute | solution.py:323
  134.1 9.0 %collective-permute-start.16 = (bf16[2,2,8,8,128]{4,3,2,1,0:T(8,128)(2,1)S(1)}, bf16[2,2,8,8,128]{4,3,2,1,0:T(8,128)(2,1)S(1)}, u32[]{:S(2)}, u32[]{:S(2)}) collective-permute-start(bf16[2,2,8,8,128]{4,3,2,1,0:T(8,128)(2,1)S(1)} %get-tuple-element.58), channel_id=1, source_target_pairs={{0,12},{1,13},{2,14},{3,15},{4,8},{5,9},{6,10},{7,11},{8,4},{9,5},... | collective-permute-start | bytes 196616 | tf_op jit(solution)/shard_map/ppermute | solution.py:318
  144.4 17.2 %all-to-all-start.3 = ((bf16[32,2,2,2,4,128]{5,4,3,2,1,0:T(4,128)(2,1)}), bf16[32,2,2,2,4,128]{5,4,3,2,1,0:T(4,128)(2,1)S(1)}, u32[]{:S(2)}, u32[]{:S(2)}) async-start(bf16[32,2,2,2,4,128]{5,4,3,2,1,0:T(4,128)(2,1)} %bitcast.22), calls=%async_computation.3 | async-start | bytes 524288 | tf_op jit(solution)/shard_map/all_to_all | solution.py:356

commit v13 on v12

--- a/solution.py
+++ b/solution.py
@@ -15,7 +15,7 @@
 LOG2E = 1.4426950408889634
 PLANE = ("dp", "xh")
 MIRROR = 12
-ACROSS = 7
+ACROSS = 6
 NEAR = 4
 
 
@@ -78,7 +78,7 @@
         kt_all[block] = k_all[block].astype(jnp.float32).T.astype(jnp.bfloat16)
         return 0
 
-    lax.fori_loop(0, blocks, stage, 0, unroll=2)
+    lax.fori_loop(0, blocks, stage, 0, unroll=4)
 
     row = lax.broadcasted_iota(jnp.int32, (width, 1), 0)
     holder = (place_ref[0] & 12) | ((place_ref[0] - (row >> 6)) & 3)
@@ -204,7 +204,7 @@
             ref[:, :, 1, block] = dv_all[block, rows].reshape(shape).astype(jnp.bfloat16)
         return 0
 
-    lax.fori_loop(0, blocks, unstage, 0, unroll=2)
+    lax.fori_loop(0, blocks, unstage, 0, unroll=4)
 
 
 def attention(my_recv, start, place, qg, chunks):

time: 164 us -> 164 us (level)
  no operation moved by 1% of the time
where the time goes in v13:
time: 164 us; the launch traced here: 163 us
  starting transfers between devices  99.5 us (61%)
  waiting for transfers between devices  37.8 us (23%)
  Pallas kernels  16.9 us (10%)
  local copies, waits for them, and re-layouts  7.24 us (4%)
    ppermute x12, starting transfers between devices, near_shift(): return lax.ppermute(values, 'z', pairs)  41 us
    ppermute x5, starting transfers between devices, far_swap(): lax.ppermute(values, 'z', [(place, place ^ flip) for place in range(16)])  31.2 us
    ppermute x12, waiting for transfers between devices, near_shift(): return lax.ppermute(values, 'z', pairs)  22.7 us
    all_to_all x2, starting transfers between devices, over_plane(): lax.all_to_all(values.reshape((2 * n_replicas,) + values.shape[2:]), PLAN...  18.5 us
    all_to_all x2, waiting for transfers between devices, over_plane(): lax.all_to_all(values.reshape((2 * n_replicas,) + values.shape[2:]), PLAN...  11.4 us
    pallas_call x1, Pallas kernels, attention(): pl.pallas_call(attention_kernel, out_shape=(jax.ShapeDtypeStruct((slots,...  10.1 us
    unnamed x20, local copies, waits for them, and re-layouts  5.82 us
    all_to_all x1, starting transfers between devices, on_device(): lax.all_to_all(query_back.reshape(n_replicas, slot_cap, tile_rows, row_wi...  4.81 us
  transfers between devices with their start and end apart: 21, of which 8 were waited for; matrix products, arithmetic and copies ran while one was open for 1% of the time, Pallas kernels for 2%

profile of v13, /device:TPU:1, one launch (start us, length us, event | category | flops | bytes accessed | tf_op | source)
XLA Modules:
  0.0 163.1 jit_solution(7979647537398623619)
XLA Ops:
  2.2 1.4 kv_pack.1
  3.7 10.4 %all-to-all-start = ((bf16[32,2,2,2,4,128]{5,4,3,2,1,0:T(4,128)(2,1)}), bf16[32,2,2,2,4,128]{5,4,3,2,1,0:T(4,128)(2,1)S(1)}, u32[]{:S(2)}, u32[]{:S(2)}) async-start(bf16[32,2,2,2,4,128]{5,4,3,2,1,0:T(4,128)(2,1)} %bitcast.7), calls=%async_computation | async-start | bytes 524288 | tf_op jit(solution)/shard_map/all_to_all | solution.py:356
  16.8 2.1 %pack_rows.1 = bf16[32,2,128,128]{3,2,1,0:T(8,128)(2,1)} custom-call(s32[2,16]{1,0:T(2,128)S(1)} %bitcast.38, bf16[16,128,128]{2,1,0:T(8,128)(2,1)S(1)} %copy-done, bf16[16,128,128]{2,1,0:T(8,128)(2,1)S(1)} %copy-done.1), custom_call_target="tpu_custom_call" | custom-call | tf_op jit(solution)/shard_map/pack_rows/pallas_call | solution.py:38
  19.0 4.0 %all-to-all-done = bf16[32,2,2,2,4,128]{5,4,3,2,1,0:T(4,128)(2,1)S(1)} async-done(((bf16[32,2,2,2,4,128]{5,4,3,2,1,0:T(4,128)(2,1)}), bf16[32,2,2,2,4,128]{5,4,3,2,1,0:T(4,128)(2,1)S(1)}, u32[]{:S(2)}, u32[]{:S(2)}) %all-to-all-start) | async-done | bytes 262176 | tf_op jit(solution)/shard_map/all_to_all | solution.py:356
  23.0 4.1 %all-to-all-start.1 = ((bf16[16,2,2,128,128]{4,3,2,1,0:T(8,128)(2,1)}), bf16[16,2,2,128,128]{4,3,2,1,0:T(8,128)(2,1)S(1)}, u32[]{:S(2)}, u32[]{:S(2)}) async-start(bf16[16,2,2,128,128]{4,3,2,1,0:T(8,128)(2,1)} %bitcast.14), calls=%async_computation.1 | async-start | bytes 4194304 | tf_op jit(solution)/shard_map/all_to_all | solution.py:369
  27.7 9.6 %collective-permute-start.1 = (bf16[2,2,8,8,128]{4,3,2,1,0:T(8,128)(2,1)S(1)}, bf16[2,2,8,8,128]{4,3,2,1,0:T(8,128)(2,1)S(1)}, u32[]{:S(2)}, u32[]{:S(2)}) collective-permute-start(bf16[2,2,8,8,128]{4,3,2,1,0:T(8,128)(2,1)S(1)} %get-tuple-element.31), channel_id=1, source_target_pairs={{0,6},{1,7},{2,4},{3,5},{4,2},{5,3},{6,0},{7,1},{8,14},{9,15},{10,... | collective-permute-start | bytes 196616 | tf_op jit(solution)/shard_map/ppermute | solution.py:318
  37.3 6.1 %collective-permute-start.2 = (bf16[2,2,8,8,128]{4,3,2,1,0:T(8,128)(2,1)S(1)}, bf16[2,2,8,8,128]{4,3,2,1,0:T(8,128)(2,1)S(1)}, u32[]{:S(2)}, u32[]{:S(2)}) collective-permute-start(bf16[2,2,8,8,128]{4,3,2,1,0:T(8,128)(2,1)S(1)} %get-tuple-element.30), channel_id=1, source_target_pairs={{0,10},{1,11},{2,8},{3,9},{4,14},{5,15},{6,12},{7,13},{8,2},{9,3},... | collective-permute-start | bytes 196616 | tf_op jit(solution)/shard_map/ppermute | solution.py:318
  43.5 1.9 %collective-permute-start = (bf16[2,2,8,8,128]{4,3,2,1,0:T(8,128)(2,1)S(1)}, bf16[2,2,8,8,128]{4,3,2,1,0:T(8,128)(2,1)S(1)}, u32[]{:S(2)}, u32[]{:S(2)}) collective-permute-start(bf16[2,2,8,8,128]{4,3,2,1,0:T(8,128)(2,1)S(1)} %get-tuple-element.30), channel_id=1, source_target_pairs={{0,12},{1,13},{2,14},{3,15},{4,8},{5,9},{6,10},{7,11},{8,4},{9,5},... | collective-permute-start | bytes 196616 | tf_op jit(solution)/shard_map/ppermute | solution.py:318
  45.4 2.6 %collective-permute-start.3 = (bf16[1,2,2,8,8,128]{5,4,3,2,1,0:T(8,128)(2,1)S(1)}, bf16[1,2,2,8,8,128]{5,4,3,2,1,0:T(8,128)(2,1)S(1)}, u32[]{:S(2)}, u32[]{:S(2)}) collective-permute-start(bf16[1,2,2,8,8,128]{5,4,3,2,1,0:T(8,128)(2,1)S(1)} %bitcast.40), channel_id=1, source_target_pairs={{0,1},{1,2},{2,3},{3,0},{4,5},{5,6},{6,7},{7,4},{8,9},{9,10},{10,1... | collective-permute-start | bytes 196616 | tf_op jit(solution)/shard_map/ppermute | solution.py:323
  48.1 4.9 %collective-permute-start.4 = (bf16[1,2,2,8,8,128]{5,4,3,2,1,0:T(8,128)(2,1)S(1)}, bf16[1,2,2,8,8,128]{5,4,3,2,1,0:T(8,128)(2,1)S(1)}, u32[]{:S(2)}, u32[]{:S(2)}) collective-permute-start(bf16[1,2,2,8,8,128]{5,4,3,2,1,0:T(8,128)(2,1)S(1)} %bitcast.41), channel_id=1, source_target_pairs={{0,2},{1,3},{2,0},{3,1},{4,6},{5,7},{6,4},{7,5},{8,10},{9,11},{10,... | collective-permute-start | bytes 196616 | tf_op jit(solution)/shard_map/ppermute | solution.py:323
  53.0 3.5 %collective-permute-start.5 = (bf16[1,2,2,8,8,128]{5,4,3,2,1,0:T(8,128)(2,1)S(1)}, bf16[1,2,2,8,8,128]{5,4,3,2,1,0:T(8,128)(2,1)S(1)}, u32[]{:S(2)}, u32[]{:S(2)}) collective-permute-start(bf16[1,2,2,8,8,128]{5,4,3,2,1,0:T(8,128)(2,1)S(1)} %bitcast.42), channel_id=1, source_target_pairs={{0,3},{1,0},{2,1},{3,2},{4,7},{5,4},{6,5},{7,6},{8,11},{9,8},{10,9... | collective-permute-start | bytes 196616 | tf_op jit(solution)/shard_map/ppermute | solution.py:323
  56.6 2.2 %collective-permute-done.4.refs_2_ = bf16[1,2,2,8,8,128]{5,4,3,2,1,0:T(8,128)(2,1)S(1)} collective-permute-done((bf16[1,2,2,8,8,128]{5,4,3,2,1,0:T(8,128)(2,1)S(1)}, bf16[1,2,2,8,8,128]{5,4,3,2,1,0:T(8,128)(2,1)S(1)}, u32[]{:S(2)}, u32[]{:S(2)}) %collective-permute-start.4) | collective-permute-done | bytes 65568 | tf_op jit(solution)/shard_map/ppermute | solution.py:323
  59.7 3.3 %collective-permute-start.6 = (bf16[3,2,2,8,8,128]{5,4,3,2,1,0:T(8,128)(2,1)S(1)}, bf16[3,2,2,8,8,128]{5,4,3,2,1,0:T(8,128)(2,1)S(1)}, u32[]{:S(2)}, u32[]{:S(2)}) collective-permute-start(bf16[3,2,2,8,8,128]{5,4,3,2,1,0:T(8,128)(2,1)S(1)} %pad_maximum_fusion.refs_4_), channel_id=1, source_target_pairs={{0,1},{1,2},{2,3},{3,0},{4,5},{5,6},{6,7},{7,4},{8,9},{9,10},{10,1... | collective-permute-start | bytes 589832 | tf_op jit(solution)/shard_map/ppermute | solution.py:323
  63.0 3.7 %collective-permute-start.7 = (bf16[3,2,2,8,8,128]{5,4,3,2,1,0:T(8,128)(2,1)S(1)}, bf16[3,2,2,8,8,128]{5,4,3,2,1,0:T(8,128)(2,1)S(1)}, u32[]{:S(2)}, u32[]{:S(2)}) collective-permute-start(bf16[3,2,2,8,8,128]{5,4,3,2,1,0:T(8,128)(2,1)S(1)} %pad_maximum_fusion.refs_4_), channel_id=1, source_target_pairs={{0,2},{1,3},{2,0},{3,1},{4,6},{5,7},{6,4},{7,5},{8,10},{9,11},{10,... | collective-permute-start | bytes 589832 | tf_op jit(solution)/shard_map/ppermute | solution.py:323
  66.7 2.4 %collective-permute-start.8 = (bf16[3,2,2,8,8,128]{5,4,3,2,1,0:T(8,128)(2,1)S(1)}, bf16[3,2,2,8,8,128]{5,4,3,2,1,0:T(8,128)(2,1)S(1)}, u32[]{:S(2)}, u32[]{:S(2)}) collective-permute-start(bf16[3,2,2,8,8,128]{5,4,3,2,1,0:T(8,128)(2,1)S(1)} %pad_maximum_fusion.refs_4_), channel_id=1, source_target_pairs={{0,3},{1,0},{2,1},{3,2},{4,7},{5,4},{6,5},{7,6},{8,11},{9,8},{10,9... | collective-permute-start | bytes 589832 | tf_op jit(solution)/shard_map/ppermute | solution.py:323
  69.3 9.5 %collective-permute-done.7.refs_6_ = bf16[3,2,2,8,8,128]{5,4,3,2,1,0:T(8,128)(2,1)S(1)} collective-permute-done((bf16[3,2,2,8,8,128]{5,4,3,2,1,0:T(8,128)(2,1)S(1)}, bf16[3,2,2,8,8,128]{5,4,3,2,1,0:T(8,128)(2,1)S(1)}, u32[]{:S(2)}, u32[]{:S(2)}) %collective-permute-start.7) | collective-permute-done | bytes 196640 | tf_op jit(solution)/shard_map/ppermute | solution.py:323
  79.6 10.1 %attention_backward.1 = (bf16[32,128,128]{2,1,0:T(8,128)(2,1)}, bf16[2,2,2,8,8,128]{5,4,3,2,1,0:T(8,128)(2,1)S(1)}, bf16[2,2,2,8,8,128]{5,4,3,2,1,0:T(8,128)(2,1...) custom-call(s32[16]{0:T(128)S(1)} %dynamic-slice_bitcast_fusion.recv, ...), custom_call_target="tpu_custom_call" | custom-call | flops 2000000000 | bytes 6291456 | tf_op jit(solution)/shard_map/attention_backward/pallas_call | solution.py:216
  89.7 5.4 %collective-permute-start.10 = (bf16[2,2,2,8,8,128]{5,4,3,2,1,0:T(8,128)(2,1)S(1)}, bf16[2,2,2,8,8,128]{5,4,3,2,1,0:T(8,128)(2,1)S(1)}, u32[]{:S(2)}, u32[]{:S(2)}) collective-permute-start(bf16[2,2,2,8,8,128]{5,4,3,2,1,0:T(8,128)(2,1)S(1)} %get-tuple-element.44), channel_id=1, source_target_pairs={{0,2},{1,3},{2,0},{3,1},{4,6},{5,7},{6,4},{7,5},{8,10},{9,11},{10,... | collective-permute-start | bytes 393224 | tf_op jit(solution)/shard_map/ppermute | solution.py:323
  95.1 2.9 %collective-permute-start.11 = (bf16[2,2,2,8,8,128]{5,4,3,2,1,0:T(8,128)(2,1)S(1)}, bf16[2,2,2,8,8,128]{5,4,3,2,1,0:T(8,128)(2,1)S(1)}, u32[]{:S(2)}, u32[]{:S(2)}) collective-permute-start(bf16[2,2,2,8,8,128]{5,4,3,2,1,0:T(8,128)(2,1)S(1)} %get-tuple-element.45), channel_id=1, source_target_pairs={{0,1},{1,2},{2,3},{3,0},{4,5},{5,6},{6,7},{7,4},{8,9},{9,10},{10,1... | collective-permute-start | bytes 393224 | tf_op jit(solution)/shard_map/ppermute | solution.py:323
  98.0 4.2 %collective-permute-start.9 = (bf16[2,2,2,8,8,128]{5,4,3,2,1,0:T(8,128)(2,1)S(1)}, bf16[2,2,2,8,8,128]{5,4,3,2,1,0:T(8,128)(2,1)S(1)}, u32[]{:S(2)}, u32[]{:S(2)}) collective-permute-start(bf16[2,2,2,8,8,128]{5,4,3,2,1,0:T(8,128)(2,1)S(1)} %get-tuple-element.43), channel_id=1, source_target_pairs={{0,3},{1,0},{2,1},{3,2},{4,7},{5,4},{6,5},{7,6},{8,11},{9,8},{10,9... | collective-permute-start | bytes 393224 | tf_op jit(solution)/shard_map/ppermute | solution.py:323
  102.2 4.8 %all-to-all-start.2 = ((bf16[16,2,128,128]{3,2,1,0:T(8,128)(2,1)}), bf16[16,2,128,128]{3,2,1,0:T(8,128)(2,1)S(1)}, u32[]{:S(2)}, u32[]{:S(2)}) async-start(bf16[16,2,128,128]{3,2,1,0:T(8,128)(2,1)} %bitcast.18), calls=%async_computation.2 | async-start | bytes 2097152 | tf_op jit(solution)/shard_map/all_to_all | solution.py:383
  107.2 8.3 %collective-permute-start.12 = (bf16[2,2,2,8,8,128]{5,4,3,2,1,0:T(8,128)(2,1)S(1)}, bf16[2,2,2,8,8,128]{5,4,3,2,1,0:T(8,128)(2,1)S(1)}, u32[]{:S(2)}, u32[]{:S(2)}) collective-permute-start(bf16[2,2,2,8,8,128]{5,4,3,2,1,0:T(8,128)(2,1)S(1)} %add_convert_fusion.1), channel_id=1, source_target_pairs={{0,6},{1,7},{2,4},{3,5},{4,2},{5,3},{6,0},{7,1},{8,14},{9,15},{10,... | collective-permute-start | bytes 393224 | tf_op jit(solution)/shard_map/ppermute | solution.py:318
  115.7 1.9 %collective-permute-start.13 = (bf16[2,2,2,8,8,128]{5,4,3,2,1,0:T(8,128)(2,1)S(1)}, bf16[2,2,2,8,8,128]{5,4,3,2,1,0:T(8,128)(2,1)S(1)}, u32[]{:S(2)}, u32[]{:S(2)}) collective-permute-start(bf16[2,2,2,8,8,128]{5,4,3,2,1,0:T(8,128)(2,1)S(1)} %get-tuple-element.51), channel_id=1, source_target_pairs={{0,3},{1,0},{2,1},{3,2},{4,7},{5,4},{6,5},{7,6},{8,11},{9,8},{10,9... | collective-permute-start | bytes 393224 | tf_op jit(solution)/shard_map/ppermute | solution.py:323
  117.6 4.2 %collective-permute-start.14 = (bf16[2,2,2,8,8,128]{5,4,3,2,1,0:T(8,128)(2,1)S(1)}, bf16[2,2,2,8,8,128]{5,4,3,2,1,0:T(8,128)(2,1)S(1)}, u32[]{:S(2)}, u32[]{:S(2)}) collective-permute-start(bf16[2,2,2,8,8,128]{5,4,3,2,1,0:T(8,128)(2,1)S(1)} %get-tuple-element.52), channel_id=1, source_target_pairs={{0,2},{1,3},{2,0},{3,1},{4,6},{5,7},{6,4},{7,5},{8,10},{9,11},{10,... | collective-permute-start | bytes 393224 | tf_op jit(solution)/shard_map/ppermute | solution.py:323
  121.8 1.9 %collective-permute-start.15 = (bf16[2,2,2,8,8,128]{5,4,3,2,1,0:T(8,128)(2,1)S(1)}, bf16[2,2,2,8,8,128]{5,4,3,2,1,0:T(8,128)(2,1)S(1)}, u32[]{:S(2)}, u32[]{:S(2)}) collective-permute-start(bf16[2,2,2,8,8,128]{5,4,3,2,1,0:T(8,128)(2,1)S(1)} %get-tuple-element.53), channel_id=1, source_target_pairs={{0,1},{1,2},{2,3},{3,0},{4,5},{5,6},{6,7},{7,4},{8,9},{9,10},{10,1... | collective-permute-start | bytes 393224 | tf_op jit(solution)/shard_map/ppermute | solution.py:323
  125.1 9.4 %collective-permute-done.14 = bf16[2,2,2,8,8,128]{5,4,3,2,1,0:T(8,128)(2,1)S(1)} collective-permute-done((bf16[2,2,2,8,8,128]{5,4,3,2,1,0:T(8,128)(2,1)S(1)}, bf16[2,2,2,8,8,128]{5,4,3,2,1,0:T(8,128)(2,1)S(1)}, u32[]{:S(2)}, u32[]{:S(2)}) %collective-permute-start.14) | collective-permute-done | bytes 131104 | tf_op jit(solution)/shard_map/ppermute | solution.py:323
  134.6 5.1 %collective-permute-start.16 = (bf16[2,2,8,8,128]{4,3,2,1,0:T(8,128)(2,1)S(1)}, bf16[2,2,8,8,128]{4,3,2,1,0:T(8,128)(2,1)S(1)}, u32[]{:S(2)}, u32[]{:S(2)}) collective-permute-start(bf16[2,2,8,8,128]{4,3,2,1,0:T(8,128)(2,1)S(1)} %get-tuple-element.58), channel_id=1, source_target_pairs={{0,12},{1,13},{2,14},{3,15},{4,8},{5,9},{6,10},{7,11},{8,4},{9,5},... | collective-permute-start | bytes 196616 | tf_op jit(solution)/shard_map/ppermute | solution.py:318
  139.8 3.7 %collective-permute-done.16.other_ref = bf16[2,2,8,8,128]{4,3,2,1,0:T(8,128)(2,1)S(1)} collective-permute-done((bf16[2,2,8,8,128]{4,3,2,1,0:T(8,128)(2,1)S(1)}, bf16[2,2,8,8,128]{4,3,2,1,0:T(8,128)(2,1)S(1)}, u32[]{:S(2)}, u32[]{:S(2)}) %collective-permute-start.16) | collective-permute-done | bytes 65568 | tf_op jit(solution)/shard_map/ppermute | solution.py:318
  143.6 1.3 kv_back.1
  144.9 8.1 %all-to-all-start.3 = ((bf16[32,2,2,2,4,128]{5,4,3,2,1,0:T(4,128)(2,1)}), bf16[32,2,2,2,4,128]{5,4,3,2,1,0:T(4,128)(2,1)S(1)}, u32[]{:S(2)}, u32[]{:S(2)}) async-start(bf16[32,2,2,2,4,128]{5,4,3,2,1,0:T(4,128)(2,1)} %bitcast.22), calls=%async_computation.3 | async-start | bytes 524288 | tf_op jit(solution)/shard_map/all_to_all | solution.py:356
  153.0 1.4 gather_fusion
  154.4 7.4 %all-to-all-done.3 = bf16[32,2,2,2,4,128]{5,4,3,2,1,0:T(4,128)(2,1)S(1)} async-done(((bf16[32,2,2,2,4,128]{5,4,3,2,1,0:T(4,128)(2,1)}), bf16[32,2,2,2,4,128]{5,4,3,2,1,0:T(4,128)(2,1)S(1)}, u32[]{:S(2)}, u32[]{:S(2)}) %all-to-all-start.3) | async-done | bytes 262176 | tf_op jit(solution)/shard_map/all_to_all | solution.py:356
  (50 shorter events, 10.0 us)
Async XLA Ops:
  0.6 0.9 copy-start.2
  1.5 0.7 copy-start.3
  3.7 19.3 %all-to-all-start = ((bf16[32,2,2,2,4,128]{5,4,3,2,1,0:T(4,128)(2,1)}), bf16[32,2,2,2,4,128]{5,4,3,2,1,0:T(4,128)(2,1)S(1)}, u32[]{:S(2)}, u32[]{:S(2)}) async-start(bf16[32,2,2,2,4,128]{5,4,3,2,1,0:T(4,128)(2,1)} %bitcast.7), calls=%async_computation | async-start | bytes 524288 | tf_op jit(solution)/shard_map/all_to_all | solution.py:356
  14.1 1.0 copy-start
  15.1 1.0 copy-start.1
  16.2 0.7 copy-start.4
  23.0 4.1 %copy-start.8 = (s32[16,16]{1,0:T(8,128)S(1)}, s32[16,16]{1,0:T(8,128)}, u32[]{:S(2)}) copy-start(s32[16,16]{1,0:T(8,128)} %param.10) | copy-start | bytes 3076
  23.0 46.1 %copy-start.9 = (s32[1,16]{1,0:T(1,128)S(1)}, s32[1,16]{1,0:T(1,128)}, u32[]{:S(2)}) copy-start(s32[1,16]{1,0:T(1,128)} %param.11) | copy-start | bytes 196
  23.0 36.7 %all-to-all-start.1 = ((bf16[16,2,2,128,128]{4,3,2,1,0:T(8,128)(2,1)}), bf16[16,2,2,128,128]{4,3,2,1,0:T(8,128)(2,1)S(1)}, u32[]{:S(2)}, u32[]{:S(2)}) async-start(bf16[16,2,2,128,128]{4,3,2,1,0:T(8,128)(2,1)} %bitcast.14), calls=%async_computation.1 | async-start | bytes 4194304 | tf_op jit(solution)/shard_map/all_to_all | solution.py:369
  27.7 25.3 %collective-permute-start.1 = (bf16[2,2,8,8,128]{4,3,2,1,0:T(8,128)(2,1)S(1)}, bf16[2,2,8,8,128]{4,3,2,1,0:T(8,128)(2,1)S(1)}, u32[]{:S(2)}, u32[]{:S(2)}) collective-permute-start(bf16[2,2,8,8,128]{4,3,2,1,0:T(8,128)(2,1)S(1)} %get-tuple-element.31), channel_id=1, source_target_pairs={{0,6},{1,7},{2,4},{3,5},{4,2},{5,3},{6,0},{7,1},{8,14},{9,15},{10,... | collective-permute-start | bytes 196616 | tf_op jit(solution)/shard_map/ppermute | solution.py:318
  37.3 19.2 %collective-permute-start.2 = (bf16[2,2,8,8,128]{4,3,2,1,0:T(8,128)(2,1)S(1)}, bf16[2,2,8,8,128]{4,3,2,1,0:T(8,128)(2,1)S(1)}, u32[]{:S(2)}, u32[]{:S(2)}) collective-permute-start(bf16[2,2,8,8,128]{4,3,2,1,0:T(8,128)(2,1)S(1)} %get-tuple-element.30), channel_id=1, source_target_pairs={{0,10},{1,11},{2,8},{3,9},{4,14},{5,15},{6,12},{7,13},{8,2},{9,3},... | collective-permute-start | bytes 196616 | tf_op jit(solution)/shard_map/ppermute | solution.py:318
  43.5 13.1 %collective-permute-start = (bf16[2,2,8,8,128]{4,3,2,1,0:T(8,128)(2,1)S(1)}, bf16[2,2,8,8,128]{4,3,2,1,0:T(8,128)(2,1)S(1)}, u32[]{:S(2)}, u32[]{:S(2)}) collective-permute-start(bf16[2,2,8,8,128]{4,3,2,1,0:T(8,128)(2,1)S(1)} %get-tuple-element.30), channel_id=1, source_target_pairs={{0,12},{1,13},{2,14},{3,15},{4,8},{5,9},{6,10},{7,11},{8,4},{9,5},... | collective-permute-start | bytes 196616 | tf_op jit(solution)/shard_map/ppermute | solution.py:318
  45.4 11.2 %collective-permute-start.3 = (bf16[1,2,2,8,8,128]{5,4,3,2,1,0:T(8,128)(2,1)S(1)}, bf16[1,2,2,8,8,128]{5,4,3,2,1,0:T(8,128)(2,1)S(1)}, u32[]{:S(2)}, u32[]{:S(2)}) collective-permute-start(bf16[1,2,2,8,8,128]{5,4,3,2,1,0:T(8,128)(2,1)S(1)} %bitcast.40), channel_id=1, source_target_pairs={{0,1},{1,2},{2,3},{3,0},{4,5},{5,6},{6,7},{7,4},{8,9},{9,10},{10,1... | collective-permute-start | bytes 196616 | tf_op jit(solution)/shard_map/ppermute | solution.py:323
  48.1 10.8 %collective-permute-start.4 = (bf16[1,2,2,8,8,128]{5,4,3,2,1,0:T(8,128)(2,1)S(1)}, bf16[1,2,2,8,8,128]{5,4,3,2,1,0:T(8,128)(2,1)S(1)}, u32[]{:S(2)}, u32[]{:S(2)}) collective-permute-start(bf16[1,2,2,8,8,128]{5,4,3,2,1,0:T(8,128)(2,1)S(1)} %bitcast.41), channel_id=1, source_target_pairs={{0,2},{1,3},{2,0},{3,1},{4,6},{5,7},{6,4},{7,5},{8,10},{9,11},{10,... | collective-permute-start | bytes 196616 | tf_op jit(solution)/shard_map/ppermute | solution.py:323
  53.0 6.1 %collective-permute-start.5 = (bf16[1,2,2,8,8,128]{5,4,3,2,1,0:T(8,128)(2,1)S(1)}, bf16[1,2,2,8,8,128]{5,4,3,2,1,0:T(8,128)(2,1)S(1)}, u32[]{:S(2)}, u32[]{:S(2)}) collective-permute-start(bf16[1,2,2,8,8,128]{5,4,3,2,1,0:T(8,128)(2,1)S(1)} %bitcast.42), channel_id=1, source_target_pairs={{0,3},{1,0},{2,1},{3,2},{4,7},{5,4},{6,5},{7,6},{8,11},{9,8},{10,9... | collective-permute-start | bytes 196616 | tf_op jit(solution)/shard_map/ppermute | solution.py:323
  59.1 0.6 copy-start.6
  59.7 9.6 %collective-permute-start.6 = (bf16[3,2,2,8,8,128]{5,4,3,2,1,0:T(8,128)(2,1)S(1)}, bf16[3,2,2,8,8,128]{5,4,3,2,1,0:T(8,128)(2,1)S(1)}, u32[]{:S(2)}, u32[]{:S(2)}) collective-permute-start(bf16[3,2,2,8,8,128]{5,4,3,2,1,0:T(8,128)(2,1)S(1)} %pad_maximum_fusion.refs_4_), channel_id=1, source_target_pairs={{0,1},{1,2},{2,3},{3,0},{4,5},{5,6},{6,7},{7,4},{8,9},{9,10},{10,1... | collective-permute-start | bytes 589832 | tf_op jit(solution)/shard_map/ppermute | solution.py:323
  63.0 15.7 %collective-permute-start.7 = (bf16[3,2,2,8,8,128]{5,4,3,2,1,0:T(8,128)(2,1)S(1)}, bf16[3,2,2,8,8,128]{5,4,3,2,1,0:T(8,128)(2,1)S(1)}, u32[]{:S(2)}, u32[]{:S(2)}) collective-permute-start(bf16[3,2,2,8,8,128]{5,4,3,2,1,0:T(8,128)(2,1)S(1)} %pad_maximum_fusion.refs_4_), channel_id=1, source_target_pairs={{0,2},{1,3},{2,0},{3,1},{4,6},{5,7},{6,4},{7,5},{8,10},{9,11},{10,... | collective-permute-start | bytes 589832 | tf_op jit(solution)/shard_map/ppermute | solution.py:323
  66.7 12.1 %collective-permute-start.8 = (bf16[3,2,2,8,8,128]{5,4,3,2,1,0:T(8,128)(2,1)S(1)}, bf16[3,2,2,8,8,128]{5,4,3,2,1,0:T(8,128)(2,1)S(1)}, u32[]{:S(2)}, u32[]{:S(2)}) collective-permute-start(bf16[3,2,2,8,8,128]{5,4,3,2,1,0:T(8,128)(2,1)S(1)} %pad_maximum_fusion.refs_4_), channel_id=1, source_target_pairs={{0,3},{1,0},{2,1},{3,2},{4,7},{5,4},{6,5},{7,6},{8,11},{9,8},{10,9... | collective-permute-start | bytes 589832 | tf_op jit(solution)/shard_map/ppermute | solution.py:323
  78.8 0.8 copy-start.7
  89.7 17.3 %collective-permute-start.10 = (bf16[2,2,2,8,8,128]{5,4,3,2,1,0:T(8,128)(2,1)S(1)}, bf16[2,2,2,8,8,128]{5,4,3,2,1,0:T(8,128)(2,1)S(1)}, u32[]{:S(2)}, u32[]{:S(2)}) collective-permute-start(bf16[2,2,2,8,8,128]{5,4,3,2,1,0:T(8,128)(2,1)S(1)} %get-tuple-element.44), channel_id=1, source_target_pairs={{0,2},{1,3},{2,0},{3,1},{4,6},{5,7},{6,4},{7,5},{8,10},{9,11},{10,... | collective-permute-start | bytes 393224 | tf_op jit(solution)/shard_map/ppermute | solution.py:323
  95.1 11.9 %collective-permute-start.11 = (bf16[2,2,2,8,8,128]{5,4,3,2,1,0:T(8,128)(2,1)S(1)}, bf16[2,2,2,8,8,128]{5,4,3,2,1,0:T(8,128)(2,1)S(1)}, u32[]{:S(2)}, u32[]{:S(2)}) collective-permute-start(bf16[2,2,2,8,8,128]{5,4,3,2,1,0:T(8,128)(2,1)S(1)} %get-tuple-element.45), channel_id=1, source_target_pairs={{0,1},{1,2},{2,3},{3,0},{4,5},{5,6},{6,7},{7,4},{8,9},{9,10},{10,1... | collective-permute-start | bytes 393224 | tf_op jit(solution)/shard_map/ppermute | solution.py:323
  98.0 9.0 %collective-permute-start.9 = (bf16[2,2,2,8,8,128]{5,4,3,2,1,0:T(8,128)(2,1)S(1)}, bf16[2,2,2,8,8,128]{5,4,3,2,1,0:T(8,128)(2,1)S(1)}, u32[]{:S(2)}, u32[]{:S(2)}) collective-permute-start(bf16[2,2,2,8,8,128]{5,4,3,2,1,0:T(8,128)(2,1)S(1)} %get-tuple-element.43), channel_id=1, source_target_pairs={{0,3},{1,0},{2,1},{3,2},{4,7},{5,4},{6,5},{7,6},{8,11},{9,8},{10,9... | collective-permute-start | bytes 393224 | tf_op jit(solution)/shard_map/ppermute | solution.py:323
  102.2 37.5 %copy-start.5 = (s32[1,16,2]{1,2,0:T(2,128)S(1)}, s32[1,16,2]{1,2,0:T(2,128)}, u32[]{:S(2)}) copy-start(s32[1,16,2]{1,2,0:T(2,128)} %param.9) | copy-start | bytes 388
  102.2 41.3 %all-to-all-start.2 = ((bf16[16,2,128,128]{3,2,1,0:T(8,128)(2,1)}), bf16[16,2,128,128]{3,2,1,0:T(8,128)(2,1)S(1)}, u32[]{:S(2)}, u32[]{:S(2)}) async-start(bf16[16,2,128,128]{3,2,1,0:T(8,128)(2,1)} %bitcast.18), calls=%async_computation.2 | async-start | bytes 2097152 | tf_op jit(solution)/shard_map/all_to_all | solution.py:383
  107.2 16.6 %collective-permute-start.12 = (bf16[2,2,2,8,8,128]{5,4,3,2,1,0:T(8,128)(2,1)S(1)}, bf16[2,2,2,8,8,128]{5,4,3,2,1,0:T(8,128)(2,1)S(1)}, u32[]{:S(2)}, u32[]{:S(2)}) collective-permute-start(bf16[2,2,2,8,8,128]{5,4,3,2,1,0:T(8,128)(2,1)S(1)} %add_convert_fusion.1), channel_id=1, source_target_pairs={{0,6},{1,7},{2,4},{3,5},{4,2},{5,3},{6,0},{7,1},{8,14},{9,15},{10,... | collective-permute-start | bytes 393224 | tf_op jit(solution)/shard_map/ppermute | solution.py:318
  115.7 9.4 %collective-permute-start.13 = (bf16[2,2,2,8,8,128]{5,4,3,2,1,0:T(8,128)(2,1)S(1)}, bf16[2,2,2,8,8,128]{5,4,3,2,1,0:T(8,128)(2,1)S(1)}, u32[]{:S(2)}, u32[]{:S(2)}) collective-permute-start(bf16[2,2,2,8,8,128]{5,4,3,2,1,0:T(8,128)(2,1)S(1)} %get-tuple-element.51), channel_id=1, source_target_pairs={{0,3},{1,0},{2,1},{3,2},{4,7},{5,4},{6,5},{7,6},{8,11},{9,8},{10,9... | collective-permute-start | bytes 393224 | tf_op jit(solution)/shard_map/ppermute | solution.py:323
  117.6 16.9 %collective-permute-start.14 = (bf16[2,2,2,8,8,128]{5,4,3,2,1,0:T(8,128)(2,1)S(1)}, bf16[2,2,2,8,8,128]{5,4,3,2,1,0:T(8,128)(2,1)S(1)}, u32[]{:S(2)}, u32[]{:S(2)}) collective-permute-start(bf16[2,2,2,8,8,128]{5,4,3,2,1,0:T(8,128)(2,1)S(1)} %get-tuple-element.52), channel_id=1, source_target_pairs={{0,2},{1,3},{2,0},{3,1},{4,6},{5,7},{6,4},{7,5},{8,10},{9,11},{10,... | collective-permute-start | bytes 393224 | tf_op jit(solution)/shard_map/ppermute | solution.py:323
  121.8 12.7 %collective-permute-start.15 = (bf16[2,2,2,8,8,128]{5,4,3,2,1,0:T(8,128)(2,1)S(1)}, bf16[2,2,2,8,8,128]{5,4,3,2,1,0:T(8,128)(2,1)S(1)}, u32[]{:S(2)}, u32[]{:S(2)}) collective-permute-start(bf16[2,2,2,8,8,128]{5,4,3,2,1,0:T(8,128)(2,1)S(1)} %get-tuple-element.53), channel_id=1, source_target_pairs={{0,1},{1,2},{2,3},{3,0},{4,5},{5,6},{6,7},{7,4},{8,9},{9,10},{10,1... | collective-permute-start | bytes 393224 | tf_op jit(solution)/shard_map/ppermute | solution.py:323
  134.6 9.0 %collective-permute-start.16 = (bf16[2,2,8,8,128]{4,3,2,1,0:T(8,128)(2,1)S(1)}, bf16[2,2,8,8,128]{4,3,2,1,0:T(8,128)(2,1)S(1)}, u32[]{:S(2)}, u32[]{:S(2)}) collective-permute-start(bf16[2,2,8,8,128]{4,3,2,1,0:T(8,128)(2,1)S(1)} %get-tuple-element.58), channel_id=1, source_target_pairs={{0,12},{1,13},{2,14},{3,15},{4,8},{5,9},{6,10},{7,11},{8,4},{9,5},... | collective-permute-start | bytes 196616 | tf_op jit(solution)/shard_map/ppermute | solution.py:318
  144.9 17.0 %all-to-all-start.3 = ((bf16[32,2,2,2,4,128]{5,4,3,2,1,0:T(4,128)(2,1)}), bf16[32,2,2,2,4,128]{5,4,3,2,1,0:T(4,128)(2,1)S(1)}, u32[]{:S(2)}, u32[]{:S(2)}) async-start(bf16[32,2,2,2,4,128]{5,4,3,2,1,0:T(4,128)(2,1)} %bitcast.22), calls=%async_computation.3 | async-start | bytes 524288 | tf_op jit(solution)/shard_map/all_to_all | solution.py:356

commit v14 on v13

--- a/solution.py
+++ b/solution.py
@@ -198,7 +198,7 @@
 
     def unstage(block, _):
         for slot, ref in enumerate(dkv_refs):
-            rows = rows_of(slot, part // 2)
+            rows = rows_of(slot, part // 4)
             shape = ref.shape[:2] + ref.shape[4:]
             ref[:, :, 0, block] = (dk_all[block, rows] * SCALING).reshape(shape).astype(jnp.bfloat16)
             ref[:, :, 1, block] = dv_all[block, rows].reshape(shape).astype(jnp.bfloat16)
@@ -216,7 +216,7 @@
     return pl.pallas_call(
         attention_kernel,
         out_shape=(jax.ShapeDtypeStruct((slots, tile_rows, HD), jnp.bfloat16),)
-        + (jax.ShapeDtypeStruct((2,) + chunks[0].shape[1:], jnp.bfloat16),) * (2 * NEAR),
+        + tuple(jax.ShapeDtypeStruct(chunk.shape, jnp.bfloat16) for chunk in chunks),
         in_specs=[smem] * 3 + [vmem] * (1 + 2 * NEAR),
         out_specs=(vmem,) * (1 + 2 * NEAR),
         scratch_shapes=[
@@ -384,12 +384,13 @@
         query_back.reshape(n_replicas, slot_cap, tile_rows, row_width),
         "dp", split_axis=0, concat_axis=0, tiled=True,
     )
-    across_terms = near_terms(terms[NEAR:])
-    own_terms, across_terms = lax.optimization_barrier((terms[:NEAR], across_terms))
-    arrived = far_swap(total(across_terms).astype(jnp.bfloat16), ACROSS)
-    base = lax.optimization_barrier(total([arrived, own_terms[0]]))
-    summed = total([base] + near_terms(own_terms)[1:]).astype(jnp.bfloat16)
-    swapped = [summed[0], far_swap(summed[1], MIRROR)]
+    far_terms = near_terms(terms[NEAR:])
+    own_terms, far_terms = lax.optimization_barrier((terms[:NEAR], far_terms))
+    across = total([term[1:] for term in far_terms]).astype(jnp.bfloat16)
+    arrived = far_swap(across, ACROSS)
+    crossing = total([term[0] for term in far_terms] + [arrived[1]]).astype(jnp.bfloat16)
+    own_sum = total([term[0] for term in near_terms(own_terms)] + [arrived[0]]).astype(jnp.bfloat16)
+    swapped = [own_sum, far_swap(crossing, MIRROR)]
     swapped, query_returned = lax.optimization_barrier((swapped, query_returned))
     kv_returned = over_plane(
         local_call(kv_back_kernel, "kv_back", [my_recv, place], swapped, traveling)

time: 164 us -> 165 us (level)
  starting transfers between devices: 99.5 us -> 105 us
  waiting for transfers between devices: 37.8 us -> 34.2 us
    ppermute x12, waiting for transfers between devices: 22.7 us -> 17.6 us  [near_shift(): return lax.ppermute(values, 'z', pairs)]
    all_to_all x1, starting transfers between devices: 4.81 us -> 7.29 us  [on_device(): lax.all_to_all(query_back.reshape(n_replicas, slot_cap, tile_rows, row_wi...]
    ppermute x5, starting transfers between devices: 31.2 us -> 33.4 us  [far_swap(): lax.ppermute(values, 'z', [(place, place ^ flip) for place in range(16)])]
    all_to_all x2, starting transfers between devices: 18.5 us -> 20.2 us  [over_plane(): lax.all_to_all(values.reshape((2 * n_replicas,) + values.shape[2:]), PLAN...]
  transfers between devices with their start and end apart: 21 -> 21, of which waited for: 8 -> 9; matrix products, arithmetic and copies ran while one was open for 1% -> 1% of each run, Pallas kernels for 2% -> 2%
where the time goes in v14:
time: 165 us; the launch traced here: 164 us
  starting transfers between devices  105 us (64%)
  waiting for transfers between devices  34.2 us (21%)
  Pallas kernels  15.9 us (10%)
  local copies, waits for them, and re-layouts  7.23 us (4%)
    ppermute x12, starting transfers between devices, near_shift(): return lax.ppermute(values, 'z', pairs)  40.2 us
    ppermute x5, starting transfers between devices, far_swap(): lax.ppermute(values, 'z', [(place, place ^ flip) for place in range(16)])  33.4 us
    all_to_all x2, starting transfers between devices, over_plane(): lax.all_to_all(values.reshape((2 * n_replicas,) + values.shape[2:]), PLAN...  20.2 us
    ppermute x12, waiting for transfers between devices, near_shift(): return lax.ppermute(values, 'z', pairs)  17.6 us
    all_to_all x2, waiting for transfers between devices, over_plane(): lax.all_to_all(values.reshape((2 * n_replicas,) + values.shape[2:]), PLAN...  11.4 us
    pallas_call x1, Pallas kernels, attention(): pl.pallas_call(attention_kernel, out_shape=(jax.ShapeDtypeStruct((slots,...  9.09 us
    all_to_all x1, starting transfers between devices, on_device(): lax.all_to_all(query_back.reshape(n_replicas, slot_cap, tile_rows, row_wi...  7.29 us
    unnamed x20, local copies, waits for them, and re-layouts  5.81 us
  transfers between devices with their start and end apart: 21, of which 9 were waited for; matrix products, arithmetic and copies ran while one was open for 1% of the time, Pallas kernels for 2%

profile of v14, /device:TPU:1, one launch (start us, length us, event | category | flops | bytes accessed | tf_op | source)
XLA Modules:
  0.0 164.1 jit_solution(18002642559843836433)
XLA Ops:
  2.2 1.4 kv_pack.1
  3.7 10.4 %all-to-all-start = ((bf16[32,2,2,2,4,128]{5,4,3,2,1,0:T(4,128)(2,1)}), bf16[32,2,2,2,4,128]{5,4,3,2,1,0:T(4,128)(2,1)S(1)}, u32[]{:S(2)}, u32[]{:S(2)}) async-start(bf16[32,2,2,2,4,128]{5,4,3,2,1,0:T(4,128)(2,1)} %bitcast.7), calls=%async_computation | async-start | bytes 524288 | tf_op jit(solution)/shard_map/all_to_all | solution.py:356
  16.8 2.1 %pack_rows.1 = bf16[32,2,128,128]{3,2,1,0:T(8,128)(2,1)} custom-call(s32[2,16]{1,0:T(2,128)S(1)} %bitcast.38, bf16[16,128,128]{2,1,0:T(8,128)(2,1)S(1)} %copy-done, bf16[16,128,128]{2,1,0:T(8,128)(2,1)S(1)} %copy-done.1), custom_call_target="tpu_custom_call" | custom-call | tf_op jit(solution)/shard_map/pack_rows/pallas_call | solution.py:38
  19.0 4.0 %all-to-all-done = bf16[32,2,2,2,4,128]{5,4,3,2,1,0:T(4,128)(2,1)S(1)} async-done(((bf16[32,2,2,2,4,128]{5,4,3,2,1,0:T(4,128)(2,1)}), bf16[32,2,2,2,4,128]{5,4,3,2,1,0:T(4,128)(2,1)S(1)}, u32[]{:S(2)}, u32[]{:S(2)}) %all-to-all-start) | async-done | bytes 262176 | tf_op jit(solution)/shard_map/all_to_all | solution.py:356
  23.0 4.1 %all-to-all-start.1 = ((bf16[16,2,2,128,128]{4,3,2,1,0:T(8,128)(2,1)}), bf16[16,2,2,128,128]{4,3,2,1,0:T(8,128)(2,1)S(1)}, u32[]{:S(2)}, u32[]{:S(2)}) async-start(bf16[16,2,2,128,128]{4,3,2,1,0:T(8,128)(2,1)} %bitcast.14), calls=%async_computation.1 | async-start | bytes 4194304 | tf_op jit(solution)/shard_map/all_to_all | solution.py:369
  27.7 9.6 %collective-permute-start.1 = (bf16[2,2,8,8,128]{4,3,2,1,0:T(8,128)(2,1)S(1)}, bf16[2,2,8,8,128]{4,3,2,1,0:T(8,128)(2,1)S(1)}, u32[]{:S(2)}, u32[]{:S(2)}) collective-permute-start(bf16[2,2,8,8,128]{4,3,2,1,0:T(8,128)(2,1)S(1)} %get-tuple-element.31), channel_id=1, source_target_pairs={{0,6},{1,7},{2,4},{3,5},{4,2},{5,3},{6,0},{7,1},{8,14},{9,15},{10,... | collective-permute-start | bytes 196616 | tf_op jit(solution)/shard_map/ppermute | solution.py:318
  37.3 6.1 %collective-permute-start.2 = (bf16[2,2,8,8,128]{4,3,2,1,0:T(8,128)(2,1)S(1)}, bf16[2,2,8,8,128]{4,3,2,1,0:T(8,128)(2,1)S(1)}, u32[]{:S(2)}, u32[]{:S(2)}) collective-permute-start(bf16[2,2,8,8,128]{4,3,2,1,0:T(8,128)(2,1)S(1)} %get-tuple-element.30), channel_id=1, source_target_pairs={{0,10},{1,11},{2,8},{3,9},{4,14},{5,15},{6,12},{7,13},{8,2},{9,3},... | collective-permute-start | bytes 196616 | tf_op jit(solution)/shard_map/ppermute | solution.py:318
  43.5 1.9 %collective-permute-start = (bf16[2,2,8,8,128]{4,3,2,1,0:T(8,128)(2,1)S(1)}, bf16[2,2,8,8,128]{4,3,2,1,0:T(8,128)(2,1)S(1)}, u32[]{:S(2)}, u32[]{:S(2)}) collective-permute-start(bf16[2,2,8,8,128]{4,3,2,1,0:T(8,128)(2,1)S(1)} %get-tuple-element.30), channel_id=1, source_target_pairs={{0,12},{1,13},{2,14},{3,15},{4,8},{5,9},{6,10},{7,11},{8,4},{9,5},... | collective-permute-start | bytes 196616 | tf_op jit(solution)/shard_map/ppermute | solution.py:318
  45.4 2.6 %collective-permute-start.3 = (bf16[1,2,2,8,8,128]{5,4,3,2,1,0:T(8,128)(2,1)S(1)}, bf16[1,2,2,8,8,128]{5,4,3,2,1,0:T(8,128)(2,1)S(1)}, u32[]{:S(2)}, u32[]{:S(2)}) collective-permute-start(bf16[1,2,2,8,8,128]{5,4,3,2,1,0:T(8,128)(2,1)S(1)} %bitcast.40), channel_id=1, source_target_pairs={{0,1},{1,2},{2,3},{3,0},{4,5},{5,6},{6,7},{7,4},{8,9},{9,10},{10,1... | collective-permute-start | bytes 196616 | tf_op jit(solution)/shard_map/ppermute | solution.py:323
  48.1 4.9 %collective-permute-start.4 = (bf16[1,2,2,8,8,128]{5,4,3,2,1,0:T(8,128)(2,1)S(1)}, bf16[1,2,2,8,8,128]{5,4,3,2,1,0:T(8,128)(2,1)S(1)}, u32[]{:S(2)}, u32[]{:S(2)}) collective-permute-start(bf16[1,2,2,8,8,128]{5,4,3,2,1,0:T(8,128)(2,1)S(1)} %bitcast.41), channel_id=1, source_target_pairs={{0,2},{1,3},{2,0},{3,1},{4,6},{5,7},{6,4},{7,5},{8,10},{9,11},{10,... | collective-permute-start | bytes 196616 | tf_op jit(solution)/shard_map/ppermute | solution.py:323
  53.0 3.5 %collective-permute-start.5 = (bf16[1,2,2,8,8,128]{5,4,3,2,1,0:T(8,128)(2,1)S(1)}, bf16[1,2,2,8,8,128]{5,4,3,2,1,0:T(8,128)(2,1)S(1)}, u32[]{:S(2)}, u32[]{:S(2)}) collective-permute-start(bf16[1,2,2,8,8,128]{5,4,3,2,1,0:T(8,128)(2,1)S(1)} %bitcast.42), channel_id=1, source_target_pairs={{0,3},{1,0},{2,1},{3,2},{4,7},{5,4},{6,5},{7,6},{8,11},{9,8},{10,9... | collective-permute-start | bytes 196616 | tf_op jit(solution)/shard_map/ppermute | solution.py:323
  56.6 2.2 %collective-permute-done.4.refs_2_ = bf16[1,2,2,8,8,128]{5,4,3,2,1,0:T(8,128)(2,1)S(1)} collective-permute-done((bf16[1,2,2,8,8,128]{5,4,3,2,1,0:T(8,128)(2,1)S(1)}, bf16[1,2,2,8,8,128]{5,4,3,2,1,0:T(8,128)(2,1)S(1)}, u32[]{:S(2)}, u32[]{:S(2)}) %collective-permute-start.4) | collective-permute-done | bytes 65568 | tf_op jit(solution)/shard_map/ppermute | solution.py:323
  59.7 3.3 %collective-permute-start.6 = (bf16[3,2,2,8,8,128]{5,4,3,2,1,0:T(8,128)(2,1)S(1)}, bf16[3,2,2,8,8,128]{5,4,3,2,1,0:T(8,128)(2,1)S(1)}, u32[]{:S(2)}, u32[]{:S(2)}) collective-permute-start(bf16[3,2,2,8,8,128]{5,4,3,2,1,0:T(8,128)(2,1)S(1)} %pad_maximum_fusion.refs_4_), channel_id=1, source_target_pairs={{0,1},{1,2},{2,3},{3,0},{4,5},{5,6},{6,7},{7,4},{8,9},{9,10},{10,1... | collective-permute-start | bytes 589832 | tf_op jit(solution)/shard_map/ppermute | solution.py:323
  63.0 3.7 %collective-permute-start.7 = (bf16[3,2,2,8,8,128]{5,4,3,2,1,0:T(8,128)(2,1)S(1)}, bf16[3,2,2,8,8,128]{5,4,3,2,1,0:T(8,128)(2,1)S(1)}, u32[]{:S(2)}, u32[]{:S(2)}) collective-permute-start(bf16[3,2,2,8,8,128]{5,4,3,2,1,0:T(8,128)(2,1)S(1)} %pad_maximum_fusion.refs_4_), channel_id=1, source_target_pairs={{0,2},{1,3},{2,0},{3,1},{4,6},{5,7},{6,4},{7,5},{8,10},{9,11},{10,... | collective-permute-start | bytes 589832 | tf_op jit(solution)/shard_map/ppermute | solution.py:323
  66.7 2.4 %collective-permute-start.8 = (bf16[3,2,2,8,8,128]{5,4,3,2,1,0:T(8,128)(2,1)S(1)}, bf16[3,2,2,8,8,128]{5,4,3,2,1,0:T(8,128)(2,1)S(1)}, u32[]{:S(2)}, u32[]{:S(2)}) collective-permute-start(bf16[3,2,2,8,8,128]{5,4,3,2,1,0:T(8,128)(2,1)S(1)} %pad_maximum_fusion.refs_4_), channel_id=1, source_target_pairs={{0,3},{1,0},{2,1},{3,2},{4,7},{5,4},{6,5},{7,6},{8,11},{9,8},{10,9... | collective-permute-start | bytes 589832 | tf_op jit(solution)/shard_map/ppermute | solution.py:323
  69.3 9.5 %collective-permute-done.7.refs_6_ = bf16[3,2,2,8,8,128]{5,4,3,2,1,0:T(8,128)(2,1)S(1)} collective-permute-done((bf16[3,2,2,8,8,128]{5,4,3,2,1,0:T(8,128)(2,1)S(1)}, bf16[3,2,2,8,8,128]{5,4,3,2,1,0:T(8,128)(2,1)S(1)}, u32[]{:S(2)}, u32[]{:S(2)}) %collective-permute-start.7) | collective-permute-done | bytes 196640 | tf_op jit(solution)/shard_map/ppermute | solution.py:323
  79.6 9.1 %attention_backward.1 = (bf16[32,128,128]{2,1,0:T(8,128)(2,1)}, bf16[1,2,2,8,8,128]{5,4,3,2,1,0:T(8,128)(2,1)S(1)}, bf16[1,2,2,8,8,128]{5,4,3,2,1,0:T(8,128)(2,1...) custom-call(s32[16]{0:T(128)S(1)} %dynamic-slice_bitcast_fusion.recv, ...), custom_call_target="tpu_custom_call" | custom-call | flops 2000000000 | bytes 6291456 | tf_op jit(solution)/shard_map/attention_backward/pallas_call | solution.py:216
  88.7 5.5 %collective-permute-start.10 = (bf16[3,2,2,8,8,128]{5,4,3,2,1,0:T(8,128)(2,1)S(1)}, bf16[3,2,2,8,8,128]{5,4,3,2,1,0:T(8,128)(2,1)S(1)}, u32[]{:S(2)}, u32[]{:S(2)}) collective-permute-start(bf16[3,2,2,8,8,128]{5,4,3,2,1,0:T(8,128)(2,1)S(1)} %get-tuple-element.44), channel_id=1, source_target_pairs={{0,2},{1,3},{2,0},{3,1},{4,6},{5,7},{6,4},{7,5},{8,10},{9,11},{10,... | collective-permute-start | bytes 589832 | tf_op jit(solution)/shard_map/ppermute | solution.py:323
  94.3 2.9 %collective-permute-start.11 = (bf16[3,2,2,8,8,128]{5,4,3,2,1,0:T(8,128)(2,1)S(1)}, bf16[3,2,2,8,8,128]{5,4,3,2,1,0:T(8,128)(2,1)S(1)}, u32[]{:S(2)}, u32[]{:S(2)}) collective-permute-start(bf16[3,2,2,8,8,128]{5,4,3,2,1,0:T(8,128)(2,1)S(1)} %get-tuple-element.45), channel_id=1, source_target_pairs={{0,1},{1,2},{2,3},{3,0},{4,5},{5,6},{6,7},{7,4},{8,9},{9,10},{10,1... | collective-permute-start | bytes 589832 | tf_op jit(solution)/shard_map/ppermute | solution.py:323
  97.2 4.2 %collective-permute-start.9 = (bf16[3,2,2,8,8,128]{5,4,3,2,1,0:T(8,128)(2,1)S(1)}, bf16[3,2,2,8,8,128]{5,4,3,2,1,0:T(8,128)(2,1)S(1)}, u32[]{:S(2)}, u32[]{:S(2)}) collective-permute-start(bf16[3,2,2,8,8,128]{5,4,3,2,1,0:T(8,128)(2,1)S(1)} %get-tuple-element.43), channel_id=1, source_target_pairs={{0,3},{1,0},{2,1},{3,2},{4,7},{5,4},{6,5},{7,6},{8,11},{9,8},{10,9... | collective-permute-start | bytes 589832 | tf_op jit(solution)/shard_map/ppermute | solution.py:323
  101.4 7.3 %all-to-all-start.2 = ((bf16[16,2,128,128]{3,2,1,0:T(8,128)(2,1)}), bf16[16,2,128,128]{3,2,1,0:T(8,128)(2,1)S(1)}, u32[]{:S(2)}, u32[]{:S(2)}) async-start(bf16[16,2,128,128]{3,2,1,0:T(8,128)(2,1)} %bitcast.18), calls=%async_computation.2 | async-start | bytes 2097152 | tf_op jit(solution)/shard_map/all_to_all | solution.py:383
  108.8 11.9 %collective-permute-start.15 = (bf16[2,2,2,8,8,128]{5,4,3,2,1,0:T(8,128)(2,1)S(1)}, bf16[2,2,2,8,8,128]{5,4,3,2,1,0:T(8,128)(2,1)S(1)}, u32[]{:S(2)}, u32[]{:S(2)}) collective-permute-start(bf16[2,2,2,8,8,128]{5,4,3,2,1,0:T(8,128)(2,1)S(1)} %add_convert_fusion), channel_id=1, source_target_pairs={{0,6},{1,7},{2,4},{3,5},{4,2},{5,3},{6,0},{7,1},{8,14},{9,15},{10,... | collective-permute-start | bytes 393224 | tf_op jit(solution)/shard_map/ppermute | solution.py:318
  120.9 1.9 %collective-permute-start.12 = (bf16[1,2,2,8,8,128]{5,4,3,2,1,0:T(8,128)(2,1)S(1)}, bf16[1,2,2,8,8,128]{5,4,3,2,1,0:T(8,128)(2,1)S(1)}, u32[]{:S(2)}, u32[]{:S(2)}) collective-permute-start(bf16[1,2,2,8,8,128]{5,4,3,2,1,0:T(8,128)(2,1)S(1)} %get-tuple-element.47), channel_id=1, source_target_pairs={{0,3},{1,0},{2,1},{3,2},{4,7},{5,4},{6,5},{7,6},{8,11},{9,8},{10,9... | collective-permute-start | bytes 196616 | tf_op jit(solution)/shard_map/ppermute | solution.py:323
  122.8 1.9 %collective-permute-start.13 = (bf16[1,2,2,8,8,128]{5,4,3,2,1,0:T(8,128)(2,1)S(1)}, bf16[1,2,2,8,8,128]{5,4,3,2,1,0:T(8,128)(2,1)S(1)}, u32[]{:S(2)}, u32[]{:S(2)}) collective-permute-start(bf16[1,2,2,8,8,128]{5,4,3,2,1,0:T(8,128)(2,1)S(1)} %get-tuple-element.48), channel_id=1, source_target_pairs={{0,2},{1,3},{2,0},{3,1},{4,6},{5,7},{6,4},{7,5},{8,10},{9,11},{10,... | collective-permute-start | bytes 196616 | tf_op jit(solution)/shard_map/ppermute | solution.py:323
  124.7 3.4 %collective-permute-start.14 = (bf16[1,2,2,8,8,128]{5,4,3,2,1,0:T(8,128)(2,1)S(1)}, bf16[1,2,2,8,8,128]{5,4,3,2,1,0:T(8,128)(2,1)S(1)}, u32[]{:S(2)}, u32[]{:S(2)}) collective-permute-start(bf16[1,2,2,8,8,128]{5,4,3,2,1,0:T(8,128)(2,1)S(1)} %get-tuple-element.49), channel_id=1, source_target_pairs={{0,1},{1,2},{2,3},{3,0},{4,5},{5,6},{6,7},{7,4},{8,9},{9,10},{10,1... | collective-permute-start | bytes 196616 | tf_op jit(solution)/shard_map/ppermute | solution.py:323
  128.3 1.4 collective-permute-done.13
  129.7 4.0 %collective-permute-done.14 = bf16[1,2,2,8,8,128]{5,4,3,2,1,0:T(8,128)(2,1)S(1)} collective-permute-done((bf16[1,2,2,8,8,128]{5,4,3,2,1,0:T(8,128)(2,1)S(1)}, bf16[1,2,2,8,8,128]{5,4,3,2,1,0:T(8,128)(2,1)S(1)}, u32[]{:S(2)}, u32[]{:S(2)}) %collective-permute-start.14) | collective-permute-done | bytes 65568 | tf_op jit(solution)/shard_map/ppermute | solution.py:323
  133.8 3.8 %collective-permute-start.16 = (bf16[2,2,8,8,128]{4,3,2,1,0:T(8,128)(2,1)S(1)}, bf16[2,2,8,8,128]{4,3,2,1,0:T(8,128)(2,1)S(1)}, u32[]{:S(2)}, u32[]{:S(2)}) collective-permute-start(bf16[2,2,8,8,128]{4,3,2,1,0:T(8,128)(2,1)S(1)} %get-tuple-element.58), channel_id=1, source_target_pairs={{0,12},{1,13},{2,14},{3,15},{4,8},{5,9},{6,10},{7,11},{8,4},{9,5},... | collective-permute-start | bytes 196616 | tf_op jit(solution)/shard_map/ppermute | solution.py:318
  137.7 5.2 %collective-permute-done.16.other_ref = bf16[2,2,8,8,128]{4,3,2,1,0:T(8,128)(2,1)S(1)} collective-permute-done((bf16[2,2,8,8,128]{4,3,2,1,0:T(8,128)(2,1)S(1)}, bf16[2,2,8,8,128]{4,3,2,1,0:T(8,128)(2,1)S(1)}, u32[]{:S(2)}, u32[]{:S(2)}) %collective-permute-start.16) | collective-permute-done | bytes 65568 | tf_op jit(solution)/shard_map/ppermute | solution.py:318
  144.2 9.8 %all-to-all-start.3 = ((bf16[32,2,2,2,4,128]{5,4,3,2,1,0:T(4,128)(2,1)}), bf16[32,2,2,2,4,128]{5,4,3,2,1,0:T(4,128)(2,1)S(1)}, u32[]{:S(2)}, u32[]{:S(2)}) async-start(bf16[32,2,2,2,4,128]{5,4,3,2,1,0:T(4,128)(2,1)} %bitcast.22), calls=%async_computation.3 | async-start | bytes 524288 | tf_op jit(solution)/shard_map/all_to_all | solution.py:356
  154.0 1.4 gather_fusion
  155.4 7.4 %all-to-all-done.3 = bf16[32,2,2,2,4,128]{5,4,3,2,1,0:T(4,128)(2,1)S(1)} async-done(((bf16[32,2,2,2,4,128]{5,4,3,2,1,0:T(4,128)(2,1)}), bf16[32,2,2,2,4,128]{5,4,3,2,1,0:T(4,128)(2,1)S(1)}, u32[]{:S(2)}, u32[]{:S(2)}) %all-to-all-start.3) | async-done | bytes 262176 | tf_op jit(solution)/shard_map/all_to_all | solution.py:356
  (48 shorter events, 10.2 us)
Async XLA Ops:
  0.6 0.9 copy-start.2
  1.5 0.7 copy-start.3
  3.7 19.3 %all-to-all-start = ((bf16[32,2,2,2,4,128]{5,4,3,2,1,0:T(4,128)(2,1)}), bf16[32,2,2,2,4,128]{5,4,3,2,1,0:T(4,128)(2,1)S(1)}, u32[]{:S(2)}, u32[]{:S(2)}) async-start(bf16[32,2,2,2,4,128]{5,4,3,2,1,0:T(4,128)(2,1)} %bitcast.7), calls=%async_computation | async-start | bytes 524288 | tf_op jit(solution)/shard_map/all_to_all | solution.py:356
  14.1 1.0 copy-start
  15.1 1.0 copy-start.1
  16.2 0.7 copy-start.4
  23.0 4.1 %copy-start.8 = (s32[16,16]{1,0:T(8,128)S(1)}, s32[16,16]{1,0:T(8,128)}, u32[]{:S(2)}) copy-start(s32[16,16]{1,0:T(8,128)} %param.10) | copy-start | bytes 3076
  23.0 46.1 %copy-start.9 = (s32[1,16]{1,0:T(1,128)S(1)}, s32[1,16]{1,0:T(1,128)}, u32[]{:S(2)}) copy-start(s32[1,16]{1,0:T(1,128)} %param.11) | copy-start | bytes 196
  23.0 36.7 %all-to-all-start.1 = ((bf16[16,2,2,128,128]{4,3,2,1,0:T(8,128)(2,1)}), bf16[16,2,2,128,128]{4,3,2,1,0:T(8,128)(2,1)S(1)}, u32[]{:S(2)}, u32[]{:S(2)}) async-start(bf16[16,2,2,128,128]{4,3,2,1,0:T(8,128)(2,1)} %bitcast.14), calls=%async_computation.1 | async-start | bytes 4194304 | tf_op jit(solution)/shard_map/all_to_all | solution.py:369
  27.7 25.3 %collective-permute-start.1 = (bf16[2,2,8,8,128]{4,3,2,1,0:T(8,128)(2,1)S(1)}, bf16[2,2,8,8,128]{4,3,2,1,0:T(8,128)(2,1)S(1)}, u32[]{:S(2)}, u32[]{:S(2)}) collective-permute-start(bf16[2,2,8,8,128]{4,3,2,1,0:T(8,128)(2,1)S(1)} %get-tuple-element.31), channel_id=1, source_target_pairs={{0,6},{1,7},{2,4},{3,5},{4,2},{5,3},{6,0},{7,1},{8,14},{9,15},{10,... | collective-permute-start | bytes 196616 | tf_op jit(solution)/shard_map/ppermute | solution.py:318
  37.3 19.2 %collective-permute-start.2 = (bf16[2,2,8,8,128]{4,3,2,1,0:T(8,128)(2,1)S(1)}, bf16[2,2,8,8,128]{4,3,2,1,0:T(8,128)(2,1)S(1)}, u32[]{:S(2)}, u32[]{:S(2)}) collective-permute-start(bf16[2,2,8,8,128]{4,3,2,1,0:T(8,128)(2,1)S(1)} %get-tuple-element.30), channel_id=1, source_target_pairs={{0,10},{1,11},{2,8},{3,9},{4,14},{5,15},{6,12},{7,13},{8,2},{9,3},... | collective-permute-start | bytes 196616 | tf_op jit(solution)/shard_map/ppermute | solution.py:318
  43.5 13.1 %collective-permute-start = (bf16[2,2,8,8,128]{4,3,2,1,0:T(8,128)(2,1)S(1)}, bf16[2,2,8,8,128]{4,3,2,1,0:T(8,128)(2,1)S(1)}, u32[]{:S(2)}, u32[]{:S(2)}) collective-permute-start(bf16[2,2,8,8,128]{4,3,2,1,0:T(8,128)(2,1)S(1)} %get-tuple-element.30), channel_id=1, source_target_pairs={{0,12},{1,13},{2,14},{3,15},{4,8},{5,9},{6,10},{7,11},{8,4},{9,5},... | collective-permute-start | bytes 196616 | tf_op jit(solution)/shard_map/ppermute | solution.py:318
  45.4 11.2 %collective-permute-start.3 = (bf16[1,2,2,8,8,128]{5,4,3,2,1,0:T(8,128)(2,1)S(1)}, bf16[1,2,2,8,8,128]{5,4,3,2,1,0:T(8,128)(2,1)S(1)}, u32[]{:S(2)}, u32[]{:S(2)}) collective-permute-start(bf16[1,2,2,8,8,128]{5,4,3,2,1,0:T(8,128)(2,1)S(1)} %bitcast.40), channel_id=1, source_target_pairs={{0,1},{1,2},{2,3},{3,0},{4,5},{5,6},{6,7},{7,4},{8,9},{9,10},{10,1... | collective-permute-start | bytes 196616 | tf_op jit(solution)/shard_map/ppermute | solution.py:323
  48.1 10.8 %collective-permute-start.4 = (bf16[1,2,2,8,8,128]{5,4,3,2,1,0:T(8,128)(2,1)S(1)}, bf16[1,2,2,8,8,128]{5,4,3,2,1,0:T(8,128)(2,1)S(1)}, u32[]{:S(2)}, u32[]{:S(2)}) collective-permute-start(bf16[1,2,2,8,8,128]{5,4,3,2,1,0:T(8,128)(2,1)S(1)} %bitcast.41), channel_id=1, source_target_pairs={{0,2},{1,3},{2,0},{3,1},{4,6},{5,7},{6,4},{7,5},{8,10},{9,11},{10,... | collective-permute-start | bytes 196616 | tf_op jit(solution)/shard_map/ppermute | solution.py:323
  53.0 6.1 %collective-permute-start.5 = (bf16[1,2,2,8,8,128]{5,4,3,2,1,0:T(8,128)(2,1)S(1)}, bf16[1,2,2,8,8,128]{5,4,3,2,1,0:T(8,128)(2,1)S(1)}, u32[]{:S(2)}, u32[]{:S(2)}) collective-permute-start(bf16[1,2,2,8,8,128]{5,4,3,2,1,0:T(8,128)(2,1)S(1)} %bitcast.42), channel_id=1, source_target_pairs={{0,3},{1,0},{2,1},{3,2},{4,7},{5,4},{6,5},{7,6},{8,11},{9,8},{10,9... | collective-permute-start | bytes 196616 | tf_op jit(solution)/shard_map/ppermute | solution.py:323
  59.1 0.6 copy-start.6
  59.7 9.6 %collective-permute-start.6 = (bf16[3,2,2,8,8,128]{5,4,3,2,1,0:T(8,128)(2,1)S(1)}, bf16[3,2,2,8,8,128]{5,4,3,2,1,0:T(8,128)(2,1)S(1)}, u32[]{:S(2)}, u32[]{:S(2)}) collective-permute-start(bf16[3,2,2,8,8,128]{5,4,3,2,1,0:T(8,128)(2,1)S(1)} %pad_maximum_fusion.refs_4_), channel_id=1, source_target_pairs={{0,1},{1,2},{2,3},{3,0},{4,5},{5,6},{6,7},{7,4},{8,9},{9,10},{10,1... | collective-permute-start | bytes 589832 | tf_op jit(solution)/shard_map/ppermute | solution.py:323
  63.0 15.7 %collective-permute-start.7 = (bf16[3,2,2,8,8,128]{5,4,3,2,1,0:T(8,128)(2,1)S(1)}, bf16[3,2,2,8,8,128]{5,4,3,2,1,0:T(8,128)(2,1)S(1)}, u32[]{:S(2)}, u32[]{:S(2)}) collective-permute-start(bf16[3,2,2,8,8,128]{5,4,3,2,1,0:T(8,128)(2,1)S(1)} %pad_maximum_fusion.refs_4_), channel_id=1, source_target_pairs={{0,2},{1,3},{2,0},{3,1},{4,6},{5,7},{6,4},{7,5},{8,10},{9,11},{10,... | collective-permute-start | bytes 589832 | tf_op jit(solution)/shard_map/ppermute | solution.py:323
  66.7 12.1 %collective-permute-start.8 = (bf16[3,2,2,8,8,128]{5,4,3,2,1,0:T(8,128)(2,1)S(1)}, bf16[3,2,2,8,8,128]{5,4,3,2,1,0:T(8,128)(2,1)S(1)}, u32[]{:S(2)}, u32[]{:S(2)}) collective-permute-start(bf16[3,2,2,8,8,128]{5,4,3,2,1,0:T(8,128)(2,1)S(1)} %pad_maximum_fusion.refs_4_), channel_id=1, source_target_pairs={{0,3},{1,0},{2,1},{3,2},{4,7},{5,4},{6,5},{7,6},{8,11},{9,8},{10,9... | collective-permute-start | bytes 589832 | tf_op jit(solution)/shard_map/ppermute | solution.py:323
  78.8 0.8 copy-start.7
  88.7 48.8 %copy-start.5 = (s32[1,16,2]{1,2,0:T(2,128)S(1)}, s32[1,16,2]{1,2,0:T(2,128)}, u32[]{:S(2)}) copy-start(s32[1,16,2]{1,2,0:T(2,128)} %param.9) | copy-start | bytes 388
  88.7 19.9 %collective-permute-start.10 = (bf16[3,2,2,8,8,128]{5,4,3,2,1,0:T(8,128)(2,1)S(1)}, bf16[3,2,2,8,8,128]{5,4,3,2,1,0:T(8,128)(2,1)S(1)}, u32[]{:S(2)}, u32[]{:S(2)}) collective-permute-start(bf16[3,2,2,8,8,128]{5,4,3,2,1,0:T(8,128)(2,1)S(1)} %get-tuple-element.44), channel_id=1, source_target_pairs={{0,2},{1,3},{2,0},{3,1},{4,6},{5,7},{6,4},{7,5},{8,10},{9,11},{10,... | collective-permute-start | bytes 589832 | tf_op jit(solution)/shard_map/ppermute | solution.py:323
  94.3 14.4 %collective-permute-start.11 = (bf16[3,2,2,8,8,128]{5,4,3,2,1,0:T(8,128)(2,1)S(1)}, bf16[3,2,2,8,8,128]{5,4,3,2,1,0:T(8,128)(2,1)S(1)}, u32[]{:S(2)}, u32[]{:S(2)}) collective-permute-start(bf16[3,2,2,8,8,128]{5,4,3,2,1,0:T(8,128)(2,1)S(1)} %get-tuple-element.45), channel_id=1, source_target_pairs={{0,1},{1,2},{2,3},{3,0},{4,5},{5,6},{6,7},{7,4},{8,9},{9,10},{10,1... | collective-permute-start | bytes 589832 | tf_op jit(solution)/shard_map/ppermute | solution.py:323
  97.2 11.5 %collective-permute-start.9 = (bf16[3,2,2,8,8,128]{5,4,3,2,1,0:T(8,128)(2,1)S(1)}, bf16[3,2,2,8,8,128]{5,4,3,2,1,0:T(8,128)(2,1)S(1)}, u32[]{:S(2)}, u32[]{:S(2)}) collective-permute-start(bf16[3,2,2,8,8,128]{5,4,3,2,1,0:T(8,128)(2,1)S(1)} %get-tuple-element.43), channel_id=1, source_target_pairs={{0,3},{1,0},{2,1},{3,2},{4,7},{5,4},{6,5},{7,6},{8,11},{9,8},{10,9... | collective-permute-start | bytes 589832 | tf_op jit(solution)/shard_map/ppermute | solution.py:323
  101.4 41.6 %all-to-all-start.2 = ((bf16[16,2,128,128]{3,2,1,0:T(8,128)(2,1)}), bf16[16,2,128,128]{3,2,1,0:T(8,128)(2,1)S(1)}, u32[]{:S(2)}, u32[]{:S(2)}) async-start(bf16[16,2,128,128]{3,2,1,0:T(8,128)(2,1)} %bitcast.18), calls=%async_computation.2 | async-start | bytes 2097152 | tf_op jit(solution)/shard_map/all_to_all | solution.py:383
  108.8 24.9 %collective-permute-start.15 = (bf16[2,2,2,8,8,128]{5,4,3,2,1,0:T(8,128)(2,1)S(1)}, bf16[2,2,2,8,8,128]{5,4,3,2,1,0:T(8,128)(2,1)S(1)}, u32[]{:S(2)}, u32[]{:S(2)}) collective-permute-start(bf16[2,2,2,8,8,128]{5,4,3,2,1,0:T(8,128)(2,1)S(1)} %add_convert_fusion), channel_id=1, source_target_pairs={{0,6},{1,7},{2,4},{3,5},{4,2},{5,3},{6,0},{7,1},{8,14},{9,15},{10,... | collective-permute-start | bytes 393224 | tf_op jit(solution)/shard_map/ppermute | solution.py:318
  120.9 7.4 %collective-permute-start.12 = (bf16[1,2,2,8,8,128]{5,4,3,2,1,0:T(8,128)(2,1)S(1)}, bf16[1,2,2,8,8,128]{5,4,3,2,1,0:T(8,128)(2,1)S(1)}, u32[]{:S(2)}, u32[]{:S(2)}) collective-permute-start(bf16[1,2,2,8,8,128]{5,4,3,2,1,0:T(8,128)(2,1)S(1)} %get-tuple-element.47), channel_id=1, source_target_pairs={{0,3},{1,0},{2,1},{3,2},{4,7},{5,4},{6,5},{7,6},{8,11},{9,8},{10,9... | collective-permute-start | bytes 196616 | tf_op jit(solution)/shard_map/ppermute | solution.py:323
  122.8 6.9 %collective-permute-start.13 = (bf16[1,2,2,8,8,128]{5,4,3,2,1,0:T(8,128)(2,1)S(1)}, bf16[1,2,2,8,8,128]{5,4,3,2,1,0:T(8,128)(2,1)S(1)}, u32[]{:S(2)}, u32[]{:S(2)}) collective-permute-start(bf16[1,2,2,8,8,128]{5,4,3,2,1,0:T(8,128)(2,1)S(1)} %get-tuple-element.48), channel_id=1, source_target_pairs={{0,2},{1,3},{2,0},{3,1},{4,6},{5,7},{6,4},{7,5},{8,10},{9,11},{10,... | collective-permute-start | bytes 196616 | tf_op jit(solution)/shard_map/ppermute | solution.py:323
  124.7 8.9 %collective-permute-start.14 = (bf16[1,2,2,8,8,128]{5,4,3,2,1,0:T(8,128)(2,1)S(1)}, bf16[1,2,2,8,8,128]{5,4,3,2,1,0:T(8,128)(2,1)S(1)}, u32[]{:S(2)}, u32[]{:S(2)}) collective-permute-start(bf16[1,2,2,8,8,128]{5,4,3,2,1,0:T(8,128)(2,1)S(1)} %get-tuple-element.49), channel_id=1, source_target_pairs={{0,1},{1,2},{2,3},{3,0},{4,5},{5,6},{6,7},{7,4},{8,9},{9,10},{10,1... | collective-permute-start | bytes 196616 | tf_op jit(solution)/shard_map/ppermute | solution.py:323
  133.8 9.1 %collective-permute-start.16 = (bf16[2,2,8,8,128]{4,3,2,1,0:T(8,128)(2,1)S(1)}, bf16[2,2,8,8,128]{4,3,2,1,0:T(8,128)(2,1)S(1)}, u32[]{:S(2)}, u32[]{:S(2)}) collective-permute-start(bf16[2,2,8,8,128]{4,3,2,1,0:T(8,128)(2,1)S(1)} %get-tuple-element.58), channel_id=1, source_target_pairs={{0,12},{1,13},{2,14},{3,15},{4,8},{5,9},{6,10},{7,11},{8,4},{9,5},... | collective-permute-start | bytes 196616 | tf_op jit(solution)/shard_map/ppermute | solution.py:318
  144.2 18.6 %all-to-all-start.3 = ((bf16[32,2,2,2,4,128]{5,4,3,2,1,0:T(4,128)(2,1)}), bf16[32,2,2,2,4,128]{5,4,3,2,1,0:T(4,128)(2,1)S(1)}, u32[]{:S(2)}, u32[]{:S(2)}) async-start(bf16[32,2,2,2,4,128]{5,4,3,2,1,0:T(4,128)(2,1)} %bitcast.22), calls=%async_computation.3 | async-start | bytes 524288 | tf_op jit(solution)/shard_map/all_to_all | solution.py:356

commit v15 on v14

--- a/solution.py
+++ b/solution.py
@@ -270,7 +270,8 @@
     lax.fori_loop(0, recv_ref.shape[0] // PAIR, body, 0, unroll=4)
 
 
-def kv_back_kernel(recv_ref, place_ref, own_ref, other_ref, out_ref):
+def kv_back_kernel(recv_ref, place_ref, *refs):
+    own_refs, (across_ref, other_ref, out_ref) = refs[:NEAR], refs[NEAR:]
     head = place_ref[0] >> 3
     sliver = out_ref.shape[-2]
 
@@ -278,8 +279,11 @@
         slots = (recv_ref[PAIR * pair], recv_ref[PAIR * pair + 1])
         for half in range(2):
             for kind in range(2):
-                for ref, which in ((own_ref, head), (other_ref, 1 - head)):
-                    total = ref[half, kind, pair].astype(jnp.float32)
+                own = across_ref[0, half, kind, pair].astype(jnp.float32)
+                for ref in own_refs:
+                    own += ref[0, half, kind, pair].astype(jnp.float32)
+                other = other_ref[half, kind, pair].astype(jnp.float32)
+                for total, which in ((own, head), (other, 1 - head)):
                     for order, slot in enumerate(slots):
                         rows = total[order * sliver : (order + 1) * sliver]
                         out_ref[slot >> 1, half, slot & 1, kind, which] = rows.astype(jnp.bfloat16)
@@ -389,11 +393,11 @@
     across = total([term[1:] for term in far_terms]).astype(jnp.bfloat16)
     arrived = far_swap(across, ACROSS)
     crossing = total([term[0] for term in far_terms] + [arrived[1]]).astype(jnp.bfloat16)
-    own_sum = total([term[0] for term in near_terms(own_terms)] + [arrived[0]]).astype(jnp.bfloat16)
-    swapped = [own_sum, far_swap(crossing, MIRROR)]
-    swapped, query_returned = lax.optimization_barrier((swapped, query_returned))
+    other = far_swap(crossing, MIRROR)
+    last = near_terms(own_terms) + [arrived, other]
+    last, query_returned = lax.optimization_barrier((last, query_returned))
     kv_returned = over_plane(
-        local_call(kv_back_kernel, "kv_back", [my_recv, place], swapped, traveling)
+        local_call(kv_back_kernel, "kv_back", [my_recv, place], last, traveling)
     )
 
     flat_slots = jnp.arange(slots)

time: 165 us -> 160 us (0.970)
  waiting for transfers between devices: 34.2 us -> 30.2 us
  starting transfers between devices: 105 us -> 102 us
    all_to_all x2, starting transfers between devices: 20.2 us -> 15.5 us  [over_plane(): lax.all_to_all(values.reshape((2 * n_replicas,) + values.shape[2:]), PLAN...]
    ppermute x12, waiting for transfers between devices: 17.6 us -> 14.5 us  [near_shift(): return lax.ppermute(values, 'z', pairs)]
    ppermute x5, starting transfers between devices: 33.4 us -> 35.1 us  [far_swap(): lax.ppermute(values, 'z', [(place, place ^ flip) for place in range(16)])]
  transfers between devices with their start and end apart: 21 -> 21, of which waited for: 9 -> 7; matrix products, arithmetic and copies ran while one was open for 1% -> 1% of each run, Pallas kernels for 2% -> 2%
where the time goes in v15:
time: 160 us; the launch traced here: 158 us
  starting transfers between devices  102 us (64%)
  waiting for transfers between devices  30.2 us (19%)
  Pallas kernels  16.9 us (11%)
  local copies, waits for them, and re-layouts  7.23 us (5%)
    ppermute x12, starting transfers between devices, near_shift(): return lax.ppermute(values, 'z', pairs)  40.3 us
    ppermute x5, starting transfers between devices, far_swap(): lax.ppermute(values, 'z', [(place, place ^ flip) for place in range(16)])  35.1 us
    all_to_all x2, starting transfers between devices, over_plane(): lax.all_to_all(values.reshape((2 * n_replicas,) + values.shape[2:]), PLAN...  15.5 us
    ppermute x12, waiting for transfers between devices, near_shift(): return lax.ppermute(values, 'z', pairs)  14.5 us
    all_to_all x2, waiting for transfers between devices, over_plane(): lax.all_to_all(values.reshape((2 * n_replicas,) + values.shape[2:]), PLAN...  11.4 us
    pallas_call x1, Pallas kernels, attention(): pl.pallas_call(attention_kernel, out_shape=(jax.ShapeDtypeStruct((slots,...  10.1 us
    all_to_all x1, starting transfers between devices, on_device(): lax.all_to_all(query_back.reshape(n_replicas, slot_cap, tile_rows, row_wi...  7.39 us
    unnamed x20, local copies, waits for them, and re-layouts  5.81 us
  transfers between devices with their start and end apart: 21, of which 7 were waited for; matrix products, arithmetic and copies ran while one was open for 1% of the time, Pallas kernels for 2%

profile of v15, /device:TPU:1, one launch (start us, length us, event | category | flops | bytes accessed | tf_op | source)
XLA Modules:
  0.0 158.3 jit_solution(16688054331585269334)
XLA Ops:
  2.2 1.4 kv_pack.1
  3.7 10.4 %all-to-all-start = ((bf16[32,2,2,2,4,128]{5,4,3,2,1,0:T(4,128)(2,1)}), bf16[32,2,2,2,4,128]{5,4,3,2,1,0:T(4,128)(2,1)S(1)}, u32[]{:S(2)}, u32[]{:S(2)}) async-start(bf16[32,2,2,2,4,128]{5,4,3,2,1,0:T(4,128)(2,1)} %bitcast.7), calls=%async_computation | async-start | bytes 524288 | tf_op jit(solution)/shard_map/all_to_all | solution.py:360
  16.8 2.2 %pack_rows.1 = bf16[32,2,128,128]{3,2,1,0:T(8,128)(2,1)} custom-call(s32[2,16]{1,0:T(2,128)S(1)} %bitcast.36, bf16[16,128,128]{2,1,0:T(8,128)(2,1)S(1)} %copy-done, bf16[16,128,128]{2,1,0:T(8,128)(2,1)S(1)} %copy-done.1), custom_call_target="tpu_custom_call" | custom-call | tf_op jit(solution)/shard_map/pack_rows/pallas_call | solution.py:38
  19.0 4.0 %all-to-all-done = bf16[32,2,2,2,4,128]{5,4,3,2,1,0:T(4,128)(2,1)S(1)} async-done(((bf16[32,2,2,2,4,128]{5,4,3,2,1,0:T(4,128)(2,1)}), bf16[32,2,2,2,4,128]{5,4,3,2,1,0:T(4,128)(2,1)S(1)}, u32[]{:S(2)}, u32[]{:S(2)}) %all-to-all-start) | async-done | bytes 262176 | tf_op jit(solution)/shard_map/all_to_all | solution.py:360
  23.0 4.1 %all-to-all-start.1 = ((bf16[16,2,2,128,128]{4,3,2,1,0:T(8,128)(2,1)}), bf16[16,2,2,128,128]{4,3,2,1,0:T(8,128)(2,1)S(1)}, u32[]{:S(2)}, u32[]{:S(2)}) async-start(bf16[16,2,2,128,128]{4,3,2,1,0:T(8,128)(2,1)} %bitcast.14), calls=%async_computation.1 | async-start | bytes 4194304 | tf_op jit(solution)/shard_map/all_to_all | solution.py:373
  27.7 9.6 %collective-permute-start.1 = (bf16[2,2,8,8,128]{4,3,2,1,0:T(8,128)(2,1)S(1)}, bf16[2,2,8,8,128]{4,3,2,1,0:T(8,128)(2,1)S(1)}, u32[]{:S(2)}, u32[]{:S(2)}) collective-permute-start(bf16[2,2,8,8,128]{4,3,2,1,0:T(8,128)(2,1)S(1)} %get-tuple-element.35), channel_id=1, source_target_pairs={{0,6},{1,7},{2,4},{3,5},{4,2},{5,3},{6,0},{7,1},{8,14},{9,15},{10,... | collective-permute-start | bytes 196616 | tf_op jit(solution)/shard_map/ppermute | solution.py:322
  37.3 6.1 %collective-permute-start.2 = (bf16[2,2,8,8,128]{4,3,2,1,0:T(8,128)(2,1)S(1)}, bf16[2,2,8,8,128]{4,3,2,1,0:T(8,128)(2,1)S(1)}, u32[]{:S(2)}, u32[]{:S(2)}) collective-permute-start(bf16[2,2,8,8,128]{4,3,2,1,0:T(8,128)(2,1)S(1)} %get-tuple-element.34), channel_id=1, source_target_pairs={{0,10},{1,11},{2,8},{3,9},{4,14},{5,15},{6,12},{7,13},{8,2},{9,3},... | collective-permute-start | bytes 196616 | tf_op jit(solution)/shard_map/ppermute | solution.py:322
  43.5 1.9 %collective-permute-start = (bf16[2,2,8,8,128]{4,3,2,1,0:T(8,128)(2,1)S(1)}, bf16[2,2,8,8,128]{4,3,2,1,0:T(8,128)(2,1)S(1)}, u32[]{:S(2)}, u32[]{:S(2)}) collective-permute-start(bf16[2,2,8,8,128]{4,3,2,1,0:T(8,128)(2,1)S(1)} %get-tuple-element.34), channel_id=1, source_target_pairs={{0,12},{1,13},{2,14},{3,15},{4,8},{5,9},{6,10},{7,11},{8,4},{9,5},... | collective-permute-start | bytes 196616 | tf_op jit(solution)/shard_map/ppermute | solution.py:322
  45.4 2.6 %collective-permute-start.3 = (bf16[1,2,2,8,8,128]{5,4,3,2,1,0:T(8,128)(2,1)S(1)}, bf16[1,2,2,8,8,128]{5,4,3,2,1,0:T(8,128)(2,1)S(1)}, u32[]{:S(2)}, u32[]{:S(2)}) collective-permute-start(bf16[1,2,2,8,8,128]{5,4,3,2,1,0:T(8,128)(2,1)S(1)} %bitcast.38), channel_id=1, source_target_pairs={{0,1},{1,2},{2,3},{3,0},{4,5},{5,6},{6,7},{7,4},{8,9},{9,10},{10,1... | collective-permute-start | bytes 196616 | tf_op jit(solution)/shard_map/ppermute | solution.py:327
  48.1 4.9 %collective-permute-start.4 = (bf16[1,2,2,8,8,128]{5,4,3,2,1,0:T(8,128)(2,1)S(1)}, bf16[1,2,2,8,8,128]{5,4,3,2,1,0:T(8,128)(2,1)S(1)}, u32[]{:S(2)}, u32[]{:S(2)}) collective-permute-start(bf16[1,2,2,8,8,128]{5,4,3,2,1,0:T(8,128)(2,1)S(1)} %bitcast.39), channel_id=1, source_target_pairs={{0,2},{1,3},{2,0},{3,1},{4,6},{5,7},{6,4},{7,5},{8,10},{9,11},{10,... | collective-permute-start | bytes 196616 | tf_op jit(solution)/shard_map/ppermute | solution.py:327
  53.0 3.5 %collective-permute-start.5 = (bf16[1,2,2,8,8,128]{5,4,3,2,1,0:T(8,128)(2,1)S(1)}, bf16[1,2,2,8,8,128]{5,4,3,2,1,0:T(8,128)(2,1)S(1)}, u32[]{:S(2)}, u32[]{:S(2)}) collective-permute-start(bf16[1,2,2,8,8,128]{5,4,3,2,1,0:T(8,128)(2,1)S(1)} %bitcast.40), channel_id=1, source_target_pairs={{0,3},{1,0},{2,1},{3,2},{4,7},{5,4},{6,5},{7,6},{8,11},{9,8},{10,9... | collective-permute-start | bytes 196616 | tf_op jit(solution)/shard_map/ppermute | solution.py:327
  56.6 2.2 %collective-permute-done.4.refs_2_ = bf16[1,2,2,8,8,128]{5,4,3,2,1,0:T(8,128)(2,1)S(1)} collective-permute-done((bf16[1,2,2,8,8,128]{5,4,3,2,1,0:T(8,128)(2,1)S(1)}, bf16[1,2,2,8,8,128]{5,4,3,2,1,0:T(8,128)(2,1)S(1)}, u32[]{:S(2)}, u32[]{:S(2)}) %collective-permute-start.4) | collective-permute-done | bytes 65568 | tf_op jit(solution)/shard_map/ppermute | solution.py:327
  59.7 3.3 %collective-permute-start.6 = (bf16[3,2,2,8,8,128]{5,4,3,2,1,0:T(8,128)(2,1)S(1)}, bf16[3,2,2,8,8,128]{5,4,3,2,1,0:T(8,128)(2,1)S(1)}, u32[]{:S(2)}, u32[]{:S(2)}) collective-permute-start(bf16[3,2,2,8,8,128]{5,4,3,2,1,0:T(8,128)(2,1)S(1)} %pad_maximum_fusion.refs_4_), channel_id=1, source_target_pairs={{0,1},{1,2},{2,3},{3,0},{4,5},{5,6},{6,7},{7,4},{8,9},{9,10},{10,1... | collective-permute-start | bytes 589832 | tf_op jit(solution)/shard_map/ppermute | solution.py:327
  63.0 3.7 %collective-permute-start.7 = (bf16[3,2,2,8,8,128]{5,4,3,2,1,0:T(8,128)(2,1)S(1)}, bf16[3,2,2,8,8,128]{5,4,3,2,1,0:T(8,128)(2,1)S(1)}, u32[]{:S(2)}, u32[]{:S(2)}) collective-permute-start(bf16[3,2,2,8,8,128]{5,4,3,2,1,0:T(8,128)(2,1)S(1)} %pad_maximum_fusion.refs_4_), channel_id=1, source_target_pairs={{0,2},{1,3},{2,0},{3,1},{4,6},{5,7},{6,4},{7,5},{8,10},{9,11},{10,... | collective-permute-start | bytes 589832 | tf_op jit(solution)/shard_map/ppermute | solution.py:327
  66.7 2.4 %collective-permute-start.8 = (bf16[3,2,2,8,8,128]{5,4,3,2,1,0:T(8,128)(2,1)S(1)}, bf16[3,2,2,8,8,128]{5,4,3,2,1,0:T(8,128)(2,1)S(1)}, u32[]{:S(2)}, u32[]{:S(2)}) collective-permute-start(bf16[3,2,2,8,8,128]{5,4,3,2,1,0:T(8,128)(2,1)S(1)} %pad_maximum_fusion.refs_4_), channel_id=1, source_target_pairs={{0,3},{1,0},{2,1},{3,2},{4,7},{5,4},{6,5},{7,6},{8,11},{9,8},{10,9... | collective-permute-start | bytes 589832 | tf_op jit(solution)/shard_map/ppermute | solution.py:327
  69.3 9.5 %collective-permute-done.7.refs_6_ = bf16[3,2,2,8,8,128]{5,4,3,2,1,0:T(8,128)(2,1)S(1)} collective-permute-done((bf16[3,2,2,8,8,128]{5,4,3,2,1,0:T(8,128)(2,1)S(1)}, bf16[3,2,2,8,8,128]{5,4,3,2,1,0:T(8,128)(2,1)S(1)}, u32[]{:S(2)}, u32[]{:S(2)}) %collective-permute-start.7) | collective-permute-done | bytes 196640 | tf_op jit(solution)/shard_map/ppermute | solution.py:327
  79.6 10.1 %attention_backward.1 = (bf16[32,128,128]{2,1,0:T(8,128)(2,1)}, bf16[1,2,2,8,8,128]{5,4,3,2,1,0:T(8,128)(2,1)S(1)}, bf16[1,2,2,8,8,128]{5,4,3,2,1,0:T(8,128)(2,1...) custom-call(s32[16]{0:T(128)S(1)} %dynamic-slice_bitcast_fusion.recv, ...), custom_call_target="tpu_custom_call" | custom-call | flops 2000000000 | bytes 6291456 | tf_op jit(solution)/shard_map/attention_backward/pallas_call | solution.py:216
  89.7 5.5 %collective-permute-start.10 = (bf16[3,2,2,8,8,128]{5,4,3,2,1,0:T(8,128)(2,1)S(1)}, bf16[3,2,2,8,8,128]{5,4,3,2,1,0:T(8,128)(2,1)S(1)}, u32[]{:S(2)}, u32[]{:S(2)}) collective-permute-start(bf16[3,2,2,8,8,128]{5,4,3,2,1,0:T(8,128)(2,1)S(1)} %get-tuple-element.48), channel_id=1, source_target_pairs={{0,2},{1,3},{2,0},{3,1},{4,6},{5,7},{6,4},{7,5},{8,10},{9,11},{10,... | collective-permute-start | bytes 589832 | tf_op jit(solution)/shard_map/ppermute | solution.py:327
  95.3 2.9 %collective-permute-start.11 = (bf16[3,2,2,8,8,128]{5,4,3,2,1,0:T(8,128)(2,1)S(1)}, bf16[3,2,2,8,8,128]{5,4,3,2,1,0:T(8,128)(2,1)S(1)}, u32[]{:S(2)}, u32[]{:S(2)}) collective-permute-start(bf16[3,2,2,8,8,128]{5,4,3,2,1,0:T(8,128)(2,1)S(1)} %get-tuple-element.49), channel_id=1, source_target_pairs={{0,1},{1,2},{2,3},{3,0},{4,5},{5,6},{6,7},{7,4},{8,9},{9,10},{10,1... | collective-permute-start | bytes 589832 | tf_op jit(solution)/shard_map/ppermute | solution.py:327
  98.2 4.2 %collective-permute-start.9 = (bf16[3,2,2,8,8,128]{5,4,3,2,1,0:T(8,128)(2,1)S(1)}, bf16[3,2,2,8,8,128]{5,4,3,2,1,0:T(8,128)(2,1)S(1)}, u32[]{:S(2)}, u32[]{:S(2)}) collective-permute-start(bf16[3,2,2,8,8,128]{5,4,3,2,1,0:T(8,128)(2,1)S(1)} %get-tuple-element.47), channel_id=1, source_target_pairs={{0,3},{1,0},{2,1},{3,2},{4,7},{5,4},{6,5},{7,6},{8,11},{9,8},{10,9... | collective-permute-start | bytes 589832 | tf_op jit(solution)/shard_map/ppermute | solution.py:327
  102.4 7.4 %all-to-all-start.2 = ((bf16[16,2,128,128]{3,2,1,0:T(8,128)(2,1)}), bf16[16,2,128,128]{3,2,1,0:T(8,128)(2,1)S(1)}, u32[]{:S(2)}, u32[]{:S(2)}) async-start(bf16[16,2,128,128]{3,2,1,0:T(8,128)(2,1)} %bitcast.17), calls=%async_computation.2 | async-start | bytes 2097152 | tf_op jit(solution)/shard_map/all_to_all | solution.py:387
  109.8 2.5 %collective-permute-done.9 = bf16[3,2,2,8,8,128]{5,4,3,2,1,0:T(8,128)(2,1)S(1)} collective-permute-done((bf16[3,2,2,8,8,128]{5,4,3,2,1,0:T(8,128)(2,1)S(1)}, bf16[3,2,2,8,8,128]{5,4,3,2,1,0:T(8,128)(2,1)S(1)}, u32[]{:S(2)}, u32[]{:S(2)}) %collective-permute-start.9) | collective-permute-done | bytes 196640 | tf_op jit(solution)/shard_map/ppermute | solution.py:327
  112.4 9.5 %collective-permute-start.15 = (bf16[2,2,2,8,8,128]{5,4,3,2,1,0:T(8,128)(2,1)S(1)}, bf16[2,2,2,8,8,128]{5,4,3,2,1,0:T(8,128)(2,1)S(1)}, u32[]{:S(2)}, u32[]{:S(2)}) collective-permute-start(bf16[2,2,2,8,8,128]{5,4,3,2,1,0:T(8,128)(2,1)S(1)} %add_convert_fusion), channel_id=1, source_target_pairs={{0,6},{1,7},{2,4},{3,5},{4,2},{5,3},{6,0},{7,1},{8,14},{9,15},{10,... | collective-permute-start | bytes 393224 | tf_op jit(solution)/shard_map/ppermute | solution.py:322
  122.1 1.9 %collective-permute-start.12 = (bf16[1,2,2,8,8,128]{5,4,3,2,1,0:T(8,128)(2,1)S(1)}, bf16[1,2,2,8,8,128]{5,4,3,2,1,0:T(8,128)(2,1)S(1)}, u32[]{:S(2)}, u32[]{:S(2)}) collective-permute-start(bf16[1,2,2,8,8,128]{5,4,3,2,1,0:T(8,128)(2,1)S(1)} %get-tuple-element.51), channel_id=1, source_target_pairs={{0,3},{1,0},{2,1},{3,2},{4,7},{5,4},{6,5},{7,6},{8,11},{9,8},{10,9... | collective-permute-start | bytes 196616 | tf_op jit(solution)/shard_map/ppermute | solution.py:327
  124.0 3.4 %collective-permute-start.13 = (bf16[1,2,2,8,8,128]{5,4,3,2,1,0:T(8,128)(2,1)S(1)}, bf16[1,2,2,8,8,128]{5,4,3,2,1,0:T(8,128)(2,1)S(1)}, u32[]{:S(2)}, u32[]{:S(2)}) collective-permute-start(bf16[1,2,2,8,8,128]{5,4,3,2,1,0:T(8,128)(2,1)S(1)} %get-tuple-element.52), channel_id=1, source_target_pairs={{0,2},{1,3},{2,0},{3,1},{4,6},{5,7},{6,4},{7,5},{8,10},{9,11},{10,... | collective-permute-start | bytes 196616 | tf_op jit(solution)/shard_map/ppermute | solution.py:327
  127.4 1.9 %collective-permute-start.14 = (bf16[1,2,2,8,8,128]{5,4,3,2,1,0:T(8,128)(2,1)S(1)}, bf16[1,2,2,8,8,128]{5,4,3,2,1,0:T(8,128)(2,1)S(1)}, u32[]{:S(2)}, u32[]{:S(2)}) collective-permute-start(bf16[1,2,2,8,8,128]{5,4,3,2,1,0:T(8,128)(2,1)S(1)} %get-tuple-element.53), channel_id=1, source_target_pairs={{0,1},{1,2},{2,3},{3,0},{4,5},{5,6},{6,7},{7,4},{8,9},{9,10},{10,1... | collective-permute-start | bytes 196616 | tf_op jit(solution)/shard_map/ppermute | solution.py:327
  129.4 7.9 %collective-permute-start.16 = (bf16[2,2,8,8,128]{4,3,2,1,0:T(8,128)(2,1)S(1)}, bf16[2,2,8,8,128]{4,3,2,1,0:T(8,128)(2,1)S(1)}, u32[]{:S(2)}, u32[]{:S(2)}) collective-permute-start(bf16[2,2,8,8,128]{4,3,2,1,0:T(8,128)(2,1)S(1)} %fusion), channel_id=1, source_target_pairs={{0,12},{1,13},{2,14},{3,15},{4,8},{5,9},{6,10},{7,11},{8,4},{9,5},... | collective-permute-start | bytes 196616 | tf_op jit(solution)/shard_map/ppermute | solution.py:322
  137.5 4.2 %collective-permute-done.16.refs_5_ = bf16[2,2,8,8,128]{4,3,2,1,0:T(8,128)(2,1)S(1)} collective-permute-done((bf16[2,2,8,8,128]{4,3,2,1,0:T(8,128)(2,1)S(1)}, bf16[2,2,8,8,128]{4,3,2,1,0:T(8,128)(2,1)S(1)}, u32[]{:S(2)}, u32[]{:S(2)}) %collective-permute-start.16) | collective-permute-done | bytes 65568 | tf_op jit(solution)/shard_map/ppermute | solution.py:322
  141.7 1.4 kv_back.1
  143.1 5.1 %all-to-all-start.3 = ((bf16[32,2,2,2,4,128]{5,4,3,2,1,0:T(4,128)(2,1)}), bf16[32,2,2,2,4,128]{5,4,3,2,1,0:T(4,128)(2,1)S(1)}, u32[]{:S(2)}, u32[]{:S(2)}) async-start(bf16[32,2,2,2,4,128]{5,4,3,2,1,0:T(4,128)(2,1)} %bitcast.21), calls=%async_computation.3 | async-start | bytes 524288 | tf_op jit(solution)/shard_map/all_to_all | solution.py:360
  148.2 1.4 gather_fusion
  149.6 7.4 %all-to-all-done.3 = bf16[32,2,2,2,4,128]{5,4,3,2,1,0:T(4,128)(2,1)S(1)} async-done(((bf16[32,2,2,2,4,128]{5,4,3,2,1,0:T(4,128)(2,1)}), bf16[32,2,2,2,4,128]{5,4,3,2,1,0:T(4,128)(2,1)S(1)}, u32[]{:S(2)}, u32[]{:S(2)}) %all-to-all-start.3) | async-done | bytes 262176 | tf_op jit(solution)/shard_map/all_to_all | solution.py:360
  (48 shorter events, 8.6 us)
Async XLA Ops:
  0.6 0.9 copy-start.2
  1.5 0.7 copy-start.3
  3.7 19.3 %all-to-all-start = ((bf16[32,2,2,2,4,128]{5,4,3,2,1,0:T(4,128)(2,1)}), bf16[32,2,2,2,4,128]{5,4,3,2,1,0:T(4,128)(2,1)S(1)}, u32[]{:S(2)}, u32[]{:S(2)}) async-start(bf16[32,2,2,2,4,128]{5,4,3,2,1,0:T(4,128)(2,1)} %bitcast.7), calls=%async_computation | async-start | bytes 524288 | tf_op jit(solution)/shard_map/all_to_all | solution.py:360
  14.1 1.0 copy-start
  15.1 1.0 copy-start.1
  16.2 0.7 copy-start.4
  23.0 4.1 %copy-start.8 = (s32[16,16]{1,0:T(8,128)S(1)}, s32[16,16]{1,0:T(8,128)}, u32[]{:S(2)}) copy-start(s32[16,16]{1,0:T(8,128)} %param.10) | copy-start | bytes 3076
  23.0 46.1 %copy-start.9 = (s32[1,16]{1,0:T(1,128)S(1)}, s32[1,16]{1,0:T(1,128)}, u32[]{:S(2)}) copy-start(s32[1,16]{1,0:T(1,128)} %param.11) | copy-start | bytes 196
  23.0 36.7 %all-to-all-start.1 = ((bf16[16,2,2,128,128]{4,3,2,1,0:T(8,128)(2,1)}), bf16[16,2,2,128,128]{4,3,2,1,0:T(8,128)(2,1)S(1)}, u32[]{:S(2)}, u32[]{:S(2)}) async-start(bf16[16,2,2,128,128]{4,3,2,1,0:T(8,128)(2,1)} %bitcast.14), calls=%async_computation.1 | async-start | bytes 4194304 | tf_op jit(solution)/shard_map/all_to_all | solution.py:373
  27.7 25.3 %collective-permute-start.1 = (bf16[2,2,8,8,128]{4,3,2,1,0:T(8,128)(2,1)S(1)}, bf16[2,2,8,8,128]{4,3,2,1,0:T(8,128)(2,1)S(1)}, u32[]{:S(2)}, u32[]{:S(2)}) collective-permute-start(bf16[2,2,8,8,128]{4,3,2,1,0:T(8,128)(2,1)S(1)} %get-tuple-element.35), channel_id=1, source_target_pairs={{0,6},{1,7},{2,4},{3,5},{4,2},{5,3},{6,0},{7,1},{8,14},{9,15},{10,... | collective-permute-start | bytes 196616 | tf_op jit(solution)/shard_map/ppermute | solution.py:322
  37.3 19.2 %collective-permute-start.2 = (bf16[2,2,8,8,128]{4,3,2,1,0:T(8,128)(2,1)S(1)}, bf16[2,2,8,8,128]{4,3,2,1,0:T(8,128)(2,1)S(1)}, u32[]{:S(2)}, u32[]{:S(2)}) collective-permute-start(bf16[2,2,8,8,128]{4,3,2,1,0:T(8,128)(2,1)S(1)} %get-tuple-element.34), channel_id=1, source_target_pairs={{0,10},{1,11},{2,8},{3,9},{4,14},{5,15},{6,12},{7,13},{8,2},{9,3},... | collective-permute-start | bytes 196616 | tf_op jit(solution)/shard_map/ppermute | solution.py:322
  43.5 13.1 %collective-permute-start = (bf16[2,2,8,8,128]{4,3,2,1,0:T(8,128)(2,1)S(1)}, bf16[2,2,8,8,128]{4,3,2,1,0:T(8,128)(2,1)S(1)}, u32[]{:S(2)}, u32[]{:S(2)}) collective-permute-start(bf16[2,2,8,8,128]{4,3,2,1,0:T(8,128)(2,1)S(1)} %get-tuple-element.34), channel_id=1, source_target_pairs={{0,12},{1,13},{2,14},{3,15},{4,8},{5,9},{6,10},{7,11},{8,4},{9,5},... | collective-permute-start | bytes 196616 | tf_op jit(solution)/shard_map/ppermute | solution.py:322
  45.4 11.2 %collective-permute-start.3 = (bf16[1,2,2,8,8,128]{5,4,3,2,1,0:T(8,128)(2,1)S(1)}, bf16[1,2,2,8,8,128]{5,4,3,2,1,0:T(8,128)(2,1)S(1)}, u32[]{:S(2)}, u32[]{:S(2)}) collective-permute-start(bf16[1,2,2,8,8,128]{5,4,3,2,1,0:T(8,128)(2,1)S(1)} %bitcast.38), channel_id=1, source_target_pairs={{0,1},{1,2},{2,3},{3,0},{4,5},{5,6},{6,7},{7,4},{8,9},{9,10},{10,1... | collective-permute-start | bytes 196616 | tf_op jit(solution)/shard_map/ppermute | solution.py:327
  48.1 10.8 %collective-permute-start.4 = (bf16[1,2,2,8,8,128]{5,4,3,2,1,0:T(8,128)(2,1)S(1)}, bf16[1,2,2,8,8,128]{5,4,3,2,1,0:T(8,128)(2,1)S(1)}, u32[]{:S(2)}, u32[]{:S(2)}) collective-permute-start(bf16[1,2,2,8,8,128]{5,4,3,2,1,0:T(8,128)(2,1)S(1)} %bitcast.39), channel_id=1, source_target_pairs={{0,2},{1,3},{2,0},{3,1},{4,6},{5,7},{6,4},{7,5},{8,10},{9,11},{10,... | collective-permute-start | bytes 196616 | tf_op jit(solution)/shard_map/ppermute | solution.py:327
  53.0 6.1 %collective-permute-start.5 = (bf16[1,2,2,8,8,128]{5,4,3,2,1,0:T(8,128)(2,1)S(1)}, bf16[1,2,2,8,8,128]{5,4,3,2,1,0:T(8,128)(2,1)S(1)}, u32[]{:S(2)}, u32[]{:S(2)}) collective-permute-start(bf16[1,2,2,8,8,128]{5,4,3,2,1,0:T(8,128)(2,1)S(1)} %bitcast.40), channel_id=1, source_target_pairs={{0,3},{1,0},{2,1},{3,2},{4,7},{5,4},{6,5},{7,6},{8,11},{9,8},{10,9... | collective-permute-start | bytes 196616 | tf_op jit(solution)/shard_map/ppermute | solution.py:327
  59.1 0.6 copy-start.6
  59.7 9.6 %collective-permute-start.6 = (bf16[3,2,2,8,8,128]{5,4,3,2,1,0:T(8,128)(2,1)S(1)}, bf16[3,2,2,8,8,128]{5,4,3,2,1,0:T(8,128)(2,1)S(1)}, u32[]{:S(2)}, u32[]{:S(2)}) collective-permute-start(bf16[3,2,2,8,8,128]{5,4,3,2,1,0:T(8,128)(2,1)S(1)} %pad_maximum_fusion.refs_4_), channel_id=1, source_target_pairs={{0,1},{1,2},{2,3},{3,0},{4,5},{5,6},{6,7},{7,4},{8,9},{9,10},{10,1... | collective-permute-start | bytes 589832 | tf_op jit(solution)/shard_map/ppermute | solution.py:327
  63.0 15.7 %collective-permute-start.7 = (bf16[3,2,2,8,8,128]{5,4,3,2,1,0:T(8,128)(2,1)S(1)}, bf16[3,2,2,8,8,128]{5,4,3,2,1,0:T(8,128)(2,1)S(1)}, u32[]{:S(2)}, u32[]{:S(2)}) collective-permute-start(bf16[3,2,2,8,8,128]{5,4,3,2,1,0:T(8,128)(2,1)S(1)} %pad_maximum_fusion.refs_4_), channel_id=1, source_target_pairs={{0,2},{1,3},{2,0},{3,1},{4,6},{5,7},{6,4},{7,5},{8,10},{9,11},{10,... | collective-permute-start | bytes 589832 | tf_op jit(solution)/shard_map/ppermute | solution.py:327
  66.7 12.1 %collective-permute-start.8 = (bf16[3,2,2,8,8,128]{5,4,3,2,1,0:T(8,128)(2,1)S(1)}, bf16[3,2,2,8,8,128]{5,4,3,2,1,0:T(8,128)(2,1)S(1)}, u32[]{:S(2)}, u32[]{:S(2)}) collective-permute-start(bf16[3,2,2,8,8,128]{5,4,3,2,1,0:T(8,128)(2,1)S(1)} %pad_maximum_fusion.refs_4_), channel_id=1, source_target_pairs={{0,3},{1,0},{2,1},{3,2},{4,7},{5,4},{6,5},{7,6},{8,11},{9,8},{10,9... | collective-permute-start | bytes 589832 | tf_op jit(solution)/shard_map/ppermute | solution.py:327
  78.8 0.8 copy-start.7
  89.7 47.6 %copy-start.5 = (s32[1,16,2]{1,2,0:T(2,128)S(1)}, s32[1,16,2]{1,2,0:T(2,128)}, u32[]{:S(2)}) copy-start(s32[1,16,2]{1,2,0:T(2,128)} %param.9) | copy-start | bytes 388
  89.7 20.0 %collective-permute-start.10 = (bf16[3,2,2,8,8,128]{5,4,3,2,1,0:T(8,128)(2,1)S(1)}, bf16[3,2,2,8,8,128]{5,4,3,2,1,0:T(8,128)(2,1)S(1)}, u32[]{:S(2)}, u32[]{:S(2)}) collective-permute-start(bf16[3,2,2,8,8,128]{5,4,3,2,1,0:T(8,128)(2,1)S(1)} %get-tuple-element.48), channel_id=1, source_target_pairs={{0,2},{1,3},{2,0},{3,1},{4,6},{5,7},{6,4},{7,5},{8,10},{9,11},{10,... | collective-permute-start | bytes 589832 | tf_op jit(solution)/shard_map/ppermute | solution.py:327
  95.3 14.5 %collective-permute-start.11 = (bf16[3,2,2,8,8,128]{5,4,3,2,1,0:T(8,128)(2,1)S(1)}, bf16[3,2,2,8,8,128]{5,4,3,2,1,0:T(8,128)(2,1)S(1)}, u32[]{:S(2)}, u32[]{:S(2)}) collective-permute-start(bf16[3,2,2,8,8,128]{5,4,3,2,1,0:T(8,128)(2,1)S(1)} %get-tuple-element.49), channel_id=1, source_target_pairs={{0,1},{1,2},{2,3},{3,0},{4,5},{5,6},{6,7},{7,4},{8,9},{9,10},{10,1... | collective-permute-start | bytes 589832 | tf_op jit(solution)/shard_map/ppermute | solution.py:327
  98.2 14.1 %collective-permute-start.9 = (bf16[3,2,2,8,8,128]{5,4,3,2,1,0:T(8,128)(2,1)S(1)}, bf16[3,2,2,8,8,128]{5,4,3,2,1,0:T(8,128)(2,1)S(1)}, u32[]{:S(2)}, u32[]{:S(2)}) collective-permute-start(bf16[3,2,2,8,8,128]{5,4,3,2,1,0:T(8,128)(2,1)S(1)} %get-tuple-element.47), channel_id=1, source_target_pairs={{0,3},{1,0},{2,1},{3,2},{4,7},{5,4},{6,5},{7,6},{8,11},{9,8},{10,9... | collective-permute-start | bytes 589832 | tf_op jit(solution)/shard_map/ppermute | solution.py:327
  102.4 39.3 %all-to-all-start.2 = ((bf16[16,2,128,128]{3,2,1,0:T(8,128)(2,1)}), bf16[16,2,128,128]{3,2,1,0:T(8,128)(2,1)S(1)}, u32[]{:S(2)}, u32[]{:S(2)}) async-start(bf16[16,2,128,128]{3,2,1,0:T(8,128)(2,1)} %bitcast.17), calls=%async_computation.2 | async-start | bytes 2097152 | tf_op jit(solution)/shard_map/all_to_all | solution.py:387
  112.4 16.9 %collective-permute-start.15 = (bf16[2,2,2,8,8,128]{5,4,3,2,1,0:T(8,128)(2,1)S(1)}, bf16[2,2,2,8,8,128]{5,4,3,2,1,0:T(8,128)(2,1)S(1)}, u32[]{:S(2)}, u32[]{:S(2)}) collective-permute-start(bf16[2,2,2,8,8,128]{5,4,3,2,1,0:T(8,128)(2,1)S(1)} %add_convert_fusion), channel_id=1, source_target_pairs={{0,6},{1,7},{2,4},{3,5},{4,2},{5,3},{6,0},{7,1},{8,14},{9,15},{10,... | collective-permute-start | bytes 393224 | tf_op jit(solution)/shard_map/ppermute | solution.py:322
  122.1 15.4 %collective-permute-start.12 = (bf16[1,2,2,8,8,128]{5,4,3,2,1,0:T(8,128)(2,1)S(1)}, bf16[1,2,2,8,8,128]{5,4,3,2,1,0:T(8,128)(2,1)S(1)}, u32[]{:S(2)}, u32[]{:S(2)}) collective-permute-start(bf16[1,2,2,8,8,128]{5,4,3,2,1,0:T(8,128)(2,1)S(1)} %get-tuple-element.51), channel_id=1, source_target_pairs={{0,3},{1,0},{2,1},{3,2},{4,7},{5,4},{6,5},{7,6},{8,11},{9,8},{10,9... | collective-permute-start | bytes 196616 | tf_op jit(solution)/shard_map/ppermute | solution.py:327
  124.0 13.4 %collective-permute-start.13 = (bf16[1,2,2,8,8,128]{5,4,3,2,1,0:T(8,128)(2,1)S(1)}, bf16[1,2,2,8,8,128]{5,4,3,2,1,0:T(8,128)(2,1)S(1)}, u32[]{:S(2)}, u32[]{:S(2)}) collective-permute-start(bf16[1,2,2,8,8,128]{5,4,3,2,1,0:T(8,128)(2,1)S(1)} %get-tuple-element.52), channel_id=1, source_target_pairs={{0,2},{1,3},{2,0},{3,1},{4,6},{5,7},{6,4},{7,5},{8,10},{9,11},{10,... | collective-permute-start | bytes 196616 | tf_op jit(solution)/shard_map/ppermute | solution.py:327
  127.4 10.0 %collective-permute-start.14 = (bf16[1,2,2,8,8,128]{5,4,3,2,1,0:T(8,128)(2,1)S(1)}, bf16[1,2,2,8,8,128]{5,4,3,2,1,0:T(8,128)(2,1)S(1)}, u32[]{:S(2)}, u32[]{:S(2)}) collective-permute-start(bf16[1,2,2,8,8,128]{5,4,3,2,1,0:T(8,128)(2,1)S(1)} %get-tuple-element.53), channel_id=1, source_target_pairs={{0,1},{1,2},{2,3},{3,0},{4,5},{5,6},{6,7},{7,4},{8,9},{9,10},{10,1... | collective-permute-start | bytes 196616 | tf_op jit(solution)/shard_map/ppermute | solution.py:327
  129.4 12.3 %collective-permute-start.16 = (bf16[2,2,8,8,128]{4,3,2,1,0:T(8,128)(2,1)S(1)}, bf16[2,2,8,8,128]{4,3,2,1,0:T(8,128)(2,1)S(1)}, u32[]{:S(2)}, u32[]{:S(2)}) collective-permute-start(bf16[2,2,8,8,128]{4,3,2,1,0:T(8,128)(2,1)S(1)} %fusion), channel_id=1, source_target_pairs={{0,12},{1,13},{2,14},{3,15},{4,8},{5,9},{6,10},{7,11},{8,4},{9,5},... | collective-permute-start | bytes 196616 | tf_op jit(solution)/shard_map/ppermute | solution.py:322
  143.1 14.0 %all-to-all-start.3 = ((bf16[32,2,2,2,4,128]{5,4,3,2,1,0:T(4,128)(2,1)}), bf16[32,2,2,2,4,128]{5,4,3,2,1,0:T(4,128)(2,1)S(1)}, u32[]{:S(2)}, u32[]{:S(2)}) async-start(bf16[32,2,2,2,4,128]{5,4,3,2,1,0:T(4,128)(2,1)} %bitcast.21), calls=%async_computation.3 | async-start | bytes 524288 | tf_op jit(solution)/shard_map/all_to_all | solution.py:360

commit v16 on v15

--- a/solution.py
+++ b/solution.py
@@ -121,7 +121,7 @@
         dqt[block] = jnp.zeros_like(dqt[block])
         return 0
 
-    lax.fori_loop(0, blocks, diagonal_products, 0, unroll=4)
+    lax.fori_loop(0, blocks, diagonal_products, 0, unroll=8)
 
     def sweep(begin, end, step, state):
         twice = (end - begin) >> 1
@@ -194,7 +194,7 @@
         dq_ref[recv_ref[PAIR * block + 1]] = result[tile_rows:]
         return 0
 
-    lax.fori_loop(0, blocks, diagonal_terms, 0, unroll=4)
+    lax.fori_loop(0, blocks, diagonal_terms, 0, unroll=8)
 
     def unstage(block, _):
         for slot, ref in enumerate(dkv_refs):
@@ -232,7 +232,7 @@
             pltpu.VMEM((blocks, 2, 8, width), jnp.float32),
             pltpu.VMEM((blocks, HD, width), jnp.float32),
         ],
-        compiler_params=pltpu.CompilerParams(vmem_limit_bytes=24 * 2**20),
+        compiler_params=pltpu.CompilerParams(vmem_limit_bytes=20 * 2**20),
         cost_estimate=pl.CostEstimate(
             flops=2 * 10**9, bytes_accessed=6 * 2**20, transcendentals=2 * 10**6
         ),

time: 160 us -> 160 us (level)
    all_to_all x1, starting transfers between devices: 7.39 us -> 5.38 us  [on_device(): lax.all_to_all(query_back.reshape(n_replicas, slot_cap, tile_rows, row_wi...]
where the time goes in v16:
time: 160 us; the launch traced here: 159 us
  starting transfers between devices  102 us (64%)
  waiting for transfers between devices  30.9 us (19%)
  Pallas kernels  16.9 us (11%)
  local copies, waits for them, and re-layouts  7.23 us (5%)
    ppermute x12, starting transfers between devices, near_shift(): return lax.ppermute(values, 'z', pairs)  40.2 us
    ppermute x5, starting transfers between devices, far_swap(): lax.ppermute(values, 'z', [(place, place ^ flip) for place in range(16)])  35.8 us
    all_to_all x2, starting transfers between devices, over_plane(): lax.all_to_all(values.reshape((2 * n_replicas,) + values.shape[2:]), PLAN...  16.6 us
    ppermute x12, waiting for transfers between devices, near_shift(): return lax.ppermute(values, 'z', pairs)  15.1 us
    all_to_all x2, waiting for transfers between devices, over_plane(): lax.all_to_all(values.reshape((2 * n_replicas,) + values.shape[2:]), PLAN...  11.4 us
    pallas_call x1, Pallas kernels, attention(): pl.pallas_call(attention_kernel, out_shape=(jax.ShapeDtypeStruct((slots,...  10.1 us
    unnamed x20, local copies, waits for them, and re-layouts  5.81 us
    all_to_all x1, starting transfers between devices, on_device(): lax.all_to_all(query_back.reshape(n_replicas, slot_cap, tile_rows, row_wi...  5.38 us
  transfers between devices with their start and end apart: 21, of which 7 were waited for; matrix products, arithmetic and copies ran while one was open for 1% of the time, Pallas kernels for 2%

profile of v16, /device:TPU:1, one launch (start us, length us, event | category | flops | bytes accessed | tf_op | source)
XLA Modules:
  0.0 158.7 jit_solution(15569719003860171606)
XLA Ops:
  2.2 1.4 kv_pack.1
  3.7 10.4 %all-to-all-start = ((bf16[32,2,2,2,4,128]{5,4,3,2,1,0:T(4,128)(2,1)}), bf16[32,2,2,2,4,128]{5,4,3,2,1,0:T(4,128)(2,1)S(1)}, u32[]{:S(2)}, u32[]{:S(2)}) async-start(bf16[32,2,2,2,4,128]{5,4,3,2,1,0:T(4,128)(2,1)} %bitcast.7), calls=%async_computation | async-start | bytes 524288 | tf_op jit(solution)/shard_map/all_to_all | solution.py:360
  16.8 2.2 %pack_rows.1 = bf16[32,2,128,128]{3,2,1,0:T(8,128)(2,1)} custom-call(s32[2,16]{1,0:T(2,128)S(1)} %bitcast.36, bf16[16,128,128]{2,1,0:T(8,128)(2,1)S(1)} %copy-done, bf16[16,128,128]{2,1,0:T(8,128)(2,1)S(1)} %copy-done.1), custom_call_target="tpu_custom_call" | custom-call | tf_op jit(solution)/shard_map/pack_rows/pallas_call | solution.py:38
  19.0 4.0 %all-to-all-done = bf16[32,2,2,2,4,128]{5,4,3,2,1,0:T(4,128)(2,1)S(1)} async-done(((bf16[32,2,2,2,4,128]{5,4,3,2,1,0:T(4,128)(2,1)}), bf16[32,2,2,2,4,128]{5,4,3,2,1,0:T(4,128)(2,1)S(1)}, u32[]{:S(2)}, u32[]{:S(2)}) %all-to-all-start) | async-done | bytes 262176 | tf_op jit(solution)/shard_map/all_to_all | solution.py:360
  23.0 4.1 %all-to-all-start.1 = ((bf16[16,2,2,128,128]{4,3,2,1,0:T(8,128)(2,1)}), bf16[16,2,2,128,128]{4,3,2,1,0:T(8,128)(2,1)S(1)}, u32[]{:S(2)}, u32[]{:S(2)}) async-start(bf16[16,2,2,128,128]{4,3,2,1,0:T(8,128)(2,1)} %bitcast.14), calls=%async_computation.1 | async-start | bytes 4194304 | tf_op jit(solution)/shard_map/all_to_all | solution.py:373
  27.7 9.6 %collective-permute-start.1 = (bf16[2,2,8,8,128]{4,3,2,1,0:T(8,128)(2,1)S(1)}, bf16[2,2,8,8,128]{4,3,2,1,0:T(8,128)(2,1)S(1)}, u32[]{:S(2)}, u32[]{:S(2)}) collective-permute-start(bf16[2,2,8,8,128]{4,3,2,1,0:T(8,128)(2,1)S(1)} %get-tuple-element.35), channel_id=1, source_target_pairs={{0,6},{1,7},{2,4},{3,5},{4,2},{5,3},{6,0},{7,1},{8,14},{9,15},{10,... | collective-permute-start | bytes 196616 | tf_op jit(solution)/shard_map/ppermute | solution.py:322
  37.3 6.1 %collective-permute-start.2 = (bf16[2,2,8,8,128]{4,3,2,1,0:T(8,128)(2,1)S(1)}, bf16[2,2,8,8,128]{4,3,2,1,0:T(8,128)(2,1)S(1)}, u32[]{:S(2)}, u32[]{:S(2)}) collective-permute-start(bf16[2,2,8,8,128]{4,3,2,1,0:T(8,128)(2,1)S(1)} %get-tuple-element.34), channel_id=1, source_target_pairs={{0,10},{1,11},{2,8},{3,9},{4,14},{5,15},{6,12},{7,13},{8,2},{9,3},... | collective-permute-start | bytes 196616 | tf_op jit(solution)/shard_map/ppermute | solution.py:322
  43.5 1.9 %collective-permute-start = (bf16[2,2,8,8,128]{4,3,2,1,0:T(8,128)(2,1)S(1)}, bf16[2,2,8,8,128]{4,3,2,1,0:T(8,128)(2,1)S(1)}, u32[]{:S(2)}, u32[]{:S(2)}) collective-permute-start(bf16[2,2,8,8,128]{4,3,2,1,0:T(8,128)(2,1)S(1)} %get-tuple-element.34), channel_id=1, source_target_pairs={{0,12},{1,13},{2,14},{3,15},{4,8},{5,9},{6,10},{7,11},{8,4},{9,5},... | collective-permute-start | bytes 196616 | tf_op jit(solution)/shard_map/ppermute | solution.py:322
  45.4 2.6 %collective-permute-start.3 = (bf16[1,2,2,8,8,128]{5,4,3,2,1,0:T(8,128)(2,1)S(1)}, bf16[1,2,2,8,8,128]{5,4,3,2,1,0:T(8,128)(2,1)S(1)}, u32[]{:S(2)}, u32[]{:S(2)}) collective-permute-start(bf16[1,2,2,8,8,128]{5,4,3,2,1,0:T(8,128)(2,1)S(1)} %bitcast.38), channel_id=1, source_target_pairs={{0,1},{1,2},{2,3},{3,0},{4,5},{5,6},{6,7},{7,4},{8,9},{9,10},{10,1... | collective-permute-start | bytes 196616 | tf_op jit(solution)/shard_map/ppermute | solution.py:327
  48.1 4.9 %collective-permute-start.4 = (bf16[1,2,2,8,8,128]{5,4,3,2,1,0:T(8,128)(2,1)S(1)}, bf16[1,2,2,8,8,128]{5,4,3,2,1,0:T(8,128)(2,1)S(1)}, u32[]{:S(2)}, u32[]{:S(2)}) collective-permute-start(bf16[1,2,2,8,8,128]{5,4,3,2,1,0:T(8,128)(2,1)S(1)} %bitcast.39), channel_id=1, source_target_pairs={{0,2},{1,3},{2,0},{3,1},{4,6},{5,7},{6,4},{7,5},{8,10},{9,11},{10,... | collective-permute-start | bytes 196616 | tf_op jit(solution)/shard_map/ppermute | solution.py:327
  53.0 3.5 %collective-permute-start.5 = (bf16[1,2,2,8,8,128]{5,4,3,2,1,0:T(8,128)(2,1)S(1)}, bf16[1,2,2,8,8,128]{5,4,3,2,1,0:T(8,128)(2,1)S(1)}, u32[]{:S(2)}, u32[]{:S(2)}) collective-permute-start(bf16[1,2,2,8,8,128]{5,4,3,2,1,0:T(8,128)(2,1)S(1)} %bitcast.40), channel_id=1, source_target_pairs={{0,3},{1,0},{2,1},{3,2},{4,7},{5,4},{6,5},{7,6},{8,11},{9,8},{10,9... | collective-permute-start | bytes 196616 | tf_op jit(solution)/shard_map/ppermute | solution.py:327
  56.6 2.2 %collective-permute-done.4.refs_2_ = bf16[1,2,2,8,8,128]{5,4,3,2,1,0:T(8,128)(2,1)S(1)} collective-permute-done((bf16[1,2,2,8,8,128]{5,4,3,2,1,0:T(8,128)(2,1)S(1)}, bf16[1,2,2,8,8,128]{5,4,3,2,1,0:T(8,128)(2,1)S(1)}, u32[]{:S(2)}, u32[]{:S(2)}) %collective-permute-start.4) | collective-permute-done | bytes 65568 | tf_op jit(solution)/shard_map/ppermute | solution.py:327
  59.7 3.3 %collective-permute-start.6 = (bf16[3,2,2,8,8,128]{5,4,3,2,1,0:T(8,128)(2,1)S(1)}, bf16[3,2,2,8,8,128]{5,4,3,2,1,0:T(8,128)(2,1)S(1)}, u32[]{:S(2)}, u32[]{:S(2)}) collective-permute-start(bf16[3,2,2,8,8,128]{5,4,3,2,1,0:T(8,128)(2,1)S(1)} %pad_maximum_fusion.refs_4_), channel_id=1, source_target_pairs={{0,1},{1,2},{2,3},{3,0},{4,5},{5,6},{6,7},{7,4},{8,9},{9,10},{10,1... | collective-permute-start | bytes 589832 | tf_op jit(solution)/shard_map/ppermute | solution.py:327
  63.0 3.7 %collective-permute-start.7 = (bf16[3,2,2,8,8,128]{5,4,3,2,1,0:T(8,128)(2,1)S(1)}, bf16[3,2,2,8,8,128]{5,4,3,2,1,0:T(8,128)(2,1)S(1)}, u32[]{:S(2)}, u32[]{:S(2)}) collective-permute-start(bf16[3,2,2,8,8,128]{5,4,3,2,1,0:T(8,128)(2,1)S(1)} %pad_maximum_fusion.refs_4_), channel_id=1, source_target_pairs={{0,2},{1,3},{2,0},{3,1},{4,6},{5,7},{6,4},{7,5},{8,10},{9,11},{10,... | collective-permute-start | bytes 589832 | tf_op jit(solution)/shard_map/ppermute | solution.py:327
  66.7 2.4 %collective-permute-start.8 = (bf16[3,2,2,8,8,128]{5,4,3,2,1,0:T(8,128)(2,1)S(1)}, bf16[3,2,2,8,8,128]{5,4,3,2,1,0:T(8,128)(2,1)S(1)}, u32[]{:S(2)}, u32[]{:S(2)}) collective-permute-start(bf16[3,2,2,8,8,128]{5,4,3,2,1,0:T(8,128)(2,1)S(1)} %pad_maximum_fusion.refs_4_), channel_id=1, source_target_pairs={{0,3},{1,0},{2,1},{3,2},{4,7},{5,4},{6,5},{7,6},{8,11},{9,8},{10,9... | collective-permute-start | bytes 589832 | tf_op jit(solution)/shard_map/ppermute | solution.py:327
  69.3 9.5 %collective-permute-done.7.refs_6_ = bf16[3,2,2,8,8,128]{5,4,3,2,1,0:T(8,128)(2,1)S(1)} collective-permute-done((bf16[3,2,2,8,8,128]{5,4,3,2,1,0:T(8,128)(2,1)S(1)}, bf16[3,2,2,8,8,128]{5,4,3,2,1,0:T(8,128)(2,1)S(1)}, u32[]{:S(2)}, u32[]{:S(2)}) %collective-permute-start.7) | collective-permute-done | bytes 196640 | tf_op jit(solution)/shard_map/ppermute | solution.py:327
  79.6 10.1 %attention_backward.1 = (bf16[32,128,128]{2,1,0:T(8,128)(2,1)}, bf16[1,2,2,8,8,128]{5,4,3,2,1,0:T(8,128)(2,1)S(1)}, bf16[1,2,2,8,8,128]{5,4,3,2,1,0:T(8,128)(2,1...) custom-call(s32[16]{0:T(128)S(1)} %dynamic-slice_bitcast_fusion.recv, ...), custom_call_target="tpu_custom_call" | custom-call | flops 2000000000 | bytes 6291456 | tf_op jit(solution)/shard_map/attention_backward/pallas_call | solution.py:216
  89.7 5.5 %collective-permute-start.10 = (bf16[3,2,2,8,8,128]{5,4,3,2,1,0:T(8,128)(2,1)S(1)}, bf16[3,2,2,8,8,128]{5,4,3,2,1,0:T(8,128)(2,1)S(1)}, u32[]{:S(2)}, u32[]{:S(2)}) collective-permute-start(bf16[3,2,2,8,8,128]{5,4,3,2,1,0:T(8,128)(2,1)S(1)} %get-tuple-element.48), channel_id=1, source_target_pairs={{0,2},{1,3},{2,0},{3,1},{4,6},{5,7},{6,4},{7,5},{8,10},{9,11},{10,... | collective-permute-start | bytes 589832 | tf_op jit(solution)/shard_map/ppermute | solution.py:327
  95.2 3.0 %collective-permute-start.11 = (bf16[3,2,2,8,8,128]{5,4,3,2,1,0:T(8,128)(2,1)S(1)}, bf16[3,2,2,8,8,128]{5,4,3,2,1,0:T(8,128)(2,1)S(1)}, u32[]{:S(2)}, u32[]{:S(2)}) collective-permute-start(bf16[3,2,2,8,8,128]{5,4,3,2,1,0:T(8,128)(2,1)S(1)} %get-tuple-element.49), channel_id=1, source_target_pairs={{0,1},{1,2},{2,3},{3,0},{4,5},{5,6},{6,7},{7,4},{8,9},{9,10},{10,1... | collective-permute-start | bytes 589832 | tf_op jit(solution)/shard_map/ppermute | solution.py:327
  98.2 4.1 %collective-permute-start.9 = (bf16[3,2,2,8,8,128]{5,4,3,2,1,0:T(8,128)(2,1)S(1)}, bf16[3,2,2,8,8,128]{5,4,3,2,1,0:T(8,128)(2,1)S(1)}, u32[]{:S(2)}, u32[]{:S(2)}) collective-permute-start(bf16[3,2,2,8,8,128]{5,4,3,2,1,0:T(8,128)(2,1)S(1)} %get-tuple-element.47), channel_id=1, source_target_pairs={{0,3},{1,0},{2,1},{3,2},{4,7},{5,4},{6,5},{7,6},{8,11},{9,8},{10,9... | collective-permute-start | bytes 589832 | tf_op jit(solution)/shard_map/ppermute | solution.py:327
  102.3 5.4 %all-to-all-start.2 = ((bf16[16,2,128,128]{3,2,1,0:T(8,128)(2,1)}), bf16[16,2,128,128]{3,2,1,0:T(8,128)(2,1)S(1)}, u32[]{:S(2)}, u32[]{:S(2)}) async-start(bf16[16,2,128,128]{3,2,1,0:T(8,128)(2,1)} %bitcast.17), calls=%async_computation.2 | async-start | bytes 2097152 | tf_op jit(solution)/shard_map/all_to_all | solution.py:387
  107.7 3.1 %collective-permute-done.9 = bf16[3,2,2,8,8,128]{5,4,3,2,1,0:T(8,128)(2,1)S(1)} collective-permute-done((bf16[3,2,2,8,8,128]{5,4,3,2,1,0:T(8,128)(2,1)S(1)}, bf16[3,2,2,8,8,128]{5,4,3,2,1,0:T(8,128)(2,1)S(1)}, u32[]{:S(2)}, u32[]{:S(2)}) %collective-permute-start.9) | collective-permute-done | bytes 196640 | tf_op jit(solution)/shard_map/ppermute | solution.py:327
  110.9 11.1 %collective-permute-start.15 = (bf16[2,2,2,8,8,128]{5,4,3,2,1,0:T(8,128)(2,1)S(1)}, bf16[2,2,2,8,8,128]{5,4,3,2,1,0:T(8,128)(2,1)S(1)}, u32[]{:S(2)}, u32[]{:S(2)}) collective-permute-start(bf16[2,2,2,8,8,128]{5,4,3,2,1,0:T(8,128)(2,1)S(1)} %add_convert_fusion), channel_id=1, source_target_pairs={{0,6},{1,7},{2,4},{3,5},{4,2},{5,3},{6,0},{7,1},{8,14},{9,15},{10,... | collective-permute-start | bytes 393224 | tf_op jit(solution)/shard_map/ppermute | solution.py:322
  122.2 1.9 %collective-permute-start.12 = (bf16[1,2,2,8,8,128]{5,4,3,2,1,0:T(8,128)(2,1)S(1)}, bf16[1,2,2,8,8,128]{5,4,3,2,1,0:T(8,128)(2,1)S(1)}, u32[]{:S(2)}, u32[]{:S(2)}) collective-permute-start(bf16[1,2,2,8,8,128]{5,4,3,2,1,0:T(8,128)(2,1)S(1)} %get-tuple-element.51), channel_id=1, source_target_pairs={{0,3},{1,0},{2,1},{3,2},{4,7},{5,4},{6,5},{7,6},{8,11},{9,8},{10,9... | collective-permute-start | bytes 196616 | tf_op jit(solution)/shard_map/ppermute | solution.py:327
  124.1 2.4 %collective-permute-start.13 = (bf16[1,2,2,8,8,128]{5,4,3,2,1,0:T(8,128)(2,1)S(1)}, bf16[1,2,2,8,8,128]{5,4,3,2,1,0:T(8,128)(2,1)S(1)}, u32[]{:S(2)}, u32[]{:S(2)}) collective-permute-start(bf16[1,2,2,8,8,128]{5,4,3,2,1,0:T(8,128)(2,1)S(1)} %get-tuple-element.52), channel_id=1, source_target_pairs={{0,2},{1,3},{2,0},{3,1},{4,6},{5,7},{6,4},{7,5},{8,10},{9,11},{10,... | collective-permute-start | bytes 196616 | tf_op jit(solution)/shard_map/ppermute | solution.py:327
  126.5 2.9 %collective-permute-start.14 = (bf16[1,2,2,8,8,128]{5,4,3,2,1,0:T(8,128)(2,1)S(1)}, bf16[1,2,2,8,8,128]{5,4,3,2,1,0:T(8,128)(2,1)S(1)}, u32[]{:S(2)}, u32[]{:S(2)}) collective-permute-start(bf16[1,2,2,8,8,128]{5,4,3,2,1,0:T(8,128)(2,1)S(1)} %get-tuple-element.53), channel_id=1, source_target_pairs={{0,1},{1,2},{2,3},{3,0},{4,5},{5,6},{6,7},{7,4},{8,9},{9,10},{10,1... | collective-permute-start | bytes 196616 | tf_op jit(solution)/shard_map/ppermute | solution.py:327
  129.5 7.0 %collective-permute-start.16 = (bf16[2,2,8,8,128]{4,3,2,1,0:T(8,128)(2,1)S(1)}, bf16[2,2,8,8,128]{4,3,2,1,0:T(8,128)(2,1)S(1)}, u32[]{:S(2)}, u32[]{:S(2)}) collective-permute-start(bf16[2,2,8,8,128]{4,3,2,1,0:T(8,128)(2,1)S(1)} %fusion), channel_id=1, source_target_pairs={{0,12},{1,13},{2,14},{3,15},{4,8},{5,9},{6,10},{7,11},{8,4},{9,5},... | collective-permute-start | bytes 196616 | tf_op jit(solution)/shard_map/ppermute | solution.py:322
  136.6 4.4 %collective-permute-done.16.refs_5_ = bf16[2,2,8,8,128]{4,3,2,1,0:T(8,128)(2,1)S(1)} collective-permute-done((bf16[2,2,8,8,128]{4,3,2,1,0:T(8,128)(2,1)S(1)}, bf16[2,2,8,8,128]{4,3,2,1,0:T(8,128)(2,1)S(1)}, u32[]{:S(2)}, u32[]{:S(2)}) %collective-permute-start.16) | collective-permute-done | bytes 65568 | tf_op jit(solution)/shard_map/ppermute | solution.py:322
  141.0 1.4 kv_back.1
  142.4 6.2 %all-to-all-start.3 = ((bf16[32,2,2,2,4,128]{5,4,3,2,1,0:T(4,128)(2,1)}), bf16[32,2,2,2,4,128]{5,4,3,2,1,0:T(4,128)(2,1)S(1)}, u32[]{:S(2)}, u32[]{:S(2)}) async-start(bf16[32,2,2,2,4,128]{5,4,3,2,1,0:T(4,128)(2,1)} %bitcast.21), calls=%async_computation.3 | async-start | bytes 524288 | tf_op jit(solution)/shard_map/all_to_all | solution.py:360
  148.6 1.4 gather_fusion
  150.1 7.4 %all-to-all-done.3 = bf16[32,2,2,2,4,128]{5,4,3,2,1,0:T(4,128)(2,1)S(1)} async-done(((bf16[32,2,2,2,4,128]{5,4,3,2,1,0:T(4,128)(2,1)}), bf16[32,2,2,2,4,128]{5,4,3,2,1,0:T(4,128)(2,1)S(1)}, u32[]{:S(2)}, u32[]{:S(2)}) %all-to-all-start.3) | async-done | bytes 262176 | tf_op jit(solution)/shard_map/all_to_all | solution.py:360
  (48 shorter events, 8.6 us)
Async XLA Ops:
  0.6 0.9 copy-start.2
  1.5 0.7 copy-start.3
  3.7 19.3 %all-to-all-start = ((bf16[32,2,2,2,4,128]{5,4,3,2,1,0:T(4,128)(2,1)}), bf16[32,2,2,2,4,128]{5,4,3,2,1,0:T(4,128)(2,1)S(1)}, u32[]{:S(2)}, u32[]{:S(2)}) async-start(bf16[32,2,2,2,4,128]{5,4,3,2,1,0:T(4,128)(2,1)} %bitcast.7), calls=%async_computation | async-start | bytes 524288 | tf_op jit(solution)/shard_map/all_to_all | solution.py:360
  14.1 1.0 copy-start
  15.1 1.0 copy-start.1
  16.2 0.7 copy-start.4
  23.0 4.1 %copy-start.8 = (s32[16,16]{1,0:T(8,128)S(1)}, s32[16,16]{1,0:T(8,128)}, u32[]{:S(2)}) copy-start(s32[16,16]{1,0:T(8,128)} %param.10) | copy-start | bytes 3076
  23.0 46.1 %copy-start.9 = (s32[1,16]{1,0:T(1,128)S(1)}, s32[1,16]{1,0:T(1,128)}, u32[]{:S(2)}) copy-start(s32[1,16]{1,0:T(1,128)} %param.11) | copy-start | bytes 196
  23.0 36.7 %all-to-all-start.1 = ((bf16[16,2,2,128,128]{4,3,2,1,0:T(8,128)(2,1)}), bf16[16,2,2,128,128]{4,3,2,1,0:T(8,128)(2,1)S(1)}, u32[]{:S(2)}, u32[]{:S(2)}) async-start(bf16[16,2,2,128,128]{4,3,2,1,0:T(8,128)(2,1)} %bitcast.14), calls=%async_computation.1 | async-start | bytes 4194304 | tf_op jit(solution)/shard_map/all_to_all | solution.py:373
  27.7 25.3 %collective-permute-start.1 = (bf16[2,2,8,8,128]{4,3,2,1,0:T(8,128)(2,1)S(1)}, bf16[2,2,8,8,128]{4,3,2,1,0:T(8,128)(2,1)S(1)}, u32[]{:S(2)}, u32[]{:S(2)}) collective-permute-start(bf16[2,2,8,8,128]{4,3,2,1,0:T(8,128)(2,1)S(1)} %get-tuple-element.35), channel_id=1, source_target_pairs={{0,6},{1,7},{2,4},{3,5},{4,2},{5,3},{6,0},{7,1},{8,14},{9,15},{10,... | collective-permute-start | bytes 196616 | tf_op jit(solution)/shard_map/ppermute | solution.py:322
  37.3 19.2 %collective-permute-start.2 = (bf16[2,2,8,8,128]{4,3,2,1,0:T(8,128)(2,1)S(1)}, bf16[2,2,8,8,128]{4,3,2,1,0:T(8,128)(2,1)S(1)}, u32[]{:S(2)}, u32[]{:S(2)}) collective-permute-start(bf16[2,2,8,8,128]{4,3,2,1,0:T(8,128)(2,1)S(1)} %get-tuple-element.34), channel_id=1, source_target_pairs={{0,10},{1,11},{2,8},{3,9},{4,14},{5,15},{6,12},{7,13},{8,2},{9,3},... | collective-permute-start | bytes 196616 | tf_op jit(solution)/shard_map/ppermute | solution.py:322
  43.5 13.1 %collective-permute-start = (bf16[2,2,8,8,128]{4,3,2,1,0:T(8,128)(2,1)S(1)}, bf16[2,2,8,8,128]{4,3,2,1,0:T(8,128)(2,1)S(1)}, u32[]{:S(2)}, u32[]{:S(2)}) collective-permute-start(bf16[2,2,8,8,128]{4,3,2,1,0:T(8,128)(2,1)S(1)} %get-tuple-element.34), channel_id=1, source_target_pairs={{0,12},{1,13},{2,14},{3,15},{4,8},{5,9},{6,10},{7,11},{8,4},{9,5},... | collective-permute-start | bytes 196616 | tf_op jit(solution)/shard_map/ppermute | solution.py:322
  45.4 11.2 %collective-permute-start.3 = (bf16[1,2,2,8,8,128]{5,4,3,2,1,0:T(8,128)(2,1)S(1)}, bf16[1,2,2,8,8,128]{5,4,3,2,1,0:T(8,128)(2,1)S(1)}, u32[]{:S(2)}, u32[]{:S(2)}) collective-permute-start(bf16[1,2,2,8,8,128]{5,4,3,2,1,0:T(8,128)(2,1)S(1)} %bitcast.38), channel_id=1, source_target_pairs={{0,1},{1,2},{2,3},{3,0},{4,5},{5,6},{6,7},{7,4},{8,9},{9,10},{10,1... | collective-permute-start | bytes 196616 | tf_op jit(solution)/shard_map/ppermute | solution.py:327
  48.1 10.8 %collective-permute-start.4 = (bf16[1,2,2,8,8,128]{5,4,3,2,1,0:T(8,128)(2,1)S(1)}, bf16[1,2,2,8,8,128]{5,4,3,2,1,0:T(8,128)(2,1)S(1)}, u32[]{:S(2)}, u32[]{:S(2)}) collective-permute-start(bf16[1,2,2,8,8,128]{5,4,3,2,1,0:T(8,128)(2,1)S(1)} %bitcast.39), channel_id=1, source_target_pairs={{0,2},{1,3},{2,0},{3,1},{4,6},{5,7},{6,4},{7,5},{8,10},{9,11},{10,... | collective-permute-start | bytes 196616 | tf_op jit(solution)/shard_map/ppermute | solution.py:327
  53.0 6.1 %collective-permute-start.5 = (bf16[1,2,2,8,8,128]{5,4,3,2,1,0:T(8,128)(2,1)S(1)}, bf16[1,2,2,8,8,128]{5,4,3,2,1,0:T(8,128)(2,1)S(1)}, u32[]{:S(2)}, u32[]{:S(2)}) collective-permute-start(bf16[1,2,2,8,8,128]{5,4,3,2,1,0:T(8,128)(2,1)S(1)} %bitcast.40), channel_id=1, source_target_pairs={{0,3},{1,0},{2,1},{3,2},{4,7},{5,4},{6,5},{7,6},{8,11},{9,8},{10,9... | collective-permute-start | bytes 196616 | tf_op jit(solution)/shard_map/ppermute | solution.py:327
  59.1 0.6 copy-start.6
  59.7 9.6 %collective-permute-start.6 = (bf16[3,2,2,8,8,128]{5,4,3,2,1,0:T(8,128)(2,1)S(1)}, bf16[3,2,2,8,8,128]{5,4,3,2,1,0:T(8,128)(2,1)S(1)}, u32[]{:S(2)}, u32[]{:S(2)}) collective-permute-start(bf16[3,2,2,8,8,128]{5,4,3,2,1,0:T(8,128)(2,1)S(1)} %pad_maximum_fusion.refs_4_), channel_id=1, source_target_pairs={{0,1},{1,2},{2,3},{3,0},{4,5},{5,6},{6,7},{7,4},{8,9},{9,10},{10,1... | collective-permute-start | bytes 589832 | tf_op jit(solution)/shard_map/ppermute | solution.py:327
  63.0 15.7 %collective-permute-start.7 = (bf16[3,2,2,8,8,128]{5,4,3,2,1,0:T(8,128)(2,1)S(1)}, bf16[3,2,2,8,8,128]{5,4,3,2,1,0:T(8,128)(2,1)S(1)}, u32[]{:S(2)}, u32[]{:S(2)}) collective-permute-start(bf16[3,2,2,8,8,128]{5,4,3,2,1,0:T(8,128)(2,1)S(1)} %pad_maximum_fusion.refs_4_), channel_id=1, source_target_pairs={{0,2},{1,3},{2,0},{3,1},{4,6},{5,7},{6,4},{7,5},{8,10},{9,11},{10,... | collective-permute-start | bytes 589832 | tf_op jit(solution)/shard_map/ppermute | solution.py:327
  66.7 12.1 %collective-permute-start.8 = (bf16[3,2,2,8,8,128]{5,4,3,2,1,0:T(8,128)(2,1)S(1)}, bf16[3,2,2,8,8,128]{5,4,3,2,1,0:T(8,128)(2,1)S(1)}, u32[]{:S(2)}, u32[]{:S(2)}) collective-permute-start(bf16[3,2,2,8,8,128]{5,4,3,2,1,0:T(8,128)(2,1)S(1)} %pad_maximum_fusion.refs_4_), channel_id=1, source_target_pairs={{0,3},{1,0},{2,1},{3,2},{4,7},{5,4},{6,5},{7,6},{8,11},{9,8},{10,9... | collective-permute-start | bytes 589832 | tf_op jit(solution)/shard_map/ppermute | solution.py:327
  78.8 0.8 copy-start.7
  89.7 46.8 %copy-start.5 = (s32[1,16,2]{1,2,0:T(2,128)S(1)}, s32[1,16,2]{1,2,0:T(2,128)}, u32[]{:S(2)}) copy-start(s32[1,16,2]{1,2,0:T(2,128)} %param.9) | copy-start | bytes 388
  89.7 18.0 %collective-permute-start.10 = (bf16[3,2,2,8,8,128]{5,4,3,2,1,0:T(8,128)(2,1)S(1)}, bf16[3,2,2,8,8,128]{5,4,3,2,1,0:T(8,128)(2,1)S(1)}, u32[]{:S(2)}, u32[]{:S(2)}) collective-permute-start(bf16[3,2,2,8,8,128]{5,4,3,2,1,0:T(8,128)(2,1)S(1)} %get-tuple-element.48), channel_id=1, source_target_pairs={{0,2},{1,3},{2,0},{3,1},{4,6},{5,7},{6,4},{7,5},{8,10},{9,11},{10,... | collective-permute-start | bytes 589832 | tf_op jit(solution)/shard_map/ppermute | solution.py:327
  95.2 12.5 %collective-permute-start.11 = (bf16[3,2,2,8,8,128]{5,4,3,2,1,0:T(8,128)(2,1)S(1)}, bf16[3,2,2,8,8,128]{5,4,3,2,1,0:T(8,128)(2,1)S(1)}, u32[]{:S(2)}, u32[]{:S(2)}) collective-permute-start(bf16[3,2,2,8,8,128]{5,4,3,2,1,0:T(8,128)(2,1)S(1)} %get-tuple-element.49), channel_id=1, source_target_pairs={{0,1},{1,2},{2,3},{3,0},{4,5},{5,6},{6,7},{7,4},{8,9},{9,10},{10,1... | collective-permute-start | bytes 589832 | tf_op jit(solution)/shard_map/ppermute | solution.py:327
  98.2 12.6 %collective-permute-start.9 = (bf16[3,2,2,8,8,128]{5,4,3,2,1,0:T(8,128)(2,1)S(1)}, bf16[3,2,2,8,8,128]{5,4,3,2,1,0:T(8,128)(2,1)S(1)}, u32[]{:S(2)}, u32[]{:S(2)}) collective-permute-start(bf16[3,2,2,8,8,128]{5,4,3,2,1,0:T(8,128)(2,1)S(1)} %get-tuple-element.47), channel_id=1, source_target_pairs={{0,3},{1,0},{2,1},{3,2},{4,7},{5,4},{6,5},{7,6},{8,11},{9,8},{10,9... | collective-permute-start | bytes 589832 | tf_op jit(solution)/shard_map/ppermute | solution.py:327
  102.3 38.7 %all-to-all-start.2 = ((bf16[16,2,128,128]{3,2,1,0:T(8,128)(2,1)}), bf16[16,2,128,128]{3,2,1,0:T(8,128)(2,1)S(1)}, u32[]{:S(2)}, u32[]{:S(2)}) async-start(bf16[16,2,128,128]{3,2,1,0:T(8,128)(2,1)} %bitcast.17), calls=%async_computation.2 | async-start | bytes 2097152 | tf_op jit(solution)/shard_map/all_to_all | solution.py:387
  110.9 18.5 %collective-permute-start.15 = (bf16[2,2,2,8,8,128]{5,4,3,2,1,0:T(8,128)(2,1)S(1)}, bf16[2,2,2,8,8,128]{5,4,3,2,1,0:T(8,128)(2,1)S(1)}, u32[]{:S(2)}, u32[]{:S(2)}) collective-permute-start(bf16[2,2,2,8,8,128]{5,4,3,2,1,0:T(8,128)(2,1)S(1)} %add_convert_fusion), channel_id=1, source_target_pairs={{0,6},{1,7},{2,4},{3,5},{4,2},{5,3},{6,0},{7,1},{8,14},{9,15},{10,... | collective-permute-start | bytes 393224 | tf_op jit(solution)/shard_map/ppermute | solution.py:322
  122.2 14.4 %collective-permute-start.12 = (bf16[1,2,2,8,8,128]{5,4,3,2,1,0:T(8,128)(2,1)S(1)}, bf16[1,2,2,8,8,128]{5,4,3,2,1,0:T(8,128)(2,1)S(1)}, u32[]{:S(2)}, u32[]{:S(2)}) collective-permute-start(bf16[1,2,2,8,8,128]{5,4,3,2,1,0:T(8,128)(2,1)S(1)} %get-tuple-element.51), channel_id=1, source_target_pairs={{0,3},{1,0},{2,1},{3,2},{4,7},{5,4},{6,5},{7,6},{8,11},{9,8},{10,9... | collective-permute-start | bytes 196616 | tf_op jit(solution)/shard_map/ppermute | solution.py:327
  124.1 12.5 %collective-permute-start.13 = (bf16[1,2,2,8,8,128]{5,4,3,2,1,0:T(8,128)(2,1)S(1)}, bf16[1,2,2,8,8,128]{5,4,3,2,1,0:T(8,128)(2,1)S(1)}, u32[]{:S(2)}, u32[]{:S(2)}) collective-permute-start(bf16[1,2,2,8,8,128]{5,4,3,2,1,0:T(8,128)(2,1)S(1)} %get-tuple-element.52), channel_id=1, source_target_pairs={{0,2},{1,3},{2,0},{3,1},{4,6},{5,7},{6,4},{7,5},{8,10},{9,11},{10,... | collective-permute-start | bytes 196616 | tf_op jit(solution)/shard_map/ppermute | solution.py:327
  126.5 10.1 %collective-permute-start.14 = (bf16[1,2,2,8,8,128]{5,4,3,2,1,0:T(8,128)(2,1)S(1)}, bf16[1,2,2,8,8,128]{5,4,3,2,1,0:T(8,128)(2,1)S(1)}, u32[]{:S(2)}, u32[]{:S(2)}) collective-permute-start(bf16[1,2,2,8,8,128]{5,4,3,2,1,0:T(8,128)(2,1)S(1)} %get-tuple-element.53), channel_id=1, source_target_pairs={{0,1},{1,2},{2,3},{3,0},{4,5},{5,6},{6,7},{7,4},{8,9},{9,10},{10,1... | collective-permute-start | bytes 196616 | tf_op jit(solution)/shard_map/ppermute | solution.py:327
  129.5 11.5 %collective-permute-start.16 = (bf16[2,2,8,8,128]{4,3,2,1,0:T(8,128)(2,1)S(1)}, bf16[2,2,8,8,128]{4,3,2,1,0:T(8,128)(2,1)S(1)}, u32[]{:S(2)}, u32[]{:S(2)}) collective-permute-start(bf16[2,2,8,8,128]{4,3,2,1,0:T(8,128)(2,1)S(1)} %fusion), channel_id=1, source_target_pairs={{0,12},{1,13},{2,14},{3,15},{4,8},{5,9},{6,10},{7,11},{8,4},{9,5},... | collective-permute-start | bytes 196616 | tf_op jit(solution)/shard_map/ppermute | solution.py:322
  142.4 15.1 %all-to-all-start.3 = ((bf16[32,2,2,2,4,128]{5,4,3,2,1,0:T(4,128)(2,1)}), bf16[32,2,2,2,4,128]{5,4,3,2,1,0:T(4,128)(2,1)S(1)}, u32[]{:S(2)}, u32[]{:S(2)}) async-start(bf16[32,2,2,2,4,128]{5,4,3,2,1,0:T(4,128)(2,1)} %bitcast.21), calls=%async_computation.3 | async-start | bytes 524288 | tf_op jit(solution)/shard_map/all_to_all | solution.py:360

commit v17 on v16

--- a/solution.py
+++ b/solution.py
@@ -15,7 +15,7 @@
 LOG2E = 1.4426950408889634
 PLANE = ("dp", "xh")
 MIRROR = 12
-ACROSS = 6
+ACROSS = 7
 NEAR = 4
 
 

time: 160 us -> 160 us (level)
  starting transfers between devices: 102 us -> 106 us
  waiting for transfers between devices: 30.9 us -> 28.5 us
  Pallas kernels: 16.9 us -> 14.9 us
    all_to_all x2, starting transfers between devices: 16.6 us -> 20.9 us  [over_plane(): lax.all_to_all(values.reshape((2 * n_replicas,) + values.shape[2:]), PLAN...]
    ppermute x5, starting transfers between devices: 35.8 us -> 32 us  [far_swap(): lax.ppermute(values, 'z', [(place, place ^ flip) for place in range(16)])]
    all_to_all x1, starting transfers between devices: 5.38 us -> 8.03 us  [on_device(): lax.all_to_all(query_back.reshape(n_replicas, slot_cap, tile_rows, row_wi...]
    ppermute x12, waiting for transfers between devices: 15.1 us -> 13 us  [near_shift(): return lax.ppermute(values, 'z', pairs)]
    pallas_call x1, Pallas kernels: 10.1 us -> 8.05 us  [attention(): pl.pallas_call(attention_kernel, out_shape=(jax.ShapeDtypeStruct((slots,...]
where the time goes in v17:
time: 160 us; the launch traced here: 159 us
  starting transfers between devices  106 us (66%)
  waiting for transfers between devices  28.5 us (18%)
  Pallas kernels  14.9 us (9%)
  local copies, waits for them, and re-layouts  7.23 us (5%)
    ppermute x12, starting transfers between devices, near_shift(): return lax.ppermute(values, 'z', pairs)  41.3 us
    ppermute x5, starting transfers between devices, far_swap(): lax.ppermute(values, 'z', [(place, place ^ flip) for place in range(16)])  32 us
    all_to_all x2, starting transfers between devices, over_plane(): lax.all_to_all(values.reshape((2 * n_replicas,) + values.shape[2:]), PLAN...  20.9 us
    ppermute x12, waiting for transfers between devices, near_shift(): return lax.ppermute(values, 'z', pairs)  13 us
    all_to_all x2, waiting for transfers between devices, over_plane(): lax.all_to_all(values.reshape((2 * n_replicas,) + values.shape[2:]), PLAN...  11.4 us
    pallas_call x1, Pallas kernels, attention(): pl.pallas_call(attention_kernel, out_shape=(jax.ShapeDtypeStruct((slots,...  8.05 us
    all_to_all x1, starting transfers between devices, on_device(): lax.all_to_all(query_back.reshape(n_replicas, slot_cap, tile_rows, row_wi...  8.03 us
    unnamed x20, local copies, waits for them, and re-layouts  5.81 us
  transfers between devices with their start and end apart: 21, of which 7 were waited for; matrix products, arithmetic and copies ran while one was open for 1% of the time, Pallas kernels for 2%

profile of v17, /device:TPU:1, one launch (start us, length us, event | category | flops | bytes accessed | tf_op | source)
XLA Modules:
  0.0 158.5 jit_solution(10012246541853759379)
XLA Ops:
  2.2 1.4 kv_pack.1
  3.7 10.4 %all-to-all-start = ((bf16[32,2,2,2,4,128]{5,4,3,2,1,0:T(4,128)(2,1)}), bf16[32,2,2,2,4,128]{5,4,3,2,1,0:T(4,128)(2,1)S(1)}, u32[]{:S(2)}, u32[]{:S(2)}) async-start(bf16[32,2,2,2,4,128]{5,4,3,2,1,0:T(4,128)(2,1)} %bitcast.7), calls=%async_computation | async-start | bytes 524288 | tf_op jit(solution)/shard_map/all_to_all | solution.py:360
  16.8 2.2 %pack_rows.1 = bf16[32,2,128,128]{3,2,1,0:T(8,128)(2,1)} custom-call(s32[2,16]{1,0:T(2,128)S(1)} %bitcast.36, bf16[16,128,128]{2,1,0:T(8,128)(2,1)S(1)} %copy-done, bf16[16,128,128]{2,1,0:T(8,128)(2,1)S(1)} %copy-done.1), custom_call_target="tpu_custom_call" | custom-call | tf_op jit(solution)/shard_map/pack_rows/pallas_call | solution.py:38
  19.0 4.0 %all-to-all-done = bf16[32,2,2,2,4,128]{5,4,3,2,1,0:T(4,128)(2,1)S(1)} async-done(((bf16[32,2,2,2,4,128]{5,4,3,2,1,0:T(4,128)(2,1)}), bf16[32,2,2,2,4,128]{5,4,3,2,1,0:T(4,128)(2,1)S(1)}, u32[]{:S(2)}, u32[]{:S(2)}) %all-to-all-start) | async-done | bytes 262176 | tf_op jit(solution)/shard_map/all_to_all | solution.py:360
  23.0 4.1 %all-to-all-start.1 = ((bf16[16,2,2,128,128]{4,3,2,1,0:T(8,128)(2,1)}), bf16[16,2,2,128,128]{4,3,2,1,0:T(8,128)(2,1)S(1)}, u32[]{:S(2)}, u32[]{:S(2)}) async-start(bf16[16,2,2,128,128]{4,3,2,1,0:T(8,128)(2,1)} %bitcast.14), calls=%async_computation.1 | async-start | bytes 4194304 | tf_op jit(solution)/shard_map/all_to_all | solution.py:373
  27.7 11.0 %collective-permute-start.1 = (bf16[2,2,8,8,128]{4,3,2,1,0:T(8,128)(2,1)S(1)}, bf16[2,2,8,8,128]{4,3,2,1,0:T(8,128)(2,1)S(1)}, u32[]{:S(2)}, u32[]{:S(2)}) collective-permute-start(bf16[2,2,8,8,128]{4,3,2,1,0:T(8,128)(2,1)S(1)} %get-tuple-element.35), channel_id=1, source_target_pairs={{0,7},{1,6},{2,5},{3,4},{4,3},{5,2},{6,1},{7,0},{8,15},{9,14},{10,... | collective-permute-start | bytes 196616 | tf_op jit(solution)/shard_map/ppermute | solution.py:322
  38.7 3.9 %collective-permute-start.2 = (bf16[2,2,8,8,128]{4,3,2,1,0:T(8,128)(2,1)S(1)}, bf16[2,2,8,8,128]{4,3,2,1,0:T(8,128)(2,1)S(1)}, u32[]{:S(2)}, u32[]{:S(2)}) collective-permute-start(bf16[2,2,8,8,128]{4,3,2,1,0:T(8,128)(2,1)S(1)} %get-tuple-element.34), channel_id=1, source_target_pairs={{0,11},{1,10},{2,9},{3,8},{4,15},{5,14},{6,13},{7,12},{8,3},{9,2},... | collective-permute-start | bytes 196616 | tf_op jit(solution)/shard_map/ppermute | solution.py:322
  42.6 2.3 %collective-permute-start = (bf16[2,2,8,8,128]{4,3,2,1,0:T(8,128)(2,1)S(1)}, bf16[2,2,8,8,128]{4,3,2,1,0:T(8,128)(2,1)S(1)}, u32[]{:S(2)}, u32[]{:S(2)}) collective-permute-start(bf16[2,2,8,8,128]{4,3,2,1,0:T(8,128)(2,1)S(1)} %get-tuple-element.34), channel_id=1, source_target_pairs={{0,12},{1,13},{2,14},{3,15},{4,8},{5,9},{6,10},{7,11},{8,4},{9,5},... | collective-permute-start | bytes 196616 | tf_op jit(solution)/shard_map/ppermute | solution.py:322
  44.9 4.0 %collective-permute-start.3 = (bf16[1,2,2,8,8,128]{5,4,3,2,1,0:T(8,128)(2,1)S(1)}, bf16[1,2,2,8,8,128]{5,4,3,2,1,0:T(8,128)(2,1)S(1)}, u32[]{:S(2)}, u32[]{:S(2)}) collective-permute-start(bf16[1,2,2,8,8,128]{5,4,3,2,1,0:T(8,128)(2,1)S(1)} %bitcast.38), channel_id=1, source_target_pairs={{0,1},{1,2},{2,3},{3,0},{4,5},{5,6},{6,7},{7,4},{8,9},{9,10},{10,1... | collective-permute-start | bytes 196616 | tf_op jit(solution)/shard_map/ppermute | solution.py:327
  49.0 4.0 %collective-permute-start.4 = (bf16[1,2,2,8,8,128]{5,4,3,2,1,0:T(8,128)(2,1)S(1)}, bf16[1,2,2,8,8,128]{5,4,3,2,1,0:T(8,128)(2,1)S(1)}, u32[]{:S(2)}, u32[]{:S(2)}) collective-permute-start(bf16[1,2,2,8,8,128]{5,4,3,2,1,0:T(8,128)(2,1)S(1)} %bitcast.39), channel_id=1, source_target_pairs={{0,2},{1,3},{2,0},{3,1},{4,6},{5,7},{6,4},{7,5},{8,10},{9,11},{10,... | collective-permute-start | bytes 196616 | tf_op jit(solution)/shard_map/ppermute | solution.py:327
  53.0 3.5 %collective-permute-start.5 = (bf16[1,2,2,8,8,128]{5,4,3,2,1,0:T(8,128)(2,1)S(1)}, bf16[1,2,2,8,8,128]{5,4,3,2,1,0:T(8,128)(2,1)S(1)}, u32[]{:S(2)}, u32[]{:S(2)}) collective-permute-start(bf16[1,2,2,8,8,128]{5,4,3,2,1,0:T(8,128)(2,1)S(1)} %bitcast.40), channel_id=1, source_target_pairs={{0,3},{1,0},{2,1},{3,2},{4,7},{5,4},{6,5},{7,6},{8,11},{9,8},{10,9... | collective-permute-start | bytes 196616 | tf_op jit(solution)/shard_map/ppermute | solution.py:327
  56.6 2.3 %collective-permute-done.4.refs_2_ = bf16[1,2,2,8,8,128]{5,4,3,2,1,0:T(8,128)(2,1)S(1)} collective-permute-done((bf16[1,2,2,8,8,128]{5,4,3,2,1,0:T(8,128)(2,1)S(1)}, bf16[1,2,2,8,8,128]{5,4,3,2,1,0:T(8,128)(2,1)S(1)}, u32[]{:S(2)}, u32[]{:S(2)}) %collective-permute-start.4) | collective-permute-done | bytes 65568 | tf_op jit(solution)/shard_map/ppermute | solution.py:327
  59.8 3.3 %collective-permute-start.6 = (bf16[3,2,2,8,8,128]{5,4,3,2,1,0:T(8,128)(2,1)S(1)}, bf16[3,2,2,8,8,128]{5,4,3,2,1,0:T(8,128)(2,1)S(1)}, u32[]{:S(2)}, u32[]{:S(2)}) collective-permute-start(bf16[3,2,2,8,8,128]{5,4,3,2,1,0:T(8,128)(2,1)S(1)} %pad_maximum_fusion.refs_4_), channel_id=1, source_target_pairs={{0,1},{1,2},{2,3},{3,0},{4,5},{5,6},{6,7},{7,4},{8,9},{9,10},{10,1... | collective-permute-start | bytes 589832 | tf_op jit(solution)/shard_map/ppermute | solution.py:327
  63.1 3.8 %collective-permute-start.7 = (bf16[3,2,2,8,8,128]{5,4,3,2,1,0:T(8,128)(2,1)S(1)}, bf16[3,2,2,8,8,128]{5,4,3,2,1,0:T(8,128)(2,1)S(1)}, u32[]{:S(2)}, u32[]{:S(2)}) collective-permute-start(bf16[3,2,2,8,8,128]{5,4,3,2,1,0:T(8,128)(2,1)S(1)} %pad_maximum_fusion.refs_4_), channel_id=1, source_target_pairs={{0,2},{1,3},{2,0},{3,1},{4,6},{5,7},{6,4},{7,5},{8,10},{9,11},{10,... | collective-permute-start | bytes 589832 | tf_op jit(solution)/shard_map/ppermute | solution.py:327
  67.0 2.1 %collective-permute-start.8 = (bf16[3,2,2,8,8,128]{5,4,3,2,1,0:T(8,128)(2,1)S(1)}, bf16[3,2,2,8,8,128]{5,4,3,2,1,0:T(8,128)(2,1)S(1)}, u32[]{:S(2)}, u32[]{:S(2)}) collective-permute-start(bf16[3,2,2,8,8,128]{5,4,3,2,1,0:T(8,128)(2,1)S(1)} %pad_maximum_fusion.refs_4_), channel_id=1, source_target_pairs={{0,3},{1,0},{2,1},{3,2},{4,7},{5,4},{6,5},{7,6},{8,11},{9,8},{10,9... | collective-permute-start | bytes 589832 | tf_op jit(solution)/shard_map/ppermute | solution.py:327
  69.3 9.5 %collective-permute-done.7.refs_6_ = bf16[3,2,2,8,8,128]{5,4,3,2,1,0:T(8,128)(2,1)S(1)} collective-permute-done((bf16[3,2,2,8,8,128]{5,4,3,2,1,0:T(8,128)(2,1)S(1)}, bf16[3,2,2,8,8,128]{5,4,3,2,1,0:T(8,128)(2,1)S(1)}, u32[]{:S(2)}, u32[]{:S(2)}) %collective-permute-start.7) | collective-permute-done | bytes 196640 | tf_op jit(solution)/shard_map/ppermute | solution.py:327
  79.6 8.0 %attention_backward.1 = (bf16[32,128,128]{2,1,0:T(8,128)(2,1)}, bf16[1,2,2,8,8,128]{5,4,3,2,1,0:T(8,128)(2,1)S(1)}, bf16[1,2,2,8,8,128]{5,4,3,2,1,0:T(8,128)(2,1...) custom-call(s32[16]{0:T(128)S(1)} %dynamic-slice_bitcast_fusion.recv, ...), custom_call_target="tpu_custom_call" | custom-call | flops 2000000000 | bytes 6291456 | tf_op jit(solution)/shard_map/attention_backward/pallas_call | solution.py:216
  87.7 5.5 %collective-permute-start.10 = (bf16[3,2,2,8,8,128]{5,4,3,2,1,0:T(8,128)(2,1)S(1)}, bf16[3,2,2,8,8,128]{5,4,3,2,1,0:T(8,128)(2,1)S(1)}, u32[]{:S(2)}, u32[]{:S(2)}) collective-permute-start(bf16[3,2,2,8,8,128]{5,4,3,2,1,0:T(8,128)(2,1)S(1)} %get-tuple-element.48), channel_id=1, source_target_pairs={{0,2},{1,3},{2,0},{3,1},{4,6},{5,7},{6,4},{7,5},{8,10},{9,11},{10,... | collective-permute-start | bytes 589832 | tf_op jit(solution)/shard_map/ppermute | solution.py:327
  93.2 2.9 %collective-permute-start.11 = (bf16[3,2,2,8,8,128]{5,4,3,2,1,0:T(8,128)(2,1)S(1)}, bf16[3,2,2,8,8,128]{5,4,3,2,1,0:T(8,128)(2,1)S(1)}, u32[]{:S(2)}, u32[]{:S(2)}) collective-permute-start(bf16[3,2,2,8,8,128]{5,4,3,2,1,0:T(8,128)(2,1)S(1)} %get-tuple-element.49), channel_id=1, source_target_pairs={{0,1},{1,2},{2,3},{3,0},{4,5},{5,6},{6,7},{7,4},{8,9},{9,10},{10,1... | collective-permute-start | bytes 589832 | tf_op jit(solution)/shard_map/ppermute | solution.py:327
  96.1 4.2 %collective-permute-start.9 = (bf16[3,2,2,8,8,128]{5,4,3,2,1,0:T(8,128)(2,1)S(1)}, bf16[3,2,2,8,8,128]{5,4,3,2,1,0:T(8,128)(2,1)S(1)}, u32[]{:S(2)}, u32[]{:S(2)}) collective-permute-start(bf16[3,2,2,8,8,128]{5,4,3,2,1,0:T(8,128)(2,1)S(1)} %get-tuple-element.47), channel_id=1, source_target_pairs={{0,3},{1,0},{2,1},{3,2},{4,7},{5,4},{6,5},{7,6},{8,11},{9,8},{10,9... | collective-permute-start | bytes 589832 | tf_op jit(solution)/shard_map/ppermute | solution.py:327
  100.3 8.0 %all-to-all-start.2 = ((bf16[16,2,128,128]{3,2,1,0:T(8,128)(2,1)}), bf16[16,2,128,128]{3,2,1,0:T(8,128)(2,1)S(1)}, u32[]{:S(2)}, u32[]{:S(2)}) async-start(bf16[16,2,128,128]{3,2,1,0:T(8,128)(2,1)} %bitcast.17), calls=%async_computation.2 | async-start | bytes 2097152 | tf_op jit(solution)/shard_map/all_to_all | solution.py:387
  109.3 10.0 %collective-permute-start.15 = (bf16[2,2,2,8,8,128]{5,4,3,2,1,0:T(8,128)(2,1)S(1)}, bf16[2,2,2,8,8,128]{5,4,3,2,1,0:T(8,128)(2,1)S(1)}, u32[]{:S(2)}, u32[]{:S(2)}) collective-permute-start(bf16[2,2,2,8,8,128]{5,4,3,2,1,0:T(8,128)(2,1)S(1)} %add_convert_fusion), channel_id=1, source_target_pairs={{0,7},{1,6},{2,5},{3,4},{4,3},{5,2},{6,1},{7,0},{8,15},{9,14},{10,... | collective-permute-start | bytes 393224 | tf_op jit(solution)/shard_map/ppermute | solution.py:322
  119.4 1.9 %collective-permute-start.12 = (bf16[1,2,2,8,8,128]{5,4,3,2,1,0:T(8,128)(2,1)S(1)}, bf16[1,2,2,8,8,128]{5,4,3,2,1,0:T(8,128)(2,1)S(1)}, u32[]{:S(2)}, u32[]{:S(2)}) collective-permute-start(bf16[1,2,2,8,8,128]{5,4,3,2,1,0:T(8,128)(2,1)S(1)} %get-tuple-element.51), channel_id=1, source_target_pairs={{0,3},{1,0},{2,1},{3,2},{4,7},{5,4},{6,5},{7,6},{8,11},{9,8},{10,9... | collective-permute-start | bytes 196616 | tf_op jit(solution)/shard_map/ppermute | solution.py:327
  121.4 4.1 %collective-permute-start.13 = (bf16[1,2,2,8,8,128]{5,4,3,2,1,0:T(8,128)(2,1)S(1)}, bf16[1,2,2,8,8,128]{5,4,3,2,1,0:T(8,128)(2,1)S(1)}, u32[]{:S(2)}, u32[]{:S(2)}) collective-permute-start(bf16[1,2,2,8,8,128]{5,4,3,2,1,0:T(8,128)(2,1)S(1)} %get-tuple-element.52), channel_id=1, source_target_pairs={{0,2},{1,3},{2,0},{3,1},{4,6},{5,7},{6,4},{7,5},{8,10},{9,11},{10,... | collective-permute-start | bytes 196616 | tf_op jit(solution)/shard_map/ppermute | solution.py:327
  125.5 1.9 %collective-permute-start.14 = (bf16[1,2,2,8,8,128]{5,4,3,2,1,0:T(8,128)(2,1)S(1)}, bf16[1,2,2,8,8,128]{5,4,3,2,1,0:T(8,128)(2,1)S(1)}, u32[]{:S(2)}, u32[]{:S(2)}) collective-permute-start(bf16[1,2,2,8,8,128]{5,4,3,2,1,0:T(8,128)(2,1)S(1)} %get-tuple-element.53), channel_id=1, source_target_pairs={{0,1},{1,2},{2,3},{3,0},{4,5},{5,6},{6,7},{7,4},{8,9},{9,10},{10,1... | collective-permute-start | bytes 196616 | tf_op jit(solution)/shard_map/ppermute | solution.py:327
  127.5 4.8 %collective-permute-start.16 = (bf16[2,2,8,8,128]{4,3,2,1,0:T(8,128)(2,1)S(1)}, bf16[2,2,8,8,128]{4,3,2,1,0:T(8,128)(2,1)S(1)}, u32[]{:S(2)}, u32[]{:S(2)}) collective-permute-start(bf16[2,2,8,8,128]{4,3,2,1,0:T(8,128)(2,1)S(1)} %fusion), channel_id=1, source_target_pairs={{0,12},{1,13},{2,14},{3,15},{4,8},{5,9},{6,10},{7,11},{8,4},{9,5},... | collective-permute-start | bytes 196616 | tf_op jit(solution)/shard_map/ppermute | solution.py:322
  132.4 4.1 %collective-permute-done.16.refs_5_ = bf16[2,2,8,8,128]{4,3,2,1,0:T(8,128)(2,1)S(1)} collective-permute-done((bf16[2,2,8,8,128]{4,3,2,1,0:T(8,128)(2,1)S(1)}, bf16[2,2,8,8,128]{4,3,2,1,0:T(8,128)(2,1)S(1)}, u32[]{:S(2)}, u32[]{:S(2)}) %collective-permute-start.16) | collective-permute-done | bytes 65568 | tf_op jit(solution)/shard_map/ppermute | solution.py:322
  136.6 1.4 kv_back.1
  137.9 10.5 %all-to-all-start.3 = ((bf16[32,2,2,2,4,128]{5,4,3,2,1,0:T(4,128)(2,1)}), bf16[32,2,2,2,4,128]{5,4,3,2,1,0:T(4,128)(2,1)S(1)}, u32[]{:S(2)}, u32[]{:S(2)}) async-start(bf16[32,2,2,2,4,128]{5,4,3,2,1,0:T(4,128)(2,1)} %bitcast.21), calls=%async_computation.3 | async-start | bytes 524288 | tf_op jit(solution)/shard_map/all_to_all | solution.py:360
  148.4 1.4 gather_fusion
  149.8 7.4 %all-to-all-done.3 = bf16[32,2,2,2,4,128]{5,4,3,2,1,0:T(4,128)(2,1)S(1)} async-done(((bf16[32,2,2,2,4,128]{5,4,3,2,1,0:T(4,128)(2,1)}), bf16[32,2,2,2,4,128]{5,4,3,2,1,0:T(4,128)(2,1)S(1)}, u32[]{:S(2)}, u32[]{:S(2)}) %all-to-all-start.3) | async-done | bytes 262176 | tf_op jit(solution)/shard_map/all_to_all | solution.py:360
  157.3 1.3 kv_final.1
  (48 shorter events, 8.2 us)
Async XLA Ops:
  0.6 0.9 copy-start.2
  1.5 0.7 copy-start.3
  3.7 19.3 %all-to-all-start = ((bf16[32,2,2,2,4,128]{5,4,3,2,1,0:T(4,128)(2,1)}), bf16[32,2,2,2,4,128]{5,4,3,2,1,0:T(4,128)(2,1)S(1)}, u32[]{:S(2)}, u32[]{:S(2)}) async-start(bf16[32,2,2,2,4,128]{5,4,3,2,1,0:T(4,128)(2,1)} %bitcast.7), calls=%async_computation | async-start | bytes 524288 | tf_op jit(solution)/shard_map/all_to_all | solution.py:360
  14.1 1.0 copy-start
  15.1 1.0 copy-start.1
  16.2 0.7 copy-start.4
  23.0 4.1 %copy-start.8 = (s32[16,16]{1,0:T(8,128)S(1)}, s32[16,16]{1,0:T(8,128)}, u32[]{:S(2)}) copy-start(s32[16,16]{1,0:T(8,128)} %param.10) | copy-start | bytes 3076
  23.0 46.1 %copy-start.9 = (s32[1,16]{1,0:T(1,128)S(1)}, s32[1,16]{1,0:T(1,128)}, u32[]{:S(2)}) copy-start(s32[1,16]{1,0:T(1,128)} %param.11) | copy-start | bytes 196
  23.0 36.8 %all-to-all-start.1 = ((bf16[16,2,2,128,128]{4,3,2,1,0:T(8,128)(2,1)}), bf16[16,2,2,128,128]{4,3,2,1,0:T(8,128)(2,1)S(1)}, u32[]{:S(2)}, u32[]{:S(2)}) async-start(bf16[16,2,2,128,128]{4,3,2,1,0:T(8,128)(2,1)} %bitcast.14), calls=%async_computation.1 | async-start | bytes 4194304 | tf_op jit(solution)/shard_map/all_to_all | solution.py:373
  27.7 25.3 %collective-permute-start.1 = (bf16[2,2,8,8,128]{4,3,2,1,0:T(8,128)(2,1)S(1)}, bf16[2,2,8,8,128]{4,3,2,1,0:T(8,128)(2,1)S(1)}, u32[]{:S(2)}, u32[]{:S(2)}) collective-permute-start(bf16[2,2,8,8,128]{4,3,2,1,0:T(8,128)(2,1)S(1)} %get-tuple-element.35), channel_id=1, source_target_pairs={{0,7},{1,6},{2,5},{3,4},{4,3},{5,2},{6,1},{7,0},{8,15},{9,14},{10,... | collective-permute-start | bytes 196616 | tf_op jit(solution)/shard_map/ppermute | solution.py:322
  38.7 17.8 %collective-permute-start.2 = (bf16[2,2,8,8,128]{4,3,2,1,0:T(8,128)(2,1)S(1)}, bf16[2,2,8,8,128]{4,3,2,1,0:T(8,128)(2,1)S(1)}, u32[]{:S(2)}, u32[]{:S(2)}) collective-permute-start(bf16[2,2,8,8,128]{4,3,2,1,0:T(8,128)(2,1)S(1)} %get-tuple-element.34), channel_id=1, source_target_pairs={{0,11},{1,10},{2,9},{3,8},{4,15},{5,14},{6,13},{7,12},{8,3},{9,2},... | collective-permute-start | bytes 196616 | tf_op jit(solution)/shard_map/ppermute | solution.py:322
  42.6 14.0 %collective-permute-start = (bf16[2,2,8,8,128]{4,3,2,1,0:T(8,128)(2,1)S(1)}, bf16[2,2,8,8,128]{4,3,2,1,0:T(8,128)(2,1)S(1)}, u32[]{:S(2)}, u32[]{:S(2)}) collective-permute-start(bf16[2,2,8,8,128]{4,3,2,1,0:T(8,128)(2,1)S(1)} %get-tuple-element.34), channel_id=1, source_target_pairs={{0,12},{1,13},{2,14},{3,15},{4,8},{5,9},{6,10},{7,11},{8,4},{9,5},... | collective-permute-start | bytes 196616 | tf_op jit(solution)/shard_map/ppermute | solution.py:322
  44.9 11.6 %collective-permute-start.3 = (bf16[1,2,2,8,8,128]{5,4,3,2,1,0:T(8,128)(2,1)S(1)}, bf16[1,2,2,8,8,128]{5,4,3,2,1,0:T(8,128)(2,1)S(1)}, u32[]{:S(2)}, u32[]{:S(2)}) collective-permute-start(bf16[1,2,2,8,8,128]{5,4,3,2,1,0:T(8,128)(2,1)S(1)} %bitcast.38), channel_id=1, source_target_pairs={{0,1},{1,2},{2,3},{3,0},{4,5},{5,6},{6,7},{7,4},{8,9},{9,10},{10,1... | collective-permute-start | bytes 196616 | tf_op jit(solution)/shard_map/ppermute | solution.py:327
  49.0 10.0 %collective-permute-start.4 = (bf16[1,2,2,8,8,128]{5,4,3,2,1,0:T(8,128)(2,1)S(1)}, bf16[1,2,2,8,8,128]{5,4,3,2,1,0:T(8,128)(2,1)S(1)}, u32[]{:S(2)}, u32[]{:S(2)}) collective-permute-start(bf16[1,2,2,8,8,128]{5,4,3,2,1,0:T(8,128)(2,1)S(1)} %bitcast.39), channel_id=1, source_target_pairs={{0,2},{1,3},{2,0},{3,1},{4,6},{5,7},{6,4},{7,5},{8,10},{9,11},{10,... | collective-permute-start | bytes 196616 | tf_op jit(solution)/shard_map/ppermute | solution.py:327
  53.0 6.2 %collective-permute-start.5 = (bf16[1,2,2,8,8,128]{5,4,3,2,1,0:T(8,128)(2,1)S(1)}, bf16[1,2,2,8,8,128]{5,4,3,2,1,0:T(8,128)(2,1)S(1)}, u32[]{:S(2)}, u32[]{:S(2)}) collective-permute-start(bf16[1,2,2,8,8,128]{5,4,3,2,1,0:T(8,128)(2,1)S(1)} %bitcast.40), channel_id=1, source_target_pairs={{0,3},{1,0},{2,1},{3,2},{4,7},{5,4},{6,5},{7,6},{8,11},{9,8},{10,9... | collective-permute-start | bytes 196616 | tf_op jit(solution)/shard_map/ppermute | solution.py:327
  59.2 0.6 copy-start.6
  59.8 9.4 %collective-permute-start.6 = (bf16[3,2,2,8,8,128]{5,4,3,2,1,0:T(8,128)(2,1)S(1)}, bf16[3,2,2,8,8,128]{5,4,3,2,1,0:T(8,128)(2,1)S(1)}, u32[]{:S(2)}, u32[]{:S(2)}) collective-permute-start(bf16[3,2,2,8,8,128]{5,4,3,2,1,0:T(8,128)(2,1)S(1)} %pad_maximum_fusion.refs_4_), channel_id=1, source_target_pairs={{0,1},{1,2},{2,3},{3,0},{4,5},{5,6},{6,7},{7,4},{8,9},{9,10},{10,1... | collective-permute-start | bytes 589832 | tf_op jit(solution)/shard_map/ppermute | solution.py:327
  63.1 15.6 %collective-permute-start.7 = (bf16[3,2,2,8,8,128]{5,4,3,2,1,0:T(8,128)(2,1)S(1)}, bf16[3,2,2,8,8,128]{5,4,3,2,1,0:T(8,128)(2,1)S(1)}, u32[]{:S(2)}, u32[]{:S(2)}) collective-permute-start(bf16[3,2,2,8,8,128]{5,4,3,2,1,0:T(8,128)(2,1)S(1)} %pad_maximum_fusion.refs_4_), channel_id=1, source_target_pairs={{0,2},{1,3},{2,0},{3,1},{4,6},{5,7},{6,4},{7,5},{8,10},{9,11},{10,... | collective-permute-start | bytes 589832 | tf_op jit(solution)/shard_map/ppermute | solution.py:327
  67.0 11.8 %collective-permute-start.8 = (bf16[3,2,2,8,8,128]{5,4,3,2,1,0:T(8,128)(2,1)S(1)}, bf16[3,2,2,8,8,128]{5,4,3,2,1,0:T(8,128)(2,1)S(1)}, u32[]{:S(2)}, u32[]{:S(2)}) collective-permute-start(bf16[3,2,2,8,8,128]{5,4,3,2,1,0:T(8,128)(2,1)S(1)} %pad_maximum_fusion.refs_4_), channel_id=1, source_target_pairs={{0,3},{1,0},{2,1},{3,2},{4,7},{5,4},{6,5},{7,6},{8,11},{9,8},{10,9... | collective-permute-start | bytes 589832 | tf_op jit(solution)/shard_map/ppermute | solution.py:327
  78.8 0.8 copy-start.7
  87.7 44.6 %copy-start.5 = (s32[1,16,2]{1,2,0:T(2,128)S(1)}, s32[1,16,2]{1,2,0:T(2,128)}, u32[]{:S(2)}) copy-start(s32[1,16,2]{1,2,0:T(2,128)} %param.9) | copy-start | bytes 388
  87.7 20.7 %collective-permute-start.10 = (bf16[3,2,2,8,8,128]{5,4,3,2,1,0:T(8,128)(2,1)S(1)}, bf16[3,2,2,8,8,128]{5,4,3,2,1,0:T(8,128)(2,1)S(1)}, u32[]{:S(2)}, u32[]{:S(2)}) collective-permute-start(bf16[3,2,2,8,8,128]{5,4,3,2,1,0:T(8,128)(2,1)S(1)} %get-tuple-element.48), channel_id=1, source_target_pairs={{0,2},{1,3},{2,0},{3,1},{4,6},{5,7},{6,4},{7,5},{8,10},{9,11},{10,... | collective-permute-start | bytes 589832 | tf_op jit(solution)/shard_map/ppermute | solution.py:327
  93.2 15.1 %collective-permute-start.11 = (bf16[3,2,2,8,8,128]{5,4,3,2,1,0:T(8,128)(2,1)S(1)}, bf16[3,2,2,8,8,128]{5,4,3,2,1,0:T(8,128)(2,1)S(1)}, u32[]{:S(2)}, u32[]{:S(2)}) collective-permute-start(bf16[3,2,2,8,8,128]{5,4,3,2,1,0:T(8,128)(2,1)S(1)} %get-tuple-element.49), channel_id=1, source_target_pairs={{0,1},{1,2},{2,3},{3,0},{4,5},{5,6},{6,7},{7,4},{8,9},{9,10},{10,1... | collective-permute-start | bytes 589832 | tf_op jit(solution)/shard_map/ppermute | solution.py:327
  96.1 13.1 %collective-permute-start.9 = (bf16[3,2,2,8,8,128]{5,4,3,2,1,0:T(8,128)(2,1)S(1)}, bf16[3,2,2,8,8,128]{5,4,3,2,1,0:T(8,128)(2,1)S(1)}, u32[]{:S(2)}, u32[]{:S(2)}) collective-permute-start(bf16[3,2,2,8,8,128]{5,4,3,2,1,0:T(8,128)(2,1)S(1)} %get-tuple-element.47), channel_id=1, source_target_pairs={{0,3},{1,0},{2,1},{3,2},{4,7},{5,4},{6,5},{7,6},{8,11},{9,8},{10,9... | collective-permute-start | bytes 589832 | tf_op jit(solution)/shard_map/ppermute | solution.py:327
  100.3 36.2 %all-to-all-start.2 = ((bf16[16,2,128,128]{3,2,1,0:T(8,128)(2,1)}), bf16[16,2,128,128]{3,2,1,0:T(8,128)(2,1)S(1)}, u32[]{:S(2)}, u32[]{:S(2)}) async-start(bf16[16,2,128,128]{3,2,1,0:T(8,128)(2,1)} %bitcast.17), calls=%async_computation.2 | async-start | bytes 2097152 | tf_op jit(solution)/shard_map/all_to_all | solution.py:387
  109.3 18.1 %collective-permute-start.15 = (bf16[2,2,2,8,8,128]{5,4,3,2,1,0:T(8,128)(2,1)S(1)}, bf16[2,2,2,8,8,128]{5,4,3,2,1,0:T(8,128)(2,1)S(1)}, u32[]{:S(2)}, u32[]{:S(2)}) collective-permute-start(bf16[2,2,2,8,8,128]{5,4,3,2,1,0:T(8,128)(2,1)S(1)} %add_convert_fusion), channel_id=1, source_target_pairs={{0,7},{1,6},{2,5},{3,4},{4,3},{5,2},{6,1},{7,0},{8,15},{9,14},{10,... | collective-permute-start | bytes 393224 | tf_op jit(solution)/shard_map/ppermute | solution.py:322
  119.4 13.0 %collective-permute-start.12 = (bf16[1,2,2,8,8,128]{5,4,3,2,1,0:T(8,128)(2,1)S(1)}, bf16[1,2,2,8,8,128]{5,4,3,2,1,0:T(8,128)(2,1)S(1)}, u32[]{:S(2)}, u32[]{:S(2)}) collective-permute-start(bf16[1,2,2,8,8,128]{5,4,3,2,1,0:T(8,128)(2,1)S(1)} %get-tuple-element.51), channel_id=1, source_target_pairs={{0,3},{1,0},{2,1},{3,2},{4,7},{5,4},{6,5},{7,6},{8,11},{9,8},{10,9... | collective-permute-start | bytes 196616 | tf_op jit(solution)/shard_map/ppermute | solution.py:327
  121.4 11.1 %collective-permute-start.13 = (bf16[1,2,2,8,8,128]{5,4,3,2,1,0:T(8,128)(2,1)S(1)}, bf16[1,2,2,8,8,128]{5,4,3,2,1,0:T(8,128)(2,1)S(1)}, u32[]{:S(2)}, u32[]{:S(2)}) collective-permute-start(bf16[1,2,2,8,8,128]{5,4,3,2,1,0:T(8,128)(2,1)S(1)} %get-tuple-element.52), channel_id=1, source_target_pairs={{0,2},{1,3},{2,0},{3,1},{4,6},{5,7},{6,4},{7,5},{8,10},{9,11},{10,... | collective-permute-start | bytes 196616 | tf_op jit(solution)/shard_map/ppermute | solution.py:327
  125.5 7.0 %collective-permute-start.14 = (bf16[1,2,2,8,8,128]{5,4,3,2,1,0:T(8,128)(2,1)S(1)}, bf16[1,2,2,8,8,128]{5,4,3,2,1,0:T(8,128)(2,1)S(1)}, u32[]{:S(2)}, u32[]{:S(2)}) collective-permute-start(bf16[1,2,2,8,8,128]{5,4,3,2,1,0:T(8,128)(2,1)S(1)} %get-tuple-element.53), channel_id=1, source_target_pairs={{0,1},{1,2},{2,3},{3,0},{4,5},{5,6},{6,7},{7,4},{8,9},{9,10},{10,1... | collective-permute-start | bytes 196616 | tf_op jit(solution)/shard_map/ppermute | solution.py:327
  127.5 9.1 %collective-permute-start.16 = (bf16[2,2,8,8,128]{4,3,2,1,0:T(8,128)(2,1)S(1)}, bf16[2,2,8,8,128]{4,3,2,1,0:T(8,128)(2,1)S(1)}, u32[]{:S(2)}, u32[]{:S(2)}) collective-permute-start(bf16[2,2,8,8,128]{4,3,2,1,0:T(8,128)(2,1)S(1)} %fusion), channel_id=1, source_target_pairs={{0,12},{1,13},{2,14},{3,15},{4,8},{5,9},{6,10},{7,11},{8,4},{9,5},... | collective-permute-start | bytes 196616 | tf_op jit(solution)/shard_map/ppermute | solution.py:322
  137.9 19.4 %all-to-all-start.3 = ((bf16[32,2,2,2,4,128]{5,4,3,2,1,0:T(4,128)(2,1)}), bf16[32,2,2,2,4,128]{5,4,3,2,1,0:T(4,128)(2,1)S(1)}, u32[]{:S(2)}, u32[]{:S(2)}) async-start(bf16[32,2,2,2,4,128]{5,4,3,2,1,0:T(4,128)(2,1)} %bitcast.21), calls=%async_computation.3 | async-start | bytes 524288 | tf_op jit(solution)/shard_map/all_to_all | solution.py:360
